TPU v7x, 32 devices: a whole 2x2x4 slice. The times are simulated.
32 devices in a mesh: grp: 2 (over core), dev: 16 (over z, y, x).
Axes of the slice: x: 2, y: 2, z: 4, core: 2. Of those that a mesh axis runs over, the one named last changes fastest.
Arguments:
- features: bfloat16 [2, 256, 128, 256], P('grp', 'dev'), may hold values from -6 to 6
- offsets: float32 [2, 256, 3, 128], P('grp', 'dev'), may hold values from 0 to 1
- radial: bfloat16 [2, 256, 8, 128, 128], P('grp', 'dev'), may hold values from -0.25 to 0.25
- neighbours: int32 [2, 256, 8], P('grp', 'dev'), may hold values from 0 to 8, as said below
- counts: int32 [2, 256], P('grp', 'dev'), may hold values from 16 to 128
- wavevectors: int32 [3, 1024], replicated, may hold values from -8 to 8
- w_msg: bfloat16 [256, 256], replicated, may hold values from -0.375 to 0.375
- w_mix: bfloat16 [256, 256], replicated, may hold values from -0.375 to 0.375
Outputs:
- updated: bfloat16 [2, 256, 128, 256], P('grp', 'dev')
Inputs may be any that keep to these rules, and one draw needn't show every extreme that they name: `neighbours`: A cell's 8 codes are distinct; code c names the cell at (c // 3 - 1) slabs and (c % 3 - 1) cells away along the slab.
All inputs are finite; a program needn't handle non-finite values.
Results may differ from a plain program's by a relative error of at most 0.018.
Values may be sent and summed in bfloat16 or wider, within the bound.
No kernel may reach another device: no remote copies, remote signals or barrier semaphores. Data moves between devices by JAX's collectives and lax.ppermute only.
A program may use at most 128 MiB of HBM per device.

v0:
```python
import math

import jax
import jax.numpy as jnp
from jax import lax
from jax.sharding import PartitionSpec as P


def extended(array, sides, width):
    for axis, dim in sides:
        devices, length = (lax.axis_size(axis), array.shape[dim])
        up = [(i, (i + 1) % devices) for i in range(devices - 1)]
        down = [(j, i) for i, j in up]
        last = lax.slice_in_dim(array, length - width, length, axis=dim)
        first = lax.slice_in_dim(array, 0, width, axis=dim)
        before = lax.ppermute(last, axis, up)
        after = lax.ppermute(first, axis, down)
        array = jnp.concatenate([before, array, after], axis=dim)
    return array


def wave_kernel(wavevectors):
    waves = wavevectors.astype(jnp.float32)
    square = jnp.sum(waves * waves, axis=0)
    kernel = jnp.exp(-square / 128.0) / (1.0 + square / 64.0)
    return jnp.concatenate([kernel, kernel])


def body(features, offsets, radial, neighbours, counts, wavevectors, w_msg, w_mix):
    cells_here = features.shape[1]
    atom_slots = features.shape[2]
    channels = features.shape[3]
    wave_count = wavevectors.shape[1]
    dev_count = lax.axis_size("dev")
    cell_line = cells_here * dev_count
    total_slots = lax.axis_size("grp") * cell_line * atom_slots
    slot_ids = jnp.arange(atom_slots, dtype=jnp.int32)
    masking = (slot_ids[None, None, :] < counts[:, :, None]).astype(jnp.bfloat16)
    masked = features * masking[..., None]
    window = extended(masked, (("grp", 0), ("dev", 1)), 1)
    flat_window = window.reshape(3 * (cells_here + 2), atom_slots, channels)
    codes = neighbours[0]
    local_ids = jnp.arange(cells_here, dtype=jnp.int32)
    gathered = jnp.zeros((cells_here, atom_slots, channels), jnp.float32)
    for neighbour in range(neighbours.shape[2]):
        code = codes[:, neighbour]
        rows_taken = code // 3 * (cells_here + 2) + local_ids + code % 3
        picked = flat_window[rows_taken]
        gathered = gathered + jnp.einsum(
            "kab,kbc->kac", radial[0, :, neighbour], picked, preferred_element_type=jnp.float32
        )
    waves = wavevectors.astype(jnp.float32)
    cell_pos = (lax.axis_index("dev") * cells_here + local_ids).astype(jnp.float32)
    along_x = (cell_pos[:, None] + offsets[0, :, 0, :]) / cell_line
    along_y = offsets[0, :, 1, :]
    along_z = (lax.axis_index("grp").astype(jnp.float32) + offsets[0, :, 2, :]) / lax.axis_size(
        "grp"
    )
    phase = (
        2.0
        * math.pi
        * (
            along_x[..., None] * waves[0]
            + along_y[..., None] * waves[1]
            + along_z[..., None] * waves[2]
        )
    )
    table = jnp.concatenate([jnp.cos(phase), jnp.sin(phase)], axis=-1).astype(jnp.bfloat16)
    table = table.reshape(cells_here * atom_slots, 2 * wave_count)
    masked_rows = masked.reshape(cells_here * atom_slots, channels)
    partial_sums = lax.dot_general(
        table, masked_rows, (((0,), (0,)), ((), ())), preferred_element_type=jnp.float32
    )
    kernel = wave_kernel(wavevectors)
    factor_scale = 1.0 / math.sqrt(total_slots)
    owned = lax.psum_scatter(
        partial_sums.astype(jnp.bfloat16), "dev", scatter_dimension=0, tiled=True
    ).astype(jnp.float32)
    owned = lax.psum(owned.astype(jnp.bfloat16), "grp").astype(jnp.float32)
    row_count = owned.shape[0]
    start = lax.axis_index("dev") * row_count
    kernel_rows = lax.dynamic_slice_in_dim(kernel, start, row_count, 0)
    factors = (owned * factor_scale).astype(jnp.bfloat16)
    energy_rows = (
        jnp.dot(factors, w_mix, preferred_element_type=jnp.float32) * kernel_rows[:, None]
    ).astype(jnp.bfloat16)
    energy = lax.all_gather(energy_rows, "dev", axis=0, tiled=True)
    longrange = jnp.dot(table, energy, preferred_element_type=jnp.float32) * (
        8.0 / math.sqrt(wave_count)
    )
    message = jnp.dot(
        gathered.reshape(cells_here * atom_slots, channels).astype(jnp.bfloat16),
        w_msg,
        preferred_element_type=jnp.float32,
    )
    result = masked_rows.astype(jnp.float32) + jax.nn.silu(message + longrange)
    result = result * masking.reshape(cells_here * atom_slots, 1).astype(jnp.float32)
    return result.astype(jnp.bfloat16).reshape(1, cells_here, atom_slots, channels)


def solution(mesh):
    in_specs = (
        P("grp", "dev", None, None),
        P("grp", "dev", None, None),
        P("grp", "dev", None, None, None),
        P("grp", "dev", None),
        P("grp", "dev"),
        P(),
        P(),
        P(),
    )
    out_specs = P("grp", "dev", None, None)
    return jax.shard_map(body, mesh=mesh, in_specs=in_specs, out_specs=out_specs, check_vma=False)
```

profile of v0, /device:TPU:0, one launch (start us, length us, event | category | flops | bytes accessed | tf_op | source)
XLA Modules:
  0.0 230.8 jit_solution(12604834691746285215)
XLA Ops:
  7.3 1.6 broadcast_multiply_fusion
  8.9 1.3 collective-permute-start.1
  10.2 3.2 %collective-permute-start = (bf16[1,16,128,256]{3,2,1,0:T(8,128)(2,1)S(1)}, bf16[1,16,128,256]{3,2,1,0:T(8,128)(2,1)S(1)}, u32[]{:S(2)}, u32[]{:S(2)}) collective-permute-start(bf16[1,16,128,256]{3,2,1,0:T(8,128)(2,1)S(1)} %broadcast_multiply_fusion), channel_id=1, source_target_pairs={{0,16},{1,17},{2,18},{3,19},{4,20},{5,21},{6,22},{7,23},{8,24},{9,... | collective-permute-start | bytes 3145736 | tf_op jit(solution)/shard_map/ppermute | solution.py:16
  15.6 33.8 %cosine_convert_fusion = (bf16[2048,1024]{1,0:T(8,128)(2,1)S(1)}, bf16[2048,1024]{1,0:T(8,128)(2,1)S(1)}) fusion(f32[1024]{0:T(1024)S(1)} %bitcast.110, f32[2048]{0:T(1024)S(1)} %get-tuple-element.10, f32[1024]{0:T(1024)S(1)} %bitcast.111, f32[2048]{0:T(1024)S(1)} %get-tuple-element.9, f32[1024]{0:T(1024)S(1)} %bitcast.109, f32[2048]{0:T(1024)S(1)} %fusion.29), kind=kLoop, calls=%fused_computation.10 | loop fusion | flops 16777216 | bytes 8425472 | tf_op jit(solution)/shard_map/convert
  49.5 2.0 copy-done.8
  52.7 6.8 %fusion.3 = bf16[2048,256]{1,0:T(8,128)(2,1)} fusion(bf16[2048,256]{1,0:T(8,128)(2,1)S(1)} %bitcast.105, bf16[2048,1024]{1,0:T(8,128)(2,1)S(1)} %get-tuple-element.8, bf16[2048,1024]{1,0:T(8,128)(2,1)S(1)} %get-tuple-element.7), kind=kOutput, calls=%fused_computation.17 | convolution fusion | flops 2164785152 | bytes 10485760 | tf_op jit(solution)/shard_map/dot_general | solution.py:71
  59.9 4.9 %collective-permute-start.2 = (bf16[3,1,128,256]{3,2,1,0:T(8,128)(2,1)S(1)}, bf16[3,1,128,256]{3,2,1,0:T(8,128)(2,1)S(1)}, u32[]{:S(2)}, u32[]{:S(2)}) collective-permute-start(bf16[3,1,128,256]{3,2,1,0:T(8,128)(2,1)S(1)} %get-tuple-element.5), channel_id=1, source_target_pairs={{0,1},{1,2},{2,3},{3,4},{4,5},{5,6},{6,7},{7,8},{8,9},{9,10},{10,1... | collective-permute-start | bytes 589832 | tf_op jit(solution)/shard_map/ppermute | solution.py:16
  64.7 1.3 collective-permute-start.3
  66.1 2.5 %collective-permute-done.2 = bf16[3,1,128,256]{3,2,1,0:T(8,128)(2,1)S(1)} collective-permute-done((bf16[3,1,128,256]{3,2,1,0:T(8,128)(2,1)S(1)}, bf16[3,1,128,256]{3,2,1,0:T(8,128)(2,1)S(1)}, u32[]{:S(2)}, u32[]{:S(2)}) %collective-permute-start.2) | collective-permute-done | bytes 196640 | tf_op jit(solution)/shard_map/ppermute | solution.py:16
  68.7 8.7 %collective-permute-done.3 = bf16[3,1,128,256]{3,2,1,0:T(8,128)(2,1)S(1)} collective-permute-done((bf16[3,1,128,256]{3,2,1,0:T(8,128)(2,1)S(1)}, bf16[3,1,128,256]{3,2,1,0:T(8,128)(2,1)S(1)}, u32[]{:S(2)}, u32[]{:S(2)}) %collective-permute-start.3) | collective-permute-done | bytes 196640 | tf_op jit(solution)/shard_map/ppermute | solution.py:17
  77.3 2.2 pad_maximum_fusion.3
  79.5 3.6 %gather_fusion.2 = bf16[16,128,256]{2,1,0:T(8,128)(2,1)} fusion(bf16[54,128,256]{2,1,0:T(8,128)(2,1)} %bitcast.97, s32[1024]{0:T(1024)S(1)} %get-tuple-element.27), kind=kCustom, calls=%fused_computation.2 | custom fusion | bytes 2097216 | tf_op jit(solution)/shard_map/gather | solution.py:48
  83.1 3.6 %gather_fusion.1 = bf16[16,128,256]{2,1,0:T(8,128)(2,1)} fusion(bf16[54,128,256]{2,1,0:T(8,128)(2,1)} %bitcast.98, s32[1024]{0:T(1024)S(1)} %get-tuple-element.28), kind=kCustom, calls=%fused_computation.1 | custom fusion | bytes 2097216 | tf_op jit(solution)/shard_map/gather | solution.py:48
  86.7 3.6 %gather_fusion = bf16[16,128,256]{2,1,0:T(8,128)(2,1)} fusion(bf16[54,128,256]{2,1,0:T(8,128)(2,1)} %bitcast.99, s32[1024]{0:T(1024)S(1)} %get-tuple-element.29), kind=kCustom, calls=%fused_computation | custom fusion | bytes 2097216 | tf_op jit(solution)/shard_map/gather | solution.py:48
  90.3 1.9 fusion.18
  92.2 2.8 %fusion.16 = f32[16,256,128]{1,2,0:T(8,128)} fusion(bf16[16,128,256]{2,1,0:T(8,128)(2,1)S(1)} %copy-done.7, bf16[1,16,8,128,128]{4,3,2,1,0:T(8,128)(2,1)} %param.10), kind=kOutput, calls=%fused_computation.33 | convolution fusion | flops 134217728 | bytes 3670016 | tf_op jit(solution)/shard_map/kab,kbc->kac/dot_general | solution.py:49
  95.1 45.0 %reduce-scatter.2.cloned.1.call-done = bf16[128,256]{1,0:T(8,128)(2,1)} async-done(((bf16[2048,256]{1,0:T(8,128)(2,1)}), bf16[128,256]{1,0:T(8,128)(2,1)}) %reduce-scatter.2.cloned.1.call-update) | async-done | bytes 65552 | tf_op jit(solution)/shard_map/reduce_scatter | solution.py:76
  140.4 3.1 %fusion.14 = f32[16,256,128]{1,2,0:T(8,128)} fusion(bf16[16,128,256]{2,1,0:T(8,128)(2,1)} %gather_fusion.2, bf16[1,16,8,128,128]{4,3,2,1,0:T(8,128)(2,1)} %param.10), kind=kOutput, calls=%fused_computation.31 | convolution fusion | flops 134217728 | bytes 3670016 | tf_op jit(solution)/shard_map/kab,kbc->kac/dot_general | solution.py:49
  143.5 3.6 %gather_fusion.7 = bf16[16,128,256]{2,1,0:T(8,128)(2,1)} fusion(bf16[54,128,256]{2,1,0:T(8,128)(2,1)} %bitcast.100, s32[1024]{0:T(1024)S(1)} %get-tuple-element.22), kind=kCustom, calls=%fused_computation.7 | custom fusion | bytes 2097216 | tf_op jit(solution)/shard_map/gather | solution.py:48
  147.1 3.6 %gather_fusion.6 = bf16[16,128,256]{2,1,0:T(8,128)(2,1)} fusion(bf16[54,128,256]{2,1,0:T(8,128)(2,1)} %bitcast.101, s32[1024]{0:T(1024)S(1)} %get-tuple-element.23), kind=kCustom, calls=%fused_computation.6 | custom fusion | bytes 2097216 | tf_op jit(solution)/shard_map/gather | solution.py:48
  150.7 3.6 %gather_fusion.5 = bf16[16,128,256]{2,1,0:T(8,128)(2,1)} fusion(bf16[54,128,256]{2,1,0:T(8,128)(2,1)} %bitcast.102, s32[1024]{0:T(1024)S(1)} %get-tuple-element.24), kind=kCustom, calls=%fused_computation.5 | custom fusion | bytes 2097216 | tf_op jit(solution)/shard_map/gather | solution.py:48
  154.3 3.6 %gather_fusion.4 = bf16[16,128,256]{2,1,0:T(8,128)(2,1)} fusion(bf16[54,128,256]{2,1,0:T(8,128)(2,1)} %bitcast.103, s32[1024]{0:T(1024)S(1)} %get-tuple-element.25), kind=kCustom, calls=%fused_computation.4 | custom fusion | bytes 2097216 | tf_op jit(solution)/shard_map/gather | solution.py:48
  158.0 3.6 %gather_fusion.3 = bf16[16,128,256]{2,1,0:T(8,128)(2,1)} fusion(bf16[54,128,256]{2,1,0:T(8,128)(2,1)} %bitcast.104, s32[1024]{0:T(1024)S(1)} %get-tuple-element.26), kind=kCustom, calls=%fused_computation.3 | custom fusion | bytes 2097216 | tf_op jit(solution)/shard_map/gather | solution.py:48
  161.6 1.6 fusion.4
  163.2 2.0 fusion.12
  165.2 1.6 fusion.10
  166.8 1.6 fusion.8
  168.4 1.5 fusion.6
  170.0 3.0 %add_convert_fusion = bf16[16,256,128]{1,2,0:T(8,128)(2,1)} fusion(f32[16,256,128]{1,2,0:T(8,128)S(1)} %fusion.6, f32[16,256,128]{1,2,0:T(8,128)S(1)} %fusion.8, f32[16,256,128]{1,2,0:T(8,128)S(1)} %fusion.10, f32[16,256,128]{1,2,0:T(8,128)S(1)} %fusion.12, f32[16,256,128]{1,2,0:T(8,128)S(1)} %copy-done.2, f32[16,256,128]{1,2,0:T(8,128)S(1)} %fusion.18, ...), kind=kOutput, calls=%fused_computation.18 | convolution fusion | flops 138412032 | bytes 17301504 | tf_op jit(solution)/shard_map/kab,kbc->kac/dot_general | solution.py:49
  173.0 44.3 %all-gather.2.cloned.1.call-done = bf16[2048,256]{1,0:T(8,128)(2,1)} async-done(((bf16[128,256]{1,0:T(8,128)(2,1)}), bf16[2048,256]{1,0:T(8,128)(2,1)}) %all-gather.2.cloned.1.call-update) | async-done | bytes 1048592 | tf_op jit(solution)/shard_map/all_gather | solution.py:87
  217.3 5.0 %fusion.2 = f32[2048,256]{1,0:T(8,128)S(1)} fusion(bf16[2048,256]{1,0:T(8,128)(2,1)} %all-gather.2.cloned.1.call-done, bf16[2048,1024]{1,0:T(8,128)(2,1)} %copy-done.9, bf16[2048,1024]{1,0:T(8,128)(2,1)} %copy-done.8), kind=kOutput, calls=%fused_computation.16 | convolution fusion | flops 2164785152 | bytes 11534336 | tf_op jit(solution)/shard_map/dot_general | solution.py:88
  222.4 1.9 multiply_convert_fusion
  (55 shorter events, 4.9 us)
Async XLA Ops:
  6.5 215.8 %copy-start = (bf16[256,256]{1,0:T(8,128)(2,1)S(1)}, bf16[256,256]{1,0:T(8,128)(2,1)}, u32[]{:S(2)}) copy-start(bf16[256,256]{1,0:T(8,128)(2,1)} %param.14) | copy-start | bytes 393220
  6.5 133.6 %reduce-scatter.2.cloned.1.call-start = ((), (), s32[]{:S(2)}) async-start(), calls=%async_computation.1 | async-start | bytes 1114112 | tf_op jit(solution)/shard_map/reduce_scatter | solution.py:76
  8.9 50.9 %collective-permute-start.1 = (bf16[1,16,128,256]{3,2,1,0:T(8,128)(2,1)S(1)}, bf16[1,16,128,256]{3,2,1,0:T(8,128)(2,1)S(1)}, u32[]{:S(2)}, u32[]{:S(2)}) collective-permute-start(bf16[1,16,128,256]{3,2,1,0:T(8,128)(2,1)S(1)} %broadcast_multiply_fusion), channel_id=1, source_target_pairs={{16,0},{17,1},{18,2},{19,3},{20,4},{21,5},{22,6},{23,7},{24,8},{25... | collective-permute-start | bytes 3145736 | tf_op jit(solution)/shard_map/ppermute | solution.py:17
  10.2 49.6 %collective-permute-start = (bf16[1,16,128,256]{3,2,1,0:T(8,128)(2,1)S(1)}, bf16[1,16,128,256]{3,2,1,0:T(8,128)(2,1)S(1)}, u32[]{:S(2)}, u32[]{:S(2)}) collective-permute-start(bf16[1,16,128,256]{3,2,1,0:T(8,128)(2,1)S(1)} %broadcast_multiply_fusion), channel_id=1, source_target_pairs={{0,16},{1,17},{2,18},{3,19},{4,20},{5,21},{6,22},{7,23},{8,24},{9,... | collective-permute-start | bytes 3145736 | tf_op jit(solution)/shard_map/ppermute | solution.py:16
  49.4 2.0 copy-start.8
  49.4 3.3 %copy-start.9 = (bf16[2048,1024]{1,0:T(8,128)(2,1)}, bf16[2048,1024]{1,0:T(8,128)(2,1)S(1)}, u32[]{:S(2)}) copy-start(bf16[2048,1024]{1,0:T(8,128)(2,1)S(1)} %get-tuple-element.8) | copy-start | bytes 12582916
  52.7 6.8 %copy-start.12 = (s32[3,1024]{1,0:T(4,128)S(1)}, s32[3,1024]{1,0:T(4,128)}, u32[]{:S(2)}) copy-start(s32[3,1024]{1,0:T(4,128)} %param.13) | copy-start | bytes 36868
  52.7 7.0 %copy-start.13 = (s32[1,16,8]{1,2,0:T(8,128)S(1)}, s32[1,16,8]{1,2,0:T(8,128)}, u32[]{:S(2)}) copy-start(s32[1,16,8]{1,2,0:T(8,128)} %param.11) | copy-start | bytes 1540
  59.5 6.6 %copy-start.14 = (s32[1,16]{1,0:T(1,128)S(1)}, s32[1,16]{1,0:T(1,128)}, u32[]{:S(2)}) copy-start(s32[1,16]{1,0:T(1,128)} %param.12) | copy-start | bytes 196
  59.5 102.1 %all-reduce.2.cloned.1.call-start = ((), (), s32[]{:S(2)}) async-start(), calls=%async_computation.2 | async-start | bytes 131072 | tf_op jit(solution)/shard_map/psum | solution.py:79
  59.9 8.8 %collective-permute-start.2 = (bf16[3,1,128,256]{3,2,1,0:T(8,128)(2,1)S(1)}, bf16[3,1,128,256]{3,2,1,0:T(8,128)(2,1)S(1)}, u32[]{:S(2)}, u32[]{:S(2)}) collective-permute-start(bf16[3,1,128,256]{3,2,1,0:T(8,128)(2,1)S(1)} %get-tuple-element.5), channel_id=1, source_target_pairs={{0,1},{1,2},{2,3},{3,4},{4,5},{5,6},{6,7},{7,8},{8,9},{9,10},{10,1... | collective-permute-start | bytes 589832 | tf_op jit(solution)/shard_map/ppermute | solution.py:16
  64.7 12.6 %collective-permute-start.3 = (bf16[3,1,128,256]{3,2,1,0:T(8,128)(2,1)S(1)}, bf16[3,1,128,256]{3,2,1,0:T(8,128)(2,1)S(1)}, u32[]{:S(2)}, u32[]{:S(2)}) collective-permute-start(bf16[3,1,128,256]{3,2,1,0:T(8,128)(2,1)S(1)} %get-tuple-element.6), channel_id=1, source_target_pairs={{1,0},{2,1},{3,2},{4,3},{5,4},{6,5},{7,6},{8,7},{9,8},{10,9},{11,1... | collective-permute-start | bytes 589832 | tf_op jit(solution)/shard_map/ppermute | solution.py:17
  90.3 1.9 copy-start.7
  140.1 77.1 %all-gather.2.cloned.1.call-start = ((), (), s32[]{:S(2)}) async-start(), calls=%async_computation.3 | async-start | bytes 1114112 | tf_op jit(solution)/shard_map/all_gather | solution.py:87
  150.7 10.9 %copy-start.11 = (bf16[256,256]{1,0:T(8,128)(2,1)S(1)}, bf16[256,256]{1,0:T(8,128)(2,1)}, u32[]{:S(2)}) copy-start(bf16[256,256]{1,0:T(8,128)(2,1)} %param.15) | copy-start | bytes 393220
  163.2 2.0 copy-start.6
  163.2 3.5 %copy-start.5 = (bf16[16,128,256]{2,1,0:T(8,128)(2,1)S(1)}, bf16[16,128,256]{2,1,0:T(8,128)(2,1)}, u32[]{:S(2)}) copy-start(bf16[16,128,256]{2,1,0:T(8,128)(2,1)} %gather_fusion.5) | copy-start | bytes 3145732
  165.2 3.2 %copy-start.4 = (bf16[16,128,256]{2,1,0:T(8,128)(2,1)S(1)}, bf16[16,128,256]{2,1,0:T(8,128)(2,1)}, u32[]{:S(2)}) copy-start(bf16[16,128,256]{2,1,0:T(8,128)(2,1)} %gather_fusion.6) | copy-start | bytes 3145732
  166.8 3.2 %copy-start.1 = (f32[16,256,128]{1,2,0:T(8,128)S(1)}, f32[16,256,128]{1,2,0:T(8,128)}, u32[]{:S(2)}) copy-start(f32[16,256,128]{1,2,0:T(8,128)} %fusion.16) | copy-start | bytes 6291460
  166.8 3.2 %copy-start.2 = (f32[16,256,128]{1,2,0:T(8,128)S(1)}, f32[16,256,128]{1,2,0:T(8,128)}, u32[]{:S(2)}) copy-start(f32[16,256,128]{1,2,0:T(8,128)} %fusion.14) | copy-start | bytes 6291460
  166.8 3.2 %copy-start.3 = (bf16[16,128,256]{2,1,0:T(8,128)(2,1)S(1)}, bf16[16,128,256]{2,1,0:T(8,128)(2,1)}, u32[]{:S(2)}) copy-start(bf16[16,128,256]{2,1,0:T(8,128)(2,1)} %gather_fusion.7) | copy-start | bytes 3145732
  173.0 49.3 %copy-start.10 = (bf16[16,256,128]{1,2,0:T(8,128)(2,1)S(1)}, bf16[16,256,128]{1,2,0:T(8,128)(2,1)}, u32[]{:S(2)}) copy-start(bf16[16,256,128]{1,2,0:T(8,128)(2,1)} %add_convert_fusion) | copy-start | bytes 3145732
Sparse Core Ops, SparseCore 0:
  59.6 80.4 reduce-scatter.1
  142.5 15.0 all-reduce.1
  163.3 53.9 all-gather.1
where the time goes:
time: 232 us; the launch traced here: 231 us
  waiting for transfers between devices  101 us (44%)
  other arithmetic  40.8 us (18%)
  matrix products  32.8 us (14%)
  local copies, waits for them, and re-layouts  32.3 us (14%)
  between operations  13.4 us (6%)
  starting transfers between devices  10.9 us (5%)
    reduce_scatter x1, waiting for transfers between devices, body(): lax.psum_scatter(partial_sums.astype(jnp.bfloat16), 'dev', scatter_dimens...  45 us
    all_gather x1, waiting for transfers between devices, body(): energy = lax.all_gather(energy_rows, 'dev', axis=0, tiled=True)  44.3 us
    another operation x1, other arithmetic  33.8 us
    gather x8, local copies, waits for them, and re-layouts, body(): picked = flat_window[rows_taken]  28.9 us
    dot_general x8, matrix products, body(): jnp.einsum('kab,kbc->kac', radial[0, :, neighbour], picked, preferred_ele...  17.5 us
    ppermute x2, waiting for transfers between devices, extended(): after = lax.ppermute(first, axis, down)  8.65 us
    ppermute x2, starting transfers between devices, extended(): before = lax.ppermute(last, axis, up)  8.02 us
    dot_general x1, matrix products, body(): lax.dot_general(table, masked_rows, (((0,), (0,)), ((), ())), preferred_e...  6.76 us
  transfers between devices with their start and end apart: 7, of which 4 were waited for; matrix products, arithmetic and copies ran while one was open for 40% of the time, Pallas kernels for 0%

commit v1 on v0

v1 whole, which is shorter than its diff:
```python
import functools
import math

import jax
import jax.numpy as jnp
from jax import lax
from jax.experimental import pallas as pl
from jax.experimental.pallas import tpu as pltpu
from jax.sharding import PartitionSpec as P

F32 = jnp.float32
BF16 = jnp.bfloat16
VMEM = pl.BlockSpec(memory_space=pltpu.VMEM)
SMEM = pl.BlockSpec(memory_space=pltpu.SMEM)
PARAMS = pltpu.CompilerParams(vmem_limit_bytes=56 * 1024 * 1024)
SIN = (4.44287957, -7.30781668, 3.59777418, -0.79119939)
COS = (1.41420401, -6.97763732, 5.71518787, -1.72821389)


def radices(count):
    digits = []
    stride = 1
    while stride < count:
        rest = count // stride
        radix = 4 if rest % 4 == 0 else 2 if rest % 2 == 0 else rest
        digits.append((stride, radix))
        stride *= radix
    return digits


def to_offset(axis, stride, radix, offset):
    pairs = []
    for place in range(lax.axis_size(axis)):
        digit = place // stride % radix
        pairs.append((place, place + ((digit + offset) % radix - digit) * stride))
    return pairs


def cosine_sine(turns):
    part = turns - jnp.round(turns)
    square = part * part
    sine = part * (SIN[0] + square * (SIN[1] + square * (SIN[2] + square * SIN[3])))
    cosine = COS[0] + square * (COS[1] + square * (COS[2] + square * COS[3]))
    return 1.0 - sine * sine, sine * cosine


def table_kernel(tile, lengths, has_rows, has_start, keeps, *refs):
    refs = list(refs)
    place_ref, offsets_ref, waves_ref = refs[:3]
    refs = refs[3:]
    rows_ref = refs.pop(0) if has_rows else None
    start_ref = refs.pop(0) if has_start else None
    table_ref = refs.pop(0) if keeps else None
    sums_ref = refs.pop(0) if has_rows else None
    places_ref = refs.pop(0)
    cell_line, slabs = lengths
    cells, _, slots = offsets_ref.shape

    @pl.when(pl.program_id(0) == 0)
    def _():
        line = lax.broadcasted_iota(jnp.int32, (8, slots), 0)
        for cell in range(cells):
            own = offsets_ref[cell]
            first = (place_ref[0] + cell).astype(F32)
            along_x = (first + own[0:1]) / cell_line
            along_z = (place_ref[1].astype(F32) + own[2:3]) / slabs
            full = jnp.where(
                line == 0, along_x, jnp.where(line == 1, own[1:2], jnp.where(line == 2, along_z, 0.0))
            )
            high = full.astype(BF16).astype(F32)
            middle = (full - high).astype(BF16).astype(F32)
            low = full - high - middle
            parts = jnp.concatenate([high, middle, low, jnp.zeros_like(low)], axis=0)
            places_ref[:, cell * slots : (cell + 1) * slots] = parts.astype(BF16)

    waves = waves_ref[...]
    block = waves.shape[0]
    total = start_ref[0] if has_start else None
    for first in range(0, cells * slots, tile):
        span = slice(first, first + tile)
        turns = jnp.dot(waves, places_ref[:, span], preferred_element_type=F32)
        cosine, sine = cosine_sine(turns)
        both = jnp.concatenate([cosine.astype(BF16), sine.astype(BF16)], axis=0)
        if keeps:
            table_ref[0, :, span] = both
        if has_rows:
            part = jnp.dot(both, rows_ref[span, :], preferred_element_type=F32)
            total = part if total is None else total + part
    if has_rows:
        sums_ref[0] = total.astype(sums_ref.dtype)


def table_call(place, offsets, waves, blocks, lengths, rows=None, start=None, keeps=True, sums_type=F32):
    cells, _, slots = offsets.shape
    atoms = cells * slots
    block = waves.shape[0] // blocks
    operands = [place, offsets, waves]
    in_specs = [
        SMEM,
        pl.BlockSpec(offsets.shape, lambda i: (0, 0, 0)),
        pl.BlockSpec((block, waves.shape[1]), lambda i: (i, 0)),
    ]
    out_shape, out_specs = [], []
    if keeps:
        out_shape.append(jax.ShapeDtypeStruct((blocks, 2 * block, atoms), BF16))
        out_specs.append(pl.BlockSpec((1, 2 * block, atoms), lambda i: (i, 0, 0)))
    if rows is not None:
        channels = rows.shape[1]
        operands.append(rows)
        in_specs.append(pl.BlockSpec(rows.shape, lambda i: (0, 0)))
        sums_spec = pl.BlockSpec((1, 2 * block, channels), lambda i: (i, 0, 0))
        if start is not None:
            operands.append(start)
            in_specs.append(sums_spec)
        out_shape.append(jax.ShapeDtypeStruct((blocks, 2 * block, channels), sums_type))
        out_specs.append(sums_spec)
    tile = math.gcd(atoms, 256)
    return pl.pallas_call(
        functools.partial(table_kernel, tile, lengths, rows is not None, start is not None, keeps),
        grid=(blocks,),
        in_specs=in_specs,
        out_specs=out_specs,
        out_shape=out_shape,
        scratch_shapes=[pltpu.VMEM((32, atoms), BF16)],
        compiler_params=PARAMS,
    )(*operands)


def short_kernel(groups, lines, picks_ref, radial_ref, *refs):
    row_refs = refs[:lines]
    before_ref, after_ref, w_ref, message_ref, window_ref = refs[lines:]
    cells, slots, channels = row_refs[0].shape
    step = pl.program_id(0)

    @pl.when(step == 0)
    def _():
        for line in range(lines):
            base = line * (cells + 2)
            window_ref[base] = before_ref[line]
            for cell in range(cells):
                window_ref[base + 1 + cell] = row_refs[line][cell]
            window_ref[base + 1 + cells] = after_ref[line]
        window_ref[lines * (cells + 2)] = jnp.zeros((slots, channels), BF16)

    pairs = radial_ref.shape[1]
    for cell in range(groups):
        total = None
        for pair in range(0, pairs, 2):
            here = list(range(pair, min(pair + 2, pairs)))
            blocks = [radial_ref[cell, p] for p in here]
            taken = [window_ref[picks_ref[(step * groups + cell) * pairs + p]] for p in here]
            left = jnp.concatenate(blocks, axis=1)
            right = jnp.concatenate(taken, axis=0)
            part = jnp.dot(left, right, preferred_element_type=F32)
            total = part if total is None else total + part
        message_ref[cell] = jnp.dot(total.astype(BF16), w_ref[...], preferred_element_type=F32)


def short_call(picks, radial, rows, before, after, w_msg):
    cells, slots, channels = rows[0].shape
    groups = math.gcd(cells, 2)
    lines = len(rows)
    return pl.pallas_call(
        functools.partial(short_kernel, groups, lines),
        grid=(cells // groups,),
        in_specs=[
            SMEM,
            pl.BlockSpec((groups,) + radial.shape[1:], lambda i: (i, 0, 0, 0)),
            *[pl.BlockSpec(rows[0].shape, lambda i: (0, 0, 0))] * lines,
            *[pl.BlockSpec(before.shape, lambda i: (0, 0, 0))] * 2,
            pl.BlockSpec(w_msg.shape, lambda i: (0, 0)),
        ],
        out_specs=pl.BlockSpec((groups, slots, channels), lambda i: (i, 0, 0)),
        out_shape=jax.ShapeDtypeStruct((cells, slots, channels), F32),
        scratch_shapes=[pltpu.VMEM((lines * (cells + 2) + 1, slots, channels), BF16)],
        compiler_params=PARAMS,
    )(picks, radial, *rows, before, after, w_msg)


def add_kernel(count, radix, *refs):
    pieces, outs = refs[:count], refs[count:]
    total = pieces[0][...].astype(F32)
    for piece in pieces[1:]:
        total = total + piece[...].astype(F32)
    rows = total.shape[1] // radix
    for place, out in enumerate(outs):
        out[...] = total[:, place * rows : (place + 1) * rows].astype(out.dtype)


def add_and_cut(pieces, radix):
    trig, rows, channels = pieces[0].shape
    part = (trig, rows // radix, channels)
    types = [F32] + [BF16] * (radix - 1)
    if part[1] % 16:
        total = functools.reduce(jnp.add, [piece.astype(F32) for piece in pieces])
        return [
            total[:, place * part[1] : (place + 1) * part[1]].astype(kind) for place, kind in enumerate(types)
        ]
    return pl.pallas_call(
        functools.partial(add_kernel, len(pieces), radix),
        in_specs=[VMEM] * len(pieces),
        out_specs=[VMEM] * radix,
        out_shape=[jax.ShapeDtypeStruct(part, kind) for kind in types],
        compiler_params=PARAMS,
    )(*pieces)


def final_kernel(blocks, scale, energies, counts_ref, mine_ref, other_ref, message_ref, masked_ref, *refs):
    energy_refs = refs[:energies]
    out_ref, turned_ref = refs[energies:]
    cells, slots, channels = masked_ref.shape
    step = pl.program_id(0)

    @pl.when(step == 0)
    def _():
        for place, energy in enumerate(energy_refs):
            turned_ref[place] = energy[...].astype(F32).T.astype(BF16)

    total = None
    for place in range(blocks):
        part = jnp.dot(turned_ref[place], mine_ref[place], preferred_element_type=F32)
        total = part if total is None else total + part
    for place in range(blocks):
        total = total + jnp.dot(turned_ref[blocks + place], other_ref[place], preferred_element_type=F32)
    slot_ids = lax.broadcasted_iota(jnp.int32, (slots, channels), 0)
    for cell in range(cells):
        value = total[:, cell * slots : (cell + 1) * slots].T * scale + message_ref[cell]
        value = value * (0.5 + 0.5 * jnp.tanh(0.5 * value))
        result = masked_ref[cell].astype(F32) + value
        result = jnp.where(slot_ids < counts_ref[step * cells + cell], result, 0.0)
        out_ref[cell] = result.astype(BF16)


def final_call(counts, mine, other, message, masked, energies, scale):
    cells, slots, channels = masked.shape
    blocks, rows, _ = mine.shape
    group = math.gcd(cells, 4)
    table_spec = pl.BlockSpec((blocks, rows, group * slots), lambda i: (0, 0, i))
    cell_spec = pl.BlockSpec((group, slots, channels), lambda i: (i, 0, 0))
    return pl.pallas_call(
        functools.partial(final_kernel, blocks, scale, len(energies)),
        grid=(cells // group,),
        in_specs=[
            SMEM,
            table_spec,
            table_spec,
            cell_spec,
            cell_spec,
            *[pl.BlockSpec((rows, channels), lambda i: (0, 0))] * len(energies),
        ],
        out_specs=cell_spec,
        out_shape=jax.ShapeDtypeStruct(masked.shape, BF16),
        scratch_shapes=[pltpu.VMEM((len(energies), channels, rows), BF16)],
        compiler_params=PARAMS,
    )(counts, mine, other, message, masked, *energies)


def body(features, offsets, radial, neighbours, counts, wavevectors, w_msg, w_mix):
    _, cells, slots, channels = features.shape
    wave_count = wavevectors.shape[1]
    slabs, dev_count = lax.axis_size("grp"), lax.axis_size("dev")
    slab, dev = lax.axis_index("grp"), lax.axis_index("dev")
    cell_line = cells * dev_count
    total_slots = slabs * cell_line * slots
    atoms = cells * slots
    lengths = (float(cell_line), float(slabs))

    slot_ids = jnp.arange(slots, dtype=jnp.int32)
    masking = slot_ids[None, :] < counts[0][:, None]
    masked = jnp.where(masking[..., None], features[0], jnp.bfloat16(0))
    offsets = offsets[0]

    swap = to_offset("grp", 1, 2, 1)
    sibling_offsets = lax.ppermute(offsets, "grp", swap)
    if slabs == 2:
        sibling = lax.ppermute(masked, "grp", swap)
        lines = [masked, sibling]
    else:
        up = [(i, i + 1) for i in range(slabs - 1)]
        below = lax.ppermute(masked, "grp", up)
        above = lax.ppermute(masked, "grp", [(j, i) for i, j in up])
        sibling = jnp.where(slab % 2 == 0, above, below)
        lines = [masked, below, above]

    stages = [("dev", *digit) for digit in radices(dev_count)]
    stages += [("grp", 2 * stride, radix) for stride, radix in radices(slabs // 2)]
    digits = [("grp", 1, 2)] + stages

    waves = wavevectors.astype(F32).T.reshape(*[radix for _, _, radix in digits], -1, 3)
    for dim, (axis, stride, radix) in enumerate(digits):
        digit = (slab if axis == "grp" else dev) // stride % radix
        waves = jnp.roll(waves, -digit, axis=dim)
    waves = waves.reshape(wave_count, 3)
    owned_waves = wave_count // (slabs * dev_count)
    square = jnp.sum(waves[:owned_waves] ** 2, axis=1)
    kernel = jnp.exp(-square / 128.0) / (1.0 + square / 64.0)
    thrice = jnp.pad(waves, ((0, 0), (0, 5))).astype(BF16)
    thrice = jnp.concatenate([thrice, thrice, thrice, jnp.zeros_like(thrice)], axis=1)
    half = wave_count // 2
    blocks = stages[0][2]

    own_place = jnp.stack([dev * cells, slab]).astype(jnp.int32)
    other_place = jnp.stack([dev * cells, slab ^ 1]).astype(jnp.int32)
    own_rows = masked.reshape(atoms, channels)
    mine, sums = table_call(own_place, offsets, thrice[:half], blocks, lengths, rows=own_rows)
    (sums,) = table_call(
        other_place, sibling_offsets, thrice[:half], blocks, lengths,
        rows=sibling.reshape(atoms, channels), start=sums, keeps=False,
    )

    rows = half // blocks
    parts = [sums[0].reshape(2, rows, channels)]
    parts += [sums[place].astype(BF16).reshape(2, rows, channels) for place in range(1, blocks)]
    for stage, (axis, stride, radix) in enumerate(stages):
        received = [
            lax.ppermute(parts[place], axis, to_offset(axis, stride, radix, place)) for place in range(1, radix)
        ]
        cut = stages[stage + 1][2] if stage + 1 < len(stages) else 1
        parts = add_and_cut([parts[0], *received], cut)
    owned = parts[0].reshape(2 * owned_waves, channels)
    factors = (owned * (1.0 / math.sqrt(total_slots))).astype(BF16)
    energy = jnp.dot(factors, w_mix, preferred_element_type=F32).reshape(2, owned_waves, channels)
    energy = (energy * kernel[None, :, None]).astype(BF16)

    (other,) = table_call(own_place, offsets, thrice[half:], blocks, lengths)
    first = jnp.stack([line[0] for line in lines])
    last = jnp.stack([line[cells - 1] for line in lines])
    right = [(i, i + 1) for i in range(dev_count - 1)]
    before = lax.ppermute(last, "dev", right)
    after = lax.ppermute(first, "dev", [(j, i) for i, j in right])
    codes = neighbours[0]
    level = codes // 3 - 1
    if slabs == 2:
        line = jnp.where(level == 0, 0, 1)
    else:
        line = jnp.where(level == 0, 0, jnp.where(level < 0, 1, 2))
    inside = (slab + level >= 0) & (slab + level < slabs)
    picks = line * (cells + 2) + jnp.arange(cells, dtype=jnp.int32)[:, None] + codes % 3
    picks = jnp.where(inside, picks, len(lines) * (cells + 2)).reshape(-1)
    message = short_call(picks, radial[0], lines, before, after, w_msg)

    for axis, stride, radix in reversed(stages[1:]):
        pieces = [energy]
        for place in range(1, radix):
            pieces.append(lax.ppermute(energy, axis, to_offset(axis, stride, radix, -place)))
        energy = jnp.concatenate(pieces, axis=1)
    axis, stride, radix = stages[0]
    energies = [energy]
    for place in range(1, radix):
        energies.append(lax.ppermute(energy, axis, to_offset(axis, stride, radix, -place)))
    energies += [lax.ppermute(piece, "grp", swap) for piece in energies]
    energies = [piece.reshape(2 * rows, channels) for piece in energies]

    scale = 8.0 / math.sqrt(wave_count)
    result = final_call(counts[0], mine, other, message, masked, energies, scale)
    return result[None]


def solution(mesh):
    in_specs = (
        P("grp", "dev", None, None),
        P("grp", "dev", None, None),
        P("grp", "dev", None, None, None),
        P("grp", "dev", None),
        P("grp", "dev"),
        P(),
        P(),
        P(),
    )
    out_specs = P("grp", "dev", None, None)
    return jax.shard_map(body, mesh=mesh, in_specs=in_specs, out_specs=out_specs, check_vma=False)
```

time: 232 us -> 98.6 us (0.42)
  waiting for transfers between devices: 101 us -> 10.4 us
  Pallas kernels: 0 us -> 41.9 us
  other arithmetic: 40.8 us -> 8.45 us
  matrix products: 32.8 us -> 0.95 us
  local copies, waits for them, and re-layouts: 32.3 us -> 9.56 us
  starting transfers between devices: 10.9 us -> 25.5 us
  between operations: 13.4 us -> 0.43 us
    reduce_scatter x1 -> x0, waiting for transfers between devices: 45 us -> none  [body(): lax.psum_scatter(partial_sums.astype(jnp.bfloat16), 'dev', scatter_dimens...]
    all_gather x1 -> x0, waiting for transfers between devices: 44.3 us -> none  [body(): energy = lax.all_gather(energy_rows, 'dev', axis=0, tiled=True)]
    pallas_call x0 -> x7, Pallas kernels: none -> 41.9 us  [the longest x3 20.6 us: table_call(): pl.pallas_call(functools.partial(table_kernel, tile, lengths, rows is not...]
    dot_general x12 -> x1, matrix products: 32.8 us -> 0.95 us  [body(): jnp.dot(factors, w_mix, preferred_element_type=F32)]
    another operation x1 -> x6, other arithmetic: 33.8 us -> 2.61 us
    gather x8 -> x0, local copies, waits for them, and re-layouts: 28.9 us -> none  [body(): picked = flat_window[rows_taken]]
    ppermute x4 -> x20, starting transfers between devices: 10.6 us -> 25.5 us  [the longest x6 11.4 us: body(): lax.ppermute(parts[place], axis, to_offset(axis, stride, radix, place))]
    select_n x1 -> x3, other arithmetic: 0.05 us -> 3.32 us  [the longest x2 2.8 us: body(): masked = jnp.where(masking[..., None], features[0], jnp.bfloat16(0))]
  transfers between devices with their start and end apart: 7 -> 20, of which waited for: 4 -> 8; matrix products, arithmetic and copies ran while one was open for 40% -> 11% of each run, Pallas kernels for 0% -> 23%
where the time goes in v1:
time: 98.6 us; the launch traced here: 97.2 us
  Pallas kernels  41.9 us (42%)
  starting transfers between devices  25.5 us (26%)
  waiting for transfers between devices  10.4 us (11%)
  local copies, waits for them, and re-layouts  9.56 us (10%)
  other arithmetic  8.45 us (9%)
    pallas_call x3, Pallas kernels, table_call(): pl.pallas_call(functools.partial(table_kernel, tile, lengths, rows is not...  20.6 us
    ppermute x6, starting transfers between devices, body(): lax.ppermute(parts[place], axis, to_offset(axis, stride, radix, place))  11.4 us
    pallas_call x1, Pallas kernels, short_call(): pl.pallas_call(functools.partial(short_kernel, groups, lines), grid=(cell...  9.63 us
    pallas_call x1, Pallas kernels, final_call(): pl.pallas_call(functools.partial(final_kernel, blocks, scale, len(energie...  8.38 us
    ppermute x6, starting transfers between devices, body(): lax.ppermute(energy, axis, to_offset(axis, stride, radix, -place))  7.38 us
    unnamed x49, local copies, waits for them, and re-layouts  6.04 us
    ppermute x6, waiting for transfers between devices, body(): lax.ppermute(parts[place], axis, to_offset(axis, stride, radix, place))  5.04 us
    ppermute x1, waiting for transfers between devices, body(): after = lax.ppermute(first, 'dev', [(j, i) for i, j in right])  3.98 us
  transfers between devices with their start and end apart: 20, of which 8 were waited for; matrix products, arithmetic and copies ran while one was open for 11% of the time, Pallas kernels for 23%

profile of v1, /device:TPU:0, one launch (start us, length us, event | category | flops | bytes accessed | tf_op | source)
XLA Modules:
  0.0 97.2 jit_solution(7646123713728145045)
XLA Ops:
  0.0 0.8 iota_compare_fusion
  0.8 1.5 %bitcast_select_fusion.refs_0_.masked_ref = bf16[16,128,256]{2,1,0:T(8,128)(2,1)S(1)} fusion(bf16[1,16,128,256]{3,2,1,0:T(8,128)(2,1)} %param.8, pred[16,128]{1,0:T(8,128)(4,1)S(1)} %get-tuple-element.28), kind=kLoop, calls=%fused_computation.2 | loop fusion | flops 524288 | bytes 2099200 | tf_op jit(solution)/shard_map/jit(_where)/select_n | solution.py:270
  2.8 0.8 copy.50
  6.6 1.3 %bitcast_select_fusion.1.refs_3_ = bf16[2048,256]{1,0:T(8,128)(2,1)} fusion(bf16[1,16,128,256]{3,2,1,0:T(8,128)(2,1)S(1)} %copy-done.3, pred[2048]{0:T(1024)(128)(4,1)S(1)} %get-tuple-element.29), kind=kLoop, calls=%fused_computation.3 | loop fusion | flops 524288 | bytes 2099200 | tf_op jit(solution)/shard_map/jit(_where)/select_n | solution.py:270
  8.5 0.8 copy.46.refs_2_
  9.3 7.6 %shard_map.82 = (bf16[4,256,2048]{2,1,0:T(8,128)(2,1)}, f32[4,256,256]{2,1,0:T(8,128)}) custom-call(s32[2]{0:T(128)} %pad_add_fusion.refs_0_, f32[16,3,128]{2,1,0:T(4,128)} %bitcast.42, bf16[512,32]{1,0:T(8,128)(2,1)} %copy.46.refs_2_, bf16[2048,256]{1,0:T(8,128)(2,1)} %bitcast_select_fusion.1.refs_3_), custom_call_target="tpu_custom_call" | custom-call | tf_op jit(solution)/shard_map/pallas_call | solution.py:118
  17.9 7.6 %shard_map.85 = f32[4,256,256]{2,1,0:T(8,128)} custom-call(s32[2]{0:T(128)} %pad_add_fusion.1.refs_0_, f32[16,3,128]{2,1,0:T(4,128)} %copy-done.18, bf16[512,32]{1,0:T(8,128)(2,1)} %copy.46.refs_2_, bf16[2048,256]{1,0:T(8,128)(2,1)} %bitcast.37, f32[4,256,256]{2,1,0:T(8,128)} %get-tuple-element.12.refs_4_), custom_call_target="tpu_custom_call" | custom-call | tf_op jit(solution)/shard_map/pallas_call | solution.py:118
  25.5 1.3 %convert.10 = bf16[4,256,256]{2,1,0:T(8,128)(2,1)S(1)} convert(f32[4,256,256]{2,1,0:T(8,128)} %shard_map.85) | non-fusion elementwise | flops 262144 | bytes 1572864 | tf_op jit(solution)/shard_map/convert.2
  26.8 2.9 %collective-permute-start.4 = (bf16[2,128,256]{2,1,0:T(8,128)(2,1)S(1)}, bf16[2,128,256]{2,1,0:T(8,128)(2,1)S(1)}, u32[]{:S(2)}, u32[]{:S(2)}) collective-permute-start(bf16[2,128,256]{2,1,0:T(8,128)(2,1)S(1)} %bitcast.53), channel_id=1, source_target_pairs={{0,1},{1,2},{2,3},{3,0},{4,5},{5,6},{6,7},{7,4},{8,9},{9,10},{10,1... | collective-permute-start | bytes 393224 | tf_op jit(solution)/shard_map/ppermute | solution.py:316
  29.8 1.5 %collective-permute-start.5 = (bf16[2,128,256]{2,1,0:T(8,128)(2,1)S(1)}, bf16[2,128,256]{2,1,0:T(8,128)(2,1)S(1)}, u32[]{:S(2)}, u32[]{:S(2)}) collective-permute-start(bf16[2,128,256]{2,1,0:T(8,128)(2,1)S(1)} %bitcast.52), channel_id=1, source_target_pairs={{0,2},{1,3},{2,0},{3,1},{4,6},{5,7},{6,4},{7,5},{8,10},{9,11},{10,... | collective-permute-start | bytes 393224 | tf_op jit(solution)/shard_map/ppermute | solution.py:316
  31.3 1.4 %collective-permute-start.6 = (bf16[2,128,256]{2,1,0:T(8,128)(2,1)S(1)}, bf16[2,128,256]{2,1,0:T(8,128)(2,1)S(1)}, u32[]{:S(2)}, u32[]{:S(2)}) collective-permute-start(bf16[2,128,256]{2,1,0:T(8,128)(2,1)S(1)} %bitcast.51), channel_id=1, source_target_pairs={{0,3},{1,0},{2,1},{3,2},{4,7},{5,4},{6,5},{7,6},{8,11},{9,8},{10,9... | collective-permute-start | bytes 393224 | tf_op jit(solution)/shard_map/ppermute | solution.py:316
  32.7 1.7 %slice.54 = f32[1,256,256]{2,1,0:T(8,128)} slice(f32[4,256,256]{2,1,0:T(8,128)} %shard_map.85), slice={[0:1], [0:256], [0:256]} | slice | bytes 524288 | tf_op jit(solution)/shard_map/slice | solution.py:312
  35.0 2.3 %collective-permute-done.5.refs_2_ = bf16[2,128,256]{2,1,0:T(8,128)(2,1)S(1)} collective-permute-done((bf16[2,128,256]{2,1,0:T(8,128)(2,1)S(1)}, bf16[2,128,256]{2,1,0:T(8,128)(2,1)S(1)}, u32[]{:S(2)}, u32[]{:S(2)}) %collective-permute-start.5) | collective-permute-done | bytes 131104 | tf_op jit(solution)/shard_map/ppermute | solution.py:316
  38.3 1.8 %shard_map.86 = (f32[2,32,256]{2,1,0:T(8,128)}, bf16[2,32,256]{2,1,0:T(8,128)(2,1)}, bf16[2,32,256]{2,1,0:T(8,128)(2,1)}, bf16[2,32,256]{2,1,0:T(8,128)(2,1)}) custom-call(f32[2,128,256]{2,1,0:T(8,128)} %bitcast.39, bf16[2,128,256]{2,1,0:T(8,128)(2,1)} %copy-done.15, bf16[2,128,256]{2,1,0:T(8,128)(2,1)} %copy-done.16, bf16[2,128,256]{2,1,0:T(8,128)(2,1)} %copy-done.17), custom_call_target="tpu_custom_call" | custom-call | tf_op jit(solution)/shard_map/pallas_call | solution.py:199
  40.1 1.6 %collective-permute-start.7 = (bf16[2,32,256]{2,1,0:T(8,128)(2,1)}, bf16[2,32,256]{2,1,0:T(8,128)(2,1)S(1)}, u32[]{:S(2)}, u32[]{:S(2)}) collective-permute-start(bf16[2,32,256]{2,1,0:T(8,128)(2,1)} %get-tuple-element.14), channel_id=1, source_target_pairs={{0,4},{1,5},{2,6},{3,7},{4,8},{5,9},{6,10},{7,11},{8,12},{9,13},{1... | collective-permute-start | bytes 98312 | tf_op jit(solution)/shard_map/ppermute | solution.py:316
  41.6 2.6 %collective-permute-start.8 = (bf16[2,32,256]{2,1,0:T(8,128)(2,1)}, bf16[2,32,256]{2,1,0:T(8,128)(2,1)S(1)}, u32[]{:S(2)}, u32[]{:S(2)}) collective-permute-start(bf16[2,32,256]{2,1,0:T(8,128)(2,1)} %get-tuple-element.15), channel_id=1, source_target_pairs={{0,8},{1,9},{2,10},{3,11},{4,12},{5,13},{6,14},{7,15},{8,0},{9,1},... | collective-permute-start | bytes 98312 | tf_op jit(solution)/shard_map/ppermute | solution.py:316
  44.2 1.3 %collective-permute-start.9 = (bf16[2,32,256]{2,1,0:T(8,128)(2,1)}, bf16[2,32,256]{2,1,0:T(8,128)(2,1)S(1)}, u32[]{:S(2)}, u32[]{:S(2)}) collective-permute-start(bf16[2,32,256]{2,1,0:T(8,128)(2,1)} %get-tuple-element.16), channel_id=1, source_target_pairs={{0,12},{1,13},{2,14},{3,15},{4,0},{5,1},{6,2},{7,3},{8,4},{9,5},{1... | collective-permute-start | bytes 98312 | tf_op jit(solution)/shard_map/ppermute | solution.py:316
  45.6 0.9 fusion.13
  47.1 1.2 %collective-permute-done.9.refs_3_ = bf16[2,32,256]{2,1,0:T(8,128)(2,1)S(1)} collective-permute-done((bf16[2,32,256]{2,1,0:T(8,128)(2,1)}, bf16[2,32,256]{2,1,0:T(8,128)(2,1)S(1)}, u32[]{:S(2)}, u32[]{:S(2)}) %collective-permute-start.9) | collective-permute-done | bytes 32800 | tf_op jit(solution)/shard_map/ppermute | solution.py:316
  49.0 1.5 %shard_map.87 = f32[2,32,256]{2,1,0:T(8,128)} custom-call(f32[2,32,256]{2,1,0:T(8,128)} %get-tuple-element.13.refs_0_, bf16[2,32,256]{2,1,0:T(8,128)(2,1)} %copy-done.19, bf16[2,32,256]{2,1,0:T(8,128)(2,1)} %copy-done.20, bf16[2,32,256]{2,1,0:T(8,128)(2,1)} %copy-done.21), custom_call_target="tpu_custom_call" | custom-call | tf_op jit(solution)/shard_map/pallas_call | solution.py:199
  50.5 0.9 fusion
  51.4 3.2 %collective-permute-start.10 = (bf16[2,32,256]{2,1,0:T(8,128)(2,1)S(1)}, bf16[2,32,256]{2,1,0:T(8,128)(2,1)S(1)}, u32[]{:S(2)}, u32[]{:S(2)}) collective-permute-start(bf16[2,32,256]{2,1,0:T(8,128)(2,1)S(1)} %fusion), channel_id=1, source_target_pairs={{0,12},{1,13},{2,14},{3,15},{4,0},{5,1},{6,2},{7,3},{8,4},{9,5},{1... | collective-permute-start | bytes 98312 | tf_op jit(solution)/shard_map/ppermute | solution.py:345
  55.3 3.7 %collective-permute-start.1 = (bf16[2,128,256]{2,1,0:T(8,128)(2,1)S(1)}, bf16[2,128,256]{2,1,0:T(8,128)(2,1)S(1)}, u32[]{:S(2)}, u32[]{:S(2)}) collective-permute-start(bf16[2,128,256]{2,1,0:T(8,128)(2,1)S(1)} %pad_maximum_fusion), channel_id=1, source_target_pairs={{0,1},{1,2},{2,3},{3,4},{4,5},{5,6},{6,7},{7,8},{8,9},{9,10},{10,1... | collective-permute-start | bytes 393224 | tf_op jit(solution)/shard_map/ppermute | solution.py:329
  59.4 0.9 collective-permute-done.12
  60.4 2.2 %collective-permute-start.13 = (bf16[2,128,256]{2,1,0:T(8,128)(2,1)S(1)}, bf16[2,128,256]{2,1,0:T(8,128)(2,1)S(1)}, u32[]{:S(2)}, u32[]{:S(2)}) collective-permute-start(bf16[2,128,256]{2,1,0:T(8,128)(2,1)S(1)} %pad_maximum_fusion.2), channel_id=1, source_target_pairs={{0,3},{1,0},{2,1},{3,2},{4,7},{5,4},{6,5},{7,6},{8,11},{9,8},{10,9... | collective-permute-start | bytes 393224 | tf_op jit(solution)/shard_map/ppermute | solution.py:350
  62.5 1.1 %collective-permute-start.14 = (bf16[2,128,256]{2,1,0:T(8,128)(2,1)S(1)}, bf16[2,128,256]{2,1,0:T(8,128)(2,1)S(1)}, u32[]{:S(2)}, u32[]{:S(2)}) collective-permute-start(bf16[2,128,256]{2,1,0:T(8,128)(2,1)S(1)} %pad_maximum_fusion.2), channel_id=1, source_target_pairs={{0,2},{1,3},{2,0},{3,1},{4,6},{5,7},{6,4},{7,5},{8,10},{9,11},{10,... | collective-permute-start | bytes 393224 | tf_op jit(solution)/shard_map/ppermute | solution.py:350
  63.9 0.8 copy.47.refs_2_
  64.7 5.4 %shard_map.83.other_ref = bf16[4,256,2048]{2,1,0:T(8,128)(2,1)} custom-call(s32[2]{0:T(128)} %pad_add_fusion.refs_0_, f32[16,3,128]{2,1,0:T(4,128)} %bitcast.43, bf16[512,32]{1,0:T(8,128)(2,1)} %copy.47.refs_2_), custom_call_target="tpu_custom_call" | custom-call | tf_op jit(solution)/shard_map/pallas_call | solution.py:118
  70.7 1.3 %collective-permute-start.2 = (bf16[2,128,256]{2,1,0:T(8,128)(2,1)S(1)}, bf16[2,128,256]{2,1,0:T(8,128)(2,1)S(1)}, u32[]{:S(2)}, u32[]{:S(2)}) collective-permute-start(bf16[2,128,256]{2,1,0:T(8,128)(2,1)S(1)} %pad_maximum_fusion.1), channel_id=1, source_target_pairs={{1,0},{2,1},{3,2},{4,3},{5,4},{6,5},{7,6},{8,7},{9,8},{10,9},{11,1... | collective-permute-start | bytes 393224 | tf_op jit(solution)/shard_map/ppermute | solution.py:330
  73.7 4.0 %collective-permute-done.2.refs_3_ = bf16[2,128,256]{2,1,0:T(8,128)(2,1)S(1)} collective-permute-done((bf16[2,128,256]{2,1,0:T(8,128)(2,1)S(1)}, bf16[2,128,256]{2,1,0:T(8,128)(2,1)S(1)}, u32[]{:S(2)}, u32[]{:S(2)}) %collective-permute-start.2) | collective-permute-done | bytes 131104 | tf_op jit(solution)/shard_map/ppermute | solution.py:330
  78.3 9.6 %shard_map.84.message_ref = f32[16,128,256]{2,1,0:T(8,128)} custom-call(s32[128]{0:T(128)} %and_select_fusion.1.picks_ref, bf16[16,8,128,128]{3,2,1,0:T(8,128)(2,1)} %bitcast.38, bf16[16,128,256]{2,1,0:T(8,128)(2,1)} %copy-done.1, bf16[16,128,256]{2,1,0:T(8,128)(2,1)} %copy-done.2, bf16[2,128,256]{2,1,0:T(8,128)(2,1)} %copy-done.7, ...), custom_call_target="tpu_custom_call" | custom-call | tf_op jit(solution)/shard_map/pallas_call | solution.py:163
  88.9 8.4 %shard_map.88 = bf16[16,128,256]{2,1,0:T(8,128)(2,1)} custom-call(s32[16]{0:T(128)} %bitcast.55, bf16[4,256,2048]{2,1,0:T(8,128)(2,1)} %get-tuple-element.11.mine_ref, bf16[4,256,2048]{2,1,0:T(8,128)(2,1)} %shard_map.83.other_ref, f32[16,128,256]{2,1,0:T(8,128)} %shard_map.84.message_ref, bf16[16,128,256]{2,1,0:T(8,128)(2,1)} %copy-done.1, ...), custom_call_target="tpu_custom_call" | custom-call | tf_op jit(solution)/shard_map/pallas_call | solution.py:240
  (106 shorter events, 13.0 us)
Async XLA Ops:
  0.0 50.5 %copy-start = (bf16[256,256]{1,0:T(8,128)(2,1)S(1)}, bf16[256,256]{1,0:T(8,128)(2,1)}, u32[]{:S(2)}) copy-start(bf16[256,256]{1,0:T(8,128)(2,1)} %param.15) | copy-start | bytes 393220
  0.0 6.6 %copy-start.3 = (bf16[1,16,128,256]{3,2,1,0:T(8,128)(2,1)S(1)}, bf16[1,16,128,256]{3,2,1,0:T(8,128)(2,1)}, u32[]{:S(2)}) copy-start(bf16[1,16,128,256]{3,2,1,0:T(8,128)(2,1)} %param.8) | copy-start | bytes 3145732
  2.3 24.5 %copy-start.1 = (bf16[16,128,256]{2,1,0:T(8,128)(2,1)}, bf16[16,128,256]{2,1,0:T(8,128)(2,1)S(1)}, u32[]{:S(2)}) copy-start(bf16[16,128,256]{2,1,0:T(8,128)(2,1)S(1)} %bitcast_select_fusion.refs_0_.masked_ref) | copy-start | bytes 3145732
  2.3 14.6 %collective-permute-start = (bf16[16,128,256]{2,1,0:T(8,128)(2,1)S(1)}, bf16[16,128,256]{2,1,0:T(8,128)(2,1)S(1)}, u32[]{:S(2)}, u32[]{:S(2)}) collective-permute-start(bf16[16,128,256]{2,1,0:T(8,128)(2,1)S(1)} %bitcast_select_fusion.refs_0_.masked_ref), channel_id=1, source_target_pairs={{0,16},{16,0},{1,17},{17,1},{2,18},{18,2},{3,19},{19,3},{4,20},{20... | collective-permute-start | bytes 3145736 | tf_op jit(solution)/shard_map/ppermute | solution.py:276
  3.6 5.7 %copy-start.5 = (f32[1,16,3,128]{3,2,1,0:T(4,128)}, f32[1,16,3,128]{3,2,1,0:T(4,128)S(1)}, u32[]{:S(2)}) copy-start(f32[1,16,3,128]{3,2,1,0:T(4,128)S(1)} %copy.50) | copy-start | bytes 73732
  3.6 13.3 %collective-permute-start.3 = (f32[16,3,128]{2,1,0:T(4,128)S(1)}, f32[16,3,128]{2,1,0:T(4,128)S(1)}, u32[]{:S(2)}, u32[]{:S(2)}) collective-permute-start(f32[16,3,128]{2,1,0:T(4,128)S(1)} %bitcast.41), channel_id=1, source_target_pairs={{0,16},{16,0},{1,17},{17,1},{2,18},{18,2},{3,19},{19,3},{4,20},{20... | collective-permute-start | bytes 73736 | tf_op jit(solution)/shard_map/ppermute | solution.py:274
  16.9 47.0 %copy-start.22 = (s32[1,16,8]{1,2,0:T(8,128)S(1)}, s32[1,16,8]{1,2,0:T(8,128)}, u32[]{:S(2)}) copy-start(s32[1,16,8]{1,2,0:T(8,128)} %param.11) | copy-start | bytes 1540
  26.8 8.2 %collective-permute-start.4 = (bf16[2,128,256]{2,1,0:T(8,128)(2,1)S(1)}, bf16[2,128,256]{2,1,0:T(8,128)(2,1)S(1)}, u32[]{:S(2)}, u32[]{:S(2)}) collective-permute-start(bf16[2,128,256]{2,1,0:T(8,128)(2,1)S(1)} %bitcast.53), channel_id=1, source_target_pairs={{0,1},{1,2},{2,3},{3,0},{4,5},{5,6},{6,7},{7,4},{8,9},{9,10},{10,1... | collective-permute-start | bytes 393224 | tf_op jit(solution)/shard_map/ppermute | solution.py:316
  29.8 7.5 %collective-permute-start.5 = (bf16[2,128,256]{2,1,0:T(8,128)(2,1)S(1)}, bf16[2,128,256]{2,1,0:T(8,128)(2,1)S(1)}, u32[]{:S(2)}, u32[]{:S(2)}) collective-permute-start(bf16[2,128,256]{2,1,0:T(8,128)(2,1)S(1)} %bitcast.52), channel_id=1, source_target_pairs={{0,2},{1,3},{2,0},{3,1},{4,6},{5,7},{6,4},{7,5},{8,10},{9,11},{10,... | collective-permute-start | bytes 393224 | tf_op jit(solution)/shard_map/ppermute | solution.py:316
  31.3 6.3 %collective-permute-start.6 = (bf16[2,128,256]{2,1,0:T(8,128)(2,1)S(1)}, bf16[2,128,256]{2,1,0:T(8,128)(2,1)S(1)}, u32[]{:S(2)}, u32[]{:S(2)}) collective-permute-start(bf16[2,128,256]{2,1,0:T(8,128)(2,1)S(1)} %bitcast.51), channel_id=1, source_target_pairs={{0,3},{1,0},{2,1},{3,2},{4,7},{5,4},{6,5},{7,6},{8,11},{9,8},{10,9... | collective-permute-start | bytes 393224 | tf_op jit(solution)/shard_map/ppermute | solution.py:316
  35.0 2.5 %copy-start.15 = (bf16[2,128,256]{2,1,0:T(8,128)(2,1)}, bf16[2,128,256]{2,1,0:T(8,128)(2,1)S(1)}, u32[]{:S(2)}) copy-start(bf16[2,128,256]{2,1,0:T(8,128)(2,1)S(1)} %collective-permute-done.4.refs_1_) | copy-start | bytes 393220
  40.1 6.4 %collective-permute-start.7 = (bf16[2,32,256]{2,1,0:T(8,128)(2,1)}, bf16[2,32,256]{2,1,0:T(8,128)(2,1)S(1)}, u32[]{:S(2)}, u32[]{:S(2)}) collective-permute-start(bf16[2,32,256]{2,1,0:T(8,128)(2,1)} %get-tuple-element.14), channel_id=1, source_target_pairs={{0,4},{1,5},{2,6},{3,7},{4,8},{5,9},{6,10},{7,11},{8,12},{9,13},{1... | collective-permute-start | bytes 98312 | tf_op jit(solution)/shard_map/ppermute | solution.py:316
  41.6 5.5 %collective-permute-start.8 = (bf16[2,32,256]{2,1,0:T(8,128)(2,1)}, bf16[2,32,256]{2,1,0:T(8,128)(2,1)S(1)}, u32[]{:S(2)}, u32[]{:S(2)}) collective-permute-start(bf16[2,32,256]{2,1,0:T(8,128)(2,1)} %get-tuple-element.15), channel_id=1, source_target_pairs={{0,8},{1,9},{2,10},{3,11},{4,12},{5,13},{6,14},{7,15},{8,0},{9,1},... | collective-permute-start | bytes 98312 | tf_op jit(solution)/shard_map/ppermute | solution.py:316
  44.2 4.1 %collective-permute-start.9 = (bf16[2,32,256]{2,1,0:T(8,128)(2,1)}, bf16[2,32,256]{2,1,0:T(8,128)(2,1)S(1)}, u32[]{:S(2)}, u32[]{:S(2)}) collective-permute-start(bf16[2,32,256]{2,1,0:T(8,128)(2,1)} %get-tuple-element.16), channel_id=1, source_target_pairs={{0,12},{1,13},{2,14},{3,15},{4,0},{5,1},{6,2},{7,3},{8,4},{9,5},{1... | collective-permute-start | bytes 98312 | tf_op jit(solution)/shard_map/ppermute | solution.py:316
  46.5 1.9 %copy-start.19 = (bf16[2,32,256]{2,1,0:T(8,128)(2,1)}, bf16[2,32,256]{2,1,0:T(8,128)(2,1)S(1)}, u32[]{:S(2)}) copy-start(bf16[2,32,256]{2,1,0:T(8,128)(2,1)S(1)} %collective-permute-done.7.refs_1_) | copy-start | bytes 98308
  51.4 7.5 %collective-permute-start.10 = (bf16[2,32,256]{2,1,0:T(8,128)(2,1)S(1)}, bf16[2,32,256]{2,1,0:T(8,128)(2,1)S(1)}, u32[]{:S(2)}, u32[]{:S(2)}) collective-permute-start(bf16[2,32,256]{2,1,0:T(8,128)(2,1)S(1)} %fusion), channel_id=1, source_target_pairs={{0,12},{1,13},{2,14},{3,15},{4,0},{5,1},{6,2},{7,3},{8,4},{9,5},{1... | collective-permute-start | bytes 98312 | tf_op jit(solution)/shard_map/ppermute | solution.py:345
  54.6 4.8 %collective-permute-start.11 = (bf16[2,32,256]{2,1,0:T(8,128)(2,1)S(1)}, bf16[2,32,256]{2,1,0:T(8,128)(2,1)S(1)}, u32[]{:S(2)}, u32[]{:S(2)}) collective-permute-start(bf16[2,32,256]{2,1,0:T(8,128)(2,1)S(1)} %fusion), channel_id=1, source_target_pairs={{0,8},{1,9},{2,10},{3,11},{4,12},{5,13},{6,14},{7,15},{8,0},{9,1},... | collective-permute-start | bytes 98312 | tf_op jit(solution)/shard_map/ppermute | solution.py:345
  54.6 5.7 %collective-permute-start.12 = (bf16[2,32,256]{2,1,0:T(8,128)(2,1)S(1)}, bf16[2,32,256]{2,1,0:T(8,128)(2,1)S(1)}, u32[]{:S(2)}, u32[]{:S(2)}) collective-permute-start(bf16[2,32,256]{2,1,0:T(8,128)(2,1)S(1)} %fusion), channel_id=1, source_target_pairs={{0,4},{1,5},{2,6},{3,7},{4,8},{5,9},{6,10},{7,11},{8,12},{9,13},{1... | collective-permute-start | bytes 98312 | tf_op jit(solution)/shard_map/ppermute | solution.py:345
  55.3 16.8 %collective-permute-start.1 = (bf16[2,128,256]{2,1,0:T(8,128)(2,1)S(1)}, bf16[2,128,256]{2,1,0:T(8,128)(2,1)S(1)}, u32[]{:S(2)}, u32[]{:S(2)}) collective-permute-start(bf16[2,128,256]{2,1,0:T(8,128)(2,1)S(1)} %pad_maximum_fusion), channel_id=1, source_target_pairs={{0,1},{1,2},{2,3},{3,4},{4,5},{5,6},{6,7},{7,8},{8,9},{9,10},{10,1... | collective-permute-start | bytes 393224 | tf_op jit(solution)/shard_map/ppermute | solution.py:329
  60.4 27.6 %copy-start.4 = (bf16[2,128,256]{2,1,0:T(8,128)(2,1)}, bf16[2,128,256]{2,1,0:T(8,128)(2,1)S(1)}, u32[]{:S(2)}) copy-start(bf16[2,128,256]{2,1,0:T(8,128)(2,1)S(1)} %pad_maximum_fusion.2) | copy-start | bytes 393220
  60.4 11.8 %collective-permute-start.13 = (bf16[2,128,256]{2,1,0:T(8,128)(2,1)S(1)}, bf16[2,128,256]{2,1,0:T(8,128)(2,1)S(1)}, u32[]{:S(2)}, u32[]{:S(2)}) collective-permute-start(bf16[2,128,256]{2,1,0:T(8,128)(2,1)S(1)} %pad_maximum_fusion.2), channel_id=1, source_target_pairs={{0,3},{1,0},{2,1},{3,2},{4,7},{5,4},{6,5},{7,6},{8,11},{9,8},{10,9... | collective-permute-start | bytes 393224 | tf_op jit(solution)/shard_map/ppermute | solution.py:350
  62.5 10.1 %collective-permute-start.14 = (bf16[2,128,256]{2,1,0:T(8,128)(2,1)S(1)}, bf16[2,128,256]{2,1,0:T(8,128)(2,1)S(1)}, u32[]{:S(2)}, u32[]{:S(2)}) collective-permute-start(bf16[2,128,256]{2,1,0:T(8,128)(2,1)S(1)} %pad_maximum_fusion.2), channel_id=1, source_target_pairs={{0,2},{1,3},{2,0},{3,1},{4,6},{5,7},{6,4},{7,5},{8,10},{9,11},{10,... | collective-permute-start | bytes 393224 | tf_op jit(solution)/shard_map/ppermute | solution.py:350
  63.6 9.1 %collective-permute-start.15 = (bf16[2,128,256]{2,1,0:T(8,128)(2,1)S(1)}, bf16[2,128,256]{2,1,0:T(8,128)(2,1)S(1)}, u32[]{:S(2)}, u32[]{:S(2)}) collective-permute-start(bf16[2,128,256]{2,1,0:T(8,128)(2,1)S(1)} %pad_maximum_fusion.2), channel_id=1, source_target_pairs={{0,1},{1,2},{2,3},{3,0},{4,5},{5,6},{6,7},{7,4},{8,9},{9,10},{10,1... | collective-permute-start | bytes 393224 | tf_op jit(solution)/shard_map/ppermute | solution.py:350
  70.7 6.9 %collective-permute-start.2 = (bf16[2,128,256]{2,1,0:T(8,128)(2,1)S(1)}, bf16[2,128,256]{2,1,0:T(8,128)(2,1)S(1)}, u32[]{:S(2)}, u32[]{:S(2)}) collective-permute-start(bf16[2,128,256]{2,1,0:T(8,128)(2,1)S(1)} %pad_maximum_fusion.1), channel_id=1, source_target_pairs={{1,0},{2,1},{3,2},{4,3},{5,4},{6,5},{7,6},{8,7},{9,8},{10,9},{11,1... | collective-permute-start | bytes 393224 | tf_op jit(solution)/shard_map/ppermute | solution.py:330
  72.1 5.6 %copy-start.7 = (bf16[2,128,256]{2,1,0:T(8,128)(2,1)}, bf16[2,128,256]{2,1,0:T(8,128)(2,1)S(1)}, u32[]{:S(2)}) copy-start(bf16[2,128,256]{2,1,0:T(8,128)(2,1)S(1)} %collective-permute-done.1.refs_2_) | copy-start | bytes 393220
  72.1 15.9 %collective-permute-start.16 = (bf16[2,128,256]{2,1,0:T(8,128)(2,1)S(1)}, bf16[2,128,256]{2,1,0:T(8,128)(2,1)S(1)}, u32[]{:S(2)}, u32[]{:S(2)}) collective-permute-start(bf16[2,128,256]{2,1,0:T(8,128)(2,1)S(1)} %pad_maximum_fusion.2), channel_id=1, source_target_pairs={{0,16},{16,0},{1,17},{17,1},{2,18},{18,2},{3,19},{19,3},{4,20},{20... | collective-permute-start | bytes 393224 | tf_op jit(solution)/shard_map/ppermute | solution.py:351
  72.2 15.8 %copy-start.6 = (bf16[2,128,256]{2,1,0:T(8,128)(2,1)}, bf16[2,128,256]{2,1,0:T(8,128)(2,1)S(1)}, u32[]{:S(2)}) copy-start(bf16[2,128,256]{2,1,0:T(8,128)(2,1)S(1)} %collective-permute-done.13) | copy-start | bytes 393220
  72.2 15.9 %collective-permute-start.17 = (bf16[2,128,256]{2,1,0:T(8,128)(2,1)S(1)}, bf16[2,128,256]{2,1,0:T(8,128)(2,1)S(1)}, u32[]{:S(2)}, u32[]{:S(2)}) collective-permute-start(bf16[2,128,256]{2,1,0:T(8,128)(2,1)S(1)} %collective-permute-done.13), channel_id=1, source_target_pairs={{0,16},{16,0},{1,17},{17,1},{2,18},{18,2},{3,19},{19,3},{4,20},{20... | collective-permute-start | bytes 393224 | tf_op jit(solution)/shard_map/ppermute | solution.py:351
  72.7 15.3 %copy-start.8 = (bf16[2,128,256]{2,1,0:T(8,128)(2,1)}, bf16[2,128,256]{2,1,0:T(8,128)(2,1)S(1)}, u32[]{:S(2)}) copy-start(bf16[2,128,256]{2,1,0:T(8,128)(2,1)S(1)} %collective-permute-done.14) | copy-start | bytes 393220
  72.7 15.4 %collective-permute-start.18 = (bf16[2,128,256]{2,1,0:T(8,128)(2,1)S(1)}, bf16[2,128,256]{2,1,0:T(8,128)(2,1)S(1)}, u32[]{:S(2)}, u32[]{:S(2)}) collective-permute-start(bf16[2,128,256]{2,1,0:T(8,128)(2,1)S(1)} %collective-permute-done.14), channel_id=1, source_target_pairs={{0,16},{16,0},{1,17},{17,1},{2,18},{18,2},{3,19},{19,3},{4,20},{20... | collective-permute-start | bytes 393224 | tf_op jit(solution)/shard_map/ppermute | solution.py:351
  72.8 15.2 %copy-start.9 = (bf16[2,128,256]{2,1,0:T(8,128)(2,1)}, bf16[2,128,256]{2,1,0:T(8,128)(2,1)S(1)}, u32[]{:S(2)}) copy-start(bf16[2,128,256]{2,1,0:T(8,128)(2,1)S(1)} %collective-permute-done.15) | copy-start | bytes 393220
  72.8 15.3 %collective-permute-start.19 = (bf16[2,128,256]{2,1,0:T(8,128)(2,1)S(1)}, bf16[2,128,256]{2,1,0:T(8,128)(2,1)S(1)}, u32[]{:S(2)}, u32[]{:S(2)}) collective-permute-start(bf16[2,128,256]{2,1,0:T(8,128)(2,1)S(1)} %collective-permute-done.15), channel_id=1, source_target_pairs={{0,16},{16,0},{1,17},{17,1},{2,18},{18,2},{3,19},{19,3},{4,20},{20... | collective-permute-start | bytes 393224 | tf_op jit(solution)/shard_map/ppermute | solution.py:351
  (11 other events, 8.3 us)

commit v2 on v0

v2 whole, which is shorter than its diff:
```python
import functools
import math

import jax
import jax.numpy as jnp
from jax import lax
from jax.experimental import pallas as pl
from jax.experimental.pallas import tpu as pltpu
from jax.sharding import PartitionSpec as P

F32 = jnp.float32
BF16 = jnp.bfloat16
VMEM = pl.BlockSpec(memory_space=pltpu.VMEM)
SMEM = pl.BlockSpec(memory_space=pltpu.SMEM)
PARAMS = pltpu.CompilerParams(vmem_limit_bytes=16 * 1024 * 1024)
LANES = 128
SIN = (4.44287957, -7.30781668, 3.59777418, -0.79119939)
COS = (1.41420401, -6.97763732, 5.71518787, -1.72821389)


def here(array):
    return pltpu.with_memory_space_constraint(array, pltpu.VMEM)


def call(kernel, outs, vmem, smem=(), scratch=()):
    return pl.pallas_call(
        kernel,
        in_specs=[SMEM] * len(smem) + [VMEM] * len(vmem),
        out_specs=[VMEM] * len(outs),
        out_shape=[pltpu.VMEM(shape, kind) for shape, kind in outs],
        scratch_shapes=list(scratch),
        compiler_params=PARAMS,
    )(*smem, *[here(array) for array in vmem])


def radices(count):
    digits = []
    stride = 1
    while stride < count:
        radix = 4 if count // stride % 4 == 0 else 2
        digits.append((stride, radix))
        stride *= radix
    return digits


def pairs_at(axis, stride, offset):
    return [(place, place ^ (offset * stride)) for place in range(lax.axis_size(axis))]


def fill_places(offsets_ref, places_ref, first, slab, cell_line, slabs):
    cells, _, slots = offsets_ref.shape
    line = lax.broadcasted_iota(jnp.int32, (8, slots), 0)
    along_z_base = slab.astype(F32)
    for cell in range(cells):
        own = offsets_ref[cell]
        along_x = ((first + cell).astype(F32) + own[0:1]) / cell_line
        along_z = (along_z_base + own[2:3]) / slabs
        full = jnp.where(line == 0, along_x, jnp.where(line == 1, own[1:2], jnp.where(line == 2, along_z, 0.0)))
        high = full.astype(BF16).astype(F32)
        middle = (full - high).astype(BF16).astype(F32)
        low = full - high - middle
        parts = jnp.concatenate([high, middle, low, jnp.zeros_like(low)], axis=0)
        places_ref[:, cell * slots : (cell + 1) * slots] = parts.astype(BF16)


def fill_masked(counts_ref, features_ref, masked_ref):
    cells, slots, channels = features_ref.shape
    slot_ids = lax.broadcasted_iota(jnp.int32, (slots, channels), 0)
    for cell in range(cells):
        kept = jnp.where(slot_ids < counts_ref[cell], features_ref[cell].astype(F32), 0.0)
        masked_ref[cell * slots : (cell + 1) * slots, :] = kept.astype(BF16)


def fill_waves(waves_ref, padded_ref, turned_ref, flips):
    count = waves_ref.shape[1]
    waves = waves_ref[...].astype(F32)
    padded_ref[...] = jnp.zeros_like(padded_ref)
    for part in range(3):
        padded_ref[8 * part : 8 * part + 3, :] = waves
    rows = lax.broadcasted_iota(jnp.int32, (LANES, LANES), 0)
    columns = lax.broadcasted_iota(jnp.int32, (LANES, LANES), 1)
    order = jnp.where((rows ^ (flips & (LANES - 1))) == columns, 1.0, 0.0).astype(BF16)
    for block in range(count // LANES):
        source = pl.multiple_of((block ^ (flips // LANES)) * LANES, LANES)
        taken = padded_ref[:, pl.ds(source, LANES)].astype(BF16)
        turned = lax.dot_general(order, taken, (((1,), (1,)), ((), ())), preferred_element_type=F32)
        turned_ref[block * LANES : (block + 1) * LANES, :] = turned.astype(BF16)


def fill_table(waves, places_ref, table_ref):
    block = waves.shape[0]
    atoms = places_ref.shape[1]
    tile = math.gcd(atoms, 256)
    for start in range(0, atoms, tile):
        span = slice(start, start + tile)
        turns = jnp.dot(waves, places_ref[:, span], preferred_element_type=F32)
        part = turns - jnp.round(turns)
        square = part * part
        sine = part * (SIN[0] + square * (SIN[1] + square * (SIN[2] + square * SIN[3])))
        cosine = COS[0] + square * (COS[1] + square * (COS[2] + square * COS[3]))
        table_ref[:block, span] = (1.0 - sine * sine).astype(BF16)
        table_ref[block:, span] = (sine * cosine).astype(BF16)


def sums_of(table_ref, rows_ref):
    return jnp.dot(table_ref[...], rows_ref[...], preferred_element_type=F32)


def own_kernel(early, block, digits, lengths, counts_ref, features_ref, offsets_ref, waves_ref, *refs):
    masked_ref, places_ref, turned_ref = refs[:3]
    tables, sums = refs[3 : 3 + len(early)], refs[3 + len(early) : 3 + 2 * len(early)]
    padded_ref = refs[-1]
    cells = features_ref.shape[0]
    dev, slab = lax.axis_index("dev"), lax.axis_index("grp")
    flips = jnp.int32(0)
    weight = waves_ref.shape[1]
    for axis, stride, radix in digits:
        weight //= radix
        flips += ((slab if axis == "grp" else dev) // stride % radix) * weight
    fill_waves(waves_ref, padded_ref, turned_ref, flips)
    fill_places(offsets_ref, places_ref, dev * cells, slab, *lengths)
    fill_masked(counts_ref, features_ref, masked_ref)
    for place, table_ref, sums_ref in zip(early, tables, sums):
        fill_table(turned_ref[place * block : (place + 1) * block, :], places_ref, table_ref)
        sums_ref[...] = sums_of(table_ref, masked_ref)


def sibling_kernel(
    place, block, lengths, counts_ref, features_ref, offsets_ref, turned_ref, own_ref, start_ref,
    masked_ref, places_ref, first_ref, last_ref, piece_ref, table_ref,
):
    cells, slots, _ = features_ref.shape
    fill_places(offsets_ref, places_ref, lax.axis_index("dev") * cells, lax.axis_index("grp") ^ 1, *lengths)
    fill_masked(counts_ref, features_ref, masked_ref)
    for line, rows_ref in enumerate((own_ref, masked_ref)):
        first_ref[line] = rows_ref[:slots, :]
        last_ref[line] = rows_ref[(cells - 1) * slots :, :]
    fill_table(turned_ref[place * block : (place + 1) * block, :], places_ref, table_ref)
    piece_ref[...] = (start_ref[...] + sums_of(table_ref, masked_ref)).astype(piece_ref.dtype)


def continued_kernel(place, block, turned_ref, places_ref, masked_ref, start_ref, piece_ref, table_ref):
    fill_table(turned_ref[place * block : (place + 1) * block, :], places_ref, table_ref)
    piece_ref[...] = (start_ref[...] + sums_of(table_ref, masked_ref)).astype(piece_ref.dtype)


def both_kernel(
    place, block, turned_ref, own_places_ref, own_ref, places_ref, masked_ref, kept_ref, piece_ref, table_ref
):
    waves = turned_ref[place * block : (place + 1) * block, :]
    fill_table(waves, own_places_ref, kept_ref)
    total = sums_of(kept_ref, own_ref)
    fill_table(waves, places_ref, table_ref)
    piece_ref[...] = (total + sums_of(table_ref, masked_ref)).astype(piece_ref.dtype)


def rest_kernel(first, block, turned_ref, places_ref, _, *tables):
    for place, table_ref in enumerate(tables):
        start = first + place * block
        fill_table(turned_ref[start : start + block, :], places_ref, table_ref)


def short_kernel(lines, codes_ref, radial_ref, *refs):
    row_refs = refs[:lines]
    before_ref, after_ref, w_ref, _, message_ref, window_ref, starts_ref = refs[lines:]
    cells, slots, channels = message_ref.shape
    pairs = radial_ref.shape[1]
    slab, slabs = lax.axis_index("grp"), lax.axis_size("grp")
    for line in range(lines):
        base = line * (cells + 2)
        window_ref[base] = before_ref[line]
        for cell in range(cells):
            window_ref[base + 1 + cell] = row_refs[line][cell * slots : (cell + 1) * slots, :]
        window_ref[base + 1 + cells] = after_ref[line]
    nothing = lines * (cells + 2)
    window_ref[nothing] = jnp.zeros((slots, channels), BF16)
    for level in range(3):
        line = 0 if level == 1 else 1 if lines == 2 else 1 + level // 2
        inside = (slab + level >= 1) & (slab + level - 1 < slabs)
        for along in range(3):
            starts_ref[3 * level + along] = jnp.where(inside, line * (cells + 2) + along, -1)

    for cell in range(cells):
        total = None
        for pair in range(0, pairs, 2):
            blocks, taken = [], []
            for p in range(pair, min(pair + 2, pairs)):
                start = starts_ref[codes_ref[cell, p]]
                blocks.append(radial_ref[cell, p])
                taken.append(window_ref[jnp.where(start < 0, nothing, start + cell)])
            part = jnp.dot(
                jnp.concatenate(blocks, axis=1), jnp.concatenate(taken, axis=0), preferred_element_type=F32
            )
            total = part if total is None else total + part
        message_ref[cell] = jnp.dot(total.astype(BF16), w_ref[...], preferred_element_type=F32)


def add_kernel(count, radix, *refs):
    pieces, outs = refs[:count], refs[count:]
    total = pieces[0][...].astype(F32)
    for piece in pieces[1:]:
        total = total + piece[...].astype(F32)
    rows = total.shape[1] // radix
    for place, out in enumerate(outs):
        out[...] = total[:, place * rows : (place + 1) * rows].astype(out.dtype)


def add_and_cut(pieces, radix):
    trig, rows, channels = pieces[0].shape
    part = (trig, rows // radix, channels)
    types = [F32] + [BF16] * (radix - 1)
    if part[1] % 16:
        total = functools.reduce(jnp.add, [piece.astype(F32) for piece in pieces])
        return [
            total[:, place * part[1] : (place + 1) * part[1]].astype(kind) for place, kind in enumerate(types)
        ]
    return call(functools.partial(add_kernel, len(pieces), radix), [(part, kind) for kind in types], pieces)


def mixed(owned, waves, w_mix, factor_scale):
    waves = jnp.where(lax.broadcasted_iota(jnp.int32, waves.shape, 1) < 3, waves, 0.0)
    square = jnp.sum(waves * waves, axis=1, keepdims=True)
    kernel = jnp.exp(-square / 128.0) / (1.0 + square / 64.0)
    factors = (owned * factor_scale).astype(BF16)
    energy = jnp.dot(factors, w_mix, preferred_element_type=F32)
    return (energy * jnp.concatenate([kernel, kernel], axis=0)).astype(BF16)


def energy_kernel(count, factor_scale, *refs):
    pieces = refs[:count]
    turned_ref, w_mix_ref, _, energy_ref = refs[count:]
    trig, rows, channels = energy_ref.shape
    total = pieces[0][...].astype(F32)
    for piece in pieces[1:]:
        total = total + piece[...].astype(F32)
    owned = total.reshape(trig * rows, channels)
    energy = mixed(owned, turned_ref[:rows, :].astype(F32), w_mix_ref[...], factor_scale)
    energy_ref[...] = energy.reshape(trig, rows, channels)


def energy_of(pieces, turned, w_mix, factor_scale, after):
    trig, rows, channels = pieces[0].shape
    if rows % 16:
        total = functools.reduce(jnp.add, [piece.astype(F32) for piece in pieces])
        energy = mixed(total.reshape(trig * rows, channels), turned[:rows].astype(F32), w_mix, factor_scale)
        return energy.reshape(trig, rows, channels)
    (energy,) = call(
        functools.partial(energy_kernel, len(pieces), factor_scale),
        [((trig, rows, channels), BF16)],
        [*pieces, turned, w_mix, after],
    )
    return energy


def join_kernel(*refs):
    pieces, out_ref = refs[:-2], refs[-1]
    rows = pieces[0].shape[1]
    for place, piece in enumerate(pieces):
        out_ref[:, place * rows : (place + 1) * rows, :] = piece[...]


def joined(pieces, after):
    trig, rows, channels = pieces[0].shape
    if rows % 16:
        return jnp.concatenate(pieces, axis=1)
    (whole,) = call(join_kernel, [((trig, rows * len(pieces), channels), BF16)], [*pieces, after])
    return whole


def near_kernel(blocks, *refs):
    energies, tables = refs[:blocks], refs[blocks : 2 * blocks]
    out_ref, turned_ref = refs[2 * blocks :]
    for place, energy in enumerate(energies):
        turned_ref[place] = energy[...].astype(F32).T.astype(BF16)
    atoms = out_ref.shape[1]
    tile = math.gcd(atoms, 512)
    for start in range(0, atoms, tile):
        total = None
        for place, table_ref in enumerate(tables):
            part = jnp.dot(turned_ref[place], table_ref[:, start : start + tile], preferred_element_type=F32)
            total = part if total is None else total + part
        out_ref[:, start : start + tile] = total


def final_kernel(blocks, scale, counts_ref, near_ref, message_ref, masked_ref, *refs):
    energies, tables = refs[:blocks], refs[blocks : 2 * blocks]
    out_ref, turned_ref = refs[2 * blocks :]
    cells, slots, channels = out_ref.shape
    step = pl.program_id(0)

    @pl.when(step == 0)
    def _():
        for place, energy in enumerate(energies):
            turned_ref[place] = energy[...].astype(F32).T.astype(BF16)

    atoms = cells * slots
    span = pl.ds(pl.multiple_of(step * atoms, atoms), atoms)
    total = near_ref[:, span]
    for place, table_ref in enumerate(tables):
        total = total + jnp.dot(turned_ref[place], table_ref[:, span], preferred_element_type=F32)
    slot_ids = lax.broadcasted_iota(jnp.int32, (slots, channels), 0)
    for cell in range(cells):
        index = step * cells + cell
        rows = pl.ds(pl.multiple_of(index * slots, slots), slots)
        value = total[:, cell * slots : (cell + 1) * slots].T * scale + message_ref[index]
        value = value * (0.5 + 0.5 * jnp.tanh(0.5 * value))
        result = masked_ref[rows, :].astype(F32) + value
        out_ref[cell] = jnp.where(slot_ids < counts_ref[index], result, 0.0).astype(BF16)


def final_call(counts, near, message, masked, energies, tables, scale):
    cells, slots, channels = message.shape
    rows = tables[0].shape[0]
    blocks = len(tables)
    group = math.gcd(cells, 4)
    operands = [near, message, masked, *energies, *tables]
    return pl.pallas_call(
        functools.partial(final_kernel, blocks, scale),
        grid=(cells // group,),
        in_specs=[SMEM] + [VMEM] * len(operands),
        out_specs=pl.BlockSpec((group, slots, channels), lambda i: (i, 0, 0)),
        out_shape=jax.ShapeDtypeStruct(message.shape, BF16),
        scratch_shapes=[pltpu.VMEM((blocks, channels, rows), BF16)],
        compiler_params=PARAMS,
    )(counts, *[here(array) for array in operands])


def body(features, offsets, radial, neighbours, counts, wavevectors, w_msg, w_mix):
    _, cells, slots, channels = features.shape
    wave_count = wavevectors.shape[1]
    slabs, dev_count = lax.axis_size("grp"), lax.axis_size("dev")
    slab = lax.axis_index("grp")
    cell_line = cells * dev_count
    total_slots = slabs * cell_line * slots
    atoms = cells * slots
    lengths = (float(cell_line), float(slabs))
    features, offsets, counts = features[0], offsets[0], counts[0]

    swap = pairs_at("grp", 1, 1)
    sibling_offsets = lax.ppermute(offsets, "grp", swap)
    if slabs == 2:
        sibling_counts = lax.ppermute(counts, "grp", swap)
        sibling_features = lax.ppermute(features, "grp", swap)
    else:
        up = [(i, i + 1) for i in range(slabs - 1)]
        down = [(j, i) for i, j in up]
        near = [(lax.ppermute(counts, "grp", way), lax.ppermute(features, "grp", way)) for way in (up, down)]
        even = slab % 2 == 0
        sibling_counts = jnp.where(even, near[1][0], near[0][0])
        sibling_features = jnp.where(even, near[1][1], near[0][1])

    stages = [("dev", *digit) for digit in radices(dev_count)]
    stages += [("grp", 2 * stride, radix) for stride, radix in radices(slabs // 2)]
    digits = [("grp", 1, 2)] + stages
    half = wave_count // 2
    axis, stride, blocks = stages[0]
    block = half // blocks
    table = ((2 * block, atoms), BF16)
    sums = ((2 * block, channels), F32)
    piece = ((2 * block, channels), BF16)
    places_type = ((32, atoms), BF16)
    rows_type = ((atoms, channels), BF16)
    edge = ((2, slots, channels), BF16)
    scratch = [pltpu.VMEM(*table)]

    def sent(part, place):
        return lax.ppermute(part.reshape(2, block, channels), axis, pairs_at(axis, stride, place))

    early = list(range(1, blocks))[:2]
    masked, places, turned, *outs = call(
        functools.partial(own_kernel, early, block, digits, lengths),
        [rows_type, places_type, ((wave_count, 32), BF16)] + [table] * len(early) + [sums] * len(early),
        [features, offsets, wavevectors],
        [counts],
        [pltpu.VMEM((32, wave_count), F32)],
    )
    tables = dict(zip(early, outs))
    started = dict(zip(early, outs[len(early) :]))
    sibling, sibling_places, first, last, part = call(
        functools.partial(sibling_kernel, early[0], block, lengths),
        [rows_type, places_type, edge, edge, piece],
        [sibling_features, sibling_offsets, turned, masked, started[early[0]]],
        [sibling_counts],
        scratch,
    )
    received = {early[0]: sent(part, early[0])}
    for place in early[1:]:
        (part,) = call(
            functools.partial(continued_kernel, place, block),
            [piece],
            [turned, sibling_places, sibling, started[place]],
            scratch=scratch,
        )
        received[place] = sent(part, place)
    for place in [*range(1 + len(early), blocks), 0]:
        tables[place], part = call(
            functools.partial(both_kernel, place, block),
            [table, piece if place else sums],
            [turned, places, masked, sibling_places, sibling],
            scratch=scratch,
        )
        if place:
            received[place] = sent(part, place)
    pieces = [part.reshape(2, block, channels)] + [received[place] for place in range(1, blocks)]

    for axis, stride, radix in stages[1:]:
        parts = add_and_cut(pieces, radix)
        pieces = [parts[0]] + [
            lax.ppermute(parts[place], axis, pairs_at(axis, stride, place)) for place in range(1, radix)
        ]

    others = call(
        functools.partial(rest_kernel, half, block), [table] * blocks, [turned, places, parts[0]]
    )
    energy = energy_of(pieces, turned, w_mix, 1.0 / math.sqrt(total_slots), others[0])

    right = [(i, i + 1) for i in range(dev_count - 1)]
    if slabs == 2:
        lines = [masked, sibling]
    else:
        kept = [
            jnp.where(jnp.arange(slots)[None, :, None] < count[:, None, None], cell, jnp.bfloat16(0))
            for count, cell in near
        ]
        first = jnp.stack([masked[:slots]] + [line[0] for line in kept])
        last = jnp.stack([masked[-slots:]] + [line[-1] for line in kept])
        lines = [masked] + [line.reshape(atoms, channels) for line in kept]
    before = lax.ppermute(last, "dev", right)
    after = lax.ppermute(first, "dev", [(j, i) for i, j in right])
    window = (len(lines) * (cells + 2) + 1, slots, channels)
    (message,) = call(
        functools.partial(short_kernel, len(lines)),
        [((cells, slots, channels), F32)],
        [radial[0], *lines, before, after, w_msg, energy],
        [neighbours[0]],
        [pltpu.VMEM(window, BF16), pltpu.SMEM((9,), jnp.int32)],
    )

    for axis, stride, radix in reversed(stages[1:]):
        gathered = [energy] + [
            lax.ppermute(energy, axis, pairs_at(axis, stride, place)) for place in range(1, radix)
        ]
        energy = joined(gathered, message)
    axis, stride, blocks = stages[0]
    energies = [energy] + [
        lax.ppermute(energy, axis, pairs_at(axis, stride, place)) for place in range(1, blocks)
    ]
    others_energies = [lax.ppermute(part, "grp", swap) for part in energies]
    energies = [part.reshape(2 * block, channels) for part in energies]
    others_energies = [part.reshape(2 * block, channels) for part in others_energies]
    turned_energies = [pltpu.VMEM((blocks, channels, 2 * block), BF16)]
    (near_sum,) = call(
        functools.partial(near_kernel, blocks),
        [((channels, atoms), F32)],
        [*energies, *[tables[place] for place in range(blocks)]],
        scratch=turned_energies,
    )
    scale = 8.0 / math.sqrt(wave_count)
    result = final_call(counts, near_sum, message, masked, others_energies, others, scale)
    return result[None]


def solution(mesh):
    in_specs = (
        P("grp", "dev", None, None),
        P("grp", "dev", None, None),
        P("grp", "dev", None, None, None),
        P("grp", "dev", None),
        P("grp", "dev"),
        P(),
        P(),
        P(),
    )
    out_specs = P("grp", "dev", None, None)
    return jax.shard_map(body, mesh=mesh, in_specs=in_specs, out_specs=out_specs, check_vma=False)
```

time: 232 us -> 68.4 us (0.29)
  waiting for transfers between devices: 101 us -> 4.4 us
  other arithmetic: 40.8 us -> 0 us
  matrix products: 32.8 us -> 0 us
  Pallas kernels: 0 us -> 25 us
  local copies, waits for them, and re-layouts: 32.3 us -> 12 us
  starting transfers between devices: 10.9 us -> 26.2 us
  between operations: 13.4 us -> 0.33 us
    reduce_scatter x1 -> x0, waiting for transfers between devices: 45 us -> none  [body(): lax.psum_scatter(partial_sums.astype(jnp.bfloat16), 'dev', scatter_dimens...]
    all_gather x1 -> x0, waiting for transfers between devices: 44.3 us -> none  [body(): energy = lax.all_gather(energy_rows, 'dev', axis=0, tiled=True)]
    another operation x1 -> x0, other arithmetic: 33.8 us -> none
    dot_general x12 -> x0, matrix products: 32.8 us -> none  [the longest x8 17.5 us: body(): jnp.einsum('kab,kbc->kac', radial[0, :, neighbour], picked, preferred_ele...]
    gather x8 -> x0, local copies, waits for them, and re-layouts: 28.9 us -> none  [body(): picked = flat_window[rows_taken]]
    pallas_call x0 -> x12, Pallas kernels: none -> 25 us  [the longest x11 20.8 us: call(): pl.pallas_call(kernel, in_specs=[SMEM] * len(smem) + [VMEM] * len(vmem),...]
    ppermute x4 -> x21, starting transfers between devices: 10.6 us -> 26.2 us  [the longest x6 7.93 us: body(): lax.ppermute(energy, axis, pairs_at(axis, stride, place))]
    unnamed x30 -> x45, local copies, waits for them, and re-layouts: 3.31 us -> 12 us
  transfers between devices with their start and end apart: 7 -> 21, of which waited for: 4 -> 4; matrix products, arithmetic and copies ran while one was open for 40% -> 1% of each run, Pallas kernels for 0% -> 24%
where the time goes in v2:
time: 68.4 us; the launch traced here: 68 us
  starting transfers between devices  26.2 us (38%)
  Pallas kernels  25 us (37%)
  local copies, waits for them, and re-layouts  12 us (18%)
  waiting for transfers between devices  4.4 us (6%)
    pallas_call x11, Pallas kernels, call(): pl.pallas_call(kernel, in_specs=[SMEM] * len(smem) + [VMEM] * len(vmem),...  20.8 us
    unnamed x45, local copies, waits for them, and re-layouts  12 us
    ppermute x6, starting transfers between devices, body(): lax.ppermute(energy, axis, pairs_at(axis, stride, place))  7.93 us
    ppermute x3, starting transfers between devices, body(): lax.ppermute(parts[place], axis, pairs_at(axis, stride, place))  7.19 us
    pallas_call x1, Pallas kernels, final_call(): pl.pallas_call(functools.partial(final_kernel, blocks, scale), grid=(cell...  4.22 us
    ppermute x3, starting transfers between devices, sent(): lax.ppermute(part.reshape(2, block, channels), axis, pairs_at(axis, strid...  4.18 us
    ppermute x1, starting transfers between devices, body(): before = lax.ppermute(last, 'dev', right)  3.84 us
    ppermute x6, waiting for transfers between devices, body(): lax.ppermute(energy, axis, pairs_at(axis, stride, place))  3.63 us
  transfers between devices with their start and end apart: 21, of which 4 were waited for; matrix products, arithmetic and copies ran while one was open for 1% of the time, Pallas kernels for 24%

profile of v2, /device:TPU:0, one launch (start us, length us, event | category | flops | bytes accessed | tf_op | source)
XLA Modules:
  0.0 68.0 jit_solution(13830605844158562360)
XLA Ops:
  0.5 0.8 %copy.12 = f32[1,16,3,128]{3,2,1,0:T(4,128)S(1)} copy(f32[1,16,3,128]{3,1,2,0:T(8,128)} %param.9) | data formatting | bytes 49152 | tf_op args[1]
  1.8 1.2 %copy-done.1 = bf16[1,16,128,256]{3,2,1,0:T(8,128)(2,1)S(1)} copy-done((bf16[1,16,128,256]{3,2,1,0:T(8,128)(2,1)S(1)}, bf16[1,16,128,256]{3,2,1,0:T(8,128)(2,1)}, u32[]{:S(2)}) %copy-start.1) | copy-done | bytes 1048600
  3.0 0.7 %copy-done.18 = s32[3,1024]{1,0:T(4,128)S(1)} copy-done((s32[3,1024]{1,0:T(4,128)S(1)}, s32[3,1024]{1,0:T(4,128)}, u32[]{:S(2)}) %copy-start.18) | copy-done | bytes 12312
  3.7 0.7 copy-done.19
  4.4 2.9 %shard_map.82 = (bf16[2048,256]{1,0:T(8,128)(2,1)S(1)}, bf16[32,2048]{1,0:T(8,128)(2,1)S(1)}, bf16[1024,32]{1,0:T(8,128)(2,1)S(1)}, bf16[256,2048]{1,0:T(8,128)(...) custom-call(s32[16]{0:T(128)S(1)} %bitcast.36, ...), custom_call_target="tpu_custom_call" | custom-call | tf_op jit(solution)/shard_map/pallas_call | solution.py:26
  7.3 1.0 %copy-done.2 = bf16[256,2048]{1,0:T(8,128)(2,1)} copy-done((bf16[256,2048]{1,0:T(8,128)(2,1)}, bf16[256,2048]{1,0:T(8,128)(2,1)S(1)}, u32[]{:S(2)}) %copy-start.2) | copy-done | bytes 1048600
  8.3 1.0 %copy-done.4 = bf16[256,2048]{1,0:T(8,128)(2,1)} copy-done((bf16[256,2048]{1,0:T(8,128)(2,1)}, bf16[256,2048]{1,0:T(8,128)(2,1)S(1)}, u32[]{:S(2)}) %copy-start.4) | copy-done | bytes 1048600
  9.3 2.5 %shard_map.83 = (bf16[2048,256]{1,0:T(8,128)(2,1)S(1)}, bf16[32,2048]{1,0:T(8,128)(2,1)S(1)}, bf16[2,128,256]{2,1,0:T(8,128)(2,1)}, bf16[2,128,256]{2,1,0:T(8,128)(2,1)}, bf16[256,256]{1,0:T(8,128)(2,1)S(1)}) custom-call(s32[16]{0:T(128)S(1)} %collective-permute-done.counts_ref, bf16[16,128,256]{2,1,0:T(8,128)(2,1)S(1)} %collective-permute-done.1.features_ref, ...), custom_call_target="tpu_custom_call" | custom-call | tf_op jit(solution)/shard_map/pallas_call | solution.py:26
  11.8 2.1 %shard_map.86 = (bf16[256,2048]{1,0:T(8,128)(2,1)S(1)}, bf16[256,256]{1,0:T(8,128)(2,1)S(1)}) custom-call(bf16[1024,32]{1,0:T(8,128)(2,1)S(1)} %get-tuple-element.29.turned_ref.refs_4_, bf16[32,2048]{1,0:T(8,128)(2,1)S(1)} %get-tuple-element.30.own_places_ref.places_ref, bf16[2048,256]{1,0:T(8,128)(2,1)S(1)} %get-tuple-element.31.own_ref.refs_0_.masked_ref, ...), custom_call_target="tpu_custom_call" | custom-call | tf_op jit(solution)/shard_map/pallas_call | solution.py:26
  14.0 1.0 %copy-done.6 = bf16[256,2048]{1,0:T(8,128)(2,1)} copy-done((bf16[256,2048]{1,0:T(8,128)(2,1)}, bf16[256,2048]{1,0:T(8,128)(2,1)S(1)}, u32[]{:S(2)}) %copy-start.6) | copy-done | bytes 1048600
  14.9 3.5 %collective-permute-start.5 = (bf16[2,128,256]{2,1,0:T(8,128)(2,1)S(1)}, bf16[2,128,256]{2,1,0:T(8,128)(2,1)S(1)}, u32[]{:S(2)}, u32[]{:S(2)}) collective-permute-start(bf16[2,128,256]{2,1,0:T(8,128)(2,1)S(1)} %bitcast.39), channel_id=1, source_target_pairs={{0,3},{1,2},{2,1},{3,0},{4,7},{5,6},{6,5},{7,4},{8,11},{9,10},{10,... | collective-permute-start | bytes 393224 | tf_op jit(solution)/shard_map/ppermute | solution.py:367
  18.4 1.1 %shard_map.85 = bf16[256,256]{1,0:T(8,128)(2,1)S(1)} custom-call(bf16[1024,32]{1,0:T(8,128)(2,1)S(1)} %get-tuple-element.29.turned_ref.refs_4_, bf16[32,2048]{1,0:T(8,128)(2,1)S(1)} %get-tuple-element.33.places_ref, bf16[2048,256]{1,0:T(8,128)(2,1)S(1)} %get-tuple-element.34.masked_ref.refs_1_, f32[256,256]{1,0:T(8,128)S(1)} %get-tuple-element.37.start_ref), custom_call_target="tpu_custom_call" | custom-call | tf_op jit(solution)/shard_map/pallas_call | solution.py:26
  20.2 3.8 %collective-permute-start.12 = (bf16[2,128,256]{2,1,0:T(8,128)(2,1)}, bf16[2,128,256]{2,1,0:T(8,128)(2,1)S(1)}, u32[]{:S(2)}, u32[]{:S(2)}) collective-permute-start(bf16[2,128,256]{2,1,0:T(8,128)(2,1)} %get-tuple-element.44), channel_id=1, source_target_pairs={{0,1},{1,2},{2,3},{3,4},{4,5},{5,6},{6,7},{7,8},{8,9},{9,10},{10,1... | collective-permute-start | bytes 393224 | tf_op jit(solution)/shard_map/ppermute | solution.py:428
  24.1 1.6 %collective-permute-start.13 = (bf16[2,128,256]{2,1,0:T(8,128)(2,1)}, bf16[2,128,256]{2,1,0:T(8,128)(2,1)}, u32[]{:S(2)}, u32[]{:S(2)}) collective-permute-start(bf16[2,128,256]{2,1,0:T(8,128)(2,1)} %get-tuple-element.45), channel_id=1, source_target_pairs={{1,0},{2,1},{3,2},{4,3},{5,4},{6,5},{7,6},{8,7},{9,8},{10,9},{11,1... | collective-permute-start | bytes 393224 | tf_op jit(solution)/shard_map/ppermute | solution.py:429
  25.7 2.1 %shard_map.84 = (bf16[256,2048]{1,0:T(8,128)(2,1)S(1)}, f32[256,256]{1,0:T(8,128)S(1)}) custom-call(bf16[1024,32]{1,0:T(8,128)(2,1)S(1)} %get-tuple-element.29.turned_ref.refs_4_, bf16[32,2048]{1,0:T(8,128)(2,1)S(1)} %get-tuple-element.30.own_places_ref.places_ref, bf16[2048,256]{1,0:T(8,128)(2,1)S(1)} %get-tuple-element.31.own_ref.refs_0_.masked_ref, ...), custom_call_target="tpu_custom_call" | custom-call | tf_op jit(solution)/shard_map/pallas_call | solution.py:26
  27.8 1.0 %copy-done.8 = bf16[256,2048]{1,0:T(8,128)(2,1)} copy-done((bf16[256,2048]{1,0:T(8,128)(2,1)}, bf16[256,2048]{1,0:T(8,128)(2,1)S(1)}, u32[]{:S(2)}) %copy-start.8) | copy-done | bytes 1048600
  28.8 4.6 %collective-permute-start.6 = (bf16[2,32,256]{2,1,0:T(8,128)(2,1)S(1)}, bf16[2,32,256]{2,1,0:T(8,128)(2,1)S(1)}, u32[]{:S(2)}, u32[]{:S(2)}) collective-permute-start(bf16[2,32,256]{2,1,0:T(8,128)(2,1)S(1)} %get-tuple-element.40), channel_id=1, source_target_pairs={{0,4},{1,5},{2,6},{3,7},{4,0},{5,1},{6,2},{7,3},{8,12},{9,13},{10,... | collective-permute-start | bytes 98312 | tf_op jit(solution)/shard_map/ppermute | solution.py:409
  33.4 2.6 %collective-permute-start.7 = (bf16[2,32,256]{2,1,0:T(8,128)(2,1)S(1)}, bf16[2,32,256]{2,1,0:T(8,128)(2,1)S(1)}, u32[]{:S(2)}, u32[]{:S(2)}) collective-permute-start(bf16[2,32,256]{2,1,0:T(8,128)(2,1)S(1)} %get-tuple-element.41), channel_id=1, source_target_pairs={{0,8},{1,9},{2,10},{3,11},{4,12},{5,13},{6,14},{7,15},{8,0},{9,1},... | collective-permute-start | bytes 98312 | tf_op jit(solution)/shard_map/ppermute | solution.py:409
  36.0 3.0 %shard_map.88 = (bf16[256,2048]{1,0:T(8,128)(2,1)S(1)}, bf16[256,2048]{1,0:T(8,128)(2,1)S(1)}, bf16[256,2048]{1,0:T(8,128)(2,1)S(1)}, bf16[256,2048]{1,0:T(8,128)(2,1)S(1)}) custom-call(bf16[1024,32]{1,0:T(8,128)(2,1)S(1)} %get-tuple-element.29.turned_ref.refs_4_, bf16[32,2048]{1,0:T(8,128)(2,1)S(1)} %get-tuple-element.30.own_places_ref.places_ref, ...), custom_call_target="tpu_custom_call" | custom-call | tf_op jit(solution)/shard_map/pallas_call | solution.py:26
  39.1 1.0 %copy-done.10 = bf16[256,2048]{1,0:T(8,128)(2,1)} copy-done((bf16[256,2048]{1,0:T(8,128)(2,1)}, bf16[256,2048]{1,0:T(8,128)(2,1)S(1)}, u32[]{:S(2)}) %copy-start.10) | copy-done | bytes 1048600
  40.0 1.0 %copy-done.12 = bf16[256,2048]{1,0:T(8,128)(2,1)} copy-done((bf16[256,2048]{1,0:T(8,128)(2,1)}, bf16[256,2048]{1,0:T(8,128)(2,1)S(1)}, u32[]{:S(2)}) %copy-start.12) | copy-done | bytes 1048600
  41.0 0.7 %collective-permute-done.8.refs_3_ = bf16[2,32,256]{2,1,0:T(8,128)(2,1)S(1)} collective-permute-done((bf16[2,32,256]{2,1,0:T(8,128)(2,1)S(1)}, bf16[2,32,256]{2,1,0:T(8,128)(2,1)S(1)}, u32[]{:S(2)}, u32[]{:S(2)}) %collective-permute-start.8) | collective-permute-done | bytes 32800 | tf_op jit(solution)/shard_map/ppermute | solution.py:409
  42.0 1.9 %collective-permute-start.10 = (bf16[2,32,256]{2,1,0:T(8,128)(2,1)S(1)}, bf16[2,32,256]{2,1,0:T(8,128)(2,1)S(1)}, u32[]{:S(2)}, u32[]{:S(2)}) collective-permute-start(bf16[2,32,256]{2,1,0:T(8,128)(2,1)S(1)} %shard_map.89.refs_5_.refs_0_), channel_id=1, source_target_pairs={{0,8},{1,9},{2,10},{3,11},{4,12},{5,13},{6,14},{7,15},{8,0},{9,1},... | collective-permute-start | bytes 98312 | tf_op jit(solution)/shard_map/ppermute | solution.py:441
  43.9 1.9 %collective-permute-start.11 = (bf16[2,32,256]{2,1,0:T(8,128)(2,1)S(1)}, bf16[2,32,256]{2,1,0:T(8,128)(2,1)S(1)}, u32[]{:S(2)}, u32[]{:S(2)}) collective-permute-start(bf16[2,32,256]{2,1,0:T(8,128)(2,1)S(1)} %shard_map.89.refs_5_.refs_0_), channel_id=1, source_target_pairs={{0,12},{1,13},{2,14},{3,15},{4,8},{5,9},{6,10},{7,11},{8,4},{9,5},... | collective-permute-start | bytes 98312 | tf_op jit(solution)/shard_map/ppermute | solution.py:441
  46.5 2.2 %copy-done = bf16[1,16,8,128,128]{4,3,2,1,0:T(8,128)(2,1)S(1)} copy-done((bf16[1,16,8,128,128]{4,3,2,1,0:T(8,128)(2,1)S(1)}, bf16[1,16,8,128,128]{4,3,2,1,0:T(8,128)(2,1)}, u32[]{:S(2)}) %copy-start) | copy-done | bytes 4194328
  48.7 5.5 %shard_map.90.refs_4_.message_ref = f32[16,128,256]{2,1,0:T(8,128)S(1)} custom-call(s32[16,8]{1,0:T(8,128)S(1)} %copy.10.codes_ref, bf16[16,8,128,128]{3,2,1,0:T(8,128)(2,1)S(1)} %bitcast.20, bf16[2048,256]{1,0:T(8,128)(2,1)S(1)} %get-tuple-element.31.own_ref.refs_0_.masked_ref, bf16[2048,256]{1,0:T(8,128)(2,1)S(1)} %get-tuple-element.34.masked_ref.refs_1_, ...), custom_call_target="tpu_custom_call" | custom-call | tf_op jit(solution)/shard_map/pallas_call | solution.py:26
  54.3 1.7 %collective-permute-start.15 = (bf16[2,128,256]{2,1,0:T(8,128)(2,1)S(1)}, bf16[2,128,256]{2,1,0:T(8,128)(2,1)S(1)}, u32[]{:S(2)}, u32[]{:S(2)}) collective-permute-start(bf16[2,128,256]{2,1,0:T(8,128)(2,1)S(1)} %shard_map.91), channel_id=1, source_target_pairs={{0,2},{1,3},{2,0},{3,1},{4,6},{5,7},{6,4},{7,5},{8,10},{9,11},{10,... | collective-permute-start | bytes 393224 | tf_op jit(solution)/shard_map/ppermute | solution.py:446
  56.0 1.8 %collective-permute-start.16 = (bf16[2,128,256]{2,1,0:T(8,128)(2,1)S(1)}, bf16[2,128,256]{2,1,0:T(8,128)(2,1)S(1)}, u32[]{:S(2)}, u32[]{:S(2)}) collective-permute-start(bf16[2,128,256]{2,1,0:T(8,128)(2,1)S(1)} %shard_map.91), channel_id=1, source_target_pairs={{0,3},{1,2},{2,1},{3,0},{4,7},{5,6},{6,5},{7,4},{8,11},{9,10},{10,... | collective-permute-start | bytes 393224 | tf_op jit(solution)/shard_map/ppermute | solution.py:446
  57.8 1.5 %collective-permute-done.14 = bf16[2,128,256]{2,1,0:T(8,128)(2,1)S(1)} collective-permute-done((bf16[2,128,256]{2,1,0:T(8,128)(2,1)S(1)}, bf16[2,128,256]{2,1,0:T(8,128)(2,1)S(1)}, u32[]{:S(2)}, u32[]{:S(2)}) %collective-permute-start.14) | collective-permute-done | bytes 131104 | tf_op jit(solution)/shard_map/ppermute | solution.py:446
  59.8 2.1 %collective-permute-done.16 = bf16[2,128,256]{2,1,0:T(8,128)(2,1)S(1)} collective-permute-done((bf16[2,128,256]{2,1,0:T(8,128)(2,1)S(1)}, bf16[2,128,256]{2,1,0:T(8,128)(2,1)S(1)}, u32[]{:S(2)}, u32[]{:S(2)}) %collective-permute-start.16) | collective-permute-done | bytes 131104 | tf_op jit(solution)/shard_map/ppermute | solution.py:446
  61.9 1.3 %shard_map.92.near_ref = f32[256,2048]{1,0:T(8,128)S(1)} custom-call(bf16[256,256]{1,0:T(8,128)(2,1)S(1)} %bitcast.23, bf16[256,256]{1,0:T(8,128)(2,1)S(1)} %bitcast.32, bf16[256,256]{1,0:T(8,128)(2,1)S(1)} %bitcast.33, bf16[256,256]{1,0:T(8,128)(2,1)S(1)} %bitcast.34, bf16[256,2048]{1,0:T(8,128)(2,1)S(1)} %copy-done.9, bf16[256,2048]{1,0:T(8,128)(2,1)S(1)} %copy-done.3, ...), custom_call_target="tpu_custom_call" | custom-call | tf_op jit(solution)/shard_map/pallas_call | solution.py:26
  63.7 4.2 %shard_map.93 = bf16[16,128,256]{2,1,0:T(8,128)(2,1)} custom-call(s32[16]{0:T(128)S(1)} %bitcast.37, f32[256,2048]{1,0:T(8,128)S(1)} %shard_map.92.near_ref, f32[16,128,256]{2,1,0:T(8,128)S(1)} %shard_map.90.refs_4_.message_ref, bf16[2048,256]{1,0:T(8,128)(2,1)S(1)} %get-tuple-element.31.own_ref.refs_0_.masked_ref, bf16[256,256]{1,0:T(8,128)(2,1)S(1)} %bitcast.25, ...), custom_call_target="tpu_custom_call" | custom-call | tf_op jit(solution)/shard_map/pallas_call | solution.py:317
  (68 shorter events, 3.8 us)
Async XLA Ops:
  0.0 9.3 %collective-permute-start.1 = (bf16[16,128,256]{2,1,0:T(8,128)(2,1)}, bf16[16,128,256]{2,1,0:T(8,128)(2,1)S(1)}, u32[]{:S(2)}, u32[]{:S(2)}) collective-permute-start(bf16[16,128,256]{2,1,0:T(8,128)(2,1)} %bitcast.21), channel_id=1, source_target_pairs={{0,16},{16,0},{1,17},{17,1},{2,18},{18,2},{3,19},{19,3},{4,20},{20... | collective-permute-start | bytes 3145736 | tf_op jit(solution)/shard_map/ppermute | solution.py:343
  1.2 8.1 %collective-permute-start.2 = (f32[16,3,128]{2,1,0:T(4,128)S(1)}, f32[16,3,128]{2,1,0:T(4,128)S(1)}, u32[]{:S(2)}, u32[]{:S(2)}) collective-permute-start(f32[16,3,128]{2,1,0:T(4,128)S(1)} %bitcast.30), channel_id=1, source_target_pairs={{0,16},{16,0},{1,17},{17,1},{2,18},{18,2},{3,19},{19,3},{4,20},{20... | collective-permute-start | bytes 73736 | tf_op jit(solution)/shard_map/ppermute | solution.py:340
  1.3 8.0 %collective-permute-start = (s32[16]{0:T(128)}, s32[16]{0:T(128)S(1)}, u32[]{:S(2)}, u32[]{:S(2)}) collective-permute-start(s32[16]{0:T(128)} %bitcast.35), channel_id=1, source_target_pairs={{0,16},{16,0},{1,17},{17,1},{2,18},{18,2},{3,19},{19,3},{4,20},{20... | collective-permute-start | bytes 200 | tf_op jit(solution)/shard_map/ppermute | solution.py:342
  14.9 13.9 %collective-permute-start.5 = (bf16[2,128,256]{2,1,0:T(8,128)(2,1)S(1)}, bf16[2,128,256]{2,1,0:T(8,128)(2,1)S(1)}, u32[]{:S(2)}, u32[]{:S(2)}) collective-permute-start(bf16[2,128,256]{2,1,0:T(8,128)(2,1)S(1)} %bitcast.39), channel_id=1, source_target_pairs={{0,3},{1,2},{2,1},{3,0},{4,7},{5,6},{6,5},{7,4},{8,11},{9,10},{10,... | collective-permute-start | bytes 393224 | tf_op jit(solution)/shard_map/ppermute | solution.py:367
  19.5 22.2 %copy-start.17 = (bf16[256,256]{1,0:T(8,128)(2,1)S(1)}, bf16[256,256]{1,0:T(8,128)(2,1)}, u32[]{:S(2)}) copy-start(bf16[256,256]{1,0:T(8,128)(2,1)} %refs_5_.1) | copy-start | bytes 393220
  19.6 9.2 %collective-permute-start.4 = (bf16[2,128,256]{2,1,0:T(8,128)(2,1)S(1)}, bf16[2,128,256]{2,1,0:T(8,128)(2,1)S(1)}, u32[]{:S(2)}, u32[]{:S(2)}) collective-permute-start(bf16[2,128,256]{2,1,0:T(8,128)(2,1)S(1)} %bitcast.29), channel_id=1, source_target_pairs={{0,2},{1,3},{2,0},{3,1},{4,6},{5,7},{6,4},{7,5},{8,10},{9,11},{10,... | collective-permute-start | bytes 393224 | tf_op jit(solution)/shard_map/ppermute | solution.py:367
  20.1 8.6 %collective-permute-start.3 = (bf16[2,128,256]{2,1,0:T(8,128)(2,1)S(1)}, bf16[2,128,256]{2,1,0:T(8,128)(2,1)S(1)}, u32[]{:S(2)}, u32[]{:S(2)}) collective-permute-start(bf16[2,128,256]{2,1,0:T(8,128)(2,1)S(1)} %bitcast.38), channel_id=1, source_target_pairs={{0,1},{1,0},{2,3},{3,2},{4,5},{5,4},{6,7},{7,6},{8,9},{9,8},{10,11... | collective-permute-start | bytes 393224 | tf_op jit(solution)/shard_map/ppermute | solution.py:367
  20.2 26.2 %collective-permute-start.12 = (bf16[2,128,256]{2,1,0:T(8,128)(2,1)}, bf16[2,128,256]{2,1,0:T(8,128)(2,1)S(1)}, u32[]{:S(2)}, u32[]{:S(2)}) collective-permute-start(bf16[2,128,256]{2,1,0:T(8,128)(2,1)} %get-tuple-element.44), channel_id=1, source_target_pairs={{0,1},{1,2},{2,3},{3,4},{4,5},{5,6},{6,7},{7,8},{8,9},{9,10},{10,1... | collective-permute-start | bytes 393224 | tf_op jit(solution)/shard_map/ppermute | solution.py:428
  24.1 22.3 %copy-start.21 = (s32[1,16,8]{1,2,0:T(8,128)S(1)}, s32[1,16,8]{1,2,0:T(8,128)}, u32[]{:S(2)}) copy-start(s32[1,16,8]{1,2,0:T(8,128)} %param.11) | copy-start | bytes 1540
  24.1 22.4 %copy-start.16 = (bf16[256,256]{1,0:T(8,128)(2,1)S(1)}, bf16[256,256]{1,0:T(8,128)(2,1)}, u32[]{:S(2)}) copy-start(bf16[256,256]{1,0:T(8,128)(2,1)} %refs_4_.1) | copy-start | bytes 393220
  24.1 22.4 %collective-permute-start.13 = (bf16[2,128,256]{2,1,0:T(8,128)(2,1)}, bf16[2,128,256]{2,1,0:T(8,128)(2,1)}, u32[]{:S(2)}, u32[]{:S(2)}) collective-permute-start(bf16[2,128,256]{2,1,0:T(8,128)(2,1)} %get-tuple-element.45), channel_id=1, source_target_pairs={{1,0},{2,1},{3,2},{4,3},{5,4},{6,5},{7,6},{8,7},{9,8},{10,9},{11,1... | collective-permute-start | bytes 393224 | tf_op jit(solution)/shard_map/ppermute | solution.py:429
  28.8 12.2 %collective-permute-start.6 = (bf16[2,32,256]{2,1,0:T(8,128)(2,1)S(1)}, bf16[2,32,256]{2,1,0:T(8,128)(2,1)S(1)}, u32[]{:S(2)}, u32[]{:S(2)}) collective-permute-start(bf16[2,32,256]{2,1,0:T(8,128)(2,1)S(1)} %get-tuple-element.40), channel_id=1, source_target_pairs={{0,4},{1,5},{2,6},{3,7},{4,0},{5,1},{6,2},{7,3},{8,12},{9,13},{10,... | collective-permute-start | bytes 98312 | tf_op jit(solution)/shard_map/ppermute | solution.py:409
  33.4 7.6 %collective-permute-start.7 = (bf16[2,32,256]{2,1,0:T(8,128)(2,1)S(1)}, bf16[2,32,256]{2,1,0:T(8,128)(2,1)S(1)}, u32[]{:S(2)}, u32[]{:S(2)}) collective-permute-start(bf16[2,32,256]{2,1,0:T(8,128)(2,1)S(1)} %get-tuple-element.41), channel_id=1, source_target_pairs={{0,8},{1,9},{2,10},{3,11},{4,12},{5,13},{6,14},{7,15},{8,0},{9,1},... | collective-permute-start | bytes 98312 | tf_op jit(solution)/shard_map/ppermute | solution.py:409
  36.0 5.7 %collective-permute-start.8 = (bf16[2,32,256]{2,1,0:T(8,128)(2,1)S(1)}, bf16[2,32,256]{2,1,0:T(8,128)(2,1)S(1)}, u32[]{:S(2)}, u32[]{:S(2)}) collective-permute-start(bf16[2,32,256]{2,1,0:T(8,128)(2,1)S(1)} %get-tuple-element.42), channel_id=1, source_target_pairs={{0,12},{1,13},{2,14},{3,15},{4,8},{5,9},{6,10},{7,11},{8,4},{9,5},... | collective-permute-start | bytes 98312 | tf_op jit(solution)/shard_map/ppermute | solution.py:409
  42.0 12.2 %collective-permute-start.10 = (bf16[2,32,256]{2,1,0:T(8,128)(2,1)S(1)}, bf16[2,32,256]{2,1,0:T(8,128)(2,1)S(1)}, u32[]{:S(2)}, u32[]{:S(2)}) collective-permute-start(bf16[2,32,256]{2,1,0:T(8,128)(2,1)S(1)} %shard_map.89.refs_5_.refs_0_), channel_id=1, source_target_pairs={{0,8},{1,9},{2,10},{3,11},{4,12},{5,13},{6,14},{7,15},{8,0},{9,1},... | collective-permute-start | bytes 98312 | tf_op jit(solution)/shard_map/ppermute | solution.py:441
  43.9 10.3 %collective-permute-start.11 = (bf16[2,32,256]{2,1,0:T(8,128)(2,1)S(1)}, bf16[2,32,256]{2,1,0:T(8,128)(2,1)S(1)}, u32[]{:S(2)}, u32[]{:S(2)}) collective-permute-start(bf16[2,32,256]{2,1,0:T(8,128)(2,1)S(1)} %shard_map.89.refs_5_.refs_0_), channel_id=1, source_target_pairs={{0,12},{1,13},{2,14},{3,15},{4,8},{5,9},{6,10},{7,11},{8,4},{9,5},... | collective-permute-start | bytes 98312 | tf_op jit(solution)/shard_map/ppermute | solution.py:441
  45.8 8.4 %collective-permute-start.9 = (bf16[2,32,256]{2,1,0:T(8,128)(2,1)S(1)}, bf16[2,32,256]{2,1,0:T(8,128)(2,1)S(1)}, u32[]{:S(2)}, u32[]{:S(2)}) collective-permute-start(bf16[2,32,256]{2,1,0:T(8,128)(2,1)S(1)} %shard_map.89.refs_5_.refs_0_), channel_id=1, source_target_pairs={{0,4},{1,5},{2,6},{3,7},{4,0},{5,1},{6,2},{7,3},{8,12},{9,13},{10,... | collective-permute-start | bytes 98312 | tf_op jit(solution)/shard_map/ppermute | solution.py:441
  46.5 2.2 %copy-start = (bf16[1,16,8,128,128]{4,3,2,1,0:T(8,128)(2,1)S(1)}, bf16[1,16,8,128,128]{4,3,2,1,0:T(8,128)(2,1)}, u32[]{:S(2)}) copy-start(bf16[1,16,8,128,128]{4,3,2,1,0:T(8,128)(2,1)} %param.10) | copy-start | bytes 12582916
  48.7 13.2 %copy-start.7 = (bf16[256,2048]{1,0:T(8,128)(2,1)S(1)}, bf16[256,2048]{1,0:T(8,128)(2,1)}, u32[]{:S(2)}) copy-start(bf16[256,2048]{1,0:T(8,128)(2,1)} %copy-done.6) | copy-start | bytes 3145732
  48.7 13.2 %copy-start.9 = (bf16[256,2048]{1,0:T(8,128)(2,1)S(1)}, bf16[256,2048]{1,0:T(8,128)(2,1)}, u32[]{:S(2)}) copy-start(bf16[256,2048]{1,0:T(8,128)(2,1)} %copy-done.8) | copy-start | bytes 3145732
  54.2 7.7 %copy-start.3 = (bf16[256,2048]{1,0:T(8,128)(2,1)S(1)}, bf16[256,2048]{1,0:T(8,128)(2,1)}, u32[]{:S(2)}) copy-start(bf16[256,2048]{1,0:T(8,128)(2,1)} %copy-done.2) | copy-start | bytes 3145732
  54.2 7.7 %copy-start.5 = (bf16[256,2048]{1,0:T(8,128)(2,1)S(1)}, bf16[256,2048]{1,0:T(8,128)(2,1)}, u32[]{:S(2)}) copy-start(bf16[256,2048]{1,0:T(8,128)(2,1)} %copy-done.4) | copy-start | bytes 3145732
  54.2 5.0 %collective-permute-start.14 = (bf16[2,128,256]{2,1,0:T(8,128)(2,1)S(1)}, bf16[2,128,256]{2,1,0:T(8,128)(2,1)S(1)}, u32[]{:S(2)}, u32[]{:S(2)}) collective-permute-start(bf16[2,128,256]{2,1,0:T(8,128)(2,1)S(1)} %shard_map.91), channel_id=1, source_target_pairs={{0,1},{1,0},{2,3},{3,2},{4,5},{5,4},{6,7},{7,6},{8,9},{9,8},{10,11... | collective-permute-start | bytes 393224 | tf_op jit(solution)/shard_map/ppermute | solution.py:446
  54.3 5.0 %collective-permute-start.15 = (bf16[2,128,256]{2,1,0:T(8,128)(2,1)S(1)}, bf16[2,128,256]{2,1,0:T(8,128)(2,1)S(1)}, u32[]{:S(2)}, u32[]{:S(2)}) collective-permute-start(bf16[2,128,256]{2,1,0:T(8,128)(2,1)S(1)} %shard_map.91), channel_id=1, source_target_pairs={{0,2},{1,3},{2,0},{3,1},{4,6},{5,7},{6,4},{7,5},{8,10},{9,11},{10,... | collective-permute-start | bytes 393224 | tf_op jit(solution)/shard_map/ppermute | solution.py:446
  56.0 5.9 %collective-permute-start.16 = (bf16[2,128,256]{2,1,0:T(8,128)(2,1)S(1)}, bf16[2,128,256]{2,1,0:T(8,128)(2,1)S(1)}, u32[]{:S(2)}, u32[]{:S(2)}) collective-permute-start(bf16[2,128,256]{2,1,0:T(8,128)(2,1)S(1)} %shard_map.91), channel_id=1, source_target_pairs={{0,3},{1,2},{2,1},{3,0},{4,7},{5,6},{6,5},{7,4},{8,11},{9,10},{10,... | collective-permute-start | bytes 393224 | tf_op jit(solution)/shard_map/ppermute | solution.py:446
  57.8 5.5 %collective-permute-start.17 = (bf16[2,128,256]{2,1,0:T(8,128)(2,1)S(1)}, bf16[2,128,256]{2,1,0:T(8,128)(2,1)S(1)}, u32[]{:S(2)}, u32[]{:S(2)}) collective-permute-start(bf16[2,128,256]{2,1,0:T(8,128)(2,1)S(1)} %shard_map.91), channel_id=1, source_target_pairs={{0,16},{16,0},{1,17},{17,1},{2,18},{18,2},{3,19},{19,3},{4,20},{20... | collective-permute-start | bytes 393224 | tf_op jit(solution)/shard_map/ppermute | solution.py:448
  59.3 4.0 %collective-permute-start.18 = (bf16[2,128,256]{2,1,0:T(8,128)(2,1)S(1)}, bf16[2,128,256]{2,1,0:T(8,128)(2,1)S(1)}, u32[]{:S(2)}, u32[]{:S(2)}) collective-permute-start(bf16[2,128,256]{2,1,0:T(8,128)(2,1)S(1)} %collective-permute-done.14), channel_id=1, source_target_pairs={{0,16},{16,0},{1,17},{17,1},{2,18},{18,2},{3,19},{19,3},{4,20},{20... | collective-permute-start | bytes 393224 | tf_op jit(solution)/shard_map/ppermute | solution.py:448
  59.4 3.9 %collective-permute-start.19 = (bf16[2,128,256]{2,1,0:T(8,128)(2,1)S(1)}, bf16[2,128,256]{2,1,0:T(8,128)(2,1)S(1)}, u32[]{:S(2)}, u32[]{:S(2)}) collective-permute-start(bf16[2,128,256]{2,1,0:T(8,128)(2,1)S(1)} %collective-permute-done.15), channel_id=1, source_target_pairs={{0,16},{16,0},{1,17},{17,1},{2,18},{18,2},{3,19},{19,3},{4,20},{20... | collective-permute-start | bytes 393224 | tf_op jit(solution)/shard_map/ppermute | solution.py:448
  61.9 1.4 %collective-permute-start.20 = (bf16[2,128,256]{2,1,0:T(8,128)(2,1)S(1)}, bf16[2,128,256]{2,1,0:T(8,128)(2,1)S(1)}, u32[]{:S(2)}, u32[]{:S(2)}) collective-permute-start(bf16[2,128,256]{2,1,0:T(8,128)(2,1)S(1)} %collective-permute-done.16), channel_id=1, source_target_pairs={{0,16},{16,0},{1,17},{17,1},{2,18},{18,2},{3,19},{19,3},{4,20},{20... | collective-permute-start | bytes 393224 | tf_op jit(solution)/shard_map/ppermute | solution.py:448
  61.9 1.5 %copy-start.13 = (bf16[256,2048]{1,0:T(8,128)(2,1)S(1)}, bf16[256,2048]{1,0:T(8,128)(2,1)}, u32[]{:S(2)}) copy-start(bf16[256,2048]{1,0:T(8,128)(2,1)} %copy-done.12) | copy-start | bytes 3145732
  61.9 1.8 %copy-start.15 = (bf16[256,2048]{1,0:T(8,128)(2,1)S(1)}, bf16[256,2048]{1,0:T(8,128)(2,1)}, u32[]{:S(2)}) copy-start(bf16[256,2048]{1,0:T(8,128)(2,1)} %copy-done.14) | copy-start | bytes 3145732
  61.9 1.8 %copy-start.20 = (s32[1,16]{1,0:T(1,128)S(1)}, s32[1,16]{1,0:T(1,128)}, u32[]{:S(2)}) copy-start(s32[1,16]{1,0:T(1,128)} %param.12) | copy-start | bytes 196
  (11 other events, 10.9 us)

commit v3 on v2

--- a/solution.py
+++ b/solution.py
@@ -12,25 +12,58 @@
 BF16 = jnp.bfloat16
 VMEM = pl.BlockSpec(memory_space=pltpu.VMEM)
 SMEM = pl.BlockSpec(memory_space=pltpu.SMEM)
-PARAMS = pltpu.CompilerParams(vmem_limit_bytes=16 * 1024 * 1024)
+HBM = pl.BlockSpec(memory_space=pltpu.HBM)
+PARAMS = pltpu.CompilerParams(vmem_limit_bytes=14 * 1024 * 1024)
 LANES = 128
+COST = 0
 SIN = (4.44287957, -7.30781668, 3.59777418, -0.79119939)
 COS = (1.41420401, -6.97763732, 5.71518787, -1.72821389)
 
 
-def here(array):
-    return pltpu.with_memory_space_constraint(array, pltpu.VMEM)
-
-
-def call(kernel, outs, vmem, smem=(), scratch=()):
+def call(kernel, outs, operands, scratch=(), held=(), flops=0):
+    ahead = len(operands)
+    operands = list(operands) + [(VMEM, array) for array in held]
+
+    def without_held(*refs):
+        kernel(*refs[:ahead], *refs[len(operands) :])
+
     return pl.pallas_call(
-        kernel,
-        in_specs=[SMEM] * len(smem) + [VMEM] * len(vmem),
-        out_specs=[VMEM] * len(outs),
-        out_shape=[pltpu.VMEM(shape, kind) for shape, kind in outs],
+        without_held,
+        in_specs=[place for place, _ in operands],
+        out_specs=[place for place, _ in outs],
+        out_shape=[place.memory_space(*kind) for place, kind in outs],
         scratch_shapes=list(scratch),
         compiler_params=PARAMS,
-    )(*smem, *[here(array) for array in vmem])
+        cost_estimate=pl.CostEstimate(flops=flops, bytes_accessed=flops // 300, transcendentals=0),
+    )(
+        *[
+            array if place is SMEM else pltpu.with_memory_space_constraint(array, place.memory_space)
+            for place, array in operands
+        ]
+    )
+
+
+def in_vmem(arrays):
+    return [(VMEM, array) for array in arrays]
+
+
+def in_hbm(arrays):
+    return [(HBM, array) for array in arrays]
+
+
+def begin(sources, targets, semaphores, first=0):
+    copies = [
+        pltpu.make_async_copy(source, target, semaphores.at[first + index])
+        for index, (source, target) in enumerate(zip(sources, targets))
+    ]
+    for copy in copies:
+        copy.start()
+    return copies
+
+
+def finish(copies):
+    for copy in copies:
+        copy.wait()
 
 
 def radices(count):
@@ -106,10 +139,14 @@
     return jnp.dot(table_ref[...], rows_ref[...], preferred_element_type=F32)
 
 
-def own_kernel(early, block, digits, lengths, counts_ref, features_ref, offsets_ref, waves_ref, *refs):
+def own_kernel(early, block, digits, lengths, *refs):
+    sources, refs = refs[:4], refs[4:]
     masked_ref, places_ref, turned_ref = refs[:3]
     tables, sums = refs[3 : 3 + len(early)], refs[3 + len(early) : 3 + 2 * len(early)]
-    padded_ref = refs[-1]
+    padded_ref, waves_ref, offsets_ref, counts_ref, features_ref, kept_ref, semaphores, kept_semaphores = refs[
+        3 + 2 * len(early) :
+    ]
+    copies = begin(sources, (waves_ref, offsets_ref, counts_ref, features_ref), semaphores)
     cells = features_ref.shape[0]
     dev, slab = lax.axis_index("dev"), lax.axis_index("grp")
     flips = jnp.int32(0)
@@ -117,24 +154,29 @@
     for axis, stride, radix in digits:
         weight //= radix
         flips += ((slab if axis == "grp" else dev) // stride % radix) * weight
+    copies[0].wait()
     fill_waves(waves_ref, padded_ref, turned_ref, flips)
+    copies[1].wait()
     fill_places(offsets_ref, places_ref, dev * cells, slab, *lengths)
+    copies[2].wait()
+    copies[3].wait()
     fill_masked(counts_ref, features_ref, masked_ref)
-    for place, table_ref, sums_ref in zip(early, tables, sums):
+    leaving = []
+    for index, (place, sums_ref) in enumerate(zip(early, sums)):
+        table_ref = kept_ref.at[index]
         fill_table(turned_ref[place * block : (place + 1) * block, :], places_ref, table_ref)
+        leaving += begin([table_ref], [tables[index]], kept_semaphores, index)
         sums_ref[...] = sums_of(table_ref, masked_ref)
+    finish(leaving)
 
 
 def sibling_kernel(
-    place, block, lengths, counts_ref, features_ref, offsets_ref, turned_ref, own_ref, start_ref,
-    masked_ref, places_ref, first_ref, last_ref, piece_ref, table_ref,
+    place, block, lengths, counts_ref, features_ref, offsets_ref, turned_ref, start_ref,
+    masked_ref, places_ref, piece_ref, table_ref,
 ):
-    cells, slots, _ = features_ref.shape
+    cells = features_ref.shape[0]
     fill_places(offsets_ref, places_ref, lax.axis_index("dev") * cells, lax.axis_index("grp") ^ 1, *lengths)
     fill_masked(counts_ref, features_ref, masked_ref)
-    for line, rows_ref in enumerate((own_ref, masked_ref)):
-        first_ref[line] = rows_ref[:slots, :]
-        last_ref[line] = rows_ref[(cells - 1) * slots :, :]
     fill_table(turned_ref[place * block : (place + 1) * block, :], places_ref, table_ref)
     piece_ref[...] = (start_ref[...] + sums_of(table_ref, masked_ref)).astype(piece_ref.dtype)
 
@@ -145,33 +187,66 @@
 
 
 def both_kernel(
-    place, block, turned_ref, own_places_ref, own_ref, places_ref, masked_ref, kept_ref, piece_ref, table_ref
+    place, block, turned_ref, own_places_ref, own_ref, places_ref, masked_ref, kept_ref, piece_ref, table_ref, semaphores
 ):
     waves = turned_ref[place * block : (place + 1) * block, :]
-    fill_table(waves, own_places_ref, kept_ref)
-    total = sums_of(kept_ref, own_ref)
-    fill_table(waves, places_ref, table_ref)
-    piece_ref[...] = (total + sums_of(table_ref, masked_ref)).astype(piece_ref.dtype)
-
-
-def rest_kernel(first, block, turned_ref, places_ref, _, *tables):
-    for place, table_ref in enumerate(tables):
+    fill_table(waves, own_places_ref, table_ref.at[0])
+    leaving = begin([table_ref.at[0]], [kept_ref], semaphores)
+    total = sums_of(table_ref.at[0], own_ref)
+    fill_table(waves, places_ref, table_ref.at[1])
+    piece_ref[...] = (total + sums_of(table_ref.at[1], masked_ref)).astype(piece_ref.dtype)
+    finish(leaving)
+
+
+def rest_kernel(first, block, turned_ref, places_ref, mark_ref, *refs):
+    *tables, table_ref, semaphores = refs
+    mark_ref[...] = jnp.zeros_like(mark_ref)
+    leaving = []
+    for place, target_ref in enumerate(tables):
         start = first + place * block
-        fill_table(turned_ref[start : start + block, :], places_ref, table_ref)
-
-
-def short_kernel(lines, codes_ref, radial_ref, *refs):
-    row_refs = refs[:lines]
-    before_ref, after_ref, w_ref, _, message_ref, window_ref, starts_ref = refs[lines:]
+        fill_table(turned_ref[start : start + block, :], places_ref, table_ref.at[place])
+        leaving += begin([table_ref.at[place]], [target_ref], semaphores, place)
+    finish(leaving)
+
+
+def fill_edges(lines, outs):
+    slots = outs[0].shape[1]
+    end = lines[0].shape[0] - slots
+    if len(outs) == 1:
+        start = pl.multiple_of(jnp.where(lax.axis_index("grp") == 0, end, 0), slots)
+        for line, rows_ref in enumerate(lines):
+            outs[0][line] = rows_ref[pl.ds(start, slots), :]
+        return
+    for line, rows_ref in enumerate(lines):
+        outs[0][line] = rows_ref[end:, :]
+        outs[1][line] = rows_ref[:slots, :]
+
+
+def short_kernel(lines, chunks, codes_ref, source_ref, *refs):
+    line_refs, refs = refs[:lines], refs[lines:]
+    one_ref, two_ref, w_ref, message_ref = refs[:4]
+    window_ref, starts_ref, radial_ref, semaphores = refs[4:]
     cells, slots, channels = message_ref.shape
     pairs = radial_ref.shape[1]
     slab, slabs = lax.axis_index("grp"), lax.axis_size("grp")
+    share = cells // chunks
+    edges = []
     for line in range(lines):
-        base = line * (cells + 2)
-        window_ref[base] = before_ref[line]
-        for cell in range(cells):
-            window_ref[base + 1 + cell] = row_refs[line][cell * slots : (cell + 1) * slots, :]
-        window_ref[base + 1 + cells] = after_ref[line]
+        if slabs == 2:
+            near = slab * (cells + 1)
+            edges.append((one_ref.at[line], window_ref.at[line * (cells + 2) + near]))
+            edges.append((two_ref.at[line], window_ref.at[(1 - line) * (cells + 2) + cells + 1 - near]))
+        else:
+            edges.append((one_ref.at[line], window_ref.at[line * (cells + 2)]))
+            edges.append((two_ref.at[line], window_ref.at[line * (cells + 2) + cells + 1]))
+    edges = begin(*zip(*edges), semaphores)
+    parts = []
+    for chunk in range(chunks):
+        span = pl.ds(chunk * share, share)
+        moves = [(source_ref.at[span], radial_ref.at[span])]
+        for line, line_ref in enumerate(line_refs):
+            moves.append((line_ref.at[span], window_ref.at[pl.ds(line * (cells + 2) + 1 + chunk * share, share)]))
+        parts.append(begin(*zip(*moves), semaphores, 2 * lines + chunk * (1 + lines)))
     nothing = lines * (cells + 2)
     window_ref[nothing] = jnp.zeros((slots, channels), BF16)
     for level in range(3):
@@ -181,6 +256,11 @@
             starts_ref[3 * level + along] = jnp.where(inside, line * (cells + 2) + along, -1)
 
     for cell in range(cells):
+        if cell == 0:
+            finish(edges)
+            finish(parts[0])
+        if cell % share == 0 and cell // share + 1 < chunks:
+            finish(parts[cell // share + 1])
         total = None
         for pair in range(0, pairs, 2):
             blocks, taken = [], []
@@ -205,7 +285,7 @@
         out[...] = total[:, place * rows : (place + 1) * rows].astype(out.dtype)
 
 
-def add_and_cut(pieces, radix):
+def add_and_cut(pieces, radix, held):
     trig, rows, channels = pieces[0].shape
     part = (trig, rows // radix, channels)
     types = [F32] + [BF16] * (radix - 1)
@@ -214,7 +294,8 @@
         return [
             total[:, place * part[1] : (place + 1) * part[1]].astype(kind) for place, kind in enumerate(types)
         ]
-    return call(functools.partial(add_kernel, len(pieces), radix), [(part, kind) for kind in types], pieces)
+    kernel = functools.partial(add_kernel, len(pieces), radix)
+    return call(kernel, [(VMEM, (part, kind)) for kind in types], in_vmem(pieces), held=held)
 
 
 def mixed(owned, waves, w_mix, factor_scale):
@@ -226,9 +307,12 @@
     return (energy * jnp.concatenate([kernel, kernel], axis=0)).astype(BF16)
 
 
-def energy_kernel(count, factor_scale, *refs):
+def energy_kernel(count, lines, factor_scale, *refs):
     pieces = refs[:count]
-    turned_ref, w_mix_ref, _, energy_ref = refs[count:]
+    turned_ref, w_mix_ref = refs[count : count + 2]
+    energy_ref, *edges = refs[count + 2 + lines :]
+    if edges:
+        fill_edges(refs[count + 2 : count + 2 + lines], edges)
     trig, rows, channels = energy_ref.shape
     total = pieces[0][...].astype(F32)
     for piece in pieces[1:]:
@@ -238,38 +322,41 @@
     energy_ref[...] = energy.reshape(trig, rows, channels)
 
 
-def energy_of(pieces, turned, w_mix, factor_scale, after):
+def energy_of(pieces, turned, w_mix, factor_scale, lines, slots, held):
     trig, rows, channels = pieces[0].shape
     if rows % 16:
         total = functools.reduce(jnp.add, [piece.astype(F32) for piece in pieces])
         energy = mixed(total.reshape(trig * rows, channels), turned[:rows].astype(F32), w_mix, factor_scale)
-        return energy.reshape(trig, rows, channels)
-    (energy,) = call(
-        functools.partial(energy_kernel, len(pieces), factor_scale),
-        [((trig, rows, channels), BF16)],
-        [*pieces, turned, w_mix, after],
+        edges = [jnp.stack([line[-slots:] for line in lines]), jnp.stack([line[:slots] for line in lines])]
+        return energy.reshape(trig, rows, channels), edges
+    edge = (VMEM, ((len(lines), slots, channels), BF16))
+    energy, *edges = call(
+        functools.partial(energy_kernel, len(pieces), len(lines), factor_scale),
+        [(VMEM, ((trig, rows, channels), BF16))] + [edge] * (1 if lax.axis_size("grp") == 2 else 2),
+        in_vmem([*pieces, turned, w_mix, *lines]),
+        held=held,
     )
-    return energy
+    return energy, edges
 
 
 def join_kernel(*refs):
-    pieces, out_ref = refs[:-2], refs[-1]
+    pieces, out_ref = refs[:-1], refs[-1]
     rows = pieces[0].shape[1]
     for place, piece in enumerate(pieces):
         out_ref[:, place * rows : (place + 1) * rows, :] = piece[...]
 
 
-def joined(pieces, after):
+def joined(pieces, held):
     trig, rows, channels = pieces[0].shape
     if rows % 16:
         return jnp.concatenate(pieces, axis=1)
-    (whole,) = call(join_kernel, [((trig, rows * len(pieces), channels), BF16)], [*pieces, after])
+    whole = (VMEM, ((trig, rows * len(pieces), channels), BF16))
+    (whole,) = call(join_kernel, [whole], in_vmem(pieces), held=held)
     return whole
 
 
 def near_kernel(blocks, *refs):
-    energies, tables = refs[:blocks], refs[blocks : 2 * blocks]
-    out_ref, turned_ref = refs[2 * blocks :]
+    energies, tables, (out_ref, turned_ref) = refs[:blocks], refs[blocks : 2 * blocks], refs[2 * blocks :]
     for place, energy in enumerate(energies):
         turned_ref[place] = energy[...].astype(F32).T.astype(BF16)
     atoms = out_ref.shape[1]
@@ -282,16 +369,19 @@
         out_ref[:, start : start + tile] = total
 
 
-def final_kernel(blocks, scale, counts_ref, near_ref, message_ref, masked_ref, *refs):
-    energies, tables = refs[:blocks], refs[blocks : 2 * blocks]
-    out_ref, turned_ref = refs[2 * blocks :]
+def final_kernel(scale, counts_ref, masked_ref, near_ref, message_ref, energy_ref, rest_ref, *refs):
+    tables, (out_ref, turned_ref) = refs[:-2], refs[-2:]
     cells, slots, channels = out_ref.shape
     step = pl.program_id(0)
 
     @pl.when(step == 0)
     def _():
-        for place, energy in enumerate(energies):
-            turned_ref[place] = energy[...].astype(F32).T.astype(BF16)
+        rows = energy_ref.shape[0]
+        half = rows // 2
+        turned_ref[0] = energy_ref[...].astype(F32).T.astype(BF16)
+        for place in range(1, len(tables)):
+            taken = rest_ref[:, (place - 1) * half : place * half, :].reshape(rows, channels)
+            turned_ref[place] = taken.astype(F32).T.astype(BF16)
 
     atoms = cells * slots
     span = pl.ds(pl.multiple_of(step * atoms, atoms), atoms)
@@ -301,28 +391,28 @@
     slot_ids = lax.broadcasted_iota(jnp.int32, (slots, channels), 0)
     for cell in range(cells):
         index = step * cells + cell
-        rows = pl.ds(pl.multiple_of(index * slots, slots), slots)
         value = total[:, cell * slots : (cell + 1) * slots].T * scale + message_ref[index]
         value = value * (0.5 + 0.5 * jnp.tanh(0.5 * value))
-        result = masked_ref[rows, :].astype(F32) + value
+        result = masked_ref[index].astype(F32) + value
         out_ref[cell] = jnp.where(slot_ids < counts_ref[index], result, 0.0).astype(BF16)
 
 
-def final_call(counts, near, message, masked, energies, tables, scale):
+def final_call(counts, near, message, masked, energy, rest, tables, scale):
     cells, slots, channels = message.shape
     rows = tables[0].shape[0]
     blocks = len(tables)
     group = math.gcd(cells, 4)
-    operands = [near, message, masked, *energies, *tables]
+    cells_spec = pl.BlockSpec((group, slots, channels), lambda i: (i, 0, 0))
+    operands = [masked, near, message, energy, rest, *tables]
     return pl.pallas_call(
-        functools.partial(final_kernel, blocks, scale),
+        functools.partial(final_kernel, scale),
         grid=(cells // group,),
         in_specs=[SMEM] + [VMEM] * len(operands),
-        out_specs=pl.BlockSpec((group, slots, channels), lambda i: (i, 0, 0)),
+        out_specs=cells_spec,
         out_shape=jax.ShapeDtypeStruct(message.shape, BF16),
         scratch_shapes=[pltpu.VMEM((blocks, channels, rows), BF16)],
         compiler_params=PARAMS,
-    )(counts, *[here(array) for array in operands])
+    )(counts, *[pltpu.with_memory_space_constraint(array, pltpu.VMEM) for array in operands])
 
 
 def body(features, offsets, radial, neighbours, counts, wavevectors, w_msg, w_mix):
@@ -362,101 +452,149 @@
     rows_type = ((atoms, channels), BF16)
     edge = ((2, slots, channels), BF16)
     scratch = [pltpu.VMEM(*table)]
+    block_flops = 2 * 2 * block * atoms * channels * COST
+
+    def several(count):
+        return [pltpu.VMEM((count,) + table[0], BF16), pltpu.SemaphoreType.DMA((count,))]
 
     def sent(part, place):
         return lax.ppermute(part.reshape(2, block, channels), axis, pairs_at(axis, stride, place))
 
-    early = list(range(1, blocks))[:2]
+    order = [*range(blocks - 1, 0, -1), 0]
+    early = order[: min(2, blocks - 1)]
     masked, places, turned, *outs = call(
         functools.partial(own_kernel, early, block, digits, lengths),
-        [rows_type, places_type, ((wave_count, 32), BF16)] + [table] * len(early) + [sums] * len(early),
-        [features, offsets, wavevectors],
-        [counts],
-        [pltpu.VMEM((32, wave_count), F32)],
+        [(VMEM, rows_type), (VMEM, places_type), (VMEM, ((wave_count, 32), BF16))]
+        + [(HBM, table)] * len(early)
+        + [(VMEM, sums)] * len(early),
+        in_hbm([wavevectors, offsets, counts, features]),
+        [
+            pltpu.VMEM((32, wave_count), F32),
+            pltpu.VMEM(wavevectors.shape, jnp.int32),
+            pltpu.VMEM(offsets.shape, F32),
+            pltpu.SMEM(counts.shape, jnp.int32),
+            pltpu.VMEM(features.shape, BF16),
+            pltpu.VMEM((len(early),) + table[0], BF16),
+            pltpu.SemaphoreType.DMA((4,)),
+            pltpu.SemaphoreType.DMA((len(early),)),
+        ],
     )
     tables = dict(zip(early, outs))
     started = dict(zip(early, outs[len(early) :]))
-    sibling, sibling_places, first, last, part = call(
+    sibling, sibling_places, part = call(
         functools.partial(sibling_kernel, early[0], block, lengths),
-        [rows_type, places_type, edge, edge, piece],
-        [sibling_features, sibling_offsets, turned, masked, started[early[0]]],
-        [sibling_counts],
+        [(VMEM, rows_type), (VMEM, places_type), (VMEM, piece)],
+        [(SMEM, sibling_counts)] + in_vmem([sibling_features, sibling_offsets, turned, started[early[0]]]),
         scratch,
     )
     received = {early[0]: sent(part, early[0])}
     for place in early[1:]:
         (part,) = call(
             functools.partial(continued_kernel, place, block),
-            [piece],
-            [turned, sibling_places, sibling, started[place]],
-            scratch=scratch,
+            [(VMEM, piece)],
+            in_vmem([turned, sibling_places, sibling, started[place]]),
+            scratch,
+            flops=block_flops,
         )
         received[place] = sent(part, place)
-    for place in [*range(1 + len(early), blocks), 0]:
+    for place in order[len(early) :]:
         tables[place], part = call(
             functools.partial(both_kernel, place, block),
-            [table, piece if place else sums],
-            [turned, places, masked, sibling_places, sibling],
-            scratch=scratch,
+            [(HBM, table), (VMEM, piece if place else sums)],
+            in_vmem([turned, places, masked, sibling_places, sibling]),
+            [pltpu.VMEM((2,) + table[0], BF16), pltpu.SemaphoreType.DMA((1,))],
+            [part] if place else [],
+            2 * block_flops,
         )
         if place:
             received[place] = sent(part, place)
     pieces = [part.reshape(2, block, channels)] + [received[place] for place in range(1, blocks)]
+    tables = [tables[place] for place in range(blocks)]
+
+    def rest_of_tables(first, count, held):
+        return call(
+            functools.partial(rest_kernel, half + first * block, block),
+            [(VMEM, ((8, LANES), F32))] + [(HBM, table)] * count,
+            in_vmem([turned, places]),
+            several(count),
+            held,
+            block_flops * count,
+        )
+
+    share = blocks // 2
+    mark, *others = rest_of_tables(0, share, [part])
 
     for axis, stride, radix in stages[1:]:
-        parts = add_and_cut(pieces, radix)
+        parts = add_and_cut(pieces, radix, [mark])
         pieces = [parts[0]] + [
             lax.ppermute(parts[place], axis, pairs_at(axis, stride, place)) for place in range(1, radix)
         ]
 
-    others = call(
-        functools.partial(rest_kernel, half, block), [table] * blocks, [turned, places, parts[0]]
-    )
-    energy = energy_of(pieces, turned, w_mix, 1.0 / math.sqrt(total_slots), others[0])
-
-    right = [(i, i + 1) for i in range(dev_count - 1)]
+    mark, *more = rest_of_tables(share, blocks - share, [parts[0]])
+    others += more
+
     if slabs == 2:
         lines = [masked, sibling]
     else:
-        kept = [
-            jnp.where(jnp.arange(slots)[None, :, None] < count[:, None, None], cell, jnp.bfloat16(0))
+        lines = [masked] + [
+            jnp.where(jnp.arange(slots)[None, :, None] < count[:, None, None], cell, jnp.bfloat16(0)).reshape(
+                atoms, channels
+            )
             for count, cell in near
         ]
-        first = jnp.stack([masked[:slots]] + [line[0] for line in kept])
-        last = jnp.stack([masked[-slots:]] + [line[-1] for line in kept])
-        lines = [masked] + [line.reshape(atoms, channels) for line in kept]
-    before = lax.ppermute(last, "dev", right)
-    after = lax.ppermute(first, "dev", [(j, i) for i, j in right])
-    window = (len(lines) * (cells + 2) + 1, slots, channels)
-    (message,) = call(
-        functools.partial(short_kernel, len(lines)),
-        [((cells, slots, channels), F32)],
-        [radial[0], *lines, before, after, w_msg, energy],
-        [neighbours[0]],
-        [pltpu.VMEM(window, BF16), pltpu.SMEM((9,), jnp.int32)],
-    )
+    energy, edges = energy_of(pieces, turned, w_mix, 1.0 / math.sqrt(total_slots), lines, slots, [mark])
+
+    right = [(i, i + 1) for i in range(dev_count - 1)]
+    left = [(j, i) for i, j in right]
+    if slabs == 2:
+        ways = right + [(dev_count + i, dev_count + j) for i, j in left]
+        one = lax.ppermute(edges[0], ("grp", "dev"), ways)
+        two = lax.ppermute(one, "grp", swap)
+    else:
+        one = lax.ppermute(edges[0], "dev", right)
+        two = lax.ppermute(edges[1], "dev", left)
 
     for axis, stride, radix in reversed(stages[1:]):
-        gathered = [energy] + [
-            lax.ppermute(energy, axis, pairs_at(axis, stride, place)) for place in range(1, radix)
-        ]
-        energy = joined(gathered, message)
+        energy = joined(
+            [energy] + [lax.ppermute(energy, axis, pairs_at(axis, stride, place)) for place in range(1, radix)],
+            [],
+        )
     axis, stride, blocks = stages[0]
     energies = [energy] + [
         lax.ppermute(energy, axis, pairs_at(axis, stride, place)) for place in range(1, blocks)
     ]
-    others_energies = [lax.ppermute(part, "grp", swap) for part in energies]
+    other_energy = lax.ppermute(energy, "grp", swap)
+
+    chunks = math.gcd(cells, 4)
+    (message,) = call(
+        functools.partial(short_kernel, len(lines), chunks),
+        [(VMEM, ((cells, slots, channels), F32))],
+        [(SMEM, neighbours[0])]
+        + in_hbm([radial[0], *[line.reshape(cells, slots, channels) for line in lines], one, two])
+        + in_vmem([w_msg]),
+        [
+            pltpu.VMEM((len(lines) * (cells + 2) + 1, slots, channels), BF16),
+            pltpu.SMEM((9,), jnp.int32),
+            pltpu.VMEM(radial.shape[1:], BF16),
+            pltpu.SemaphoreType.DMA((2 * len(lines) + chunks * (1 + len(lines)),)),
+        ],
+        [energy, other_energy],
+        6 * block_flops,
+    )
+    rest = lax.ppermute(joined(energies[1:], [message]), "grp", swap)
     energies = [part.reshape(2 * block, channels) for part in energies]
-    others_energies = [part.reshape(2 * block, channels) for part in others_energies]
-    turned_energies = [pltpu.VMEM((blocks, channels, 2 * block), BF16)]
+    other_energy = other_energy.reshape(2 * block, channels)
     (near_sum,) = call(
         functools.partial(near_kernel, blocks),
-        [((channels, atoms), F32)],
-        [*energies, *[tables[place] for place in range(blocks)]],
-        scratch=turned_energies,
+        [(VMEM, ((channels, atoms), F32))],
+        in_vmem([*energies, *tables]),
+        [pltpu.VMEM((blocks, channels, 2 * block), BF16)],
+        [message],
+        2 * block_flops,
     )
+    masked = masked.reshape(cells, slots, channels)
     scale = 8.0 / math.sqrt(wave_count)
-    result = final_call(counts, near_sum, message, masked, others_energies, others, scale)
+    result = final_call(counts, near_sum, message, masked, other_energy, rest, others, scale)
     return result[None]
 
 

time: 68.4 us -> 61.7 us (0.902)
  local copies, waits for them, and re-layouts: 12 us -> 4.04 us
  Pallas kernels: 25 us -> 30 us
  starting transfers between devices: 26.2 us -> 21.7 us
  waiting for transfers between devices: 4.4 us -> 5.4 us
    unnamed x45 -> x37, local copies, waits for them, and re-layouts: 12 us -> 3.97 us
    pallas_call x12 -> x14, Pallas kernels: 25 us -> 30 us  [the longest x13 25.8 us: call(): pl.pallas_call(without_held, in_specs=[place for place, _ in operands], o...]
    ppermute x3, starting transfers between devices: 7.19 us -> 4.45 us  [body(): lax.ppermute(parts[place], axis, pairs_at(axis, stride, place))]
    ppermute x3, waiting for transfers between devices: 0.73 us -> 2.73 us  [body(): lax.ppermute(parts[place], axis, pairs_at(axis, stride, place))]
    ppermute x6 -> x4, starting transfers between devices: 5.88 us -> 4.01 us  [the longest x1 3.39 us: body(): one = lax.ppermute(edges[0], ('grp', 'dev'), ways)]
    ppermute x6, waiting for transfers between devices: 3.63 us -> 2.2 us  [body(): lax.ppermute(energy, axis, pairs_at(axis, stride, place))]
  transfers between devices with their start and end apart: 21 -> 19, of which waited for: 4 -> 5; matrix products, arithmetic and copies ran while one was open for 1% -> 1% of each run, Pallas kernels for 24% -> 37%
where the time goes in v3:
time: 61.7 us; the launch traced here: 61.5 us
  Pallas kernels  30 us (49%)
  starting transfers between devices  21.7 us (35%)
  waiting for transfers between devices  5.4 us (9%)
  local copies, waits for them, and re-layouts  4.04 us (7%)
    pallas_call x13, Pallas kernels, call(): pl.pallas_call(without_held, in_specs=[place for place, _ in operands], o...  25.8 us
    ppermute x6, starting transfers between devices, body(): lax.ppermute(energy, axis, pairs_at(axis, stride, place))  7.94 us
    ppermute x3, starting transfers between devices, body(): lax.ppermute(parts[place], axis, pairs_at(axis, stride, place))  4.45 us
    ppermute x3, starting transfers between devices, sent(): lax.ppermute(part.reshape(2, block, channels), axis, pairs_at(axis, strid...  4.24 us
    pallas_call x1, Pallas kernels, final_call(): pl.pallas_call(functools.partial(final_kernel, scale), grid=(cells // gro...  4.21 us
    unnamed x37, local copies, waits for them, and re-layouts  3.97 us
    ppermute x1, starting transfers between devices, body(): one = lax.ppermute(edges[0], ('grp', 'dev'), ways)  3.39 us
    ppermute x3, waiting for transfers between devices, body(): lax.ppermute(parts[place], axis, pairs_at(axis, stride, place))  2.73 us
  transfers between devices with their start and end apart: 19, of which 5 were waited for; matrix products, arithmetic and copies ran while one was open for 1% of the time, Pallas kernels for 37%

profile of v3, /device:TPU:0, one launch (start us, length us, event | category | flops | bytes accessed | tf_op | source)
XLA Modules:
  0.0 61.5 jit_solution(12182765095136880805)
XLA Ops:
  0.0 0.5 collective-permute-start.1
  0.5 0.8 %copy.12 = f32[1,16,3,128]{3,2,1,0:T(4,128)S(1)} copy(f32[1,16,3,128]{3,1,2,0:T(8,128)} %param.9) | data formatting | bytes 49152 | tf_op args[1]
  1.3 0.5 collective-permute-start
  1.8 4.3 %shard_map.82 = (bf16[2048,256]{1,0:T(8,128)(2,1)S(1)}, bf16[32,2048]{1,0:T(8,128)(2,1)S(1)}, bf16[1024,32]{1,0:T(8,128)(2,1)S(1)}, bf16[256,2048]{1,0:T(8,128)(...) custom-call(s32[3,1024]{1,0:T(4,128)} %refs_0_.1, f32[16,3,128]{2,1,0:T(4,128)} %bitcast.38, ...), custom_call_target="tpu_custom_call" | custom-call | tf_op jit(solution)/shard_map/pallas_call | solution.py:30
  6.2 1.9 %shard_map.83 = (bf16[2048,256]{1,0:T(8,128)(2,1)S(1)}, bf16[32,2048]{1,0:T(8,128)(2,1)S(1)}, bf16[256,256]{1,0:T(8,128)(2,1)S(1)}) custom-call(s32[16]{0:T(128)S(1)} %collective-permute-done.refs_0_, bf16[16,128,256]{2,1,0:T(8,128)(2,1)S(1)} %collective-permute-done.1.refs_1_, f32[16,3,128]{2,1,0:T(4,128)S(1)} %collective-permute-done.2.refs_2_, ...), custom_call_target="tpu_custom_call" | custom-call | tf_op jit(solution)/shard_map/pallas_call | solution.py:30
  8.1 1.1 %shard_map.85.refs_5_ = bf16[256,256]{1,0:T(8,128)(2,1)S(1)} custom-call(bf16[1024,32]{1,0:T(8,128)(2,1)S(1)} %get-tuple-element.32.refs_3_.refs_0_.refs_4_, bf16[32,2048]{1,0:T(8,128)(2,1)S(1)} %get-tuple-element.35.refs_3_.refs_1_, bf16[2048,256]{1,0:T(8,128)(2,1)S(1)} %get-tuple-element.36.refs_4_.refs_2_.refs_7_, f32[256,256]{1,0:T(8,128)S(1)} %get-tuple-element.38.refs_3_), custom_call_target="tpu_custom_call" | custom-call | tf_op jit(solution)/shard_map/pallas_call | solution.py:30
  9.2 2.6 %collective-permute-start.4 = (bf16[2,128,256]{2,1,0:T(8,128)(2,1)S(1)}, bf16[2,128,256]{2,1,0:T(8,128)(2,1)S(1)}, u32[]{:S(2)}, u32[]{:S(2)}) collective-permute-start(bf16[2,128,256]{2,1,0:T(8,128)(2,1)S(1)} %bitcast.28), channel_id=1, source_target_pairs={{0,2},{1,3},{2,0},{3,1},{4,6},{5,7},{6,4},{7,5},{8,10},{9,11},{10,... | collective-permute-start | bytes 393224 | tf_op jit(solution)/shard_map/ppermute | solution.py:461
  11.8 1.4 %collective-permute-start.5 = (bf16[2,128,256]{2,1,0:T(8,128)(2,1)S(1)}, bf16[2,128,256]{2,1,0:T(8,128)(2,1)S(1)}, u32[]{:S(2)}, u32[]{:S(2)}) collective-permute-start(bf16[2,128,256]{2,1,0:T(8,128)(2,1)S(1)} %bitcast.32), channel_id=1, source_target_pairs={{0,3},{1,2},{2,1},{3,0},{4,7},{5,6},{6,5},{7,4},{8,11},{9,10},{10,... | collective-permute-start | bytes 393224 | tf_op jit(solution)/shard_map/ppermute | solution.py:461
  13.3 2.1 %shard_map.86 = (bf16[256,2048]{1,0:T(8,128)(2,1)}, bf16[256,256]{1,0:T(8,128)(2,1)S(1)}) custom-call(bf16[1024,32]{1,0:T(8,128)(2,1)S(1)} %get-tuple-element.32.refs_3_.refs_0_.refs_4_, bf16[32,2048]{1,0:T(8,128)(2,1)S(1)} %get-tuple-element.33.refs_1_, bf16[2048,256]{1,0:T(8,128)(2,1)S(1)} %get-tuple-element.31.refs_2_.refs_6_, ...), custom_call_target="tpu_custom_call" | custom-call | tf_op jit(solution)/shard_map/pallas_call | solution.py:30
  15.6 2.1 %shard_map.84 = (bf16[256,2048]{1,0:T(8,128)(2,1)}, f32[256,256]{1,0:T(8,128)S(1)}) custom-call(bf16[1024,32]{1,0:T(8,128)(2,1)S(1)} %get-tuple-element.32.refs_3_.refs_0_.refs_4_, bf16[32,2048]{1,0:T(8,128)(2,1)S(1)} %get-tuple-element.33.refs_1_, bf16[2048,256]{1,0:T(8,128)(2,1)S(1)} %get-tuple-element.31.refs_2_.refs_6_, ...), custom_call_target="tpu_custom_call" | custom-call | tf_op jit(solution)/shard_map/pallas_call | solution.py:30
  17.7 2.5 %shard_map.87 = (f32[8,128]{1,0:T(8,128)S(1)}, bf16[256,2048]{1,0:T(8,128)(2,1)}, bf16[256,2048]{1,0:T(8,128)(2,1)}) custom-call(bf16[1024,32]{1,0:T(8,128)(2,1)S(1)} %get-tuple-element.32.refs_3_.refs_0_.refs_4_, bf16[32,2048]{1,0:T(8,128)(2,1)S(1)} %get-tuple-element.33.refs_1_, f32[256,256]{1,0:T(8,128)S(1)} %get-tuple-element.37.refs_2_), custom_call_target="tpu_custom_call" | custom-call | tf_op jit(solution)/shard_map/pallas_call | solution.py:30
  20.3 0.5 collective-permute-done.3.refs_1_
  20.8 1.6 %collective-permute-start.6 = (bf16[2,32,256]{2,1,0:T(8,128)(2,1)S(1)}, bf16[2,32,256]{2,1,0:T(8,128)(2,1)S(1)}, u32[]{:S(2)}, u32[]{:S(2)}) collective-permute-start(bf16[2,32,256]{2,1,0:T(8,128)(2,1)S(1)} %get-tuple-element.43), channel_id=1, source_target_pairs={{0,4},{1,5},{2,6},{3,7},{4,0},{5,1},{6,2},{7,3},{8,12},{9,13},{10,... | collective-permute-start | bytes 98312 | tf_op jit(solution)/shard_map/ppermute | solution.py:530
  22.5 2.6 %collective-permute-start.7 = (bf16[2,32,256]{2,1,0:T(8,128)(2,1)S(1)}, bf16[2,32,256]{2,1,0:T(8,128)(2,1)S(1)}, u32[]{:S(2)}, u32[]{:S(2)}) collective-permute-start(bf16[2,32,256]{2,1,0:T(8,128)(2,1)S(1)} %get-tuple-element.44), channel_id=1, source_target_pairs={{0,8},{1,9},{2,10},{3,11},{4,12},{5,13},{6,14},{7,15},{8,0},{9,1},... | collective-permute-start | bytes 98312 | tf_op jit(solution)/shard_map/ppermute | solution.py:530
  25.3 2.7 %shard_map.89 = (f32[8,128]{1,0:T(8,128)S(1)}, bf16[256,2048]{1,0:T(8,128)(2,1)}, bf16[256,2048]{1,0:T(8,128)(2,1)}) custom-call(bf16[1024,32]{1,0:T(8,128)(2,1)S(1)} %get-tuple-element.32.refs_3_.refs_0_.refs_4_, bf16[32,2048]{1,0:T(8,128)(2,1)S(1)} %get-tuple-element.33.refs_1_, f32[2,32,256]{2,1,0:T(8,128)S(1)} %get-tuple-element.42.refs_2_.refs_0_), custom_call_target="tpu_custom_call" | custom-call | tf_op jit(solution)/shard_map/pallas_call | solution.py:30
  28.1 2.7 %collective-permute-done.8.refs_3_ = bf16[2,32,256]{2,1,0:T(8,128)(2,1)S(1)} collective-permute-done((bf16[2,32,256]{2,1,0:T(8,128)(2,1)S(1)}, bf16[2,32,256]{2,1,0:T(8,128)(2,1)S(1)}, u32[]{:S(2)}, u32[]{:S(2)}) %collective-permute-start.8) | collective-permute-done | bytes 32800 | tf_op jit(solution)/shard_map/ppermute | solution.py:530
  31.0 3.4 %collective-permute-start.15 = (bf16[2,128,256]{2,1,0:T(8,128)(2,1)S(1)}, bf16[2,128,256]{2,1,0:T(8,128)(2,1)S(1)}, u32[]{:S(2)}, u32[]{:S(2)}) collective-permute-start(bf16[2,128,256]{2,1,0:T(8,128)(2,1)S(1)} %get-tuple-element.52), channel_id=1, source_target_pairs={{0,1},{1,2},{2,3},{3,4},{4,5},{5,6},{6,7},{7,8},{8,9},{9,10},{10,1... | collective-permute-start | bytes 393224 | tf_op jit(solution)/shard_map/ppermute | solution.py:551
  34.4 1.0 %collective-permute-start.11 = (bf16[2,32,256]{2,1,0:T(8,128)(2,1)S(1)}, bf16[2,32,256]{2,1,0:T(8,128)(2,1)S(1)}, u32[]{:S(2)}, u32[]{:S(2)}) collective-permute-start(bf16[2,32,256]{2,1,0:T(8,128)(2,1)S(1)} %get-tuple-element.47.refs_0_), channel_id=1, source_target_pairs={{0,12},{1,13},{2,14},{3,15},{4,8},{5,9},{6,10},{7,11},{8,4},{9,5},... | collective-permute-start | bytes 98312 | tf_op jit(solution)/shard_map/ppermute | solution.py:559
  35.4 3.5 %collective-permute-start.9 = (bf16[2,32,256]{2,1,0:T(8,128)(2,1)S(1)}, bf16[2,32,256]{2,1,0:T(8,128)(2,1)S(1)}, u32[]{:S(2)}, u32[]{:S(2)}) collective-permute-start(bf16[2,32,256]{2,1,0:T(8,128)(2,1)S(1)} %get-tuple-element.47.refs_0_), channel_id=1, source_target_pairs={{0,4},{1,5},{2,6},{3,7},{4,0},{5,1},{6,2},{7,3},{8,12},{9,13},{10,... | collective-permute-start | bytes 98312 | tf_op jit(solution)/shard_map/ppermute | solution.py:559
  38.9 1.4 %collective-permute-done.11.refs_3_ = bf16[2,32,256]{2,1,0:T(8,128)(2,1)S(1)} collective-permute-done((bf16[2,32,256]{2,1,0:T(8,128)(2,1)S(1)}, bf16[2,32,256]{2,1,0:T(8,128)(2,1)S(1)}, u32[]{:S(2)}, u32[]{:S(2)}) %collective-permute-start.11) | collective-permute-done | bytes 32800 | tf_op jit(solution)/shard_map/ppermute | solution.py:559
  40.2 0.8 %collective-permute-done.10.refs_2_ = bf16[2,32,256]{2,1,0:T(8,128)(2,1)S(1)} collective-permute-done((bf16[2,32,256]{2,1,0:T(8,128)(2,1)S(1)}, bf16[2,32,256]{2,1,0:T(8,128)(2,1)S(1)}, u32[]{:S(2)}, u32[]{:S(2)}) %collective-permute-start.10) | collective-permute-done | bytes 32800 | tf_op jit(solution)/shard_map/ppermute | solution.py:559
  41.2 0.5 collective-permute-start.16
  41.6 0.7 %collective-permute-start.14 = (bf16[2,128,256]{2,1,0:T(8,128)(2,1)S(1)}, bf16[2,128,256]{2,1,0:T(8,128)(2,1)S(1)}, u32[]{:S(2)}, u32[]{:S(2)}) collective-permute-start(bf16[2,128,256]{2,1,0:T(8,128)(2,1)S(1)} %shard_map.91.refs_7_), channel_id=1, source_target_pairs={{0,3},{1,2},{2,1},{3,0},{4,7},{5,6},{6,5},{7,4},{8,11},{9,10},{10,... | collective-permute-start | bytes 393224 | tf_op jit(solution)/shard_map/ppermute | solution.py:564
  42.3 2.3 %collective-permute-start.13 = (bf16[2,128,256]{2,1,0:T(8,128)(2,1)S(1)}, bf16[2,128,256]{2,1,0:T(8,128)(2,1)S(1)}, u32[]{:S(2)}, u32[]{:S(2)}) collective-permute-start(bf16[2,128,256]{2,1,0:T(8,128)(2,1)S(1)} %shard_map.91.refs_7_), channel_id=1, source_target_pairs={{0,2},{1,3},{2,0},{3,1},{4,6},{5,7},{6,4},{7,5},{8,10},{9,11},{10,... | collective-permute-start | bytes 393224 | tf_op jit(solution)/shard_map/ppermute | solution.py:564
  44.6 0.5 collective-permute-start.12
  45.2 0.6 %copy-done.15 = bf16[2,128,256]{2,1,0:T(8,128)(2,1)} copy-done((bf16[2,128,256]{2,1,0:T(8,128)(2,1)}, bf16[2,128,256]{2,1,0:T(8,128)(2,1)S(1)}, u32[]{:S(2)}) %copy-start.15) | copy-done | bytes 131096
  45.9 7.3 %shard_map.92.refs_8_.refs_3_.message_ref = f32[16,128,256]{2,1,0:T(8,128)S(1)} custom-call(s32[16,8]{1,0:T(8,128)S(1)} %copy.10.refs_0_, bf16[16,8,128,128]{3,2,1,0:T(8,128)(2,1)} %bitcast.34, bf16[16,128,256]{2,1,0:T(8,128)(2,1)} %bitcast.20, bf16[16,128,256]{2,1,0:T(8,128)(2,1)} %bitcast.19, bf16[2,128,256]{2,1,0:T(8,128)(2,1)} %copy-done.14, ...), custom_call_target="tpu_custom_call" | custom-call | tf_op jit(solution)/shard_map/pallas_call | solution.py:30
  53.4 1.0 %copy-done.3 = bf16[256,2048]{1,0:T(8,128)(2,1)S(1)} copy-done((bf16[256,2048]{1,0:T(8,128)(2,1)S(1)}, bf16[256,2048]{1,0:T(8,128)(2,1)}, u32[]{:S(2)}) %copy-start.3) | copy-done | bytes 1048600
  54.4 0.3 copy-done.4
  54.8 1.3 %shard_map.93.near_ref = f32[256,2048]{1,0:T(8,128)S(1)} custom-call(bf16[256,256]{1,0:T(8,128)(2,1)S(1)} %bitcast.22, bf16[256,256]{1,0:T(8,128)(2,1)S(1)} %bitcast.27, bf16[256,256]{1,0:T(8,128)(2,1)S(1)} %bitcast.26, bf16[256,256]{1,0:T(8,128)(2,1)S(1)} %bitcast.25, bf16[256,2048]{1,0:T(8,128)(2,1)S(1)} %copy-done.6, bf16[256,2048]{1,0:T(8,128)(2,1)S(1)} %copy-done.5, ...), custom_call_target="tpu_custom_call" | custom-call | tf_op jit(solution)/shard_map/pallas_call | solution.py:30
  56.9 0.3 copy-done.10
  57.3 4.2 %shard_map.95 = bf16[16,128,256]{2,1,0:T(8,128)(2,1)} custom-call(s32[16]{0:T(128)S(1)} %bitcast.31, bf16[16,128,256]{2,1,0:T(8,128)(2,1)S(1)} %bitcast.21, f32[256,2048]{1,0:T(8,128)S(1)} %shard_map.93.near_ref, f32[16,128,256]{2,1,0:T(8,128)S(1)} %shard_map.92.refs_8_.refs_3_.message_ref, bf16[256,256]{1,0:T(8,128)(2,1)S(1)} %bitcast.24, ...), custom_call_target="tpu_custom_call" | custom-call | tf_op jit(solution)/shard_map/pallas_call | solution.py:407
  (58 shorter events, 2.0 us)
Async XLA Ops:
  0.0 6.2 %collective-permute-start.1 = (bf16[16,128,256]{2,1,0:T(8,128)(2,1)}, bf16[16,128,256]{2,1,0:T(8,128)(2,1)S(1)}, u32[]{:S(2)}, u32[]{:S(2)}) collective-permute-start(bf16[16,128,256]{2,1,0:T(8,128)(2,1)} %bitcast.35), channel_id=1, source_target_pairs={{0,16},{16,0},{1,17},{17,1},{2,18},{18,2},{3,19},{19,3},{4,20},{20... | collective-permute-start | bytes 3145736 | tf_op jit(solution)/shard_map/ppermute | solution.py:433
  1.2 5.0 %collective-permute-start.2 = (f32[16,3,128]{2,1,0:T(4,128)S(1)}, f32[16,3,128]{2,1,0:T(4,128)S(1)}, u32[]{:S(2)}, u32[]{:S(2)}) collective-permute-start(f32[16,3,128]{2,1,0:T(4,128)S(1)} %bitcast.37), channel_id=1, source_target_pairs={{0,16},{16,0},{1,17},{17,1},{2,18},{18,2},{3,19},{19,3},{4,20},{20... | collective-permute-start | bytes 73736 | tf_op jit(solution)/shard_map/ppermute | solution.py:430
  1.3 4.8 %collective-permute-start = (s32[16]{0:T(128)}, s32[16]{0:T(128)S(1)}, u32[]{:S(2)}, u32[]{:S(2)}) collective-permute-start(s32[16]{0:T(128)} %bitcast.29), channel_id=1, source_target_pairs={{0,16},{16,0},{1,17},{17,1},{2,18},{18,2},{3,19},{19,3},{4,20},{20... | collective-permute-start | bytes 200 | tf_op jit(solution)/shard_map/ppermute | solution.py:432
  6.2 24.6 %copy-start.1 = (bf16[2048,256]{1,0:T(8,128)(2,1)}, bf16[2048,256]{1,0:T(8,128)(2,1)S(1)}, u32[]{:S(2)}) copy-start(bf16[2048,256]{1,0:T(8,128)(2,1)S(1)} %get-tuple-element.31.refs_2_.refs_6_) | copy-start | bytes 3145732
  8.1 22.7 %copy-start = (bf16[2048,256]{1,0:T(8,128)(2,1)}, bf16[2048,256]{1,0:T(8,128)(2,1)S(1)}, u32[]{:S(2)}) copy-start(bf16[2048,256]{1,0:T(8,128)(2,1)S(1)} %get-tuple-element.36.refs_4_.refs_2_.refs_7_) | copy-start | bytes 3145732
  9.2 11.1 %collective-permute-start.4 = (bf16[2,128,256]{2,1,0:T(8,128)(2,1)S(1)}, bf16[2,128,256]{2,1,0:T(8,128)(2,1)S(1)}, u32[]{:S(2)}, u32[]{:S(2)}) collective-permute-start(bf16[2,128,256]{2,1,0:T(8,128)(2,1)S(1)} %bitcast.28), channel_id=1, source_target_pairs={{0,2},{1,3},{2,0},{3,1},{4,6},{5,7},{6,4},{7,5},{8,10},{9,11},{10,... | collective-permute-start | bytes 393224 | tf_op jit(solution)/shard_map/ppermute | solution.py:461
  11.8 8.5 %collective-permute-start.5 = (bf16[2,128,256]{2,1,0:T(8,128)(2,1)S(1)}, bf16[2,128,256]{2,1,0:T(8,128)(2,1)S(1)}, u32[]{:S(2)}, u32[]{:S(2)}) collective-permute-start(bf16[2,128,256]{2,1,0:T(8,128)(2,1)S(1)} %bitcast.32), channel_id=1, source_target_pairs={{0,3},{1,2},{2,1},{3,0},{4,7},{5,6},{6,5},{7,4},{8,11},{9,10},{10,... | collective-permute-start | bytes 393224 | tf_op jit(solution)/shard_map/ppermute | solution.py:461
  15.4 15.4 %copy-start.12 = (bf16[256,256]{1,0:T(8,128)(2,1)S(1)}, bf16[256,256]{1,0:T(8,128)(2,1)}, u32[]{:S(2)}) copy-start(bf16[256,256]{1,0:T(8,128)(2,1)} %refs_5_.1) | copy-start | bytes 393220
  15.4 5.4 %collective-permute-start.3 = (bf16[2,128,256]{2,1,0:T(8,128)(2,1)S(1)}, bf16[2,128,256]{2,1,0:T(8,128)(2,1)S(1)}, u32[]{:S(2)}, u32[]{:S(2)}) collective-permute-start(bf16[2,128,256]{2,1,0:T(8,128)(2,1)S(1)} %bitcast.33), channel_id=1, source_target_pairs={{0,1},{1,0},{2,3},{3,2},{4,5},{5,4},{6,7},{7,6},{8,9},{9,8},{10,11... | collective-permute-start | bytes 393224 | tf_op jit(solution)/shard_map/ppermute | solution.py:461
  20.3 24.9 %copy-start.17 = (s32[1,16,8]{1,2,0:T(8,128)S(1)}, s32[1,16,8]{1,2,0:T(8,128)}, u32[]{:S(2)}) copy-start(s32[1,16,8]{1,2,0:T(8,128)} %param.11) | copy-start | bytes 1540
  20.3 25.6 %copy-start.11 = (bf16[256,256]{1,0:T(8,128)(2,1)S(1)}, bf16[256,256]{1,0:T(8,128)(2,1)}, u32[]{:S(2)}) copy-start(bf16[256,256]{1,0:T(8,128)(2,1)} %refs_6_.1) | copy-start | bytes 393220
  20.8 7.2 %collective-permute-start.6 = (bf16[2,32,256]{2,1,0:T(8,128)(2,1)S(1)}, bf16[2,32,256]{2,1,0:T(8,128)(2,1)S(1)}, u32[]{:S(2)}, u32[]{:S(2)}) collective-permute-start(bf16[2,32,256]{2,1,0:T(8,128)(2,1)S(1)} %get-tuple-element.43), channel_id=1, source_target_pairs={{0,4},{1,5},{2,6},{3,7},{4,0},{5,1},{6,2},{7,3},{8,12},{9,13},{10,... | collective-permute-start | bytes 98312 | tf_op jit(solution)/shard_map/ppermute | solution.py:530
  22.5 5.6 %collective-permute-start.7 = (bf16[2,32,256]{2,1,0:T(8,128)(2,1)S(1)}, bf16[2,32,256]{2,1,0:T(8,128)(2,1)S(1)}, u32[]{:S(2)}, u32[]{:S(2)}) collective-permute-start(bf16[2,32,256]{2,1,0:T(8,128)(2,1)S(1)} %get-tuple-element.44), channel_id=1, source_target_pairs={{0,8},{1,9},{2,10},{3,11},{4,12},{5,13},{6,14},{7,15},{8,0},{9,1},... | collective-permute-start | bytes 98312 | tf_op jit(solution)/shard_map/ppermute | solution.py:530
  25.1 5.7 %collective-permute-start.8 = (bf16[2,32,256]{2,1,0:T(8,128)(2,1)S(1)}, bf16[2,32,256]{2,1,0:T(8,128)(2,1)S(1)}, u32[]{:S(2)}, u32[]{:S(2)}) collective-permute-start(bf16[2,32,256]{2,1,0:T(8,128)(2,1)S(1)} %get-tuple-element.45), channel_id=1, source_target_pairs={{0,12},{1,13},{2,14},{3,15},{4,8},{5,9},{6,10},{7,11},{8,4},{9,5},... | collective-permute-start | bytes 98312 | tf_op jit(solution)/shard_map/ppermute | solution.py:530
  31.0 10.1 %collective-permute-start.15 = (bf16[2,128,256]{2,1,0:T(8,128)(2,1)S(1)}, bf16[2,128,256]{2,1,0:T(8,128)(2,1)S(1)}, u32[]{:S(2)}, u32[]{:S(2)}) collective-permute-start(bf16[2,128,256]{2,1,0:T(8,128)(2,1)S(1)} %get-tuple-element.52), channel_id=1, source_target_pairs={{0,1},{1,2},{2,3},{3,4},{4,5},{5,6},{6,7},{7,8},{8,9},{9,10},{10,1... | collective-permute-start | bytes 393224 | tf_op jit(solution)/shard_map/ppermute | solution.py:551
  34.4 5.8 %collective-permute-start.11 = (bf16[2,32,256]{2,1,0:T(8,128)(2,1)S(1)}, bf16[2,32,256]{2,1,0:T(8,128)(2,1)S(1)}, u32[]{:S(2)}, u32[]{:S(2)}) collective-permute-start(bf16[2,32,256]{2,1,0:T(8,128)(2,1)S(1)} %get-tuple-element.47.refs_0_), channel_id=1, source_target_pairs={{0,12},{1,13},{2,14},{3,15},{4,8},{5,9},{6,10},{7,11},{8,4},{9,5},... | collective-permute-start | bytes 98312 | tf_op jit(solution)/shard_map/ppermute | solution.py:559
  35.4 5.6 %collective-permute-start.10 = (bf16[2,32,256]{2,1,0:T(8,128)(2,1)S(1)}, bf16[2,32,256]{2,1,0:T(8,128)(2,1)S(1)}, u32[]{:S(2)}, u32[]{:S(2)}) collective-permute-start(bf16[2,32,256]{2,1,0:T(8,128)(2,1)S(1)} %get-tuple-element.47.refs_0_), channel_id=1, source_target_pairs={{0,8},{1,9},{2,10},{3,11},{4,12},{5,13},{6,14},{7,15},{8,0},{9,1},... | collective-permute-start | bytes 98312 | tf_op jit(solution)/shard_map/ppermute | solution.py:559
  35.4 5.7 %collective-permute-start.9 = (bf16[2,32,256]{2,1,0:T(8,128)(2,1)S(1)}, bf16[2,32,256]{2,1,0:T(8,128)(2,1)S(1)}, u32[]{:S(2)}, u32[]{:S(2)}) collective-permute-start(bf16[2,32,256]{2,1,0:T(8,128)(2,1)S(1)} %get-tuple-element.47.refs_0_), channel_id=1, source_target_pairs={{0,4},{1,5},{2,6},{3,7},{4,0},{5,1},{6,2},{7,3},{8,12},{9,13},{10,... | collective-permute-start | bytes 98312 | tf_op jit(solution)/shard_map/ppermute | solution.py:559
  41.1 4.1 %collective-permute-start.17 = (bf16[2,128,256]{2,1,0:T(8,128)(2,1)S(1)}, bf16[2,128,256]{2,1,0:T(8,128)(2,1)S(1)}, u32[]{:S(2)}, u32[]{:S(2)}) collective-permute-start(bf16[2,128,256]{2,1,0:T(8,128)(2,1)S(1)} %shard_map.91.refs_7_), channel_id=1, source_target_pairs={{0,16},{16,0},{1,17},{17,1},{2,18},{18,2},{3,19},{19,3},{4,20},{20... | collective-permute-start | bytes 393224 | tf_op jit(solution)/shard_map/ppermute | solution.py:566
  41.1 4.1 %copy-start.14 = (bf16[2,128,256]{2,1,0:T(8,128)(2,1)}, bf16[2,128,256]{2,1,0:T(8,128)(2,1)S(1)}, u32[]{:S(2)}) copy-start(bf16[2,128,256]{2,1,0:T(8,128)(2,1)S(1)} %collective-permute-done.15.refs_4_) | copy-start | bytes 393220
  41.2 4.1 %collective-permute-start.16 = (bf16[2,128,256]{2,1,0:T(8,128)(2,1)S(1)}, bf16[2,128,256]{2,1,0:T(8,128)(2,1)S(1)}, u32[]{:S(2)}, u32[]{:S(2)}) collective-permute-start(bf16[2,128,256]{2,1,0:T(8,128)(2,1)S(1)} %collective-permute-done.15.refs_4_), channel_id=1, source_target_pairs={{0,16},{16,0},{1,17},{17,1},{2,18},{18,2},{3,19},{19,3},{4,20},{20... | collective-permute-start | bytes 393224 | tf_op jit(solution)/shard_map/ppermute | solution.py:552
  41.6 11.6 %collective-permute-start.14 = (bf16[2,128,256]{2,1,0:T(8,128)(2,1)S(1)}, bf16[2,128,256]{2,1,0:T(8,128)(2,1)S(1)}, u32[]{:S(2)}, u32[]{:S(2)}) collective-permute-start(bf16[2,128,256]{2,1,0:T(8,128)(2,1)S(1)} %shard_map.91.refs_7_), channel_id=1, source_target_pairs={{0,3},{1,2},{2,1},{3,0},{4,7},{5,6},{6,5},{7,4},{8,11},{9,10},{10,... | collective-permute-start | bytes 393224 | tf_op jit(solution)/shard_map/ppermute | solution.py:564
  42.3 10.9 %collective-permute-start.13 = (bf16[2,128,256]{2,1,0:T(8,128)(2,1)S(1)}, bf16[2,128,256]{2,1,0:T(8,128)(2,1)S(1)}, u32[]{:S(2)}, u32[]{:S(2)}) collective-permute-start(bf16[2,128,256]{2,1,0:T(8,128)(2,1)S(1)} %shard_map.91.refs_7_), channel_id=1, source_target_pairs={{0,2},{1,3},{2,0},{3,1},{4,6},{5,7},{6,4},{7,5},{8,10},{9,11},{10,... | collective-permute-start | bytes 393224 | tf_op jit(solution)/shard_map/ppermute | solution.py:564
  44.6 8.7 %collective-permute-start.12 = (bf16[2,128,256]{2,1,0:T(8,128)(2,1)S(1)}, bf16[2,128,256]{2,1,0:T(8,128)(2,1)S(1)}, u32[]{:S(2)}, u32[]{:S(2)}) collective-permute-start(bf16[2,128,256]{2,1,0:T(8,128)(2,1)S(1)} %shard_map.91.refs_7_), channel_id=1, source_target_pairs={{0,1},{1,0},{2,3},{3,2},{4,5},{5,4},{6,7},{7,6},{8,9},{9,8},{10,11... | collective-permute-start | bytes 393224 | tf_op jit(solution)/shard_map/ppermute | solution.py:564
  45.9 7.5 %copy-start.5 = (bf16[256,2048]{1,0:T(8,128)(2,1)S(1)}, bf16[256,2048]{1,0:T(8,128)(2,1)}, u32[]{:S(2)}) copy-start(bf16[256,2048]{1,0:T(8,128)(2,1)} %get-tuple-element.49.refs_5_) | copy-start | bytes 3145732
  45.9 7.5 %copy-start.6 = (bf16[256,2048]{1,0:T(8,128)(2,1)S(1)}, bf16[256,2048]{1,0:T(8,128)(2,1)}, u32[]{:S(2)}) copy-start(bf16[256,2048]{1,0:T(8,128)(2,1)} %get-tuple-element.48.refs_4_) | copy-start | bytes 3145732
  53.3 2.8 %collective-permute-start.18 = (bf16[2,384,256]{2,1,0:T(8,128)(2,1)S(1)}, bf16[2,384,256]{2,1,0:T(8,128)(2,1)S(1)}, u32[]{:S(2)}, u32[]{:S(2)}) collective-permute-start(bf16[2,384,256]{2,1,0:T(8,128)(2,1)S(1)} %shard_map.94), channel_id=1, source_target_pairs={{0,16},{16,0},{1,17},{17,1},{2,18},{18,2},{3,19},{19,3},{4,20},{20... | collective-permute-start | bytes 1179656 | tf_op jit(solution)/shard_map/ppermute | solution.py:584
  54.8 1.5 %copy-start.7 = (bf16[256,2048]{1,0:T(8,128)(2,1)S(1)}, bf16[256,2048]{1,0:T(8,128)(2,1)}, u32[]{:S(2)}) copy-start(bf16[256,2048]{1,0:T(8,128)(2,1)} %get-tuple-element.53.refs_0_) | copy-start | bytes 3145732
  54.8 1.9 %copy-start.8 = (bf16[256,2048]{1,0:T(8,128)(2,1)S(1)}, bf16[256,2048]{1,0:T(8,128)(2,1)}, u32[]{:S(2)}) copy-start(bf16[256,2048]{1,0:T(8,128)(2,1)} %get-tuple-element.54.refs_1_) | copy-start | bytes 3145732
  54.8 2.2 %copy-start.9 = (bf16[256,2048]{1,0:T(8,128)(2,1)S(1)}, bf16[256,2048]{1,0:T(8,128)(2,1)}, u32[]{:S(2)}) copy-start(bf16[256,2048]{1,0:T(8,128)(2,1)} %get-tuple-element.55.refs_2_) | copy-start | bytes 3145732
  54.8 2.5 %copy-start.10 = (bf16[256,2048]{1,0:T(8,128)(2,1)S(1)}, bf16[256,2048]{1,0:T(8,128)(2,1)}, u32[]{:S(2)}) copy-start(bf16[256,2048]{1,0:T(8,128)(2,1)} %get-tuple-element.56.refs_3_) | copy-start | bytes 3145732
  54.8 2.5 %copy-start.13 = (s32[1,16]{1,0:T(1,128)S(1)}, s32[1,16]{1,0:T(1,128)}, u32[]{:S(2)}) copy-start(s32[1,16]{1,0:T(1,128)} %param.12) | copy-start | bytes 196
  (5 other events, 5.4 us)

commit v4 on v3

--- a/solution.py
+++ b/solution.py
@@ -20,7 +20,7 @@
 COS = (1.41420401, -6.97763732, 5.71518787, -1.72821389)
 
 
-def call(kernel, outs, operands, scratch=(), held=(), flops=0):
+def call(kernel, outs, operands, scratch=(), held=(), flops=0, same=()):
     ahead = len(operands)
     operands = list(operands) + [(VMEM, array) for array in held]
 
@@ -33,6 +33,7 @@
         out_specs=[place for place, _ in outs],
         out_shape=[place.memory_space(*kind) for place, kind in outs],
         scratch_shapes=list(scratch),
+        input_output_aliases=dict(same),
         compiler_params=PARAMS,
         cost_estimate=pl.CostEstimate(flops=flops, bytes_accessed=flops // 300, transcendentals=0),
     )(
@@ -81,14 +82,14 @@
 
 
 def fill_places(offsets_ref, places_ref, first, slab, cell_line, slabs):
-    cells, _, slots = offsets_ref.shape
+    _, cells, slots = offsets_ref.shape
     line = lax.broadcasted_iota(jnp.int32, (8, slots), 0)
     along_z_base = slab.astype(F32)
     for cell in range(cells):
-        own = offsets_ref[cell]
-        along_x = ((first + cell).astype(F32) + own[0:1]) / cell_line
-        along_z = (along_z_base + own[2:3]) / slabs
-        full = jnp.where(line == 0, along_x, jnp.where(line == 1, own[1:2], jnp.where(line == 2, along_z, 0.0)))
+        along_x = ((first + cell).astype(F32) + offsets_ref[0, cell : cell + 1]) / cell_line
+        along_y = offsets_ref[1, cell : cell + 1]
+        along_z = (along_z_base + offsets_ref[2, cell : cell + 1]) / slabs
+        full = jnp.where(line == 0, along_x, jnp.where(line == 1, along_y, jnp.where(line == 2, along_z, 0.0)))
         high = full.astype(BF16).astype(F32)
         middle = (full - high).astype(BF16).astype(F32)
         low = full - high - middle
@@ -141,11 +142,9 @@
 
 def own_kernel(early, block, digits, lengths, *refs):
     sources, refs = refs[:4], refs[4:]
-    masked_ref, places_ref, turned_ref = refs[:3]
-    tables, sums = refs[3 : 3 + len(early)], refs[3 + len(early) : 3 + 2 * len(early)]
-    padded_ref, waves_ref, offsets_ref, counts_ref, features_ref, kept_ref, semaphores, kept_semaphores = refs[
-        3 + 2 * len(early) :
-    ]
+    masked_ref, places_ref, turned_ref, table_ref = refs[:4]
+    sums = refs[4 : 4 + len(early)]
+    padded_ref, waves_ref, offsets_ref, counts_ref, features_ref, semaphores = refs[4 + len(early) :]
     copies = begin(sources, (waves_ref, offsets_ref, counts_ref, features_ref), semaphores)
     cells = features_ref.shape[0]
     dev, slab = lax.axis_index("dev"), lax.axis_index("grp")
@@ -161,13 +160,9 @@
     copies[2].wait()
     copies[3].wait()
     fill_masked(counts_ref, features_ref, masked_ref)
-    leaving = []
-    for index, (place, sums_ref) in enumerate(zip(early, sums)):
-        table_ref = kept_ref.at[index]
-        fill_table(turned_ref[place * block : (place + 1) * block, :], places_ref, table_ref)
-        leaving += begin([table_ref], [tables[index]], kept_semaphores, index)
-        sums_ref[...] = sums_of(table_ref, masked_ref)
-    finish(leaving)
+    for place, sums_ref in zip(early, sums):
+        fill_table(turned_ref[place * block : (place + 1) * block, :], places_ref, table_ref.at[place])
+        sums_ref[...] = sums_of(table_ref.at[place], masked_ref)
 
 
 def sibling_kernel(
@@ -187,26 +182,13 @@
 
 
 def both_kernel(
-    place, block, turned_ref, own_places_ref, own_ref, places_ref, masked_ref, kept_ref, piece_ref, table_ref, semaphores
+    place, block, turned_ref, own_places_ref, own_ref, places_ref, masked_ref, _, kept_ref, piece_ref, table_ref
 ):
     waves = turned_ref[place * block : (place + 1) * block, :]
-    fill_table(waves, own_places_ref, table_ref.at[0])
-    leaving = begin([table_ref.at[0]], [kept_ref], semaphores)
-    total = sums_of(table_ref.at[0], own_ref)
-    fill_table(waves, places_ref, table_ref.at[1])
-    piece_ref[...] = (total + sums_of(table_ref.at[1], masked_ref)).astype(piece_ref.dtype)
-    finish(leaving)
-
-
-def rest_kernel(first, block, turned_ref, places_ref, mark_ref, *refs):
-    *tables, table_ref, semaphores = refs
-    mark_ref[...] = jnp.zeros_like(mark_ref)
-    leaving = []
-    for place, target_ref in enumerate(tables):
-        start = first + place * block
-        fill_table(turned_ref[start : start + block, :], places_ref, table_ref.at[place])
-        leaving += begin([table_ref.at[place]], [target_ref], semaphores, place)
-    finish(leaving)
+    fill_table(waves, own_places_ref, kept_ref.at[place])
+    total = sums_of(kept_ref.at[place], own_ref)
+    fill_table(waves, places_ref, table_ref)
+    piece_ref[...] = (total + sums_of(table_ref, masked_ref)).astype(piece_ref.dtype)
 
 
 def fill_edges(lines, outs):
@@ -222,12 +204,20 @@
         outs[1][line] = rows_ref[:slots, :]
 
 
+def rest_kernel(blocks, block, lines, turned_ref, places_ref, _, *refs):
+    kept_ref, *edges = refs[lines:]
+    if edges:
+        fill_edges(refs[:lines], edges)
+    for place in blocks:
+        fill_table(turned_ref[place * block : (place + 1) * block, :], places_ref, kept_ref.at[place])
+
+
 def short_kernel(lines, chunks, codes_ref, source_ref, *refs):
     line_refs, refs = refs[:lines], refs[lines:]
     one_ref, two_ref, w_ref, message_ref = refs[:4]
-    window_ref, starts_ref, radial_ref, semaphores = refs[4:]
+    window_ref, found_ref, radial_ref, semaphores = refs[4:]
     cells, slots, channels = message_ref.shape
-    pairs = radial_ref.shape[1]
+    pairs = codes_ref.shape[0]
     slab, slabs = lax.axis_index("grp"), lax.axis_size("grp")
     share = cells // chunks
     edges = []
@@ -242,37 +232,48 @@
     edges = begin(*zip(*edges), semaphores)
     parts = []
     for chunk in range(chunks):
-        span = pl.ds(chunk * share, share)
+        span = pl.ds(chunk * share * pairs, share * pairs)
         moves = [(source_ref.at[span], radial_ref.at[span])]
         for line, line_ref in enumerate(line_refs):
-            moves.append((line_ref.at[span], window_ref.at[pl.ds(line * (cells + 2) + 1 + chunk * share, share)]))
+            base = line * (cells + 2) + 1 + chunk * share
+            moves.append((line_ref.at[pl.ds(chunk * share, share)], window_ref.at[pl.ds(base, share)]))
         parts.append(begin(*zip(*moves), semaphores, 2 * lines + chunk * (1 + lines)))
-    nothing = lines * (cells + 2)
-    window_ref[nothing] = jnp.zeros((slots, channels), BF16)
-    for level in range(3):
-        line = 0 if level == 1 else 1 if lines == 2 else 1 + level // 2
-        inside = (slab + level >= 1) & (slab + level - 1 < slabs)
-        for along in range(3):
-            starts_ref[3 * level + along] = jnp.where(inside, line * (cells + 2) + along, -1)
-
+    nothing = cells * pairs
+    radial_ref[nothing] = jnp.zeros((slots, slots), BF16)
     for cell in range(cells):
-        if cell == 0:
-            finish(edges)
-            finish(parts[0])
-        if cell % share == 0 and cell // share + 1 < chunks:
-            finish(parts[cell // share + 1])
+        for code in range(9):
+            found_ref[9 * cell + code] = nothing
+        for pair in range(pairs):
+            found_ref[9 * cell + codes_ref[pair, cell]] = cell * pairs + pair
+    levels = [1, 2 - 2 * slab] if slabs == 2 else [1, 0, 2]
+    finish(edges)
+    ready = 0
+    carried = None
+    for start in range(0, cells + 2, 2):
+        takers = [cell for cell in range(start - 2, start + 2) if 0 <= cell < cells]
+        while ready <= takers[-1] // share:
+            finish(parts[ready])
+            ready += 1
         total = None
-        for pair in range(0, pairs, 2):
-            blocks, taken = [], []
-            for p in range(pair, min(pair + 2, pairs)):
-                start = starts_ref[codes_ref[cell, p]]
-                blocks.append(radial_ref[cell, p])
-                taken.append(window_ref[jnp.where(start < 0, nothing, start + cell)])
-            part = jnp.dot(
-                jnp.concatenate(blocks, axis=1), jnp.concatenate(taken, axis=0), preferred_element_type=F32
-            )
+        for line, level in enumerate(levels):
+            rows = []
+            for cell in takers:
+                halves = []
+                for place in (start, start + 1):
+                    along = place - cell
+                    index = found_ref[9 * cell + 3 * level + along] if 0 <= along < 3 else nothing
+                    halves.append(radial_ref[index])
+                rows.append(jnp.concatenate(halves, axis=1))
+            base = line * (cells + 2) + start
+            taken = window_ref[base : base + 2].reshape(2 * slots, channels)
+            part = jnp.dot(jnp.concatenate(rows, axis=0), taken, preferred_element_type=F32)
             total = part if total is None else total + part
-        message_ref[cell] = jnp.dot(total.astype(BF16), w_ref[...], preferred_element_type=F32)
+        if start:
+            gathered = (carried + total[: 2 * slots]).astype(BF16)
+            message = jnp.dot(gathered, w_ref[...], preferred_element_type=F32)
+            message_ref[start - 2 : start] = message.reshape(2, slots, channels)
+            total = total[2 * slots :]
+        carried = total
 
 
 def add_kernel(count, radix, *refs):
@@ -307,12 +308,9 @@
     return (energy * jnp.concatenate([kernel, kernel], axis=0)).astype(BF16)
 
 
-def energy_kernel(count, lines, factor_scale, *refs):
+def energy_kernel(count, factor_scale, *refs):
     pieces = refs[:count]
-    turned_ref, w_mix_ref = refs[count : count + 2]
-    energy_ref, *edges = refs[count + 2 + lines :]
-    if edges:
-        fill_edges(refs[count + 2 : count + 2 + lines], edges)
+    turned_ref, w_mix_ref, energy_ref = refs[count:]
     trig, rows, channels = energy_ref.shape
     total = pieces[0][...].astype(F32)
     for piece in pieces[1:]:
@@ -322,21 +320,19 @@
     energy_ref[...] = energy.reshape(trig, rows, channels)
 
 
-def energy_of(pieces, turned, w_mix, factor_scale, lines, slots, held):
+def energy_of(pieces, turned, w_mix, factor_scale, held):
     trig, rows, channels = pieces[0].shape
     if rows % 16:
         total = functools.reduce(jnp.add, [piece.astype(F32) for piece in pieces])
         energy = mixed(total.reshape(trig * rows, channels), turned[:rows].astype(F32), w_mix, factor_scale)
-        edges = [jnp.stack([line[-slots:] for line in lines]), jnp.stack([line[:slots] for line in lines])]
-        return energy.reshape(trig, rows, channels), edges
-    edge = (VMEM, ((len(lines), slots, channels), BF16))
-    energy, *edges = call(
-        functools.partial(energy_kernel, len(pieces), len(lines), factor_scale),
-        [(VMEM, ((trig, rows, channels), BF16))] + [edge] * (1 if lax.axis_size("grp") == 2 else 2),
-        in_vmem([*pieces, turned, w_mix, *lines]),
+        return energy.reshape(trig, rows, channels)
+    (energy,) = call(
+        functools.partial(energy_kernel, len(pieces), factor_scale),
+        [(VMEM, ((trig, rows, channels), BF16))],
+        in_vmem([*pieces, turned, w_mix]),
         held=held,
     )
-    return energy, edges
+    return energy
 
 
 def join_kernel(*refs):
@@ -356,21 +352,22 @@
 
 
 def near_kernel(blocks, *refs):
-    energies, tables, (out_ref, turned_ref) = refs[:blocks], refs[blocks : 2 * blocks], refs[2 * blocks :]
+    energies, (table_ref, out_ref, turned_ref) = refs[:blocks], refs[blocks:]
     for place, energy in enumerate(energies):
         turned_ref[place] = energy[...].astype(F32).T.astype(BF16)
     atoms = out_ref.shape[1]
     tile = math.gcd(atoms, 512)
     for start in range(0, atoms, tile):
         total = None
-        for place, table_ref in enumerate(tables):
-            part = jnp.dot(turned_ref[place], table_ref[:, start : start + tile], preferred_element_type=F32)
+        for place in range(blocks):
+            part = jnp.dot(turned_ref[place], table_ref[place, :, start : start + tile], preferred_element_type=F32)
             total = part if total is None else total + part
         out_ref[:, start : start + tile] = total
 
 
-def final_kernel(scale, counts_ref, masked_ref, near_ref, message_ref, energy_ref, rest_ref, *refs):
-    tables, (out_ref, turned_ref) = refs[:-2], refs[-2:]
+def final_kernel(
+    blocks, scale, counts_ref, masked_ref, near_ref, message_ref, energy_ref, rest_ref, table_ref, out_ref, turned_ref
+):
     cells, slots, channels = out_ref.shape
     step = pl.program_id(0)
 
@@ -379,15 +376,15 @@
         rows = energy_ref.shape[0]
         half = rows // 2
         turned_ref[0] = energy_ref[...].astype(F32).T.astype(BF16)
-        for place in range(1, len(tables)):
+        for place in range(1, blocks):
             taken = rest_ref[:, (place - 1) * half : place * half, :].reshape(rows, channels)
             turned_ref[place] = taken.astype(F32).T.astype(BF16)
 
     atoms = cells * slots
     span = pl.ds(pl.multiple_of(step * atoms, atoms), atoms)
     total = near_ref[:, span]
-    for place, table_ref in enumerate(tables):
-        total = total + jnp.dot(turned_ref[place], table_ref[:, span], preferred_element_type=F32)
+    for place in range(blocks):
+        total = total + jnp.dot(turned_ref[place], table_ref[blocks + place, :, span], preferred_element_type=F32)
     slot_ids = lax.broadcasted_iota(jnp.int32, (slots, channels), 0)
     for cell in range(cells):
         index = step * cells + cell
@@ -397,15 +394,14 @@
         out_ref[cell] = jnp.where(slot_ids < counts_ref[index], result, 0.0).astype(BF16)
 
 
-def final_call(counts, near, message, masked, energy, rest, tables, scale):
+def final_call(counts, near, message, masked, energy, rest, table, scale):
     cells, slots, channels = message.shape
-    rows = tables[0].shape[0]
-    blocks = len(tables)
+    blocks, rows = table.shape[0] // 2, table.shape[1]
     group = math.gcd(cells, 4)
     cells_spec = pl.BlockSpec((group, slots, channels), lambda i: (i, 0, 0))
-    operands = [masked, near, message, energy, rest, *tables]
+    operands = [masked, near, message, energy, rest, table]
     return pl.pallas_call(
-        functools.partial(final_kernel, scale),
+        functools.partial(final_kernel, blocks, scale),
         grid=(cells // group,),
         in_specs=[SMEM] + [VMEM] * len(operands),
         out_specs=cells_spec,
@@ -424,7 +420,7 @@
     total_slots = slabs * cell_line * slots
     atoms = cells * slots
     lengths = (float(cell_line), float(slabs))
-    features, offsets, counts = features[0], offsets[0], counts[0]
+    features, offsets, counts = features[0], offsets[0].transpose(1, 0, 2), counts[0]
 
     swap = pairs_at("grp", 1, 1)
     sibling_offsets = lax.ppermute(offsets, "grp", swap)
@@ -450,22 +446,18 @@
     piece = ((2 * block, channels), BF16)
     places_type = ((32, atoms), BF16)
     rows_type = ((atoms, channels), BF16)
-    edge = ((2, slots, channels), BF16)
+    whole_table = (VMEM, ((2 * blocks,) + table[0], BF16))
     scratch = [pltpu.VMEM(*table)]
     block_flops = 2 * 2 * block * atoms * channels * COST
 
-    def several(count):
-        return [pltpu.VMEM((count,) + table[0], BF16), pltpu.SemaphoreType.DMA((count,))]
-
     def sent(part, place):
         return lax.ppermute(part.reshape(2, block, channels), axis, pairs_at(axis, stride, place))
 
     order = [*range(blocks - 1, 0, -1), 0]
     early = order[: min(2, blocks - 1)]
-    masked, places, turned, *outs = call(
+    masked, places, turned, tables, *outs = call(
         functools.partial(own_kernel, early, block, digits, lengths),
-        [(VMEM, rows_type), (VMEM, places_type), (VMEM, ((wave_count, 32), BF16))]
-        + [(HBM, table)] * len(early)
+        [(VMEM, rows_type), (VMEM, places_type), (VMEM, ((wave_count, 32), BF16)), whole_table]
         + [(VMEM, sums)] * len(early),
         in_hbm([wavevectors, offsets, counts, features]),
         [
@@ -474,13 +466,10 @@
             pltpu.VMEM(offsets.shape, F32),
             pltpu.SMEM(counts.shape, jnp.int32),
             pltpu.VMEM(features.shape, BF16),
-            pltpu.VMEM((len(early),) + table[0], BF16),
             pltpu.SemaphoreType.DMA((4,)),
-            pltpu.SemaphoreType.DMA((len(early),)),
         ],
     )
-    tables = dict(zip(early, outs))
-    started = dict(zip(early, outs[len(early) :]))
+    started = dict(zip(early, outs))
     sibling, sibling_places, part = call(
         functools.partial(sibling_kernel, early[0], block, lengths),
         [(VMEM, rows_type), (VMEM, places_type), (VMEM, piece)],
@@ -498,40 +487,18 @@
         )
         received[place] = sent(part, place)
     for place in order[len(early) :]:
-        tables[place], part = call(
+        tables, part = call(
             functools.partial(both_kernel, place, block),
-            [(HBM, table), (VMEM, piece if place else sums)],
-            in_vmem([turned, places, masked, sibling_places, sibling]),
-            [pltpu.VMEM((2,) + table[0], BF16), pltpu.SemaphoreType.DMA((1,))],
+            [whole_table, (VMEM, piece if place else sums)],
+            in_vmem([turned, places, masked, sibling_places, sibling, tables]),
+            scratch,
             [part] if place else [],
             2 * block_flops,
+            {5: 0},
         )
         if place:
             received[place] = sent(part, place)
     pieces = [part.reshape(2, block, channels)] + [received[place] for place in range(1, blocks)]
-    tables = [tables[place] for place in range(blocks)]
-
-    def rest_of_tables(first, count, held):
-        return call(
-            functools.partial(rest_kernel, half + first * block, block),
-            [(VMEM, ((8, LANES), F32))] + [(HBM, table)] * count,
-            in_vmem([turned, places]),
-            several(count),
-            held,
-            block_flops * count,
-        )
-
-    share = blocks // 2
-    mark, *others = rest_of_tables(0, share, [part])
-
-    for axis, stride, radix in stages[1:]:
-        parts = add_and_cut(pieces, radix, [mark])
-        pieces = [parts[0]] + [
-            lax.ppermute(parts[place], axis, pairs_at(axis, stride, place)) for place in range(1, radix)
-        ]
-
-    mark, *more = rest_of_tables(share, blocks - share, [parts[0]])
-    others += more
 
     if slabs == 2:
         lines = [masked, sibling]
@@ -542,7 +509,28 @@
             )
             for count, cell in near
         ]
-    energy, edges = energy_of(pieces, turned, w_mix, 1.0 / math.sqrt(total_slots), lines, slots, [mark])
+    edge = (VMEM, ((len(lines), slots, channels), BF16))
+
+    def rest_of(tables, first, last, lines, edges, held):
+        return call(
+            functools.partial(rest_kernel, range(first, last), block, len(lines)),
+            [whole_table, *edges],
+            in_vmem([turned, places, tables, *lines]),
+            held=held,
+            flops=block_flops * (last - first),
+            same={2: 0},
+        )
+
+    middle = blocks + blocks // 2
+    tables, *edges = rest_of(tables, blocks, middle, lines, [edge] * (1 if slabs == 2 else 2), [part])
+
+    for axis, stride, radix in stages[1:]:
+        parts = add_and_cut(pieces, radix, [tables])
+        pieces = [parts[0]] + [
+            lax.ppermute(parts[place], axis, pairs_at(axis, stride, place)) for place in range(1, radix)
+        ]
+
+    (tables,) = rest_of(tables, middle, 2 * blocks, [], [], [parts[0]])
 
     right = [(i, i + 1) for i in range(dev_count - 1)]
     left = [(j, i) for i, j in right]
@@ -554,10 +542,12 @@
         one = lax.ppermute(edges[0], "dev", right)
         two = lax.ppermute(edges[1], "dev", left)
 
+    energy = energy_of(pieces, turned, w_mix, 1.0 / math.sqrt(total_slots), [tables, one])
+
     for axis, stride, radix in reversed(stages[1:]):
         energy = joined(
             [energy] + [lax.ppermute(energy, axis, pairs_at(axis, stride, place)) for place in range(1, radix)],
-            [],
+            [tables],
         )
     axis, stride, blocks = stages[0]
     energies = [energy] + [
@@ -569,16 +559,16 @@
     (message,) = call(
         functools.partial(short_kernel, len(lines), chunks),
         [(VMEM, ((cells, slots, channels), F32))],
-        [(SMEM, neighbours[0])]
-        + in_hbm([radial[0], *[line.reshape(cells, slots, channels) for line in lines], one, two])
+        [(SMEM, neighbours[0].T)]
+        + in_hbm([radial.reshape(-1, slots, slots), *[line.reshape(cells, slots, channels) for line in lines], one, two])
         + in_vmem([w_msg]),
         [
-            pltpu.VMEM((len(lines) * (cells + 2) + 1, slots, channels), BF16),
-            pltpu.SMEM((9,), jnp.int32),
-            pltpu.VMEM(radial.shape[1:], BF16),
+            pltpu.VMEM((len(lines) * (cells + 2), slots, channels), BF16),
+            pltpu.SMEM((9 * cells,), jnp.int32),
+            pltpu.VMEM((cells * radial.shape[2] + 1, slots, slots), BF16),
             pltpu.SemaphoreType.DMA((2 * len(lines) + chunks * (1 + len(lines)),)),
         ],
-        [energy, other_energy],
+        [energy, other_energy, tables],
         6 * block_flops,
     )
     rest = lax.ppermute(joined(energies[1:], [message]), "grp", swap)
@@ -587,14 +577,14 @@
     (near_sum,) = call(
         functools.partial(near_kernel, blocks),
         [(VMEM, ((channels, atoms), F32))],
-        in_vmem([*energies, *tables]),
+        in_vmem([*energies, tables]),
         [pltpu.VMEM((blocks, channels, 2 * block), BF16)],
         [message],
         2 * block_flops,
     )
     masked = masked.reshape(cells, slots, channels)
     scale = 8.0 / math.sqrt(wave_count)
-    result = final_call(counts, near_sum, message, masked, other_energy, rest, others, scale)
+    result = final_call(counts, near_sum, message, masked, other_energy, rest, tables, scale)
     return result[None]
 
 

time: 61.7 us -> 54.1 us (0.88)
  Pallas kernels: 30 us -> 24.8 us
  local copies, waits for them, and re-layouts: 4.04 us -> 0.69 us
  waiting for transfers between devices: 5.4 us -> 6.32 us
    pallas_call x13, Pallas kernels: 25.8 us -> 20.6 us  [call(): pl.pallas_call(without_held, in_specs=[place for place, _ in operands], o...]
    unnamed x37 -> x18, local copies, waits for them, and re-layouts: 3.97 us -> 0.69 us
    ppermute x3, waiting for transfers between devices: 2.73 us -> 3.88 us  [body(): lax.ppermute(parts[place], axis, pairs_at(axis, stride, place))]
    ppermute x1, starting transfers between devices: 3.39 us -> 4.05 us  [body(): one = lax.ppermute(edges[0], ('grp', 'dev'), ways)]
  transfers between devices with their start and end apart: 19 -> 19, of which waited for: 5 -> 6; matrix products, arithmetic and copies ran while one was open for 1% -> 0% of each run, Pallas kernels for 37% -> 29%
where the time goes in v4:
time: 54.1 us; the launch traced here: 53.8 us
  Pallas kernels  24.8 us (46%)
  starting transfers between devices  21.7 us (40%)
  waiting for transfers between devices  6.32 us (12%)
  local copies, waits for them, and re-layouts  0.69 us (1%)
    pallas_call x13, Pallas kernels, call(): pl.pallas_call(without_held, in_specs=[place for place, _ in operands], o...  20.6 us
    ppermute x6, starting transfers between devices, body(): lax.ppermute(energy, axis, pairs_at(axis, stride, place))  8.01 us
    ppermute x3, starting transfers between devices, body(): lax.ppermute(parts[place], axis, pairs_at(axis, stride, place))  4.45 us
    pallas_call x1, Pallas kernels, final_call(): pl.pallas_call(functools.partial(final_kernel, blocks, scale), grid=(cell...  4.19 us
    ppermute x3, starting transfers between devices, sent(): lax.ppermute(part.reshape(2, block, channels), axis, pairs_at(axis, strid...  4.09 us
    ppermute x1, starting transfers between devices, body(): one = lax.ppermute(edges[0], ('grp', 'dev'), ways)  4.05 us
    ppermute x3, waiting for transfers between devices, body(): lax.ppermute(parts[place], axis, pairs_at(axis, stride, place))  3.88 us
    ppermute x6, waiting for transfers between devices, body(): lax.ppermute(energy, axis, pairs_at(axis, stride, place))  2.03 us
  transfers between devices with their start and end apart: 19, of which 6 were waited for; matrix products, arithmetic and copies ran while one was open for 0% of the time, Pallas kernels for 29%

profile of v4, /device:TPU:0, one launch (start us, length us, event | category | flops | bytes accessed | tf_op | source)
XLA Modules:
  0.0 53.8 jit_solution(15811354558918352734)
XLA Ops:
  0.0 0.5 collective-permute-start.1
  0.5 0.5 collective-permute-start
  1.0 3.5 %shard_map.82 = (bf16[2048,256]{1,0:T(8,128)(2,1)S(1)}, bf16[32,2048]{1,0:T(8,128)(2,1)S(1)}, bf16[1024,32]{1,0:T(8,128)(2,1)S(1)}, bf16[8,256,2048]{2,1,0:T(8,1...) custom-call(s32[3,1024]{1,0:T(4,128)} %refs_0_.1, f32[3,16,128]{2,1,0:T(8,128)} %bitcast.41, s32[16]{0:T(128)} %bitcast.33, ...), custom_call_target="tpu_custom_call" | custom-call | tf_op jit(solution)/shard_map/pallas_call | solution.py:30
  4.5 1.9 %shard_map.83 = (bf16[2048,256]{1,0:T(8,128)(2,1)S(1)}, bf16[32,2048]{1,0:T(8,128)(2,1)S(1)}, bf16[256,256]{1,0:T(8,128)(2,1)S(1)}) custom-call(s32[16]{0:T(128)S(1)} %collective-permute-done.refs_0_, bf16[16,128,256]{2,1,0:T(8,128)(2,1)S(1)} %collective-permute-done.1.refs_1_, f32[3,16,128]{2,1,0:T(8,128)S(1)} %collective-permute-done.2.refs_2_, ...), custom_call_target="tpu_custom_call" | custom-call | tf_op jit(solution)/shard_map/pallas_call | solution.py:30
  6.4 1.1 %shard_map.84.refs_6_ = bf16[256,256]{1,0:T(8,128)(2,1)S(1)} custom-call(bf16[1024,32]{1,0:T(8,128)(2,1)S(1)} %get-tuple-element.25.refs_3_.refs_0_.refs_4_, bf16[32,2048]{1,0:T(8,128)(2,1)S(1)} %get-tuple-element.28.refs_1_.refs_3_, bf16[2048,256]{1,0:T(8,128)(2,1)S(1)} %get-tuple-element.29.refs_2_.refs_4_, f32[256,256]{1,0:T(8,128)S(1)} %get-tuple-element.31.refs_3_), custom_call_target="tpu_custom_call" | custom-call | tf_op jit(solution)/shard_map/pallas_call | solution.py:30
  7.5 2.1 %shard_map.85 = (bf16[8,256,2048]{2,1,0:T(8,128)(2,1)S(1)}, bf16[256,256]{1,0:T(8,128)(2,1)S(1)}) custom-call(bf16[1024,32]{1,0:T(8,128)(2,1)S(1)} %get-tuple-element.25.refs_3_.refs_0_.refs_4_, bf16[32,2048]{1,0:T(8,128)(2,1)S(1)} %get-tuple-element.26.refs_1_, ...), custom_call_target="tpu_custom_call", output_to_operand_aliasing={{0}: (5, {})} | custom-call | tf_op jit(solution)/shard_map/pallas_call | solution.py:30
  9.6 2.6 %collective-permute-start.3 = (bf16[2,128,256]{2,1,0:T(8,128)(2,1)S(1)}, bf16[2,128,256]{2,1,0:T(8,128)(2,1)S(1)}, u32[]{:S(2)}, u32[]{:S(2)}) collective-permute-start(bf16[2,128,256]{2,1,0:T(8,128)(2,1)S(1)} %bitcast.36), channel_id=1, source_target_pairs={{0,1},{1,0},{2,3},{3,2},{4,5},{5,4},{6,7},{7,6},{8,9},{9,8},{10,11... | collective-permute-start | bytes 393224 | tf_op jit(solution)/shard_map/ppermute | solution.py:454
  12.1 1.5 %collective-permute-start.4 = (bf16[2,128,256]{2,1,0:T(8,128)(2,1)S(1)}, bf16[2,128,256]{2,1,0:T(8,128)(2,1)S(1)}, u32[]{:S(2)}, u32[]{:S(2)}) collective-permute-start(bf16[2,128,256]{2,1,0:T(8,128)(2,1)S(1)} %bitcast.27), channel_id=1, source_target_pairs={{0,2},{1,3},{2,0},{3,1},{4,6},{5,7},{6,4},{7,5},{8,10},{9,11},{10,... | collective-permute-start | bytes 393224 | tf_op jit(solution)/shard_map/ppermute | solution.py:454
  13.7 2.1 %shard_map.86 = (bf16[8,256,2048]{2,1,0:T(8,128)(2,1)S(1)}, f32[256,256]{1,0:T(8,128)S(1)}) custom-call(bf16[1024,32]{1,0:T(8,128)(2,1)S(1)} %get-tuple-element.25.refs_3_.refs_0_.refs_4_, bf16[32,2048]{1,0:T(8,128)(2,1)S(1)} %get-tuple-element.26.refs_1_, bf16[2048,256]{1,0:T(8,128)(2,1)S(1)} %get-tuple-element.24.refs_2_.refs_3_, ...), custom_call_target="tpu_custom_call", output_to_operand_aliasing={{0}: (5, {})} | custom-call | tf_op jit(solution)/shard_map/pallas_call | solution.py:30
  15.8 1.5 %shard_map.87 = (bf16[8,256,2048]{2,1,0:T(8,128)(2,1)S(1)}, bf16[2,128,256]{2,1,0:T(8,128)(2,1)S(1)}) custom-call(bf16[1024,32]{1,0:T(8,128)(2,1)S(1)} %get-tuple-element.25.refs_3_.refs_0_.refs_4_, bf16[32,2048]{1,0:T(8,128)(2,1)S(1)} %get-tuple-element.26.refs_1_, ...), custom_call_target="tpu_custom_call", output_to_operand_aliasing={{0}: (2, {})} | custom-call | tf_op jit(solution)/shard_map/pallas_call | solution.py:30
  17.3 4.1 %collective-permute-start.9 = (bf16[2,128,256]{2,1,0:T(8,128)(2,1)S(1)}, bf16[2,128,256]{2,1,0:T(8,128)(2,1)S(1)}, u32[]{:S(2)}, u32[]{:S(2)}) collective-permute-start(bf16[2,128,256]{2,1,0:T(8,128)(2,1)S(1)} %get-tuple-element.42), channel_id=1, source_target_pairs={{0,1},{1,2},{2,3},{3,4},{4,5},{5,6},{6,7},{7,8},{8,9},{9,10},{10,1... | collective-permute-start | bytes 393224 | tf_op jit(solution)/shard_map/ppermute | solution.py:539
  21.5 1.6 %collective-permute-start.6 = (bf16[2,32,256]{2,1,0:T(8,128)(2,1)S(1)}, bf16[2,32,256]{2,1,0:T(8,128)(2,1)S(1)}, u32[]{:S(2)}, u32[]{:S(2)}) collective-permute-start(bf16[2,32,256]{2,1,0:T(8,128)(2,1)S(1)} %get-tuple-element.39), channel_id=1, source_target_pairs={{0,4},{1,5},{2,6},{3,7},{4,0},{5,1},{6,2},{7,3},{8,12},{9,13},{10,... | collective-permute-start | bytes 98312 | tf_op jit(solution)/shard_map/ppermute | solution.py:530
  23.1 2.6 %collective-permute-start.7 = (bf16[2,32,256]{2,1,0:T(8,128)(2,1)S(1)}, bf16[2,32,256]{2,1,0:T(8,128)(2,1)S(1)}, u32[]{:S(2)}, u32[]{:S(2)}) collective-permute-start(bf16[2,32,256]{2,1,0:T(8,128)(2,1)S(1)} %get-tuple-element.40), channel_id=1, source_target_pairs={{0,8},{1,9},{2,10},{3,11},{4,12},{5,13},{6,14},{7,15},{8,0},{9,1},... | collective-permute-start | bytes 98312 | tf_op jit(solution)/shard_map/ppermute | solution.py:530
  25.7 0.2 collective-permute-start.8
  26.0 1.5 %shard_map.89.refs_6_.refs_4_.refs_9_.table_ref = bf16[8,256,2048]{2,1,0:T(8,128)(2,1)S(1)} custom-call(bf16[1024,32]{1,0:T(8,128)(2,1)S(1)} %get-tuple-element.25.refs_3_.refs_0_.refs_4_, bf16[32,2048]{1,0:T(8,128)(2,1)S(1)} %get-tuple-element.26.refs_1_, ...), custom_call_target="tpu_custom_call", output_to_operand_aliasing={{}: (2, {})} | custom-call | tf_op jit(solution)/shard_map/pallas_call | solution.py:30
  27.6 0.6 %collective-permute-done.7.refs_2_ = bf16[2,32,256]{2,1,0:T(8,128)(2,1)S(1)} collective-permute-done((bf16[2,32,256]{2,1,0:T(8,128)(2,1)S(1)}, bf16[2,32,256]{2,1,0:T(8,128)(2,1)S(1)}, u32[]{:S(2)}, u32[]{:S(2)}) %collective-permute-start.7) | collective-permute-done | bytes 32800 | tf_op jit(solution)/shard_map/ppermute | solution.py:530
  28.2 3.3 %collective-permute-done.8.refs_3_ = bf16[2,32,256]{2,1,0:T(8,128)(2,1)S(1)} collective-permute-done((bf16[2,32,256]{2,1,0:T(8,128)(2,1)S(1)}, bf16[2,32,256]{2,1,0:T(8,128)(2,1)S(1)}, u32[]{:S(2)}, u32[]{:S(2)}) %collective-permute-start.8) | collective-permute-done | bytes 32800 | tf_op jit(solution)/shard_map/ppermute | solution.py:530
  31.4 0.2 shard_map.90.refs_0_
  31.6 0.5 collective-permute-start.12
  32.1 4.0 %collective-permute-start.10 = (bf16[2,32,256]{2,1,0:T(8,128)(2,1)S(1)}, bf16[2,32,256]{2,1,0:T(8,128)(2,1)S(1)}, u32[]{:S(2)}, u32[]{:S(2)}) collective-permute-start(bf16[2,32,256]{2,1,0:T(8,128)(2,1)S(1)} %shard_map.90.refs_0_), channel_id=1, source_target_pairs={{0,4},{1,5},{2,6},{3,7},{4,0},{5,1},{6,2},{7,3},{8,12},{9,13},{10,... | collective-permute-start | bytes 98312 | tf_op jit(solution)/shard_map/ppermute | solution.py:549
  36.1 1.3 %collective-permute-done.12.refs_3_ = bf16[2,32,256]{2,1,0:T(8,128)(2,1)S(1)} collective-permute-done((bf16[2,32,256]{2,1,0:T(8,128)(2,1)S(1)}, bf16[2,32,256]{2,1,0:T(8,128)(2,1)S(1)}, u32[]{:S(2)}, u32[]{:S(2)}) %collective-permute-start.12) | collective-permute-done | bytes 32800 | tf_op jit(solution)/shard_map/ppermute | solution.py:549
  37.4 0.6 %collective-permute-done.10.refs_1_ = bf16[2,32,256]{2,1,0:T(8,128)(2,1)S(1)} collective-permute-done((bf16[2,32,256]{2,1,0:T(8,128)(2,1)S(1)}, bf16[2,32,256]{2,1,0:T(8,128)(2,1)S(1)}, u32[]{:S(2)}, u32[]{:S(2)}) %collective-permute-start.10) | collective-permute-done | bytes 32800 | tf_op jit(solution)/shard_map/ppermute | solution.py:549
  38.0 0.1 collective-permute-start.17
  38.1 1.5 %collective-permute-start.15 = (bf16[2,128,256]{2,1,0:T(8,128)(2,1)S(1)}, bf16[2,128,256]{2,1,0:T(8,128)(2,1)S(1)}, u32[]{:S(2)}, u32[]{:S(2)}) collective-permute-start(bf16[2,128,256]{2,1,0:T(8,128)(2,1)S(1)} %shard_map.91.refs_7_), channel_id=1, source_target_pairs={{0,3},{1,2},{2,1},{3,0},{4,7},{5,6},{6,5},{7,4},{8,11},{9,10},{10,... | collective-permute-start | bytes 393224 | tf_op jit(solution)/shard_map/ppermute | solution.py:554
  39.5 1.5 %collective-permute-start.14 = (bf16[2,128,256]{2,1,0:T(8,128)(2,1)S(1)}, bf16[2,128,256]{2,1,0:T(8,128)(2,1)S(1)}, u32[]{:S(2)}, u32[]{:S(2)}) collective-permute-start(bf16[2,128,256]{2,1,0:T(8,128)(2,1)S(1)} %shard_map.91.refs_7_), channel_id=1, source_target_pairs={{0,2},{1,3},{2,0},{3,1},{4,6},{5,7},{6,4},{7,5},{8,10},{9,11},{10,... | collective-permute-start | bytes 393224 | tf_op jit(solution)/shard_map/ppermute | solution.py:554
  41.1 0.5 %collective-permute-start.13 = (bf16[2,128,256]{2,1,0:T(8,128)(2,1)S(1)}, bf16[2,128,256]{2,1,0:T(8,128)(2,1)S(1)}, u32[]{:S(2)}, u32[]{:S(2)}) collective-permute-start(bf16[2,128,256]{2,1,0:T(8,128)(2,1)S(1)} %shard_map.91.refs_7_), channel_id=1, source_target_pairs={{0,1},{1,0},{2,3},{3,2},{4,5},{5,4},{6,7},{7,6},{8,9},{9,8},{10,11... | collective-permute-start | bytes 393224 | tf_op jit(solution)/shard_map/ppermute | solution.py:554
  41.6 0.6 %copy-done.8 = bf16[2,128,256]{2,1,0:T(8,128)(2,1)} copy-done((bf16[2,128,256]{2,1,0:T(8,128)(2,1)}, bf16[2,128,256]{2,1,0:T(8,128)(2,1)S(1)}, u32[]{:S(2)}) %copy-start.8) | copy-done | bytes 131096
  42.3 5.3 %shard_map.92.refs_5_.refs_3_.message_ref = f32[16,128,256]{2,1,0:T(8,128)S(1)} custom-call(s32[8,16]{1,0:T(8,128)S(1)} %bitcast.31, bf16[128,128,128]{2,1,0:T(8,128)(2,1)} %bitcast.37, bf16[16,128,256]{2,1,0:T(8,128)(2,1)} %bitcast.21, bf16[16,128,256]{2,1,0:T(8,128)(2,1)} %bitcast.23, bf16[2,128,256]{2,1,0:T(8,128)(2,1)} %copy-done.3, ...), custom_call_target="tpu_custom_call" | custom-call | tf_op jit(solution)/shard_map/pallas_call | solution.py:30
  47.7 0.1 collective-permute-done.13.refs_0_
  47.9 1.3 %shard_map.93.near_ref = f32[256,2048]{1,0:T(8,128)S(1)} custom-call(bf16[256,256]{1,0:T(8,128)(2,1)S(1)} %bitcast.24, bf16[256,256]{1,0:T(8,128)(2,1)S(1)} %bitcast.30, bf16[256,256]{1,0:T(8,128)(2,1)S(1)} %bitcast.29, bf16[256,256]{1,0:T(8,128)(2,1)S(1)} %bitcast.28, bf16[8,256,2048]{2,1,0:T(8,128)(2,1)S(1)} %shard_map.89.refs_6_.refs_4_.refs_9_.table_ref, ...), custom_call_target="tpu_custom_call" | custom-call | tf_op jit(solution)/shard_map/pallas_call | solution.py:30
  49.2 0.4 collective-permute-done.18.rest_ref
  49.6 4.2 %shard_map.95 = bf16[16,128,256]{2,1,0:T(8,128)(2,1)} custom-call(s32[16]{0:T(128)S(1)} %bitcast.34, bf16[16,128,256]{2,1,0:T(8,128)(2,1)S(1)} %bitcast.22, f32[256,2048]{1,0:T(8,128)S(1)} %shard_map.93.near_ref, f32[16,128,256]{2,1,0:T(8,128)S(1)} %shard_map.92.refs_5_.refs_3_.message_ref, bf16[256,256]{1,0:T(8,128)(2,1)S(1)} %bitcast.26, ...), custom_call_target="tpu_custom_call" | custom-call | tf_op jit(solution)/shard_map/pallas_call | solution.py:403
  (38 shorter events, 0.4 us)
Async XLA Ops:
  0.0 4.5 %collective-permute-start.1 = (bf16[16,128,256]{2,1,0:T(8,128)(2,1)}, bf16[16,128,256]{2,1,0:T(8,128)(2,1)S(1)}, u32[]{:S(2)}, u32[]{:S(2)}) collective-permute-start(bf16[16,128,256]{2,1,0:T(8,128)(2,1)} %bitcast.38), channel_id=1, source_target_pairs={{0,16},{16,0},{1,17},{17,1},{2,18},{18,2},{3,19},{19,3},{4,20},{20... | collective-permute-start | bytes 3145736 | tf_op jit(solution)/shard_map/ppermute | solution.py:429
  0.5 4.0 %collective-permute-start.2 = (f32[3,16,128]{2,1,0:T(8,128)}, f32[3,16,128]{2,1,0:T(8,128)S(1)}, u32[]{:S(2)}, u32[]{:S(2)}) collective-permute-start(f32[3,16,128]{2,1,0:T(8,128)} %bitcast.40), channel_id=1, source_target_pairs={{0,16},{16,0},{1,17},{17,1},{2,18},{18,2},{3,19},{19,3},{4,20},{20... | collective-permute-start | bytes 73736 | tf_op jit(solution)/shard_map/ppermute | solution.py:426
  0.5 3.9 %collective-permute-start = (s32[16]{0:T(128)}, s32[16]{0:T(128)S(1)}, u32[]{:S(2)}, u32[]{:S(2)}) collective-permute-start(s32[16]{0:T(128)} %bitcast.32), channel_id=1, source_target_pairs={{0,16},{16,0},{1,17},{17,1},{2,18},{18,2},{3,19},{19,3},{4,20},{20... | collective-permute-start | bytes 200 | tf_op jit(solution)/shard_map/ppermute | solution.py:428
  4.4 11.3 %copy-start = (bf16[2048,256]{1,0:T(8,128)(2,1)}, bf16[2048,256]{1,0:T(8,128)(2,1)S(1)}, u32[]{:S(2)}) copy-start(bf16[2048,256]{1,0:T(8,128)(2,1)S(1)} %get-tuple-element.24.refs_2_.refs_3_) | copy-start | bytes 3145732
  6.4 9.4 %copy-start.2 = (bf16[2048,256]{1,0:T(8,128)(2,1)}, bf16[2048,256]{1,0:T(8,128)(2,1)S(1)}, u32[]{:S(2)}) copy-start(bf16[2048,256]{1,0:T(8,128)(2,1)S(1)} %get-tuple-element.29.refs_2_.refs_4_) | copy-start | bytes 3145732
  9.6 11.8 %collective-permute-start.3 = (bf16[2,128,256]{2,1,0:T(8,128)(2,1)S(1)}, bf16[2,128,256]{2,1,0:T(8,128)(2,1)S(1)}, u32[]{:S(2)}, u32[]{:S(2)}) collective-permute-start(bf16[2,128,256]{2,1,0:T(8,128)(2,1)S(1)} %bitcast.36), channel_id=1, source_target_pairs={{0,1},{1,0},{2,3},{3,2},{4,5},{5,4},{6,7},{7,6},{8,9},{9,8},{10,11... | collective-permute-start | bytes 393224 | tf_op jit(solution)/shard_map/ppermute | solution.py:454
  12.1 9.3 %collective-permute-start.4 = (bf16[2,128,256]{2,1,0:T(8,128)(2,1)S(1)}, bf16[2,128,256]{2,1,0:T(8,128)(2,1)S(1)}, u32[]{:S(2)}, u32[]{:S(2)}) collective-permute-start(bf16[2,128,256]{2,1,0:T(8,128)(2,1)S(1)} %bitcast.27), channel_id=1, source_target_pairs={{0,2},{1,3},{2,0},{3,1},{4,6},{5,7},{6,4},{7,5},{8,10},{9,11},{10,... | collective-permute-start | bytes 393224 | tf_op jit(solution)/shard_map/ppermute | solution.py:454
  13.7 7.8 %collective-permute-start.5 = (bf16[2,128,256]{2,1,0:T(8,128)(2,1)S(1)}, bf16[2,128,256]{2,1,0:T(8,128)(2,1)S(1)}, u32[]{:S(2)}, u32[]{:S(2)}) collective-permute-start(bf16[2,128,256]{2,1,0:T(8,128)(2,1)S(1)} %bitcast.35), channel_id=1, source_target_pairs={{0,3},{1,2},{2,1},{3,0},{4,7},{5,6},{6,5},{7,4},{8,11},{9,10},{10,... | collective-permute-start | bytes 393224 | tf_op jit(solution)/shard_map/ppermute | solution.py:454
  17.3 10.2 %collective-permute-start.9 = (bf16[2,128,256]{2,1,0:T(8,128)(2,1)S(1)}, bf16[2,128,256]{2,1,0:T(8,128)(2,1)S(1)}, u32[]{:S(2)}, u32[]{:S(2)}) collective-permute-start(bf16[2,128,256]{2,1,0:T(8,128)(2,1)S(1)} %get-tuple-element.42), channel_id=1, source_target_pairs={{0,1},{1,2},{2,3},{3,4},{4,5},{5,6},{6,7},{7,8},{8,9},{9,10},{10,1... | collective-permute-start | bytes 393224 | tf_op jit(solution)/shard_map/ppermute | solution.py:539
  21.5 6.1 %collective-permute-start.6 = (bf16[2,32,256]{2,1,0:T(8,128)(2,1)S(1)}, bf16[2,32,256]{2,1,0:T(8,128)(2,1)S(1)}, u32[]{:S(2)}, u32[]{:S(2)}) collective-permute-start(bf16[2,32,256]{2,1,0:T(8,128)(2,1)S(1)} %get-tuple-element.39), channel_id=1, source_target_pairs={{0,4},{1,5},{2,6},{3,7},{4,0},{5,1},{6,2},{7,3},{8,12},{9,13},{10,... | collective-permute-start | bytes 98312 | tf_op jit(solution)/shard_map/ppermute | solution.py:530
  23.1 5.0 %collective-permute-start.7 = (bf16[2,32,256]{2,1,0:T(8,128)(2,1)S(1)}, bf16[2,32,256]{2,1,0:T(8,128)(2,1)S(1)}, u32[]{:S(2)}, u32[]{:S(2)}) collective-permute-start(bf16[2,32,256]{2,1,0:T(8,128)(2,1)S(1)} %get-tuple-element.40), channel_id=1, source_target_pairs={{0,8},{1,9},{2,10},{3,11},{4,12},{5,13},{6,14},{7,15},{8,0},{9,1},... | collective-permute-start | bytes 98312 | tf_op jit(solution)/shard_map/ppermute | solution.py:530
  25.7 5.7 %collective-permute-start.8 = (bf16[2,32,256]{2,1,0:T(8,128)(2,1)S(1)}, bf16[2,32,256]{2,1,0:T(8,128)(2,1)S(1)}, u32[]{:S(2)}, u32[]{:S(2)}) collective-permute-start(bf16[2,32,256]{2,1,0:T(8,128)(2,1)S(1)} %get-tuple-element.41), channel_id=1, source_target_pairs={{0,12},{1,13},{2,14},{3,15},{4,8},{5,9},{6,10},{7,11},{8,4},{9,5},... | collective-permute-start | bytes 98312 | tf_op jit(solution)/shard_map/ppermute | solution.py:530
  26.0 5.5 %copy-start.4 = (bf16[256,256]{1,0:T(8,128)(2,1)S(1)}, bf16[256,256]{1,0:T(8,128)(2,1)}, u32[]{:S(2)}) copy-start(bf16[256,256]{1,0:T(8,128)(2,1)} %refs_5_.1) | copy-start | bytes 393220
  27.5 14.8 %copy-start.5 = (bf16[256,256]{1,0:T(8,128)(2,1)S(1)}, bf16[256,256]{1,0:T(8,128)(2,1)}, u32[]{:S(2)}) copy-start(bf16[256,256]{1,0:T(8,128)(2,1)} %refs_6_.1) | copy-start | bytes 393220
  27.5 14.8 %copy-start.6 = (s32[1,16,8]{1,2,0:T(8,128)S(1)}, s32[1,16,8]{1,2,0:T(8,128)}, u32[]{:S(2)}) copy-start(s32[1,16,8]{1,2,0:T(8,128)} %param.11) | copy-start | bytes 1540
  27.6 10.4 %copy-start.3 = (bf16[2,128,256]{2,1,0:T(8,128)(2,1)}, bf16[2,128,256]{2,1,0:T(8,128)(2,1)S(1)}, u32[]{:S(2)}) copy-start(bf16[2,128,256]{2,1,0:T(8,128)(2,1)S(1)} %collective-permute-done.9.refs_7_.refs_4_) | copy-start | bytes 393220
  31.6 5.8 %collective-permute-start.12 = (bf16[2,32,256]{2,1,0:T(8,128)(2,1)S(1)}, bf16[2,32,256]{2,1,0:T(8,128)(2,1)S(1)}, u32[]{:S(2)}, u32[]{:S(2)}) collective-permute-start(bf16[2,32,256]{2,1,0:T(8,128)(2,1)S(1)} %shard_map.90.refs_0_), channel_id=1, source_target_pairs={{0,12},{1,13},{2,14},{3,15},{4,8},{5,9},{6,10},{7,11},{8,4},{9,5},... | collective-permute-start | bytes 98312 | tf_op jit(solution)/shard_map/ppermute | solution.py:549
  32.1 5.3 %collective-permute-start.11 = (bf16[2,32,256]{2,1,0:T(8,128)(2,1)S(1)}, bf16[2,32,256]{2,1,0:T(8,128)(2,1)S(1)}, u32[]{:S(2)}, u32[]{:S(2)}) collective-permute-start(bf16[2,32,256]{2,1,0:T(8,128)(2,1)S(1)} %shard_map.90.refs_0_), channel_id=1, source_target_pairs={{0,8},{1,9},{2,10},{3,11},{4,12},{5,13},{6,14},{7,15},{8,0},{9,1},... | collective-permute-start | bytes 98312 | tf_op jit(solution)/shard_map/ppermute | solution.py:549
  32.1 5.9 %collective-permute-start.10 = (bf16[2,32,256]{2,1,0:T(8,128)(2,1)S(1)}, bf16[2,32,256]{2,1,0:T(8,128)(2,1)S(1)}, u32[]{:S(2)}, u32[]{:S(2)}) collective-permute-start(bf16[2,32,256]{2,1,0:T(8,128)(2,1)S(1)} %shard_map.90.refs_0_), channel_id=1, source_target_pairs={{0,4},{1,5},{2,6},{3,7},{4,0},{5,1},{6,2},{7,3},{8,12},{9,13},{10,... | collective-permute-start | bytes 98312 | tf_op jit(solution)/shard_map/ppermute | solution.py:549
  36.1 5.6 %collective-permute-start.16 = (bf16[2,128,256]{2,1,0:T(8,128)(2,1)S(1)}, bf16[2,128,256]{2,1,0:T(8,128)(2,1)S(1)}, u32[]{:S(2)}, u32[]{:S(2)}) collective-permute-start(bf16[2,128,256]{2,1,0:T(8,128)(2,1)S(1)} %collective-permute-done.9.refs_7_.refs_4_), channel_id=1, source_target_pairs={{0,16},{16,0},{1,17},{17,1},{2,18},{18,2},{3,19},{19,3},{4,20},{20... | collective-permute-start | bytes 393224 | tf_op jit(solution)/shard_map/ppermute | solution.py:540
  38.0 3.6 %collective-permute-start.17 = (bf16[2,128,256]{2,1,0:T(8,128)(2,1)S(1)}, bf16[2,128,256]{2,1,0:T(8,128)(2,1)S(1)}, u32[]{:S(2)}, u32[]{:S(2)}) collective-permute-start(bf16[2,128,256]{2,1,0:T(8,128)(2,1)S(1)} %shard_map.91.refs_7_), channel_id=1, source_target_pairs={{0,16},{16,0},{1,17},{17,1},{2,18},{18,2},{3,19},{19,3},{4,20},{20... | collective-permute-start | bytes 393224 | tf_op jit(solution)/shard_map/ppermute | solution.py:556
  38.1 9.6 %collective-permute-start.15 = (bf16[2,128,256]{2,1,0:T(8,128)(2,1)S(1)}, bf16[2,128,256]{2,1,0:T(8,128)(2,1)S(1)}, u32[]{:S(2)}, u32[]{:S(2)}) collective-permute-start(bf16[2,128,256]{2,1,0:T(8,128)(2,1)S(1)} %shard_map.91.refs_7_), channel_id=1, source_target_pairs={{0,3},{1,2},{2,1},{3,0},{4,7},{5,6},{6,5},{7,4},{8,11},{9,10},{10,... | collective-permute-start | bytes 393224 | tf_op jit(solution)/shard_map/ppermute | solution.py:554
  39.5 8.2 %collective-permute-start.14 = (bf16[2,128,256]{2,1,0:T(8,128)(2,1)S(1)}, bf16[2,128,256]{2,1,0:T(8,128)(2,1)S(1)}, u32[]{:S(2)}, u32[]{:S(2)}) collective-permute-start(bf16[2,128,256]{2,1,0:T(8,128)(2,1)S(1)} %shard_map.91.refs_7_), channel_id=1, source_target_pairs={{0,2},{1,3},{2,0},{3,1},{4,6},{5,7},{6,4},{7,5},{8,10},{9,11},{10,... | collective-permute-start | bytes 393224 | tf_op jit(solution)/shard_map/ppermute | solution.py:554
  41.1 6.7 %collective-permute-start.13 = (bf16[2,128,256]{2,1,0:T(8,128)(2,1)S(1)}, bf16[2,128,256]{2,1,0:T(8,128)(2,1)S(1)}, u32[]{:S(2)}, u32[]{:S(2)}) collective-permute-start(bf16[2,128,256]{2,1,0:T(8,128)(2,1)S(1)} %shard_map.91.refs_7_), channel_id=1, source_target_pairs={{0,1},{1,0},{2,3},{3,2},{4,5},{5,4},{6,7},{7,6},{8,9},{9,8},{10,11... | collective-permute-start | bytes 393224 | tf_op jit(solution)/shard_map/ppermute | solution.py:554
  41.6 0.7 %copy-start.8 = (bf16[2,128,256]{2,1,0:T(8,128)(2,1)}, bf16[2,128,256]{2,1,0:T(8,128)(2,1)S(1)}, u32[]{:S(2)}) copy-start(bf16[2,128,256]{2,1,0:T(8,128)(2,1)S(1)} %collective-permute-done.16.refs_5_) | copy-start | bytes 393220
  47.6 2.0 %copy-start.1 = (bf16[2048,256]{1,0:T(8,128)(2,1)S(1)}, bf16[2048,256]{1,0:T(8,128)(2,1)}, u32[]{:S(2)}) copy-start(bf16[2048,256]{1,0:T(8,128)(2,1)} %copy-done) | copy-start | bytes 3145732
  47.6 2.0 %copy-start.7 = (s32[1,16]{1,0:T(1,128)S(1)}, s32[1,16]{1,0:T(1,128)}, u32[]{:S(2)}) copy-start(s32[1,16]{1,0:T(1,128)} %param.12) | copy-start | bytes 196
  47.8 1.8 %collective-permute-start.18 = (bf16[2,384,256]{2,1,0:T(8,128)(2,1)S(1)}, bf16[2,384,256]{2,1,0:T(8,128)(2,1)S(1)}, u32[]{:S(2)}, u32[]{:S(2)}) collective-permute-start(bf16[2,384,256]{2,1,0:T(8,128)(2,1)S(1)} %shard_map.94), channel_id=1, source_target_pairs={{0,16},{16,0},{1,17},{17,1},{2,18},{18,2},{3,19},{19,3},{4,20},{20... | collective-permute-start | bytes 1179656 | tf_op jit(solution)/shard_map/ppermute | solution.py:574

commit v5 on v4

--- a/solution.py
+++ b/solution.py
@@ -16,6 +16,7 @@
 PARAMS = pltpu.CompilerParams(vmem_limit_bytes=14 * 1024 * 1024)
 LANES = 128
 COST = 0
+WEIGHT = 4
 SIN = (4.44287957, -7.30781668, 3.59777418, -0.79119939)
 COS = (1.41420401, -6.97763732, 5.71518787, -1.72821389)
 
@@ -191,69 +192,51 @@
     piece_ref[...] = (total + sums_of(table_ref, masked_ref)).astype(piece_ref.dtype)
 
 
-def fill_edges(lines, outs):
-    slots = outs[0].shape[1]
-    end = lines[0].shape[0] - slots
-    if len(outs) == 1:
-        start = pl.multiple_of(jnp.where(lax.axis_index("grp") == 0, end, 0), slots)
-        for line, rows_ref in enumerate(lines):
-            outs[0][line] = rows_ref[pl.ds(start, slots), :]
-        return
+def fill_edges(lines, last_ref, first_ref):
+    slots = last_ref.shape[1]
     for line, rows_ref in enumerate(lines):
-        outs[0][line] = rows_ref[end:, :]
-        outs[1][line] = rows_ref[:slots, :]
+        last_ref[line] = rows_ref[rows_ref.shape[0] - slots :, :]
+        first_ref[line] = rows_ref[:slots, :]
 
 
 def rest_kernel(blocks, block, lines, turned_ref, places_ref, _, *refs):
-    kept_ref, *edges = refs[lines:]
-    if edges:
-        fill_edges(refs[:lines], edges)
+    kept_ref, *outs = refs[lines + 1 if lines else 0 :]
+    if lines:
+        *edges, radial_ref, semaphores = outs
+        source_ref = refs[lines]
+        count = source_ref.shape[0]
+        copies = begin([source_ref], [radial_ref.at[pl.ds(0, count)]], semaphores)
+        radial_ref[count] = jnp.zeros_like(radial_ref[count])
+        fill_edges(refs[:lines], *edges)
     for place in blocks:
         fill_table(turned_ref[place * block : (place + 1) * block, :], places_ref, kept_ref.at[place])
-
-
-def short_kernel(lines, chunks, codes_ref, source_ref, *refs):
+    if lines:
+        finish(copies)
+
+
+def short_kernel(lines, codes_ref, radial_ref, *refs):
     line_refs, refs = refs[:lines], refs[lines:]
-    one_ref, two_ref, w_ref, message_ref = refs[:4]
-    window_ref, found_ref, radial_ref, semaphores = refs[4:]
+    outer, (handed_ref, w_ref, message_ref, found_ref) = refs[:-4], refs[-4:]
     cells, slots, channels = message_ref.shape
     pairs = codes_ref.shape[0]
     slab, slabs = lax.axis_index("grp"), lax.axis_size("grp")
-    share = cells // chunks
-    edges = []
-    for line in range(lines):
+
+    def outer_cell(line, side):
         if slabs == 2:
-            near = slab * (cells + 1)
-            edges.append((one_ref.at[line], window_ref.at[line * (cells + 2) + near]))
-            edges.append((two_ref.at[line], window_ref.at[(1 - line) * (cells + 2) + cells + 1 - near]))
-        else:
-            edges.append((one_ref.at[line], window_ref.at[line * (cells + 2)]))
-            edges.append((two_ref.at[line], window_ref.at[line * (cells + 2) + cells + 1]))
-    edges = begin(*zip(*edges), semaphores)
-    parts = []
-    for chunk in range(chunks):
-        span = pl.ds(chunk * share * pairs, share * pairs)
-        moves = [(source_ref.at[span], radial_ref.at[span])]
-        for line, line_ref in enumerate(line_refs):
-            base = line * (cells + 2) + 1 + chunk * share
-            moves.append((line_ref.at[pl.ds(chunk * share, share)], window_ref.at[pl.ds(base, share)]))
-        parts.append(begin(*zip(*moves), semaphores, 2 * lines + chunk * (1 + lines)))
+            start = handed_ref.shape[0] - (4 - 2 * side - (1 - line)) * slots
+            return jnp.where(slab == 1, outer[side][line], handed_ref[start : start + slots, :])
+        return outer[side][line]
+
     nothing = cells * pairs
-    radial_ref[nothing] = jnp.zeros((slots, slots), BF16)
     for cell in range(cells):
         for code in range(9):
             found_ref[9 * cell + code] = nothing
         for pair in range(pairs):
             found_ref[9 * cell + codes_ref[pair, cell]] = cell * pairs + pair
     levels = [1, 2 - 2 * slab] if slabs == 2 else [1, 0, 2]
-    finish(edges)
-    ready = 0
     carried = None
     for start in range(0, cells + 2, 2):
         takers = [cell for cell in range(start - 2, start + 2) if 0 <= cell < cells]
-        while ready <= takers[-1] // share:
-            finish(parts[ready])
-            ready += 1
         total = None
         for line, level in enumerate(levels):
             rows = []
@@ -264,8 +247,13 @@
                     index = found_ref[9 * cell + 3 * level + along] if 0 <= along < 3 else nothing
                     halves.append(radial_ref[index])
                 rows.append(jnp.concatenate(halves, axis=1))
-            base = line * (cells + 2) + start
-            taken = window_ref[base : base + 2].reshape(2 * slots, channels)
+            span = slice(max(start - 1, 0) * slots, min(start + 1, cells) * slots)
+            taken = [line_refs[line][span, :]]
+            if start == 0:
+                taken = [outer_cell(line, 0)] + taken
+            if start == cells:
+                taken = taken + [outer_cell(line, 1)]
+            taken = jnp.concatenate(taken, axis=0)
             part = jnp.dot(jnp.concatenate(rows, axis=0), taken, preferred_element_type=F32)
             total = part if total is None else total + part
         if start:
@@ -331,15 +319,31 @@
         [(VMEM, ((trig, rows, channels), BF16))],
         in_vmem([*pieces, turned, w_mix]),
         held=held,
+        flops=WEIGHT * 10**9,
     )
     return energy
 
 
-def join_kernel(*refs):
-    pieces, out_ref = refs[:-1], refs[-1]
+def join_kernel(count, *refs):
+    pieces, out_ref = refs[:count], refs[-1]
     rows = pieces[0].shape[1]
     for place, piece in enumerate(pieces):
         out_ref[:, place * rows : (place + 1) * rows, :] = piece[...]
+
+
+def pack_kernel(count, *refs):
+    pieces, extras, (out_ref, packed_ref) = refs[:count], refs[count:-2], refs[-2:]
+    trig, rows, _ = pieces[0].shape
+    for place, piece in enumerate(pieces):
+        out_ref[:, place * rows : (place + 1) * rows, :] = piece[...]
+        for part in range(trig):
+            start = (part * count + place) * rows
+            packed_ref[start : start + rows, :] = piece[part]
+    start = trig * count * rows
+    for extra in extras:
+        for line in range(extra.shape[0]):
+            packed_ref[start : start + extra.shape[1], :] = extra[line]
+            start += extra.shape[1]
 
 
 def joined(pieces, held):
@@ -347,8 +351,19 @@
     if rows % 16:
         return jnp.concatenate(pieces, axis=1)
     whole = (VMEM, ((trig, rows * len(pieces), channels), BF16))
-    (whole,) = call(join_kernel, [whole], in_vmem(pieces), held=held)
+    (whole,) = call(functools.partial(join_kernel, len(pieces)), [whole], in_vmem(pieces), held=held)
     return whole
+
+
+def packed(pieces, extras, held):
+    trig, rows, channels = pieces[0].shape
+    count = trig * rows * len(pieces) + sum(extra.shape[0] * extra.shape[1] for extra in extras)
+    return call(
+        functools.partial(pack_kernel, len(pieces)),
+        [(VMEM, ((trig, rows * len(pieces), channels), BF16)), (VMEM, ((count, channels), BF16))],
+        in_vmem([*pieces, *extras]),
+        held=held,
+    )
 
 
 def near_kernel(blocks, *refs):
@@ -366,49 +381,50 @@
 
 
 def final_kernel(
-    blocks, scale, counts_ref, masked_ref, near_ref, message_ref, energy_ref, rest_ref, table_ref, out_ref, turned_ref
+    blocks, scale, counts_ref, masked_ref, near_ref, message_ref, energy_ref, rest_ref, table_ref, out_ref, turned_ref,
+    result_ref, semaphores,
 ):
     cells, slots, channels = out_ref.shape
-    step = pl.program_id(0)
-
-    @pl.when(step == 0)
-    def _():
-        rows = energy_ref.shape[0]
-        half = rows // 2
-        turned_ref[0] = energy_ref[...].astype(F32).T.astype(BF16)
-        for place in range(1, blocks):
-            taken = rest_ref[:, (place - 1) * half : place * half, :].reshape(rows, channels)
-            turned_ref[place] = taken.astype(F32).T.astype(BF16)
-
-    atoms = cells * slots
-    span = pl.ds(pl.multiple_of(step * atoms, atoms), atoms)
-    total = near_ref[:, span]
-    for place in range(blocks):
-        total = total + jnp.dot(turned_ref[place], table_ref[blocks + place, :, span], preferred_element_type=F32)
+    rows = table_ref.shape[1]
+    half = rows // 2
+    turned_ref[0] = energy_ref[:rows, :].astype(F32).T.astype(BF16)
+    for place in range(1, blocks):
+        taken = rest_ref[:, (place - 1) * half : place * half, :].reshape(rows, channels)
+        turned_ref[place] = taken.astype(F32).T.astype(BF16)
     slot_ids = lax.broadcasted_iota(jnp.int32, (slots, channels), 0)
-    for cell in range(cells):
-        index = step * cells + cell
-        value = total[:, cell * slots : (cell + 1) * slots].T * scale + message_ref[index]
-        value = value * (0.5 + 0.5 * jnp.tanh(0.5 * value))
-        result = masked_ref[index].astype(F32) + value
-        out_ref[cell] = jnp.where(slot_ids < counts_ref[index], result, 0.0).astype(BF16)
+    group = math.gcd(cells, 2)
+    share = math.gcd(cells, 4)
+    leaving = []
+    for first in range(0, cells, group):
+        span = slice(first * slots, (first + group) * slots)
+        total = near_ref[:, span]
+        for place in range(blocks):
+            total = total + jnp.dot(turned_ref[place], table_ref[blocks + place, :, span], preferred_element_type=F32)
+        for cell in range(first, first + group):
+            value = total[:, (cell - first) * slots : (cell - first + 1) * slots].T * scale + message_ref[cell]
+            value = value * (0.5 + 0.5 * jnp.tanh(0.5 * value))
+            result = masked_ref[cell * slots : (cell + 1) * slots, :].astype(F32) + value
+            result_ref[cell] = jnp.where(slot_ids < counts_ref[cell], result, 0.0).astype(BF16)
+        if (first + group) % share == 0:
+            done = pl.ds(first + group - share, share)
+            leaving += begin([result_ref.at[done]], [out_ref.at[done]], semaphores, first // share)
+    finish(leaving)
 
 
 def final_call(counts, near, message, masked, energy, rest, table, scale):
+    blocks, rows = table.shape[0] // 2, table.shape[1]
     cells, slots, channels = message.shape
-    blocks, rows = table.shape[0] // 2, table.shape[1]
-    group = math.gcd(cells, 4)
-    cells_spec = pl.BlockSpec((group, slots, channels), lambda i: (i, 0, 0))
-    operands = [masked, near, message, energy, rest, table]
-    return pl.pallas_call(
+    (result,) = call(
         functools.partial(final_kernel, blocks, scale),
-        grid=(cells // group,),
-        in_specs=[SMEM] + [VMEM] * len(operands),
-        out_specs=cells_spec,
-        out_shape=jax.ShapeDtypeStruct(message.shape, BF16),
-        scratch_shapes=[pltpu.VMEM((blocks, channels, rows), BF16)],
-        compiler_params=PARAMS,
-    )(counts, *[pltpu.with_memory_space_constraint(array, pltpu.VMEM) for array in operands])
+        [(HBM, (message.shape, BF16))],
+        [(SMEM, counts)] + in_vmem([masked, near, message, energy, rest, table]),
+        [
+            pltpu.VMEM((blocks, channels, rows), BF16),
+            pltpu.VMEM(message.shape, BF16),
+            pltpu.SemaphoreType.DMA((cells // math.gcd(cells, 4),)),
+        ],
+    )
+    return result
 
 
 def body(features, offsets, radial, neighbours, counts, wavevectors, w_msg, w_mix):
@@ -492,7 +508,7 @@
             [whole_table, (VMEM, piece if place else sums)],
             in_vmem([turned, places, masked, sibling_places, sibling, tables]),
             scratch,
-            [part] if place else [],
+            [part] if place else [received[early[0]]],
             2 * block_flops,
             {5: 0},
         )
@@ -511,18 +527,19 @@
         ]
     edge = (VMEM, ((len(lines), slots, channels), BF16))
 
-    def rest_of(tables, first, last, lines, edges, held):
+    def rest_of(tables, first, last, held, more=(), outs=(), scratch=(), weight=0):
         return call(
-            functools.partial(rest_kernel, range(first, last), block, len(lines)),
-            [whole_table, *edges],
-            in_vmem([turned, places, tables, *lines]),
-            held=held,
-            flops=block_flops * (last - first),
-            same={2: 0},
+            functools.partial(rest_kernel, range(first, last), block, len(more[:-1])),
+            [whole_table, *outs],
+            in_vmem([turned, places, tables, *more[:-1]]) + in_hbm(more[-1:]),
+            scratch,
+            held,
+            weight,
+            {2: 0},
         )
 
     middle = blocks + blocks // 2
-    tables, *edges = rest_of(tables, blocks, middle, lines, [edge] * (1 if slabs == 2 else 2), [part])
+    (tables,) = rest_of(tables, blocks, middle, [part])
 
     for axis, stride, radix in stages[1:]:
         parts = add_and_cut(pieces, radix, [tables])
@@ -530,50 +547,48 @@
             lax.ppermute(parts[place], axis, pairs_at(axis, stride, place)) for place in range(1, radix)
         ]
 
-    (tables,) = rest_of(tables, middle, 2 * blocks, [], [], [parts[0]])
+    radial = radial.reshape(-1, slots, slots)
+    radial_type = (VMEM, ((radial.shape[0] + 1, slots, slots), BF16))
+    tables, *edges, radial = rest_of(
+        tables, middle, 2 * blocks, [parts[0]],
+        [*lines, radial], [edge, edge, radial_type], [pltpu.SemaphoreType.DMA((1,))],
+    )
 
     right = [(i, i + 1) for i in range(dev_count - 1)]
     left = [(j, i) for i, j in right]
     if slabs == 2:
-        ways = right + [(dev_count + i, dev_count + j) for i, j in left]
-        one = lax.ppermute(edges[0], ("grp", "dev"), ways)
-        two = lax.ppermute(one, "grp", swap)
+        outer = [
+            lax.ppermute(part, ("grp", "dev"), [(dev_count + i, dev_count + j) for i, j in way])
+            for part, way in zip(edges, (right, left))
+        ]
     else:
-        one = lax.ppermute(edges[0], "dev", right)
-        two = lax.ppermute(edges[1], "dev", left)
-
-    energy = energy_of(pieces, turned, w_mix, 1.0 / math.sqrt(total_slots), [tables, one])
-
-    for axis, stride, radix in reversed(stages[1:]):
-        energy = joined(
-            [energy] + [lax.ppermute(energy, axis, pairs_at(axis, stride, place)) for place in range(1, radix)],
-            [tables],
-        )
+        outer = [lax.ppermute(part, "dev", way) for part, way in zip(edges, (right, left))]
+
+    energy = energy_of(pieces, turned, w_mix, 1.0 / math.sqrt(total_slots), [tables, radial])
+
+    for stage, (axis, stride, radix) in reversed(list(enumerate(stages))[1:]):
+        pieces = [energy] + [
+            lax.ppermute(energy, axis, pairs_at(axis, stride, place)) for place in range(1, radix)
+        ]
+        if stage > 1:
+            energy = joined(pieces, [tables, radial])
+    energy, handed = packed(pieces, outer if slabs == 2 else [], [tables, radial])
+    handed = lax.ppermute(handed, "grp", swap)
     axis, stride, blocks = stages[0]
     energies = [energy] + [
         lax.ppermute(energy, axis, pairs_at(axis, stride, place)) for place in range(1, blocks)
     ]
-    other_energy = lax.ppermute(energy, "grp", swap)
-
-    chunks = math.gcd(cells, 4)
+
     (message,) = call(
-        functools.partial(short_kernel, len(lines), chunks),
+        functools.partial(short_kernel, len(lines)),
         [(VMEM, ((cells, slots, channels), F32))],
-        [(SMEM, neighbours[0].T)]
-        + in_hbm([radial.reshape(-1, slots, slots), *[line.reshape(cells, slots, channels) for line in lines], one, two])
-        + in_vmem([w_msg]),
-        [
-            pltpu.VMEM((len(lines) * (cells + 2), slots, channels), BF16),
-            pltpu.SMEM((9 * cells,), jnp.int32),
-            pltpu.VMEM((cells * radial.shape[2] + 1, slots, slots), BF16),
-            pltpu.SemaphoreType.DMA((2 * len(lines) + chunks * (1 + len(lines)),)),
-        ],
-        [energy, other_energy, tables],
+        [(SMEM, neighbours[0].T)] + in_vmem([radial, *lines, *outer, handed, w_msg]),
+        [pltpu.SMEM((9 * cells,), jnp.int32)],
+        [energy, tables],
         6 * block_flops,
     )
     rest = lax.ppermute(joined(energies[1:], [message]), "grp", swap)
     energies = [part.reshape(2 * block, channels) for part in energies]
-    other_energy = other_energy.reshape(2 * block, channels)
     (near_sum,) = call(
         functools.partial(near_kernel, blocks),
         [(VMEM, ((channels, atoms), F32))],
@@ -582,9 +597,8 @@
         [message],
         2 * block_flops,
     )
-    masked = masked.reshape(cells, slots, channels)
     scale = 8.0 / math.sqrt(wave_count)
-    result = final_call(counts, near_sum, message, masked, other_energy, rest, tables, scale)
+    result = final_call(counts, near_sum, message, masked, handed, rest, tables, scale)
     return result[None]
 
 

time: 54.1 us -> 52.3 us (0.967)
  Pallas kernels: 24.8 us -> 21.6 us
  waiting for transfers between devices: 6.32 us -> 8.86 us
  local copies, waits for them, and re-layouts: 0.69 us -> 0.03 us
    pallas_call x1 -> x0, Pallas kernels: 4.19 us -> none  [final_call(): pl.pallas_call(functools.partial(final_kernel, blocks, scale), grid=(cell...]
    ppermute x6, waiting for transfers between devices: 2.03 us -> 4.94 us  [body(): lax.ppermute(energy, axis, pairs_at(axis, stride, place))]
    ppermute x3, waiting for transfers between devices: 3.88 us -> 1.92 us  [body(): lax.ppermute(parts[place], axis, pairs_at(axis, stride, place))]
    ppermute x3, waiting for transfers between devices: 0.01 us -> 1.6 us  [sent(): lax.ppermute(part.reshape(2, block, channels), axis, pairs_at(axis, strid...]
    pallas_call x13 -> x14, Pallas kernels: 20.6 us -> 21.6 us  [call(): pl.pallas_call(without_held, in_specs=[place for place, _ in operands], o...]
    unnamed x18 -> x8, local copies, waits for them, and re-layouts: 0.69 us -> 0.03 us
  transfers between devices with their start and end apart: 19 -> 19, of which waited for: 6 -> 9; matrix products, arithmetic and copies ran while one was open for 0% -> 0% of each run, Pallas kernels for 29% -> 32%
where the time goes in v5:
time: 52.3 us; the launch traced here: 52 us
  Pallas kernels  21.6 us (41%)
  starting transfers between devices  21.2 us (41%)
  waiting for transfers between devices  8.86 us (17%)
    pallas_call x14, Pallas kernels, call(): pl.pallas_call(without_held, in_specs=[place for place, _ in operands], o...  21.6 us
    ppermute x6, starting transfers between devices, body(): lax.ppermute(energy, axis, pairs_at(axis, stride, place))  7.94 us
    ppermute x6, waiting for transfers between devices, body(): lax.ppermute(energy, axis, pairs_at(axis, stride, place))  4.94 us
    ppermute x3, starting transfers between devices, body(): lax.ppermute(parts[place], axis, pairs_at(axis, stride, place))  4.45 us
    ppermute x3, starting transfers between devices, sent(): lax.ppermute(part.reshape(2, block, channels), axis, pairs_at(axis, strid...  4.16 us
    ppermute x1, starting transfers between devices, body(): handed = lax.ppermute(handed, 'grp', swap)  2.27 us
    ppermute x3, waiting for transfers between devices, body(): lax.ppermute(parts[place], axis, pairs_at(axis, stride, place))  1.92 us
    ppermute x3, waiting for transfers between devices, sent(): lax.ppermute(part.reshape(2, block, channels), axis, pairs_at(axis, strid...  1.6 us
  transfers between devices with their start and end apart: 19, of which 9 were waited for; matrix products, arithmetic and copies ran while one was open for 0% of the time, Pallas kernels for 32%

profile of v5, /device:TPU:0, one launch (start us, length us, event | category | flops | bytes accessed | tf_op | source)
XLA Modules:
  0.0 52.0 jit_solution(13682424219801593026)
XLA Ops:
  0.0 0.5 collective-permute-start.1
  0.5 0.5 collective-permute-start
  1.0 3.5 %shard_map.82 = (bf16[2048,256]{1,0:T(8,128)(2,1)S(1)}, bf16[32,2048]{1,0:T(8,128)(2,1)S(1)}, bf16[1024,32]{1,0:T(8,128)(2,1)S(1)}, bf16[8,256,2048]{2,1,0:T(8,1...) custom-call(s32[3,1024]{1,0:T(4,128)} %refs_0_.1, f32[3,16,128]{2,1,0:T(8,128)} %bitcast.34, s32[16]{0:T(128)} %bitcast.26, ...), custom_call_target="tpu_custom_call" | custom-call | tf_op jit(solution)/shard_map/pallas_call | solution.py:31
  4.5 1.9 %shard_map.83 = (bf16[2048,256]{1,0:T(8,128)(2,1)S(1)}, bf16[32,2048]{1,0:T(8,128)(2,1)S(1)}, bf16[256,256]{1,0:T(8,128)(2,1)S(1)}) custom-call(s32[16]{0:T(128)S(1)} %collective-permute-done.refs_0_, bf16[16,128,256]{2,1,0:T(8,128)(2,1)S(1)} %collective-permute-done.1.refs_1_, f32[3,16,128]{2,1,0:T(8,128)S(1)} %collective-permute-done.2.refs_2_, ...), custom_call_target="tpu_custom_call" | custom-call | tf_op jit(solution)/shard_map/pallas_call | solution.py:31
  6.3 3.5 %collective-permute-start.3 = (bf16[2,128,256]{2,1,0:T(8,128)(2,1)S(1)}, bf16[2,128,256]{2,1,0:T(8,128)(2,1)S(1)}, u32[]{:S(2)}, u32[]{:S(2)}) collective-permute-start(bf16[2,128,256]{2,1,0:T(8,128)(2,1)S(1)} %bitcast.28), channel_id=1, source_target_pairs={{0,3},{1,2},{2,1},{3,0},{4,7},{5,6},{6,5},{7,4},{8,11},{9,10},{10,... | collective-permute-start | bytes 393224 | tf_op jit(solution)/shard_map/ppermute | solution.py:470
  9.9 1.1 %shard_map.84.refs_6_ = bf16[256,256]{1,0:T(8,128)(2,1)S(1)} custom-call(bf16[1024,32]{1,0:T(8,128)(2,1)S(1)} %get-tuple-element.29.refs_3_.refs_0_.refs_4_, bf16[32,2048]{1,0:T(8,128)(2,1)S(1)} %get-tuple-element.32.refs_1_.refs_3_, bf16[2048,256]{1,0:T(8,128)(2,1)S(1)} %get-tuple-element.33.refs_2_.refs_4_.refs_3_, f32[256,256]{1,0:T(8,128)S(1)} %get-tuple-element.35.refs_3_), custom_call_target="tpu_custom_call" | custom-call | tf_op jit(solution)/shard_map/pallas_call | solution.py:31
  11.0 2.1 %shard_map.85 = (bf16[8,256,2048]{2,1,0:T(8,128)(2,1)S(1)}, bf16[256,256]{1,0:T(8,128)(2,1)S(1)}) custom-call(bf16[1024,32]{1,0:T(8,128)(2,1)S(1)} %get-tuple-element.29.refs_3_.refs_0_.refs_4_, bf16[32,2048]{1,0:T(8,128)(2,1)S(1)} %get-tuple-element.30.refs_1_, ...), custom_call_target="tpu_custom_call", output_to_operand_aliasing={{0}: (5, {})} | custom-call | tf_op jit(solution)/shard_map/pallas_call | solution.py:31
  13.1 0.6 %collective-permute-start.4 = (bf16[2,128,256]{2,1,0:T(8,128)(2,1)S(1)}, bf16[2,128,256]{2,1,0:T(8,128)(2,1)S(1)}, u32[]{:S(2)}, u32[]{:S(2)}) collective-permute-start(bf16[2,128,256]{2,1,0:T(8,128)(2,1)S(1)} %bitcast.29), channel_id=1, source_target_pairs={{0,1},{1,0},{2,3},{3,2},{4,5},{5,4},{6,7},{7,6},{8,9},{9,8},{10,11... | collective-permute-start | bytes 393224 | tf_op jit(solution)/shard_map/ppermute | solution.py:470
  13.7 0.3 collective-permute-done.3.refs_6_.refs_3_
  14.0 2.1 %shard_map.86 = (bf16[8,256,2048]{2,1,0:T(8,128)(2,1)S(1)}, f32[256,256]{1,0:T(8,128)S(1)}) custom-call(bf16[1024,32]{1,0:T(8,128)(2,1)S(1)} %get-tuple-element.29.refs_3_.refs_0_.refs_4_, bf16[32,2048]{1,0:T(8,128)(2,1)S(1)} %get-tuple-element.30.refs_1_, ...), custom_call_target="tpu_custom_call", output_to_operand_aliasing={{0}: (5, {})} | custom-call | tf_op jit(solution)/shard_map/pallas_call | solution.py:31
  16.2 1.5 %shard_map.87.refs_4_.refs_2_ = bf16[8,256,2048]{2,1,0:T(8,128)(2,1)S(1)} custom-call(bf16[1024,32]{1,0:T(8,128)(2,1)S(1)} %get-tuple-element.29.refs_3_.refs_0_.refs_4_, bf16[32,2048]{1,0:T(8,128)(2,1)S(1)} %get-tuple-element.30.refs_1_, bf16[8,256,2048]{2,1,0:T(8,128)(2,1)S(1)} %get-tuple-element.40.refs_2_, ...), custom_call_target="tpu_custom_call", output_to_operand_aliasing={{}: (2, {})} | custom-call | tf_op jit(solution)/shard_map/pallas_call | solution.py:31
  17.7 1.1 %collective-permute-done.4.refs_1_ = bf16[2,128,256]{2,1,0:T(8,128)(2,1)S(1)} collective-permute-done((bf16[2,128,256]{2,1,0:T(8,128)(2,1)S(1)}, bf16[2,128,256]{2,1,0:T(8,128)(2,1)S(1)}, u32[]{:S(2)}, u32[]{:S(2)}) %collective-permute-start.4) | collective-permute-done | bytes 131104 | tf_op jit(solution)/shard_map/ppermute | solution.py:470
  18.8 0.2 collective-permute-done.5.refs_2_
  19.1 1.6 %collective-permute-start.6 = (bf16[2,32,256]{2,1,0:T(8,128)(2,1)S(1)}, bf16[2,32,256]{2,1,0:T(8,128)(2,1)S(1)}, u32[]{:S(2)}, u32[]{:S(2)}) collective-permute-start(bf16[2,32,256]{2,1,0:T(8,128)(2,1)S(1)} %get-tuple-element.42), channel_id=1, source_target_pairs={{0,4},{1,5},{2,6},{3,7},{4,0},{5,1},{6,2},{7,3},{8,12},{9,13},{10,... | collective-permute-start | bytes 98312 | tf_op jit(solution)/shard_map/ppermute | solution.py:547
  20.8 2.6 %collective-permute-start.7 = (bf16[2,32,256]{2,1,0:T(8,128)(2,1)S(1)}, bf16[2,32,256]{2,1,0:T(8,128)(2,1)S(1)}, u32[]{:S(2)}, u32[]{:S(2)}) collective-permute-start(bf16[2,32,256]{2,1,0:T(8,128)(2,1)S(1)} %get-tuple-element.43), channel_id=1, source_target_pairs={{0,8},{1,9},{2,10},{3,11},{4,12},{5,13},{6,14},{7,15},{8,0},{9,1},... | collective-permute-start | bytes 98312 | tf_op jit(solution)/shard_map/ppermute | solution.py:547
  23.6 2.2 %shard_map.89 = (bf16[8,256,2048]{2,1,0:T(8,128)(2,1)S(1)}, bf16[2,128,256]{2,1,0:T(8,128)(2,1)S(1)}, bf16[2,128,256]{2,1,0:T(8,128)(2,1)S(1)}, bf16[129,128,128]{2,1,0:T(8,128)(2,1)S(1)}) custom-call(bf16[1024,32]{1,0:T(8,128)(2,1)S(1)} %get-tuple-element.29.refs_3_.refs_0_.refs_4_, ...), custom_call_target="tpu_custom_call", output_to_operand_aliasing={{0}: (2, {})} | custom-call | tf_op jit(solution)/shard_map/pallas_call | solution.py:31
  25.8 0.7 %collective-permute-start.12 = (bf16[2,128,256]{2,1,0:T(8,128)(2,1)S(1)}, bf16[2,128,256]{2,1,0:T(8,128)(2,1)S(1)}, u32[]{:S(2)}, u32[]{:S(2)}) collective-permute-start(bf16[2,128,256]{2,1,0:T(8,128)(2,1)S(1)} %get-tuple-element.47), channel_id=1, source_target_pairs={{16,17},{17,18},{18,19},{19,20},{20,21},{21,22},{22,23},{23,24},{2... | collective-permute-start | bytes 393224 | tf_op jit(solution)/shard_map/ppermute | solution.py:561
  26.5 0.7 %collective-permute-start.13 = (bf16[2,128,256]{2,1,0:T(8,128)(2,1)S(1)}, bf16[2,128,256]{2,1,0:T(8,128)(2,1)S(1)}, u32[]{:S(2)}, u32[]{:S(2)}) collective-permute-start(bf16[2,128,256]{2,1,0:T(8,128)(2,1)S(1)} %get-tuple-element.48), channel_id=1, source_target_pairs={{17,16},{18,17},{19,18},{20,19},{21,20},{22,21},{23,22},{24,23},{2... | collective-permute-start | bytes 393224 | tf_op jit(solution)/shard_map/ppermute | solution.py:561
  27.1 1.9 %collective-permute-done.8.refs_3_ = bf16[2,32,256]{2,1,0:T(8,128)(2,1)S(1)} collective-permute-done((bf16[2,32,256]{2,1,0:T(8,128)(2,1)S(1)}, bf16[2,32,256]{2,1,0:T(8,128)(2,1)S(1)}, u32[]{:S(2)}, u32[]{:S(2)}) %collective-permute-start.8) | collective-permute-done | bytes 32800 | tf_op jit(solution)/shard_map/ppermute | solution.py:547
  29.3 1.8 %collective-permute-start.11 = (bf16[2,32,256]{2,1,0:T(8,128)(2,1)S(1)}, bf16[2,32,256]{2,1,0:T(8,128)(2,1)S(1)}, u32[]{:S(2)}, u32[]{:S(2)}) collective-permute-start(bf16[2,32,256]{2,1,0:T(8,128)(2,1)S(1)} %shard_map.90.refs_0_), channel_id=1, source_target_pairs={{0,12},{1,13},{2,14},{3,15},{4,8},{5,9},{6,10},{7,11},{8,4},{9,5},... | collective-permute-start | bytes 98312 | tf_op jit(solution)/shard_map/ppermute | solution.py:571
  31.0 2.7 %collective-permute-start.9 = (bf16[2,32,256]{2,1,0:T(8,128)(2,1)S(1)}, bf16[2,32,256]{2,1,0:T(8,128)(2,1)S(1)}, u32[]{:S(2)}, u32[]{:S(2)}) collective-permute-start(bf16[2,32,256]{2,1,0:T(8,128)(2,1)S(1)} %shard_map.90.refs_0_), channel_id=1, source_target_pairs={{0,4},{1,5},{2,6},{3,7},{4,0},{5,1},{6,2},{7,3},{8,12},{9,13},{10,... | collective-permute-start | bytes 98312 | tf_op jit(solution)/shard_map/ppermute | solution.py:571
  33.7 1.4 %collective-permute-done.11.refs_3_ = bf16[2,32,256]{2,1,0:T(8,128)(2,1)S(1)} collective-permute-done((bf16[2,32,256]{2,1,0:T(8,128)(2,1)S(1)}, bf16[2,32,256]{2,1,0:T(8,128)(2,1)S(1)}, u32[]{:S(2)}, u32[]{:S(2)}) %collective-permute-start.11) | collective-permute-done | bytes 32800 | tf_op jit(solution)/shard_map/ppermute | solution.py:571
  35.1 1.1 %collective-permute-done.10.refs_2_ = bf16[2,32,256]{2,1,0:T(8,128)(2,1)S(1)} collective-permute-done((bf16[2,32,256]{2,1,0:T(8,128)(2,1)S(1)}, bf16[2,32,256]{2,1,0:T(8,128)(2,1)S(1)}, u32[]{:S(2)}, u32[]{:S(2)}) %collective-permute-start.10) | collective-permute-done | bytes 32800 | tf_op jit(solution)/shard_map/ppermute | solution.py:571
  36.3 2.3 %collective-permute-start.17 = (bf16[768,256]{1,0:T(8,128)(2,1)S(1)}, bf16[768,256]{1,0:T(8,128)(2,1)S(1)}, u32[]{:S(2)}, u32[]{:S(2)}) collective-permute-start(bf16[768,256]{1,0:T(8,128)(2,1)S(1)} %get-tuple-element.50), channel_id=1, source_target_pairs={{0,16},{16,0},{1,17},{17,1},{2,18},{18,2},{3,19},{19,3},{4,20},{20... | collective-permute-start | bytes 1179656 | tf_op jit(solution)/shard_map/ppermute | solution.py:576
  38.7 1.0 %collective-permute-start.15 = (bf16[2,128,256]{2,1,0:T(8,128)(2,1)S(1)}, bf16[2,128,256]{2,1,0:T(8,128)(2,1)S(1)}, u32[]{:S(2)}, u32[]{:S(2)}) collective-permute-start(bf16[2,128,256]{2,1,0:T(8,128)(2,1)S(1)} %get-tuple-element.49.refs_8_), channel_id=1, source_target_pairs={{0,2},{1,3},{2,0},{3,1},{4,6},{5,7},{6,4},{7,5},{8,10},{9,11},{10,... | collective-permute-start | bytes 393224 | tf_op jit(solution)/shard_map/ppermute | solution.py:579
  39.7 2.4 %collective-permute-start.14 = (bf16[2,128,256]{2,1,0:T(8,128)(2,1)S(1)}, bf16[2,128,256]{2,1,0:T(8,128)(2,1)S(1)}, u32[]{:S(2)}, u32[]{:S(2)}) collective-permute-start(bf16[2,128,256]{2,1,0:T(8,128)(2,1)S(1)} %get-tuple-element.49.refs_8_), channel_id=1, source_target_pairs={{0,1},{1,0},{2,3},{3,2},{4,5},{5,4},{6,7},{7,6},{8,9},{9,8},{10,11... | collective-permute-start | bytes 393224 | tf_op jit(solution)/shard_map/ppermute | solution.py:579
  42.1 2.5 %shard_map.92.refs_5_.refs_3_ = f32[16,128,256]{2,1,0:T(8,128)S(1)} custom-call(s32[8,16]{1,0:T(8,128)S(1)} %bitcast.24, bf16[129,128,128]{2,1,0:T(8,128)(2,1)S(1)} %get-tuple-element.46.refs_7_.refs_1_, bf16[2048,256]{1,0:T(8,128)(2,1)S(1)} %get-tuple-element.28.refs_2_.refs_3_.refs_1_, bf16[2048,256]{1,0:T(8,128)(2,1)S(1)} %get-tuple-element.33.refs_2_.refs_4_.refs_3_, ...), custom_call_target="tpu_custom_call" | custom-call | tf_op jit(solution)/shard_map/pallas_call | solution.py:31
  44.6 1.3 %collective-permute-done.16.refs_2_ = bf16[2,128,256]{2,1,0:T(8,128)(2,1)S(1)} collective-permute-done((bf16[2,128,256]{2,1,0:T(8,128)(2,1)S(1)}, bf16[2,128,256]{2,1,0:T(8,128)(2,1)S(1)}, u32[]{:S(2)}, u32[]{:S(2)}) %collective-permute-start.16) | collective-permute-done | bytes 131104 | tf_op jit(solution)/shard_map/ppermute | solution.py:579
  45.9 1.1 %collective-permute-done.15.refs_1_ = bf16[2,128,256]{2,1,0:T(8,128)(2,1)S(1)} collective-permute-done((bf16[2,128,256]{2,1,0:T(8,128)(2,1)S(1)}, bf16[2,128,256]{2,1,0:T(8,128)(2,1)S(1)}, u32[]{:S(2)}, u32[]{:S(2)}) %collective-permute-start.15) | collective-permute-done | bytes 131104 | tf_op jit(solution)/shard_map/ppermute | solution.py:579
  47.1 1.3 %shard_map.93.refs_2_ = f32[256,2048]{1,0:T(8,128)S(1)} custom-call(bf16[256,256]{1,0:T(8,128)(2,1)S(1)} %bitcast.19, bf16[256,256]{1,0:T(8,128)(2,1)S(1)} %bitcast.23, bf16[256,256]{1,0:T(8,128)(2,1)S(1)} %bitcast.22, bf16[256,256]{1,0:T(8,128)(2,1)S(1)} %bitcast.21, bf16[8,256,2048]{2,1,0:T(8,128)(2,1)S(1)} %get-tuple-element.45.refs_6_.refs_9_.refs_4_, ...), custom_call_target="tpu_custom_call" | custom-call | tf_op jit(solution)/shard_map/pallas_call | solution.py:31
  48.4 0.4 collective-permute-done.18.refs_5_
  48.8 3.1 %shard_map.95 = bf16[16,128,256]{2,1,0:T(8,128)(2,1)} custom-call(s32[16]{0:T(128)S(1)} %bitcast.27, bf16[2048,256]{1,0:T(8,128)(2,1)S(1)} %get-tuple-element.28.refs_2_.refs_3_.refs_1_, f32[256,2048]{1,0:T(8,128)S(1)} %shard_map.93.refs_2_, f32[16,128,256]{2,1,0:T(8,128)S(1)} %shard_map.92.refs_5_.refs_3_, ...), custom_call_target="tpu_custom_call" | custom-call | tf_op jit(solution)/shard_map/pallas_call | solution.py:31
  (28 shorter events, 0.8 us)
Async XLA Ops:
  0.0 4.5 %collective-permute-start.1 = (bf16[16,128,256]{2,1,0:T(8,128)(2,1)}, bf16[16,128,256]{2,1,0:T(8,128)(2,1)S(1)}, u32[]{:S(2)}, u32[]{:S(2)}) collective-permute-start(bf16[16,128,256]{2,1,0:T(8,128)(2,1)} %bitcast.31), channel_id=1, source_target_pairs={{0,16},{16,0},{1,17},{17,1},{2,18},{18,2},{3,19},{19,3},{4,20},{20... | collective-permute-start | bytes 3145736 | tf_op jit(solution)/shard_map/ppermute | solution.py:445
  0.5 4.0 %collective-permute-start.2 = (f32[3,16,128]{2,1,0:T(8,128)}, f32[3,16,128]{2,1,0:T(8,128)S(1)}, u32[]{:S(2)}, u32[]{:S(2)}) collective-permute-start(f32[3,16,128]{2,1,0:T(8,128)} %bitcast.33), channel_id=1, source_target_pairs={{0,16},{16,0},{1,17},{17,1},{2,18},{18,2},{3,19},{19,3},{4,20},{20... | collective-permute-start | bytes 73736 | tf_op jit(solution)/shard_map/ppermute | solution.py:442
  0.5 3.9 %collective-permute-start = (s32[16]{0:T(128)}, s32[16]{0:T(128)S(1)}, u32[]{:S(2)}, u32[]{:S(2)}) collective-permute-start(s32[16]{0:T(128)} %bitcast.25), channel_id=1, source_target_pairs={{0,16},{16,0},{1,17},{17,1},{2,18},{18,2},{3,19},{19,3},{4,20},{20... | collective-permute-start | bytes 200 | tf_op jit(solution)/shard_map/ppermute | solution.py:444
  6.3 7.7 %collective-permute-start.3 = (bf16[2,128,256]{2,1,0:T(8,128)(2,1)S(1)}, bf16[2,128,256]{2,1,0:T(8,128)(2,1)S(1)}, u32[]{:S(2)}, u32[]{:S(2)}) collective-permute-start(bf16[2,128,256]{2,1,0:T(8,128)(2,1)S(1)} %bitcast.28), channel_id=1, source_target_pairs={{0,3},{1,2},{2,1},{3,0},{4,7},{5,6},{6,5},{7,4},{8,11},{9,10},{10,... | collective-permute-start | bytes 393224 | tf_op jit(solution)/shard_map/ppermute | solution.py:470
  13.1 5.7 %collective-permute-start.4 = (bf16[2,128,256]{2,1,0:T(8,128)(2,1)S(1)}, bf16[2,128,256]{2,1,0:T(8,128)(2,1)S(1)}, u32[]{:S(2)}, u32[]{:S(2)}) collective-permute-start(bf16[2,128,256]{2,1,0:T(8,128)(2,1)S(1)} %bitcast.29), channel_id=1, source_target_pairs={{0,1},{1,0},{2,3},{3,2},{4,5},{5,4},{6,7},{7,6},{8,9},{9,8},{10,11... | collective-permute-start | bytes 393224 | tf_op jit(solution)/shard_map/ppermute | solution.py:470
  13.7 5.3 %collective-permute-start.5 = (bf16[2,128,256]{2,1,0:T(8,128)(2,1)S(1)}, bf16[2,128,256]{2,1,0:T(8,128)(2,1)S(1)}, u32[]{:S(2)}, u32[]{:S(2)}) collective-permute-start(bf16[2,128,256]{2,1,0:T(8,128)(2,1)S(1)} %bitcast.20), channel_id=1, source_target_pairs={{0,2},{1,3},{2,0},{3,1},{4,6},{5,7},{6,4},{7,5},{8,10},{9,11},{10,... | collective-permute-start | bytes 393224 | tf_op jit(solution)/shard_map/ppermute | solution.py:470
  19.1 10.0 %copy-start.3 = (bf16[256,256]{1,0:T(8,128)(2,1)S(1)}, bf16[256,256]{1,0:T(8,128)(2,1)}, u32[]{:S(2)}) copy-start(bf16[256,256]{1,0:T(8,128)(2,1)} %refs_5_.1) | copy-start | bytes 393220
  19.1 8.0 %collective-permute-start.6 = (bf16[2,32,256]{2,1,0:T(8,128)(2,1)S(1)}, bf16[2,32,256]{2,1,0:T(8,128)(2,1)S(1)}, u32[]{:S(2)}, u32[]{:S(2)}) collective-permute-start(bf16[2,32,256]{2,1,0:T(8,128)(2,1)S(1)} %get-tuple-element.42), channel_id=1, source_target_pairs={{0,4},{1,5},{2,6},{3,7},{4,0},{5,1},{6,2},{7,3},{8,12},{9,13},{10,... | collective-permute-start | bytes 98312 | tf_op jit(solution)/shard_map/ppermute | solution.py:547
  20.8 6.4 %collective-permute-start.7 = (bf16[2,32,256]{2,1,0:T(8,128)(2,1)S(1)}, bf16[2,32,256]{2,1,0:T(8,128)(2,1)S(1)}, u32[]{:S(2)}, u32[]{:S(2)}) collective-permute-start(bf16[2,32,256]{2,1,0:T(8,128)(2,1)S(1)} %get-tuple-element.43), channel_id=1, source_target_pairs={{0,8},{1,9},{2,10},{3,11},{4,12},{5,13},{6,14},{7,15},{8,0},{9,1},... | collective-permute-start | bytes 98312 | tf_op jit(solution)/shard_map/ppermute | solution.py:547
  23.4 5.7 %collective-permute-start.8 = (bf16[2,32,256]{2,1,0:T(8,128)(2,1)S(1)}, bf16[2,32,256]{2,1,0:T(8,128)(2,1)S(1)}, u32[]{:S(2)}, u32[]{:S(2)}) collective-permute-start(bf16[2,32,256]{2,1,0:T(8,128)(2,1)S(1)} %get-tuple-element.44), channel_id=1, source_target_pairs={{0,12},{1,13},{2,14},{3,15},{4,8},{5,9},{6,10},{7,11},{8,4},{9,5},... | collective-permute-start | bytes 98312 | tf_op jit(solution)/shard_map/ppermute | solution.py:547
  25.8 10.5 %collective-permute-start.12 = (bf16[2,128,256]{2,1,0:T(8,128)(2,1)S(1)}, bf16[2,128,256]{2,1,0:T(8,128)(2,1)S(1)}, u32[]{:S(2)}, u32[]{:S(2)}) collective-permute-start(bf16[2,128,256]{2,1,0:T(8,128)(2,1)S(1)} %get-tuple-element.47), channel_id=1, source_target_pairs={{16,17},{17,18},{18,19},{19,20},{20,21},{21,22},{22,23},{23,24},{2... | collective-permute-start | bytes 393224 | tf_op jit(solution)/shard_map/ppermute | solution.py:561
  26.5 9.8 %collective-permute-start.13 = (bf16[2,128,256]{2,1,0:T(8,128)(2,1)S(1)}, bf16[2,128,256]{2,1,0:T(8,128)(2,1)S(1)}, u32[]{:S(2)}, u32[]{:S(2)}) collective-permute-start(bf16[2,128,256]{2,1,0:T(8,128)(2,1)S(1)} %get-tuple-element.48), channel_id=1, source_target_pairs={{17,16},{18,17},{19,18},{20,19},{21,20},{22,21},{23,22},{24,23},{2... | collective-permute-start | bytes 393224 | tf_op jit(solution)/shard_map/ppermute | solution.py:561
  29.2 12.9 %copy-start = (bf16[256,256]{1,0:T(8,128)(2,1)S(1)}, bf16[256,256]{1,0:T(8,128)(2,1)}, u32[]{:S(2)}) copy-start(bf16[256,256]{1,0:T(8,128)(2,1)} %refs_7_.1) | copy-start | bytes 393220
  29.2 12.8 %copy-start.1 = (s32[1,16,8]{1,2,0:T(8,128)S(1)}, s32[1,16,8]{1,2,0:T(8,128)}, u32[]{:S(2)}) copy-start(s32[1,16,8]{1,2,0:T(8,128)} %param.11) | copy-start | bytes 1540
  29.3 5.9 %collective-permute-start.11 = (bf16[2,32,256]{2,1,0:T(8,128)(2,1)S(1)}, bf16[2,32,256]{2,1,0:T(8,128)(2,1)S(1)}, u32[]{:S(2)}, u32[]{:S(2)}) collective-permute-start(bf16[2,32,256]{2,1,0:T(8,128)(2,1)S(1)} %shard_map.90.refs_0_), channel_id=1, source_target_pairs={{0,12},{1,13},{2,14},{3,15},{4,8},{5,9},{6,10},{7,11},{8,4},{9,5},... | collective-permute-start | bytes 98312 | tf_op jit(solution)/shard_map/ppermute | solution.py:571
  31.0 5.2 %collective-permute-start.10 = (bf16[2,32,256]{2,1,0:T(8,128)(2,1)S(1)}, bf16[2,32,256]{2,1,0:T(8,128)(2,1)S(1)}, u32[]{:S(2)}, u32[]{:S(2)}) collective-permute-start(bf16[2,32,256]{2,1,0:T(8,128)(2,1)S(1)} %shard_map.90.refs_0_), channel_id=1, source_target_pairs={{0,8},{1,9},{2,10},{3,11},{4,12},{5,13},{6,14},{7,15},{8,0},{9,1},... | collective-permute-start | bytes 98312 | tf_op jit(solution)/shard_map/ppermute | solution.py:571
  31.0 5.2 %collective-permute-start.9 = (bf16[2,32,256]{2,1,0:T(8,128)(2,1)S(1)}, bf16[2,32,256]{2,1,0:T(8,128)(2,1)S(1)}, u32[]{:S(2)}, u32[]{:S(2)}) collective-permute-start(bf16[2,32,256]{2,1,0:T(8,128)(2,1)S(1)} %shard_map.90.refs_0_), channel_id=1, source_target_pairs={{0,4},{1,5},{2,6},{3,7},{4,0},{5,1},{6,2},{7,3},{8,12},{9,13},{10,... | collective-permute-start | bytes 98312 | tf_op jit(solution)/shard_map/ppermute | solution.py:571
  36.3 5.8 %collective-permute-start.17 = (bf16[768,256]{1,0:T(8,128)(2,1)S(1)}, bf16[768,256]{1,0:T(8,128)(2,1)S(1)}, u32[]{:S(2)}, u32[]{:S(2)}) collective-permute-start(bf16[768,256]{1,0:T(8,128)(2,1)S(1)} %get-tuple-element.50), channel_id=1, source_target_pairs={{0,16},{16,0},{1,17},{17,1},{2,18},{18,2},{3,19},{19,3},{4,20},{20... | collective-permute-start | bytes 1179656 | tf_op jit(solution)/shard_map/ppermute | solution.py:576
  38.6 7.3 %collective-permute-start.16 = (bf16[2,128,256]{2,1,0:T(8,128)(2,1)S(1)}, bf16[2,128,256]{2,1,0:T(8,128)(2,1)S(1)}, u32[]{:S(2)}, u32[]{:S(2)}) collective-permute-start(bf16[2,128,256]{2,1,0:T(8,128)(2,1)S(1)} %get-tuple-element.49.refs_8_), channel_id=1, source_target_pairs={{0,3},{1,2},{2,1},{3,0},{4,7},{5,6},{6,5},{7,4},{8,11},{9,10},{10,... | collective-permute-start | bytes 393224 | tf_op jit(solution)/shard_map/ppermute | solution.py:579
  38.7 8.3 %collective-permute-start.15 = (bf16[2,128,256]{2,1,0:T(8,128)(2,1)S(1)}, bf16[2,128,256]{2,1,0:T(8,128)(2,1)S(1)}, u32[]{:S(2)}, u32[]{:S(2)}) collective-permute-start(bf16[2,128,256]{2,1,0:T(8,128)(2,1)S(1)} %get-tuple-element.49.refs_8_), channel_id=1, source_target_pairs={{0,2},{1,3},{2,0},{3,1},{4,6},{5,7},{6,4},{7,5},{8,10},{9,11},{10,... | collective-permute-start | bytes 393224 | tf_op jit(solution)/shard_map/ppermute | solution.py:579
  39.7 7.3 %collective-permute-start.14 = (bf16[2,128,256]{2,1,0:T(8,128)(2,1)S(1)}, bf16[2,128,256]{2,1,0:T(8,128)(2,1)S(1)}, u32[]{:S(2)}, u32[]{:S(2)}) collective-permute-start(bf16[2,128,256]{2,1,0:T(8,128)(2,1)S(1)} %get-tuple-element.49.refs_8_), channel_id=1, source_target_pairs={{0,1},{1,0},{2,3},{3,2},{4,5},{5,4},{6,7},{7,6},{8,9},{9,8},{10,11... | collective-permute-start | bytes 393224 | tf_op jit(solution)/shard_map/ppermute | solution.py:579
  44.6 4.2 %copy-start.2 = (s32[1,16]{1,0:T(1,128)S(1)}, s32[1,16]{1,0:T(1,128)}, u32[]{:S(2)}) copy-start(s32[1,16]{1,0:T(1,128)} %param.12) | copy-start | bytes 196
  47.0 1.8 %collective-permute-start.18 = (bf16[2,384,256]{2,1,0:T(8,128)(2,1)S(1)}, bf16[2,384,256]{2,1,0:T(8,128)(2,1)S(1)}, u32[]{:S(2)}, u32[]{:S(2)}) collective-permute-start(bf16[2,384,256]{2,1,0:T(8,128)(2,1)S(1)} %shard_map.94), channel_id=1, source_target_pairs={{0,16},{16,0},{1,17},{17,1},{2,18},{18,2},{3,19},{19,3},{4,20},{20... | collective-permute-start | bytes 1179656 | tf_op jit(solution)/shard_map/ppermute | solution.py:590

commit v6 on v5

--- a/solution.py
+++ b/solution.py
@@ -16,7 +16,7 @@
 PARAMS = pltpu.CompilerParams(vmem_limit_bytes=14 * 1024 * 1024)
 LANES = 128
 COST = 0
-WEIGHT = 4
+WEIGHT = 0
 SIN = (4.44287957, -7.30781668, 3.59777418, -0.79119939)
 COS = (1.41420401, -6.97763732, 5.71518787, -1.72821389)
 
@@ -66,16 +66,6 @@
 def finish(copies):
     for copy in copies:
         copy.wait()
-
-
-def radices(count):
-    digits = []
-    stride = 1
-    while stride < count:
-        radix = 4 if count // stride % 4 == 0 else 2
-        digits.append((stride, radix))
-        stride *= radix
-    return digits
 
 
 def pairs_at(axis, stride, offset):
@@ -264,27 +254,18 @@
         carried = total
 
 
-def add_kernel(count, radix, *refs):
-    pieces, outs = refs[:count], refs[count:]
+def add_kernel(*refs):
+    pieces, (total_ref, sent_ref) = refs[:-2], refs[-2:]
     total = pieces[0][...].astype(F32)
     for piece in pieces[1:]:
         total = total + piece[...].astype(F32)
-    rows = total.shape[1] // radix
-    for place, out in enumerate(outs):
-        out[...] = total[:, place * rows : (place + 1) * rows].astype(out.dtype)
-
-
-def add_and_cut(pieces, radix, held):
-    trig, rows, channels = pieces[0].shape
-    part = (trig, rows // radix, channels)
-    types = [F32] + [BF16] * (radix - 1)
-    if part[1] % 16:
-        total = functools.reduce(jnp.add, [piece.astype(F32) for piece in pieces])
-        return [
-            total[:, place * part[1] : (place + 1) * part[1]].astype(kind) for place, kind in enumerate(types)
-        ]
-    kernel = functools.partial(add_kernel, len(pieces), radix)
-    return call(kernel, [(VMEM, (part, kind)) for kind in types], in_vmem(pieces), held=held)
+    total_ref[...] = total
+    sent_ref[...] = total.astype(sent_ref.dtype)
+
+
+def added(pieces, held):
+    shape = pieces[0].shape
+    return call(add_kernel, [(VMEM, (shape, F32)), (VMEM, (shape, BF16))], in_vmem(pieces), held=held)
 
 
 def mixed(owned, waves, w_mix, factor_scale):
@@ -309,14 +290,9 @@
 
 
 def energy_of(pieces, turned, w_mix, factor_scale, held):
-    trig, rows, channels = pieces[0].shape
-    if rows % 16:
-        total = functools.reduce(jnp.add, [piece.astype(F32) for piece in pieces])
-        energy = mixed(total.reshape(trig * rows, channels), turned[:rows].astype(F32), w_mix, factor_scale)
-        return energy.reshape(trig, rows, channels)
     (energy,) = call(
         functools.partial(energy_kernel, len(pieces), factor_scale),
-        [(VMEM, ((trig, rows, channels), BF16))],
+        [(VMEM, (pieces[0].shape, BF16))],
         in_vmem([*pieces, turned, w_mix]),
         held=held,
         flops=WEIGHT * 10**9,
@@ -324,46 +300,19 @@
     return energy
 
 
-def join_kernel(count, *refs):
-    pieces, out_ref = refs[:count], refs[-1]
-    rows = pieces[0].shape[1]
-    for place, piece in enumerate(pieces):
-        out_ref[:, place * rows : (place + 1) * rows, :] = piece[...]
-
-
-def pack_kernel(count, *refs):
-    pieces, extras, (out_ref, packed_ref) = refs[:count], refs[count:-2], refs[-2:]
-    trig, rows, _ = pieces[0].shape
-    for place, piece in enumerate(pieces):
-        out_ref[:, place * rows : (place + 1) * rows, :] = piece[...]
-        for part in range(trig):
-            start = (part * count + place) * rows
-            packed_ref[start : start + rows, :] = piece[part]
-    start = trig * count * rows
-    for extra in extras:
-        for line in range(extra.shape[0]):
-            packed_ref[start : start + extra.shape[1], :] = extra[line]
-            start += extra.shape[1]
-
-
-def joined(pieces, held):
-    trig, rows, channels = pieces[0].shape
-    if rows % 16:
-        return jnp.concatenate(pieces, axis=1)
-    whole = (VMEM, ((trig, rows * len(pieces), channels), BF16))
-    (whole,) = call(functools.partial(join_kernel, len(pieces)), [whole], in_vmem(pieces), held=held)
+def stack_kernel(*refs):
+    pieces, out_ref = refs[:-1], refs[-1]
+    start = 0
+    for piece in pieces:
+        for part in range(piece.shape[0]):
+            out_ref[start : start + piece.shape[1], :] = piece[part]
+            start += piece.shape[1]
+
+
+def stacked(pieces, held):
+    rows = sum(piece.shape[0] * piece.shape[1] for piece in pieces)
+    (whole,) = call(stack_kernel, [(VMEM, ((rows, pieces[0].shape[2]), BF16))], in_vmem(pieces), held=held)
     return whole
-
-
-def packed(pieces, extras, held):
-    trig, rows, channels = pieces[0].shape
-    count = trig * rows * len(pieces) + sum(extra.shape[0] * extra.shape[1] for extra in extras)
-    return call(
-        functools.partial(pack_kernel, len(pieces)),
-        [(VMEM, ((trig, rows * len(pieces), channels), BF16)), (VMEM, ((count, channels), BF16))],
-        in_vmem([*pieces, *extras]),
-        held=held,
-    )
 
 
 def near_kernel(blocks, *refs):
@@ -386,11 +335,9 @@
 ):
     cells, slots, channels = out_ref.shape
     rows = table_ref.shape[1]
-    half = rows // 2
     turned_ref[0] = energy_ref[:rows, :].astype(F32).T.astype(BF16)
     for place in range(1, blocks):
-        taken = rest_ref[:, (place - 1) * half : place * half, :].reshape(rows, channels)
-        turned_ref[place] = taken.astype(F32).T.astype(BF16)
+        turned_ref[place] = rest_ref[(place - 1) * rows : place * rows, :].astype(F32).T.astype(BF16)
     slot_ids = lax.broadcasted_iota(jnp.int32, (slots, channels), 0)
     group = math.gcd(cells, 2)
     share = math.gcd(cells, 4)
@@ -451,11 +398,11 @@
         sibling_counts = jnp.where(even, near[1][0], near[0][0])
         sibling_features = jnp.where(even, near[1][1], near[0][1])
 
-    stages = [("dev", *digit) for digit in radices(dev_count)]
-    stages += [("grp", 2 * stride, radix) for stride, radix in radices(slabs // 2)]
-    digits = [("grp", 1, 2)] + stages
+    blocks = 4 if dev_count % 4 == 0 else 2
+    digits = [("grp", 1, 2), ("dev", 1, blocks)]
+    twos = [("dev", blocks << bit) for bit in range((dev_count // blocks).bit_length() - 1)]
+    twos += [("grp", 2 << bit) for bit in range((slabs // 2).bit_length() - 1)]
     half = wave_count // 2
-    axis, stride, blocks = stages[0]
     block = half // blocks
     table = ((2 * block, atoms), BF16)
     sums = ((2 * block, channels), F32)
@@ -467,7 +414,7 @@
     block_flops = 2 * 2 * block * atoms * channels * COST
 
     def sent(part, place):
-        return lax.ppermute(part.reshape(2, block, channels), axis, pairs_at(axis, stride, place))
+        return lax.ppermute(part.reshape(2, block, channels), "dev", pairs_at("dev", 1, place))
 
     order = [*range(blocks - 1, 0, -1), 0]
     early = order[: min(2, blocks - 1)]
@@ -541,16 +488,11 @@
     middle = blocks + blocks // 2
     (tables,) = rest_of(tables, blocks, middle, [part])
 
-    for axis, stride, radix in stages[1:]:
-        parts = add_and_cut(pieces, radix, [tables])
-        pieces = [parts[0]] + [
-            lax.ppermute(parts[place], axis, pairs_at(axis, stride, place)) for place in range(1, radix)
-        ]
-
+    total, half_total = added(pieces, [tables])
     radial = radial.reshape(-1, slots, slots)
     radial_type = (VMEM, ((radial.shape[0] + 1, slots, slots), BF16))
     tables, *edges, radial = rest_of(
-        tables, middle, 2 * blocks, [parts[0]],
+        tables, middle, 2 * blocks, [total],
         [*lines, radial], [edge, edge, radial_type], [pltpu.SemaphoreType.DMA((1,))],
     )
 
@@ -564,20 +506,18 @@
     else:
         outer = [lax.ppermute(part, "dev", way) for part, way in zip(edges, (right, left))]
 
+    held = [tables, radial]
+    for axis, stride in twos[:-1]:
+        total, half_total = added([total, lax.ppermute(half_total, axis, pairs_at(axis, stride, 1))], held)
+        held = []
+    axis, stride = twos[-1]
+    pieces = [total, lax.ppermute(half_total, axis, pairs_at(axis, stride, 1))]
     energy = energy_of(pieces, turned, w_mix, 1.0 / math.sqrt(total_slots), [tables, radial])
 
-    for stage, (axis, stride, radix) in reversed(list(enumerate(stages))[1:]):
-        pieces = [energy] + [
-            lax.ppermute(energy, axis, pairs_at(axis, stride, place)) for place in range(1, radix)
-        ]
-        if stage > 1:
-            energy = joined(pieces, [tables, radial])
-    energy, handed = packed(pieces, outer if slabs == 2 else [], [tables, radial])
-    handed = lax.ppermute(handed, "grp", swap)
-    axis, stride, blocks = stages[0]
     energies = [energy] + [
-        lax.ppermute(energy, axis, pairs_at(axis, stride, place)) for place in range(1, blocks)
+        lax.ppermute(energy, "dev", pairs_at("dev", 1, place)) for place in range(1, blocks)
     ]
+    handed = lax.ppermute(stacked([energy, *(outer if slabs == 2 else [])], [radial]), "grp", swap)
 
     (message,) = call(
         functools.partial(short_kernel, len(lines)),
@@ -587,7 +527,7 @@
         [energy, tables],
         6 * block_flops,
     )
-    rest = lax.ppermute(joined(energies[1:], [message]), "grp", swap)
+    rest = lax.ppermute(stacked(energies[1:], [message]), "grp", swap)
     energies = [part.reshape(2 * block, channels) for part in energies]
     (near_sum,) = call(
         functools.partial(near_kernel, blocks),

time: 52.3 us -> 49.6 us (0.948)
  starting transfers between devices: 21.2 us -> 17.3 us
  waiting for transfers between devices: 8.86 us -> 10 us
    ppermute x14 -> x10, starting transfers between devices: 18.9 us -> 15.1 us  [the longest x3 4.86 us: body(): lax.ppermute(energy, 'dev', pairs_at('dev', 1, place))]
    ppermute x14 -> x10, waiting for transfers between devices: 8.85 us -> 10 us  [the longest x3 3.49 us: body(): lax.ppermute(energy, 'dev', pairs_at('dev', 1, place))]
    pallas_call x14 -> x15, Pallas kernels: 21.6 us -> 21.6 us  [call(): pl.pallas_call(without_held, in_specs=[place for place, _ in operands], o...]
  transfers between devices with their start and end apart: 19 -> 15, of which waited for: 9 -> 8; matrix products, arithmetic and copies ran while one was open for 0% -> 0% of each run, Pallas kernels for 32% -> 34%
where the time goes in v6:
time: 49.6 us; the launch traced here: 49.3 us
  Pallas kernels  21.6 us (44%)
  starting transfers between devices  17.3 us (35%)
  waiting for transfers between devices  10 us (20%)
    pallas_call x15, Pallas kernels, call(): pl.pallas_call(without_held, in_specs=[place for place, _ in operands], o...  21.6 us
    ppermute x3, starting transfers between devices, body(): lax.ppermute(energy, 'dev', pairs_at('dev', 1, place))  4.86 us
    ppermute x3, starting transfers between devices, sent(): lax.ppermute(part.reshape(2, block, channels), 'dev', pairs_at('dev', 1,...  4.17 us
    ppermute x3, waiting for transfers between devices, body(): lax.ppermute(energy, 'dev', pairs_at('dev', 1, place))  3.49 us
    ppermute x1, waiting for transfers between devices, body(): pieces = [total, lax.ppermute(half_total, axis, pairs_at(axis, stride, 1))]  3.34 us
    ppermute x1, starting transfers between devices, body(): pieces = [total, lax.ppermute(half_total, axis, pairs_at(axis, stride, 1))]  2.66 us
    ppermute x1, starting transfers between devices, body(): lax.ppermute(stacked([energy, *(outer if slabs == 2 else [])], [radial]),...  1.64 us
    ppermute x1, starting transfers between devices, body(): lax.ppermute(half_total, axis, pairs_at(axis, stride, 1))  1.64 us
  transfers between devices with their start and end apart: 15, of which 8 were waited for; matrix products, arithmetic and copies ran while one was open for 0% of the time, Pallas kernels for 34%

profile of v6, /device:TPU:0, one launch (start us, length us, event | category | flops | bytes accessed | tf_op | source)
XLA Modules:
  0.0 49.3 jit_solution(6756308907459504397)
XLA Ops:
  0.0 0.5 collective-permute-start.1
  0.5 0.5 collective-permute-start
  1.0 3.5 %shard_map.82 = (bf16[2048,256]{1,0:T(8,128)(2,1)S(1)}, bf16[32,2048]{1,0:T(8,128)(2,1)S(1)}, bf16[1024,32]{1,0:T(8,128)(2,1)S(1)}, bf16[8,256,2048]{2,1,0:T(8,1...) custom-call(s32[3,1024]{1,0:T(4,128)} %refs_0_.1, f32[3,16,128]{2,1,0:T(8,128)} %bitcast.34, s32[16]{0:T(128)} %bitcast.26, ...), custom_call_target="tpu_custom_call" | custom-call | tf_op jit(solution)/shard_map/pallas_call | solution.py:31
  4.5 1.9 %shard_map.83 = (bf16[2048,256]{1,0:T(8,128)(2,1)S(1)}, bf16[32,2048]{1,0:T(8,128)(2,1)S(1)}, bf16[256,256]{1,0:T(8,128)(2,1)S(1)}) custom-call(s32[16]{0:T(128)S(1)} %collective-permute-done.refs_0_, bf16[16,128,256]{2,1,0:T(8,128)(2,1)S(1)} %collective-permute-done.1.refs_1_, f32[3,16,128]{2,1,0:T(8,128)S(1)} %collective-permute-done.2.refs_2_, ...), custom_call_target="tpu_custom_call" | custom-call | tf_op jit(solution)/shard_map/pallas_call | solution.py:31
  6.3 3.5 %collective-permute-start.3 = (bf16[2,128,256]{2,1,0:T(8,128)(2,1)S(1)}, bf16[2,128,256]{2,1,0:T(8,128)(2,1)S(1)}, u32[]{:S(2)}, u32[]{:S(2)}) collective-permute-start(bf16[2,128,256]{2,1,0:T(8,128)(2,1)S(1)} %bitcast.28), channel_id=1, source_target_pairs={{0,3},{1,2},{2,1},{3,0},{4,7},{5,6},{6,5},{7,4},{8,11},{9,10},{10,... | collective-permute-start | bytes 393224 | tf_op jit(solution)/shard_map/ppermute | solution.py:417
  9.9 1.1 %shard_map.84.refs_6_ = bf16[256,256]{1,0:T(8,128)(2,1)S(1)} custom-call(bf16[1024,32]{1,0:T(8,128)(2,1)S(1)} %get-tuple-element.27.refs_3_.refs_0_.refs_2_, bf16[32,2048]{1,0:T(8,128)(2,1)S(1)} %get-tuple-element.30.refs_1_.refs_3_, bf16[2048,256]{1,0:T(8,128)(2,1)S(1)} %get-tuple-element.31.refs_2_.refs_4_.refs_3_, f32[256,256]{1,0:T(8,128)S(1)} %get-tuple-element.33.refs_3_), custom_call_target="tpu_custom_call" | custom-call | tf_op jit(solution)/shard_map/pallas_call | solution.py:31
  11.0 2.1 %shard_map.85 = (bf16[8,256,2048]{2,1,0:T(8,128)(2,1)S(1)}, bf16[256,256]{1,0:T(8,128)(2,1)S(1)}) custom-call(bf16[1024,32]{1,0:T(8,128)(2,1)S(1)} %get-tuple-element.27.refs_3_.refs_0_.refs_2_, bf16[32,2048]{1,0:T(8,128)(2,1)S(1)} %get-tuple-element.28.refs_1_, ...), custom_call_target="tpu_custom_call", output_to_operand_aliasing={{0}: (5, {})} | custom-call | tf_op jit(solution)/shard_map/pallas_call | solution.py:31
  13.1 0.6 %collective-permute-start.4 = (bf16[2,128,256]{2,1,0:T(8,128)(2,1)S(1)}, bf16[2,128,256]{2,1,0:T(8,128)(2,1)S(1)}, u32[]{:S(2)}, u32[]{:S(2)}) collective-permute-start(bf16[2,128,256]{2,1,0:T(8,128)(2,1)S(1)} %bitcast.29), channel_id=1, source_target_pairs={{0,1},{1,0},{2,3},{3,2},{4,5},{5,4},{6,7},{7,6},{8,9},{9,8},{10,11... | collective-permute-start | bytes 393224 | tf_op jit(solution)/shard_map/ppermute | solution.py:417
  13.7 0.3 collective-permute-done.3.refs_6_.refs_3_
  14.0 2.1 %shard_map.86 = (bf16[8,256,2048]{2,1,0:T(8,128)(2,1)S(1)}, f32[256,256]{1,0:T(8,128)S(1)}) custom-call(bf16[1024,32]{1,0:T(8,128)(2,1)S(1)} %get-tuple-element.27.refs_3_.refs_0_.refs_2_, bf16[32,2048]{1,0:T(8,128)(2,1)S(1)} %get-tuple-element.28.refs_1_, ...), custom_call_target="tpu_custom_call", output_to_operand_aliasing={{0}: (5, {})} | custom-call | tf_op jit(solution)/shard_map/pallas_call | solution.py:31
  16.2 1.5 %shard_map.87.refs_4_.refs_2_ = bf16[8,256,2048]{2,1,0:T(8,128)(2,1)S(1)} custom-call(bf16[1024,32]{1,0:T(8,128)(2,1)S(1)} %get-tuple-element.27.refs_3_.refs_0_.refs_2_, bf16[32,2048]{1,0:T(8,128)(2,1)S(1)} %get-tuple-element.28.refs_1_, bf16[8,256,2048]{2,1,0:T(8,128)(2,1)S(1)} %get-tuple-element.38.refs_2_, ...), custom_call_target="tpu_custom_call", output_to_operand_aliasing={{}: (2, {})} | custom-call | tf_op jit(solution)/shard_map/pallas_call | solution.py:31
  17.7 1.1 %collective-permute-done.4.refs_1_ = bf16[2,128,256]{2,1,0:T(8,128)(2,1)S(1)} collective-permute-done((bf16[2,128,256]{2,1,0:T(8,128)(2,1)S(1)}, bf16[2,128,256]{2,1,0:T(8,128)(2,1)S(1)}, u32[]{:S(2)}, u32[]{:S(2)}) %collective-permute-start.4) | collective-permute-done | bytes 131104 | tf_op jit(solution)/shard_map/ppermute | solution.py:417
  18.8 0.2 collective-permute-done.5.refs_2_
  19.0 0.1 shard_map.88
  19.1 1.6 %collective-permute-start.6 = (bf16[2,128,256]{2,1,0:T(8,128)(2,1)S(1)}, bf16[2,128,256]{2,1,0:T(8,128)(2,1)S(1)}, u32[]{:S(2)}, u32[]{:S(2)}) collective-permute-start(bf16[2,128,256]{2,1,0:T(8,128)(2,1)S(1)} %get-tuple-element.40), channel_id=1, source_target_pairs={{0,4},{1,5},{2,6},{3,7},{4,0},{5,1},{6,2},{7,3},{8,12},{9,13},{10,... | collective-permute-start | bytes 393224 | tf_op jit(solution)/shard_map/ppermute | solution.py:511
  20.8 2.2 %shard_map.89 = (bf16[8,256,2048]{2,1,0:T(8,128)(2,1)S(1)}, bf16[2,128,256]{2,1,0:T(8,128)(2,1)S(1)}, bf16[2,128,256]{2,1,0:T(8,128)(2,1)S(1)}, bf16[129,128,128]{2,1,0:T(8,128)(2,1)S(1)}) custom-call(bf16[1024,32]{1,0:T(8,128)(2,1)S(1)} %get-tuple-element.27.refs_3_.refs_0_.refs_2_, ...), custom_call_target="tpu_custom_call", output_to_operand_aliasing={{0}: (2, {})} | custom-call | tf_op jit(solution)/shard_map/pallas_call | solution.py:31
  23.0 1.2 %collective-permute-done.6.refs_1_ = bf16[2,128,256]{2,1,0:T(8,128)(2,1)S(1)} collective-permute-done((bf16[2,128,256]{2,1,0:T(8,128)(2,1)S(1)}, bf16[2,128,256]{2,1,0:T(8,128)(2,1)S(1)}, u32[]{:S(2)}, u32[]{:S(2)}) %collective-permute-start.6) | collective-permute-done | bytes 131104 | tf_op jit(solution)/shard_map/ppermute | solution.py:511
  24.2 2.7 %collective-permute-start.7 = (bf16[2,128,256]{2,1,0:T(8,128)(2,1)S(1)}, bf16[2,128,256]{2,1,0:T(8,128)(2,1)S(1)}, u32[]{:S(2)}, u32[]{:S(2)}) collective-permute-start(bf16[2,128,256]{2,1,0:T(8,128)(2,1)S(1)} %get-tuple-element.44), channel_id=1, source_target_pairs={{0,8},{1,9},{2,10},{3,11},{4,12},{5,13},{6,14},{7,15},{8,0},{9,1},... | collective-permute-start | bytes 393224 | tf_op jit(solution)/shard_map/ppermute | solution.py:514
  26.8 0.7 %collective-permute-start.11 = (bf16[2,128,256]{2,1,0:T(8,128)(2,1)S(1)}, bf16[2,128,256]{2,1,0:T(8,128)(2,1)S(1)}, u32[]{:S(2)}, u32[]{:S(2)}) collective-permute-start(bf16[2,128,256]{2,1,0:T(8,128)(2,1)S(1)} %get-tuple-element.45), channel_id=1, source_target_pairs={{16,17},{17,18},{18,19},{19,20},{20,21},{21,22},{22,23},{23,24},{2... | collective-permute-start | bytes 393224 | tf_op jit(solution)/shard_map/ppermute | solution.py:503
  27.5 0.7 %collective-permute-start.12 = (bf16[2,128,256]{2,1,0:T(8,128)(2,1)S(1)}, bf16[2,128,256]{2,1,0:T(8,128)(2,1)S(1)}, u32[]{:S(2)}, u32[]{:S(2)}) collective-permute-start(bf16[2,128,256]{2,1,0:T(8,128)(2,1)S(1)} %get-tuple-element.46), channel_id=1, source_target_pairs={{17,16},{18,17},{19,18},{20,19},{21,20},{22,21},{23,22},{24,23},{2... | collective-permute-start | bytes 393224 | tf_op jit(solution)/shard_map/ppermute | solution.py:503
  28.2 3.3 %collective-permute-done.7.refs_1_ = bf16[2,128,256]{2,1,0:T(8,128)(2,1)S(1)} collective-permute-done((bf16[2,128,256]{2,1,0:T(8,128)(2,1)S(1)}, bf16[2,128,256]{2,1,0:T(8,128)(2,1)S(1)}, u32[]{:S(2)}, u32[]{:S(2)}) %collective-permute-start.7) | collective-permute-done | bytes 131104 | tf_op jit(solution)/shard_map/ppermute | solution.py:514
  31.5 0.2 shard_map.91.refs_0_.refs_8_
  31.8 1.6 %collective-permute-start.13 = (bf16[768,256]{1,0:T(8,128)(2,1)S(1)}, bf16[768,256]{1,0:T(8,128)(2,1)S(1)}, u32[]{:S(2)}, u32[]{:S(2)}) collective-permute-start(bf16[768,256]{1,0:T(8,128)(2,1)S(1)} %shard_map.92), channel_id=1, source_target_pairs={{0,16},{16,0},{1,17},{17,1},{2,18},{18,2},{3,19},{19,3},{4,20},{20... | collective-permute-start | bytes 1179656 | tf_op jit(solution)/shard_map/ppermute | solution.py:520
  33.4 4.3 %collective-permute-start.10 = (bf16[2,128,256]{2,1,0:T(8,128)(2,1)S(1)}, bf16[2,128,256]{2,1,0:T(8,128)(2,1)S(1)}, u32[]{:S(2)}, u32[]{:S(2)}) collective-permute-start(bf16[2,128,256]{2,1,0:T(8,128)(2,1)S(1)} %shard_map.91.refs_0_.refs_8_), channel_id=1, source_target_pairs={{0,3},{1,2},{2,1},{3,0},{4,7},{5,6},{6,5},{7,4},{8,11},{9,10},{10,... | collective-permute-start | bytes 393224 | tf_op jit(solution)/shard_map/ppermute | solution.py:518
  37.7 0.6 %collective-permute-start.8 = (bf16[2,128,256]{2,1,0:T(8,128)(2,1)S(1)}, bf16[2,128,256]{2,1,0:T(8,128)(2,1)S(1)}, u32[]{:S(2)}, u32[]{:S(2)}) collective-permute-start(bf16[2,128,256]{2,1,0:T(8,128)(2,1)S(1)} %shard_map.91.refs_0_.refs_8_), channel_id=1, source_target_pairs={{0,1},{1,0},{2,3},{3,2},{4,5},{5,4},{6,7},{7,6},{8,9},{9,8},{10,11... | collective-permute-start | bytes 393224 | tf_op jit(solution)/shard_map/ppermute | solution.py:518
  38.3 2.5 %shard_map.93.refs_5_.refs_3_ = f32[16,128,256]{2,1,0:T(8,128)S(1)} custom-call(s32[8,16]{1,0:T(8,128)S(1)} %bitcast.24, bf16[129,128,128]{2,1,0:T(8,128)(2,1)S(1)} %get-tuple-element.42.refs_3_.refs_5_.refs_1_, bf16[2048,256]{1,0:T(8,128)(2,1)S(1)} %get-tuple-element.26.refs_2_.refs_3_.refs_1_, ...), custom_call_target="tpu_custom_call" | custom-call | tf_op jit(solution)/shard_map/pallas_call | solution.py:31
  40.8 0.9 %collective-permute-done.10.refs_2_ = bf16[2,128,256]{2,1,0:T(8,128)(2,1)S(1)} collective-permute-done((bf16[2,128,256]{2,1,0:T(8,128)(2,1)S(1)}, bf16[2,128,256]{2,1,0:T(8,128)(2,1)S(1)}, u32[]{:S(2)}, u32[]{:S(2)}) %collective-permute-start.10) | collective-permute-done | bytes 131104 | tf_op jit(solution)/shard_map/ppermute | solution.py:518
  41.6 2.6 %collective-permute-done.9.refs_1_ = bf16[2,128,256]{2,1,0:T(8,128)(2,1)S(1)} collective-permute-done((bf16[2,128,256]{2,1,0:T(8,128)(2,1)S(1)}, bf16[2,128,256]{2,1,0:T(8,128)(2,1)S(1)}, u32[]{:S(2)}, u32[]{:S(2)}) %collective-permute-start.9) | collective-permute-done | bytes 131104 | tf_op jit(solution)/shard_map/ppermute | solution.py:518
  44.3 0.1 collective-permute-start.14
  44.4 1.3 %shard_map.94.refs_2_ = f32[256,2048]{1,0:T(8,128)S(1)} custom-call(bf16[256,256]{1,0:T(8,128)(2,1)S(1)} %bitcast.18, bf16[256,256]{1,0:T(8,128)(2,1)S(1)} %bitcast.23, bf16[256,256]{1,0:T(8,128)(2,1)S(1)} %bitcast.22, bf16[256,256]{1,0:T(8,128)(2,1)S(1)} %bitcast.21, bf16[8,256,2048]{2,1,0:T(8,128)(2,1)S(1)} %get-tuple-element.41.refs_2_.refs_4_.refs_9_.refs_6_, ...), custom_call_target="tpu_custom_call" | custom-call | tf_op jit(solution)/shard_map/pallas_call | solution.py:31
  45.7 0.4 collective-permute-done.14.refs_5_
  46.1 3.1 %shard_map.96 = bf16[16,128,256]{2,1,0:T(8,128)(2,1)} custom-call(s32[16]{0:T(128)S(1)} %bitcast.27, bf16[2048,256]{1,0:T(8,128)(2,1)S(1)} %get-tuple-element.26.refs_2_.refs_3_.refs_1_, f32[256,2048]{1,0:T(8,128)S(1)} %shard_map.94.refs_2_, f32[16,128,256]{2,1,0:T(8,128)S(1)} %shard_map.93.refs_5_.refs_3_, ...), custom_call_target="tpu_custom_call" | custom-call | tf_op jit(solution)/shard_map/pallas_call | solution.py:31
  (21 shorter events, 0.2 us)
Async XLA Ops:
  0.0 4.5 %collective-permute-start.1 = (bf16[16,128,256]{2,1,0:T(8,128)(2,1)}, bf16[16,128,256]{2,1,0:T(8,128)(2,1)S(1)}, u32[]{:S(2)}, u32[]{:S(2)}) collective-permute-start(bf16[16,128,256]{2,1,0:T(8,128)(2,1)} %bitcast.31), channel_id=1, source_target_pairs={{0,16},{16,0},{1,17},{17,1},{2,18},{18,2},{3,19},{19,3},{4,20},{20... | collective-permute-start | bytes 3145736 | tf_op jit(solution)/shard_map/ppermute | solution.py:392
  0.5 4.0 %collective-permute-start.2 = (f32[3,16,128]{2,1,0:T(8,128)}, f32[3,16,128]{2,1,0:T(8,128)S(1)}, u32[]{:S(2)}, u32[]{:S(2)}) collective-permute-start(f32[3,16,128]{2,1,0:T(8,128)} %bitcast.33), channel_id=1, source_target_pairs={{0,16},{16,0},{1,17},{17,1},{2,18},{18,2},{3,19},{19,3},{4,20},{20... | collective-permute-start | bytes 73736 | tf_op jit(solution)/shard_map/ppermute | solution.py:389
  0.5 3.9 %collective-permute-start = (s32[16]{0:T(128)}, s32[16]{0:T(128)S(1)}, u32[]{:S(2)}, u32[]{:S(2)}) collective-permute-start(s32[16]{0:T(128)} %bitcast.25), channel_id=1, source_target_pairs={{0,16},{16,0},{1,17},{17,1},{2,18},{18,2},{3,19},{19,3},{4,20},{20... | collective-permute-start | bytes 200 | tf_op jit(solution)/shard_map/ppermute | solution.py:391
  6.3 7.7 %collective-permute-start.3 = (bf16[2,128,256]{2,1,0:T(8,128)(2,1)S(1)}, bf16[2,128,256]{2,1,0:T(8,128)(2,1)S(1)}, u32[]{:S(2)}, u32[]{:S(2)}) collective-permute-start(bf16[2,128,256]{2,1,0:T(8,128)(2,1)S(1)} %bitcast.28), channel_id=1, source_target_pairs={{0,3},{1,2},{2,1},{3,0},{4,7},{5,6},{6,5},{7,4},{8,11},{9,10},{10,... | collective-permute-start | bytes 393224 | tf_op jit(solution)/shard_map/ppermute | solution.py:417
  13.1 5.7 %collective-permute-start.4 = (bf16[2,128,256]{2,1,0:T(8,128)(2,1)S(1)}, bf16[2,128,256]{2,1,0:T(8,128)(2,1)S(1)}, u32[]{:S(2)}, u32[]{:S(2)}) collective-permute-start(bf16[2,128,256]{2,1,0:T(8,128)(2,1)S(1)} %bitcast.29), channel_id=1, source_target_pairs={{0,1},{1,0},{2,3},{3,2},{4,5},{5,4},{6,7},{7,6},{8,9},{9,8},{10,11... | collective-permute-start | bytes 393224 | tf_op jit(solution)/shard_map/ppermute | solution.py:417
  13.7 5.4 %collective-permute-start.5 = (bf16[2,128,256]{2,1,0:T(8,128)(2,1)S(1)}, bf16[2,128,256]{2,1,0:T(8,128)(2,1)S(1)}, u32[]{:S(2)}, u32[]{:S(2)}) collective-permute-start(bf16[2,128,256]{2,1,0:T(8,128)(2,1)S(1)} %bitcast.20), channel_id=1, source_target_pairs={{0,2},{1,3},{2,0},{3,1},{4,6},{5,7},{6,4},{7,5},{8,10},{9,11},{10,... | collective-permute-start | bytes 393224 | tf_op jit(solution)/shard_map/ppermute | solution.py:417
  19.1 5.0 %collective-permute-start.6 = (bf16[2,128,256]{2,1,0:T(8,128)(2,1)S(1)}, bf16[2,128,256]{2,1,0:T(8,128)(2,1)S(1)}, u32[]{:S(2)}, u32[]{:S(2)}) collective-permute-start(bf16[2,128,256]{2,1,0:T(8,128)(2,1)S(1)} %get-tuple-element.40), channel_id=1, source_target_pairs={{0,4},{1,5},{2,6},{3,7},{4,0},{5,1},{6,2},{7,3},{8,12},{9,13},{10,... | collective-permute-start | bytes 393224 | tf_op jit(solution)/shard_map/ppermute | solution.py:511
  23.0 8.6 %copy-start = (bf16[256,256]{1,0:T(8,128)(2,1)S(1)}, bf16[256,256]{1,0:T(8,128)(2,1)}, u32[]{:S(2)}) copy-start(bf16[256,256]{1,0:T(8,128)(2,1)} %refs_3_.1) | copy-start | bytes 393220
  24.2 7.3 %collective-permute-start.7 = (bf16[2,128,256]{2,1,0:T(8,128)(2,1)S(1)}, bf16[2,128,256]{2,1,0:T(8,128)(2,1)S(1)}, u32[]{:S(2)}, u32[]{:S(2)}) collective-permute-start(bf16[2,128,256]{2,1,0:T(8,128)(2,1)S(1)} %get-tuple-element.44), channel_id=1, source_target_pairs={{0,8},{1,9},{2,10},{3,11},{4,12},{5,13},{6,14},{7,15},{8,0},{9,1},... | collective-permute-start | bytes 393224 | tf_op jit(solution)/shard_map/ppermute | solution.py:514
  26.8 4.9 %collective-permute-start.11 = (bf16[2,128,256]{2,1,0:T(8,128)(2,1)S(1)}, bf16[2,128,256]{2,1,0:T(8,128)(2,1)S(1)}, u32[]{:S(2)}, u32[]{:S(2)}) collective-permute-start(bf16[2,128,256]{2,1,0:T(8,128)(2,1)S(1)} %get-tuple-element.45), channel_id=1, source_target_pairs={{16,17},{17,18},{18,19},{19,20},{20,21},{21,22},{22,23},{23,24},{2... | collective-permute-start | bytes 393224 | tf_op jit(solution)/shard_map/ppermute | solution.py:503
  27.5 4.2 %collective-permute-start.12 = (bf16[2,128,256]{2,1,0:T(8,128)(2,1)S(1)}, bf16[2,128,256]{2,1,0:T(8,128)(2,1)S(1)}, u32[]{:S(2)}, u32[]{:S(2)}) collective-permute-start(bf16[2,128,256]{2,1,0:T(8,128)(2,1)S(1)} %get-tuple-element.46), channel_id=1, source_target_pairs={{17,16},{18,17},{19,18},{20,19},{21,20},{22,21},{23,22},{24,23},{2... | collective-permute-start | bytes 393224 | tf_op jit(solution)/shard_map/ppermute | solution.py:503
  31.5 6.8 %copy-start.1 = (bf16[256,256]{1,0:T(8,128)(2,1)S(1)}, bf16[256,256]{1,0:T(8,128)(2,1)}, u32[]{:S(2)}) copy-start(bf16[256,256]{1,0:T(8,128)(2,1)} %refs_7_.1) | copy-start | bytes 393220
  31.5 6.8 %copy-start.2 = (s32[1,16,8]{1,2,0:T(8,128)S(1)}, s32[1,16,8]{1,2,0:T(8,128)}, u32[]{:S(2)}) copy-start(s32[1,16,8]{1,2,0:T(8,128)} %param.11) | copy-start | bytes 1540
  31.8 6.5 %collective-permute-start.13 = (bf16[768,256]{1,0:T(8,128)(2,1)S(1)}, bf16[768,256]{1,0:T(8,128)(2,1)S(1)}, u32[]{:S(2)}, u32[]{:S(2)}) collective-permute-start(bf16[768,256]{1,0:T(8,128)(2,1)S(1)} %shard_map.92), channel_id=1, source_target_pairs={{0,16},{16,0},{1,17},{17,1},{2,18},{18,2},{3,19},{19,3},{4,20},{20... | collective-permute-start | bytes 1179656 | tf_op jit(solution)/shard_map/ppermute | solution.py:520
  33.4 8.2 %collective-permute-start.10 = (bf16[2,128,256]{2,1,0:T(8,128)(2,1)S(1)}, bf16[2,128,256]{2,1,0:T(8,128)(2,1)S(1)}, u32[]{:S(2)}, u32[]{:S(2)}) collective-permute-start(bf16[2,128,256]{2,1,0:T(8,128)(2,1)S(1)} %shard_map.91.refs_0_.refs_8_), channel_id=1, source_target_pairs={{0,3},{1,2},{2,1},{3,0},{4,7},{5,6},{6,5},{7,4},{8,11},{9,10},{10,... | collective-permute-start | bytes 393224 | tf_op jit(solution)/shard_map/ppermute | solution.py:518
  37.7 6.5 %collective-permute-start.9 = (bf16[2,128,256]{2,1,0:T(8,128)(2,1)S(1)}, bf16[2,128,256]{2,1,0:T(8,128)(2,1)S(1)}, u32[]{:S(2)}, u32[]{:S(2)}) collective-permute-start(bf16[2,128,256]{2,1,0:T(8,128)(2,1)S(1)} %shard_map.91.refs_0_.refs_8_), channel_id=1, source_target_pairs={{0,2},{1,3},{2,0},{3,1},{4,6},{5,7},{6,4},{7,5},{8,10},{9,11},{10,... | collective-permute-start | bytes 393224 | tf_op jit(solution)/shard_map/ppermute | solution.py:518
  37.7 6.5 %collective-permute-start.8 = (bf16[2,128,256]{2,1,0:T(8,128)(2,1)S(1)}, bf16[2,128,256]{2,1,0:T(8,128)(2,1)S(1)}, u32[]{:S(2)}, u32[]{:S(2)}) collective-permute-start(bf16[2,128,256]{2,1,0:T(8,128)(2,1)S(1)} %shard_map.91.refs_0_.refs_8_), channel_id=1, source_target_pairs={{0,1},{1,0},{2,3},{3,2},{4,5},{5,4},{6,7},{7,6},{8,9},{9,8},{10,11... | collective-permute-start | bytes 393224 | tf_op jit(solution)/shard_map/ppermute | solution.py:518
  40.8 5.3 %copy-start.3 = (s32[1,16]{1,0:T(1,128)S(1)}, s32[1,16]{1,0:T(1,128)}, u32[]{:S(2)}) copy-start(s32[1,16]{1,0:T(1,128)} %param.12) | copy-start | bytes 196
  44.3 1.8 %collective-permute-start.14 = (bf16[768,256]{1,0:T(8,128)(2,1)S(1)}, bf16[768,256]{1,0:T(8,128)(2,1)S(1)}, u32[]{:S(2)}, u32[]{:S(2)}) collective-permute-start(bf16[768,256]{1,0:T(8,128)(2,1)S(1)} %shard_map.95), channel_id=1, source_target_pairs={{0,16},{16,0},{1,17},{17,1},{2,18},{18,2},{3,19},{19,3},{4,20},{20... | collective-permute-start | bytes 1179656 | tf_op jit(solution)/shard_map/ppermute | solution.py:530

commit v7 on v6

--- a/solution.py
+++ b/solution.py
@@ -15,13 +15,11 @@
 HBM = pl.BlockSpec(memory_space=pltpu.HBM)
 PARAMS = pltpu.CompilerParams(vmem_limit_bytes=14 * 1024 * 1024)
 LANES = 128
-COST = 0
-WEIGHT = 0
 SIN = (4.44287957, -7.30781668, 3.59777418, -0.79119939)
 COS = (1.41420401, -6.97763732, 5.71518787, -1.72821389)
 
 
-def call(kernel, outs, operands, scratch=(), held=(), flops=0, same=()):
+def call(kernel, outs, operands, scratch=(), held=(), same=()):
     ahead = len(operands)
     operands = list(operands) + [(VMEM, array) for array in held]
 
@@ -36,7 +34,7 @@
         scratch_shapes=list(scratch),
         input_output_aliases=dict(same),
         compiler_params=PARAMS,
-        cost_estimate=pl.CostEstimate(flops=flops, bytes_accessed=flops // 300, transcendentals=0),
+        cost_estimate=pl.CostEstimate(flops=0, bytes_accessed=0, transcendentals=0),
     )(
         *[
             array if place is SMEM else pltpu.with_memory_space_constraint(array, place.memory_space)
@@ -204,54 +202,72 @@
         finish(copies)
 
 
-def short_kernel(lines, codes_ref, radial_ref, *refs):
-    line_refs, refs = refs[:lines], refs[lines:]
-    outer, (handed_ref, w_ref, message_ref, found_ref) = refs[:-4], refs[-4:]
-    cells, slots, channels = message_ref.shape
-    pairs = codes_ref.shape[0]
-    slab, slabs = lax.axis_index("grp"), lax.axis_size("grp")
-
-    def outer_cell(line, side):
-        if slabs == 2:
-            start = handed_ref.shape[0] - (4 - 2 * side - (1 - line)) * slots
-            return jnp.where(slab == 1, outer[side][line], handed_ref[start : start + slots, :])
-        return outer[side][line]
-
-    nothing = cells * pairs
+def fill_found(codes_ref, found_ref):
+    pairs, cells = codes_ref.shape
     for cell in range(cells):
         for code in range(9):
-            found_ref[9 * cell + code] = nothing
+            found_ref[9 * cell + code] = cells * pairs
         for pair in range(pairs):
             found_ref[9 * cell + codes_ref[pair, cell]] = cell * pairs + pair
+
+
+def window_sum(start, radial_ref, found_ref, lines, takers):
+    slab, slabs = lax.axis_index("grp"), lax.axis_size("grp")
+    nothing = radial_ref.shape[0] - 1
     levels = [1, 2 - 2 * slab] if slabs == 2 else [1, 0, 2]
+    total = None
+    for level, taken in zip(levels, lines):
+        rows = []
+        for cell in takers:
+            halves = []
+            for place in (start, start + 1):
+                along = place - cell
+                index = found_ref[9 * cell + 3 * level + along] if 0 <= along < 3 else nothing
+                halves.append(radial_ref[index])
+            rows.append(jnp.concatenate(halves, axis=1))
+        part = jnp.dot(jnp.concatenate(rows, axis=0), taken, preferred_element_type=F32)
+        total = part if total is None else total + part
+    return total
+
+
+def short_kernel(lines, codes_ref, radial_ref, *refs):
+    line_refs, (w_ref, message_ref, found_ref) = refs[:lines], refs[lines:]
+    cells, slots, channels = message_ref.shape
+    fill_found(codes_ref, found_ref)
     carried = None
-    for start in range(0, cells + 2, 2):
-        takers = [cell for cell in range(start - 2, start + 2) if 0 <= cell < cells]
-        total = None
-        for line, level in enumerate(levels):
-            rows = []
-            for cell in takers:
-                halves = []
-                for place in (start, start + 1):
-                    along = place - cell
-                    index = found_ref[9 * cell + 3 * level + along] if 0 <= along < 3 else nothing
-                    halves.append(radial_ref[index])
-                rows.append(jnp.concatenate(halves, axis=1))
-            span = slice(max(start - 1, 0) * slots, min(start + 1, cells) * slots)
-            taken = [line_refs[line][span, :]]
-            if start == 0:
-                taken = [outer_cell(line, 0)] + taken
-            if start == cells:
-                taken = taken + [outer_cell(line, 1)]
-            taken = jnp.concatenate(taken, axis=0)
-            part = jnp.dot(jnp.concatenate(rows, axis=0), taken, preferred_element_type=F32)
-            total = part if total is None else total + part
-        if start:
-            gathered = (carried + total[: 2 * slots]).astype(BF16)
-            message = jnp.dot(gathered, w_ref[...], preferred_element_type=F32)
-            message_ref[start - 2 : start] = message.reshape(2, slots, channels)
-            total = total[2 * slots :]
-        carried = total
+    for start in range(2, cells, 2):
+        taken = [line_ref[(start - 1) * slots : (start + 1) * slots, :] for line_ref in line_refs]
+        total = window_sum(start, radial_ref, found_ref, taken, range(start - 2, start + 2))
+        gathered = total[: 2 * slots]
+        if start > 2:
+            gathered = carried + gathered
+            gathered = jnp.dot(gathered.astype(BF16), w_ref[...], preferred_element_type=F32)
+        message_ref[start - 2 : start] = gathered.reshape(2, slots, channels)
+        carried = total[2 * slots :]
+    message_ref[cells - 2 : cells] = carried.reshape(2, slots, channels)
+
+
+def fill_ends(slots, codes_ref, radial_ref, line_refs, outer, handed_ref, base, w_ref, found_ref, ends_ref):
+    slab, slabs = lax.axis_index("grp"), lax.axis_size("grp")
+    cells = codes_ref.shape[1]
+    fill_found(codes_ref, found_ref)
+    for side, start in enumerate((0, cells)):
+        taken = []
+        for line, line_ref in enumerate(line_refs):
+            cell = outer[side][line]
+            if slabs == 2:
+                first = base + (2 * side + 1 - line) * slots
+                cell = jnp.where(slab == 1, cell, handed_ref[first : first + slots, :])
+            if side == 0:
+                taken.append(jnp.concatenate([cell, line_ref[:slots, :]], axis=0))
+            else:
+                taken.append(jnp.concatenate([line_ref[(cells - 1) * slots :, :], cell], axis=0))
+        takers = (0, 1) if side == 0 else (cells - 2, cells - 1)
+        total = window_sum(start, radial_ref, found_ref, taken, takers)
+        span = slice(2 * side, 2 * side + 2)
+        gathered = ends_ref[span].reshape(total.shape) + total
+        message = jnp.dot(gathered.astype(BF16), w_ref[...], preferred_element_type=F32)
+        ends_ref[span] = message.reshape(2, slots, total.shape[1])
 
 
 def add_kernel(*refs):
@@ -295,7 +311,6 @@
         [(VMEM, (pieces[0].shape, BF16))],
         in_vmem([*pieces, turned, w_mix]),
         held=held,
-        flops=WEIGHT * 10**9,
     )
     return energy
 
@@ -329,15 +344,19 @@
         out_ref[:, start : start + tile] = total
 
 
-def final_kernel(
-    blocks, scale, counts_ref, masked_ref, near_ref, message_ref, energy_ref, rest_ref, table_ref, out_ref, turned_ref,
-    result_ref, semaphores,
-):
+def final_kernel(blocks, lines, scale, counts_ref, codes_ref, near_ref, message_ref, handed_ref, table_ref, *refs):
+    radial_ref, line_refs, outer, w_ref = refs[0], refs[1 : 1 + lines], refs[1 + lines : 3 + lines], refs[3 + lines]
+    out_ref, turned_ref, result_ref, found_ref, ends_ref, semaphores = refs[4 + lines :]
+    masked_ref = line_refs[0]
     cells, slots, channels = out_ref.shape
     rows = table_ref.shape[1]
-    turned_ref[0] = energy_ref[:rows, :].astype(F32).T.astype(BF16)
-    for place in range(1, blocks):
-        turned_ref[place] = rest_ref[(place - 1) * rows : place * rows, :].astype(F32).T.astype(BF16)
+    for place in range(blocks):
+        turned_ref[place] = handed_ref[place * rows : (place + 1) * rows, :].astype(F32).T.astype(BF16)
+    ends_ref[:2] = message_ref[:2]
+    ends_ref[2:] = message_ref[cells - 2 :]
+    fill_ends(
+        slots, codes_ref, radial_ref, line_refs, outer, handed_ref, blocks * rows, w_ref, found_ref, ends_ref
+    )
     slot_ids = lax.broadcasted_iota(jnp.int32, (slots, channels), 0)
     group = math.gcd(cells, 2)
     share = math.gcd(cells, 4)
@@ -348,7 +367,8 @@
         for place in range(blocks):
             total = total + jnp.dot(turned_ref[place], table_ref[blocks + place, :, span], preferred_element_type=F32)
         for cell in range(first, first + group):
-            value = total[:, (cell - first) * slots : (cell - first + 1) * slots].T * scale + message_ref[cell]
+            value = total[:, (cell - first) * slots : (cell - first + 1) * slots].T * scale
+            value += ends_ref[cell] if cell < 2 else ends_ref[cell - cells + 4] if cell >= cells - 2 else message_ref[cell]
             value = value * (0.5 + 0.5 * jnp.tanh(0.5 * value))
             result = masked_ref[cell * slots : (cell + 1) * slots, :].astype(F32) + value
             result_ref[cell] = jnp.where(slot_ids < counts_ref[cell], result, 0.0).astype(BF16)
@@ -358,16 +378,18 @@
     finish(leaving)
 
 
-def final_call(counts, near, message, masked, energy, rest, table, scale):
+def final_call(counts, codes, near, message, handed, table, radial, lines, outer, w_msg, scale):
     blocks, rows = table.shape[0] // 2, table.shape[1]
     cells, slots, channels = message.shape
     (result,) = call(
-        functools.partial(final_kernel, blocks, scale),
+        functools.partial(final_kernel, blocks, len(lines), scale),
         [(HBM, (message.shape, BF16))],
-        [(SMEM, counts)] + in_vmem([masked, near, message, energy, rest, table]),
+        [(SMEM, counts), (SMEM, codes)] + in_vmem([near, message, handed, table, radial, *lines, *outer, w_msg]),
         [
             pltpu.VMEM((blocks, channels, rows), BF16),
             pltpu.VMEM(message.shape, BF16),
+            pltpu.SMEM((9 * cells,), jnp.int32),
+            pltpu.VMEM((4, slots, channels), F32),
             pltpu.SemaphoreType.DMA((cells // math.gcd(cells, 4),)),
         ],
     )
@@ -411,7 +433,6 @@
     rows_type = ((atoms, channels), BF16)
     whole_table = (VMEM, ((2 * blocks,) + table[0], BF16))
     scratch = [pltpu.VMEM(*table)]
-    block_flops = 2 * 2 * block * atoms * channels * COST
 
     def sent(part, place):
         return lax.ppermute(part.reshape(2, block, channels), "dev", pairs_at("dev", 1, place))
@@ -446,7 +467,6 @@
             [(VMEM, piece)],
             in_vmem([turned, sibling_places, sibling, started[place]]),
             scratch,
-            flops=block_flops,
         )
         received[place] = sent(part, place)
     for place in order[len(early) :]:
@@ -456,8 +476,7 @@
             in_vmem([turned, places, masked, sibling_places, sibling, tables]),
             scratch,
             [part] if place else [received[early[0]]],
-            2 * block_flops,
-            {5: 0},
+            same={5: 0},
         )
         if place:
             received[place] = sent(part, place)
@@ -474,14 +493,13 @@
         ]
     edge = (VMEM, ((len(lines), slots, channels), BF16))
 
-    def rest_of(tables, first, last, held, more=(), outs=(), scratch=(), weight=0):
+    def rest_of(tables, first, last, held, more=(), outs=(), scratch=()):
         return call(
             functools.partial(rest_kernel, range(first, last), block, len(more[:-1])),
             [whole_table, *outs],
             in_vmem([turned, places, tables, *more[:-1]]) + in_hbm(more[-1:]),
             scratch,
             held,
-            weight,
             {2: 0},
         )
 
@@ -517,17 +535,16 @@
     energies = [energy] + [
         lax.ppermute(energy, "dev", pairs_at("dev", 1, place)) for place in range(1, blocks)
     ]
-    handed = lax.ppermute(stacked([energy, *(outer if slabs == 2 else [])], [radial]), "grp", swap)
-
+
+    codes = neighbours[0].T
     (message,) = call(
         functools.partial(short_kernel, len(lines)),
         [(VMEM, ((cells, slots, channels), F32))],
-        [(SMEM, neighbours[0].T)] + in_vmem([radial, *lines, *outer, handed, w_msg]),
+        [(SMEM, codes)] + in_vmem([radial, *lines, w_msg]),
         [pltpu.SMEM((9 * cells,), jnp.int32)],
         [energy, tables],
-        6 * block_flops,
-    )
-    rest = lax.ppermute(stacked(energies[1:], [message]), "grp", swap)
+    )
+    handed = lax.ppermute(stacked([*energies, *(outer if slabs == 2 else [])], [message]), "grp", swap)
     energies = [part.reshape(2 * block, channels) for part in energies]
     (near_sum,) = call(
         functools.partial(near_kernel, blocks),
@@ -535,10 +552,9 @@
         in_vmem([*energies, tables]),
         [pltpu.VMEM((blocks, channels, 2 * block), BF16)],
         [message],
-        2 * block_flops,
     )
     scale = 8.0 / math.sqrt(wave_count)
-    result = final_call(counts, near_sum, message, masked, handed, rest, tables, scale)
+    result = final_call(counts, codes, near_sum, message, handed, tables, radial, lines, outer, w_msg, scale)
     return result[None]
 
 

time: 49.6 us -> 46.5 us (0.938)
  starting transfers between devices: 17.3 us -> 14.4 us
    ppermute x2 -> x1, starting transfers between devices: 1.73 us -> 0.07 us  [body(): lax.ppermute(stacked([*energies, *(outer if slabs == 2 else [])], [messag...]
    ppermute x3, starting transfers between devices: 4.86 us -> 3.55 us  [body(): lax.ppermute(energy, 'dev', pairs_at('dev', 1, place))]
    ppermute x3, waiting for transfers between devices: 3.49 us -> 2.45 us  [body(): lax.ppermute(energy, 'dev', pairs_at('dev', 1, place))]
    ppermute x2 -> x1, waiting for transfers between devices: 0.39 us -> 0.94 us  [body(): lax.ppermute(stacked([*energies, *(outer if slabs == 2 else [])], [messag...]
    pallas_call x15 -> x14, Pallas kernels: 21.6 us -> 21.9 us  [call(): pl.pallas_call(without_held, in_specs=[place for place, _ in operands], o...]
  transfers between devices with their start and end apart: 15 -> 14, of which waited for: 8 -> 8; matrix products, arithmetic and copies ran while one was open for 0% -> 0% of each run, Pallas kernels for 34% -> 35%
where the time goes in v7:
time: 46.5 us; the launch traced here: 46.2 us
  Pallas kernels  21.9 us (47%)
  starting transfers between devices  14.4 us (31%)
  waiting for transfers between devices  9.51 us (20%)
    pallas_call x14, Pallas kernels, call(): pl.pallas_call(without_held, in_specs=[place for place, _ in operands], o...  21.9 us
    ppermute x3, starting transfers between devices, sent(): lax.ppermute(part.reshape(2, block, channels), 'dev', pairs_at('dev', 1,...  4.17 us
    ppermute x3, starting transfers between devices, body(): lax.ppermute(energy, 'dev', pairs_at('dev', 1, place))  3.55 us
    ppermute x1, waiting for transfers between devices, body(): pieces = [total, lax.ppermute(half_total, axis, pairs_at(axis, stride, 1))]  3.34 us
    ppermute x1, starting transfers between devices, body(): pieces = [total, lax.ppermute(half_total, axis, pairs_at(axis, stride, 1))]  2.66 us
    ppermute x3, waiting for transfers between devices, body(): lax.ppermute(energy, 'dev', pairs_at('dev', 1, place))  2.45 us
    ppermute x1, starting transfers between devices, body(): lax.ppermute(half_total, axis, pairs_at(axis, stride, 1))  1.65 us
    ppermute x3, waiting for transfers between devices, sent(): lax.ppermute(part.reshape(2, block, channels), 'dev', pairs_at('dev', 1,...  1.61 us
  transfers between devices with their start and end apart: 14, of which 8 were waited for; matrix products, arithmetic and copies ran while one was open for 0% of the time, Pallas kernels for 35%

profile of v7, /device:TPU:0, one launch (start us, length us, event | category | flops | bytes accessed | tf_op | source)
XLA Modules:
  0.0 46.2 jit_solution(3198472958921244273)
XLA Ops:
  0.0 0.5 collective-permute-start.1
  0.5 0.5 collective-permute-start
  1.0 3.5 %shard_map.82 = (bf16[2048,256]{1,0:T(8,128)(2,1)S(1)}, bf16[32,2048]{1,0:T(8,128)(2,1)S(1)}, bf16[1024,32]{1,0:T(8,128)(2,1)S(1)}, bf16[8,256,2048]{2,1,0:T(8,1...) custom-call(s32[3,1024]{1,0:T(4,128)} %refs_0_.1, f32[3,16,128]{2,1,0:T(8,128)} %bitcast.35, s32[16]{0:T(128)} %bitcast.27, ...), custom_call_target="tpu_custom_call" | custom-call | tf_op jit(solution)/shard_map/pallas_call | solution.py:29
  4.5 1.9 %shard_map.83 = (bf16[2048,256]{1,0:T(8,128)(2,1)S(1)}, bf16[32,2048]{1,0:T(8,128)(2,1)S(1)}, bf16[256,256]{1,0:T(8,128)(2,1)S(1)}) custom-call(s32[16]{0:T(128)S(1)} %collective-permute-done.refs_0_, bf16[16,128,256]{2,1,0:T(8,128)(2,1)S(1)} %collective-permute-done.1.refs_1_, f32[3,16,128]{2,1,0:T(8,128)S(1)} %collective-permute-done.2.refs_2_, ...), custom_call_target="tpu_custom_call" | custom-call | tf_op jit(solution)/shard_map/pallas_call | solution.py:29
  6.3 3.5 %collective-permute-start.3 = (bf16[2,128,256]{2,1,0:T(8,128)(2,1)S(1)}, bf16[2,128,256]{2,1,0:T(8,128)(2,1)S(1)}, u32[]{:S(2)}, u32[]{:S(2)}) collective-permute-start(bf16[2,128,256]{2,1,0:T(8,128)(2,1)S(1)} %bitcast.29), channel_id=1, source_target_pairs={{0,3},{1,2},{2,1},{3,0},{4,7},{5,6},{6,5},{7,4},{8,11},{9,10},{10,... | collective-permute-start | bytes 393224 | tf_op jit(solution)/shard_map/ppermute | solution.py:438
  9.9 1.1 %shard_map.84.refs_6_ = bf16[256,256]{1,0:T(8,128)(2,1)S(1)} custom-call(bf16[1024,32]{1,0:T(8,128)(2,1)S(1)} %get-tuple-element.26.refs_3_.refs_0_.refs_2_, bf16[32,2048]{1,0:T(8,128)(2,1)S(1)} %get-tuple-element.30.refs_1_.refs_3_, bf16[2048,256]{1,0:T(8,128)(2,1)S(1)} %get-tuple-element.31.refs_2_.refs_4_.refs_3_.refs_8_, ...), custom_call_target="tpu_custom_call" | custom-call | tf_op jit(solution)/shard_map/pallas_call | solution.py:29
  11.0 2.1 %shard_map.85 = (bf16[8,256,2048]{2,1,0:T(8,128)(2,1)S(1)}, bf16[256,256]{1,0:T(8,128)(2,1)S(1)}) custom-call(bf16[1024,32]{1,0:T(8,128)(2,1)S(1)} %get-tuple-element.26.refs_3_.refs_0_.refs_2_, bf16[32,2048]{1,0:T(8,128)(2,1)S(1)} %get-tuple-element.27.refs_1_, ...), custom_call_target="tpu_custom_call", output_to_operand_aliasing={{0}: (5, {})} | custom-call | tf_op jit(solution)/shard_map/pallas_call | solution.py:29
  13.1 0.6 %collective-permute-start.4 = (bf16[2,128,256]{2,1,0:T(8,128)(2,1)S(1)}, bf16[2,128,256]{2,1,0:T(8,128)(2,1)S(1)}, u32[]{:S(2)}, u32[]{:S(2)}) collective-permute-start(bf16[2,128,256]{2,1,0:T(8,128)(2,1)S(1)} %bitcast.30), channel_id=1, source_target_pairs={{0,1},{1,0},{2,3},{3,2},{4,5},{5,4},{6,7},{7,6},{8,9},{9,8},{10,11... | collective-permute-start | bytes 393224 | tf_op jit(solution)/shard_map/ppermute | solution.py:438
  13.8 0.3 collective-permute-done.3.refs_6_.refs_3_
  14.0 2.1 %shard_map.86 = (bf16[8,256,2048]{2,1,0:T(8,128)(2,1)S(1)}, f32[256,256]{1,0:T(8,128)S(1)}) custom-call(bf16[1024,32]{1,0:T(8,128)(2,1)S(1)} %get-tuple-element.26.refs_3_.refs_0_.refs_2_, bf16[32,2048]{1,0:T(8,128)(2,1)S(1)} %get-tuple-element.27.refs_1_, ...), custom_call_target="tpu_custom_call", output_to_operand_aliasing={{0}: (5, {})} | custom-call | tf_op jit(solution)/shard_map/pallas_call | solution.py:29
  16.2 1.5 %shard_map.87.refs_4_.refs_2_ = bf16[8,256,2048]{2,1,0:T(8,128)(2,1)S(1)} custom-call(bf16[1024,32]{1,0:T(8,128)(2,1)S(1)} %get-tuple-element.26.refs_3_.refs_0_.refs_2_, bf16[32,2048]{1,0:T(8,128)(2,1)S(1)} %get-tuple-element.27.refs_1_, bf16[8,256,2048]{2,1,0:T(8,128)(2,1)S(1)} %get-tuple-element.38.refs_2_, ...), custom_call_target="tpu_custom_call", output_to_operand_aliasing={{}: (2, {})} | custom-call | tf_op jit(solution)/shard_map/pallas_call | solution.py:29
  17.7 1.1 %collective-permute-done.4.refs_1_ = bf16[2,128,256]{2,1,0:T(8,128)(2,1)S(1)} collective-permute-done((bf16[2,128,256]{2,1,0:T(8,128)(2,1)S(1)}, bf16[2,128,256]{2,1,0:T(8,128)(2,1)S(1)}, u32[]{:S(2)}, u32[]{:S(2)}) %collective-permute-start.4) | collective-permute-done | bytes 131104 | tf_op jit(solution)/shard_map/ppermute | solution.py:438
  18.8 0.2 collective-permute-done.5.refs_2_
  19.0 0.1 shard_map.88
  19.1 1.6 %collective-permute-start.6 = (bf16[2,128,256]{2,1,0:T(8,128)(2,1)S(1)}, bf16[2,128,256]{2,1,0:T(8,128)(2,1)S(1)}, u32[]{:S(2)}, u32[]{:S(2)}) collective-permute-start(bf16[2,128,256]{2,1,0:T(8,128)(2,1)S(1)} %get-tuple-element.40), channel_id=1, source_target_pairs={{0,4},{1,5},{2,6},{3,7},{4,0},{5,1},{6,2},{7,3},{8,12},{9,13},{10,... | collective-permute-start | bytes 393224 | tf_op jit(solution)/shard_map/ppermute | solution.py:529
  20.8 2.2 %shard_map.89 = (bf16[8,256,2048]{2,1,0:T(8,128)(2,1)S(1)}, bf16[2,128,256]{2,1,0:T(8,128)(2,1)S(1)}, bf16[2,128,256]{2,1,0:T(8,128)(2,1)S(1)}, bf16[129,128,128]{2,1,0:T(8,128)(2,1)S(1)}) custom-call(bf16[1024,32]{1,0:T(8,128)(2,1)S(1)} %get-tuple-element.26.refs_3_.refs_0_.refs_2_, ...), custom_call_target="tpu_custom_call", output_to_operand_aliasing={{0}: (2, {})} | custom-call | tf_op jit(solution)/shard_map/pallas_call | solution.py:29
  23.0 1.2 %collective-permute-done.6.refs_1_ = bf16[2,128,256]{2,1,0:T(8,128)(2,1)S(1)} collective-permute-done((bf16[2,128,256]{2,1,0:T(8,128)(2,1)S(1)}, bf16[2,128,256]{2,1,0:T(8,128)(2,1)S(1)}, u32[]{:S(2)}, u32[]{:S(2)}) %collective-permute-start.6) | collective-permute-done | bytes 131104 | tf_op jit(solution)/shard_map/ppermute | solution.py:529
  24.2 2.7 %collective-permute-start.7 = (bf16[2,128,256]{2,1,0:T(8,128)(2,1)S(1)}, bf16[2,128,256]{2,1,0:T(8,128)(2,1)S(1)}, u32[]{:S(2)}, u32[]{:S(2)}) collective-permute-start(bf16[2,128,256]{2,1,0:T(8,128)(2,1)S(1)} %get-tuple-element.44), channel_id=1, source_target_pairs={{0,8},{1,9},{2,10},{3,11},{4,12},{5,13},{6,14},{7,15},{8,0},{9,1},... | collective-permute-start | bytes 393224 | tf_op jit(solution)/shard_map/ppermute | solution.py:532
  26.9 0.7 %collective-permute-start.11 = (bf16[2,128,256]{2,1,0:T(8,128)(2,1)S(1)}, bf16[2,128,256]{2,1,0:T(8,128)(2,1)S(1)}, u32[]{:S(2)}, u32[]{:S(2)}) collective-permute-start(bf16[2,128,256]{2,1,0:T(8,128)(2,1)S(1)} %get-tuple-element.45), channel_id=1, source_target_pairs={{16,17},{17,18},{18,19},{19,20},{20,21},{21,22},{22,23},{23,24},{2... | collective-permute-start | bytes 393224 | tf_op jit(solution)/shard_map/ppermute | solution.py:521
  27.5 0.7 %collective-permute-start.12 = (bf16[2,128,256]{2,1,0:T(8,128)(2,1)S(1)}, bf16[2,128,256]{2,1,0:T(8,128)(2,1)S(1)}, u32[]{:S(2)}, u32[]{:S(2)}) collective-permute-start(bf16[2,128,256]{2,1,0:T(8,128)(2,1)S(1)} %get-tuple-element.46), channel_id=1, source_target_pairs={{17,16},{18,17},{19,18},{20,19},{21,20},{22,21},{23,22},{24,23},{2... | collective-permute-start | bytes 393224 | tf_op jit(solution)/shard_map/ppermute | solution.py:521
  28.2 3.3 %collective-permute-done.7.refs_1_ = bf16[2,128,256]{2,1,0:T(8,128)(2,1)S(1)} collective-permute-done((bf16[2,128,256]{2,1,0:T(8,128)(2,1)S(1)}, bf16[2,128,256]{2,1,0:T(8,128)(2,1)S(1)}, u32[]{:S(2)}, u32[]{:S(2)}) %collective-permute-start.7) | collective-permute-done | bytes 131104 | tf_op jit(solution)/shard_map/ppermute | solution.py:532
  31.5 0.2 shard_map.91.refs_5_.refs_0_
  31.8 1.9 %collective-permute-start.10 = (bf16[2,128,256]{2,1,0:T(8,128)(2,1)S(1)}, bf16[2,128,256]{2,1,0:T(8,128)(2,1)S(1)}, u32[]{:S(2)}, u32[]{:S(2)}) collective-permute-start(bf16[2,128,256]{2,1,0:T(8,128)(2,1)S(1)} %shard_map.91.refs_5_.refs_0_), channel_id=1, source_target_pairs={{0,3},{1,2},{2,1},{3,0},{4,7},{5,6},{6,5},{7,4},{8,11},{9,10},{10,... | collective-permute-start | bytes 393224 | tf_op jit(solution)/shard_map/ppermute | solution.py:536
  33.7 1.1 %collective-permute-start.9 = (bf16[2,128,256]{2,1,0:T(8,128)(2,1)S(1)}, bf16[2,128,256]{2,1,0:T(8,128)(2,1)S(1)}, u32[]{:S(2)}, u32[]{:S(2)}) collective-permute-start(bf16[2,128,256]{2,1,0:T(8,128)(2,1)S(1)} %shard_map.91.refs_5_.refs_0_), channel_id=1, source_target_pairs={{0,2},{1,3},{2,0},{3,1},{4,6},{5,7},{6,4},{7,5},{8,10},{9,11},{10,... | collective-permute-start | bytes 393224 | tf_op jit(solution)/shard_map/ppermute | solution.py:536
  34.8 0.5 %collective-permute-start.8 = (bf16[2,128,256]{2,1,0:T(8,128)(2,1)S(1)}, bf16[2,128,256]{2,1,0:T(8,128)(2,1)S(1)}, u32[]{:S(2)}, u32[]{:S(2)}) collective-permute-start(bf16[2,128,256]{2,1,0:T(8,128)(2,1)S(1)} %shard_map.91.refs_5_.refs_0_), channel_id=1, source_target_pairs={{0,1},{1,0},{2,3},{3,2},{4,5},{5,4},{6,7},{7,6},{8,9},{9,8},{10,11... | collective-permute-start | bytes 393224 | tf_op jit(solution)/shard_map/ppermute | solution.py:536
  35.3 2.2 %shard_map.92.refs_5_.refs_6_.refs_3_ = f32[16,128,256]{2,1,0:T(8,128)S(1)} custom-call(s32[8,16]{1,0:T(8,128)S(1)} %bitcast.24, bf16[129,128,128]{2,1,0:T(8,128)(2,1)S(1)} %get-tuple-element.42.refs_3_.refs_5_.refs_1_.refs_6_, bf16[2048,256]{1,0:T(8,128)(2,1)S(1)} %get-tuple-element.28.refs_2_.refs_3_.refs_7_, ...), custom_call_target="tpu_custom_call" | custom-call | tf_op jit(solution)/shard_map/pallas_call | solution.py:29
  37.5 1.2 %collective-permute-done.10.refs_3_ = bf16[2,128,256]{2,1,0:T(8,128)(2,1)S(1)} collective-permute-done((bf16[2,128,256]{2,1,0:T(8,128)(2,1)S(1)}, bf16[2,128,256]{2,1,0:T(8,128)(2,1)S(1)}, u32[]{:S(2)}, u32[]{:S(2)}) %collective-permute-start.10) | collective-permute-done | bytes 131104 | tf_op jit(solution)/shard_map/ppermute | solution.py:536
  38.7 1.2 %collective-permute-done.9.refs_2_ = bf16[2,128,256]{2,1,0:T(8,128)(2,1)S(1)} collective-permute-done((bf16[2,128,256]{2,1,0:T(8,128)(2,1)S(1)}, bf16[2,128,256]{2,1,0:T(8,128)(2,1)S(1)}, u32[]{:S(2)}, u32[]{:S(2)}) %collective-permute-start.9) | collective-permute-done | bytes 131104 | tf_op jit(solution)/shard_map/ppermute | solution.py:536
  40.0 0.1 collective-permute-start.13
  40.1 1.3 %shard_map.93.refs_2_ = f32[256,2048]{1,0:T(8,128)S(1)} custom-call(bf16[256,256]{1,0:T(8,128)(2,1)S(1)} %bitcast.18, bf16[256,256]{1,0:T(8,128)(2,1)S(1)} %bitcast.23, bf16[256,256]{1,0:T(8,128)(2,1)S(1)} %bitcast.22, bf16[256,256]{1,0:T(8,128)(2,1)S(1)} %bitcast.21, bf16[8,256,2048]{2,1,0:T(8,128)(2,1)S(1)} %get-tuple-element.41.refs_2_.refs_4_.refs_6_.refs_5_, ...), custom_call_target="tpu_custom_call" | custom-call | tf_op jit(solution)/shard_map/pallas_call | solution.py:29
  41.4 0.9 %collective-permute-done.13.refs_4_ = bf16[1536,256]{1,0:T(8,128)(2,1)S(1)} collective-permute-done((bf16[1536,256]{1,0:T(8,128)(2,1)S(1)}, bf16[1536,256]{1,0:T(8,128)(2,1)S(1)}, u32[]{:S(2)}, u32[]{:S(2)}) %collective-permute-start.13) | collective-permute-done | bytes 786464 | tf_op jit(solution)/shard_map/ppermute | solution.py:547
  42.4 3.7 %shard_map.95 = bf16[16,128,256]{2,1,0:T(8,128)(2,1)} custom-call(s32[16]{0:T(128)S(1)} %bitcast.28, s32[8,16]{1,0:T(8,128)S(1)} %bitcast.25, f32[256,2048]{1,0:T(8,128)S(1)} %shard_map.93.refs_2_, f32[16,128,256]{2,1,0:T(8,128)S(1)} %shard_map.92.refs_5_.refs_6_.refs_3_, bf16[1536,256]{1,0:T(8,128)(2,1)S(1)} %collective-permute-done.13.refs_4_, ...), custom_call_target="tpu_custom_call" | custom-call | tf_op jit(solution)/shard_map/pallas_call | solution.py:29
  (18 shorter events, 0.2 us)
Async XLA Ops:
  0.0 4.5 %collective-permute-start.1 = (bf16[16,128,256]{2,1,0:T(8,128)(2,1)}, bf16[16,128,256]{2,1,0:T(8,128)(2,1)S(1)}, u32[]{:S(2)}, u32[]{:S(2)}) collective-permute-start(bf16[16,128,256]{2,1,0:T(8,128)(2,1)} %bitcast.32), channel_id=1, source_target_pairs={{0,16},{16,0},{1,17},{17,1},{2,18},{18,2},{3,19},{19,3},{4,20},{20... | collective-permute-start | bytes 3145736 | tf_op jit(solution)/shard_map/ppermute | solution.py:414
  0.5 4.0 %collective-permute-start.2 = (f32[3,16,128]{2,1,0:T(8,128)}, f32[3,16,128]{2,1,0:T(8,128)S(1)}, u32[]{:S(2)}, u32[]{:S(2)}) collective-permute-start(f32[3,16,128]{2,1,0:T(8,128)} %bitcast.34), channel_id=1, source_target_pairs={{0,16},{16,0},{1,17},{17,1},{2,18},{18,2},{3,19},{19,3},{4,20},{20... | collective-permute-start | bytes 73736 | tf_op jit(solution)/shard_map/ppermute | solution.py:411
  0.5 3.9 %collective-permute-start = (s32[16]{0:T(128)}, s32[16]{0:T(128)S(1)}, u32[]{:S(2)}, u32[]{:S(2)}) collective-permute-start(s32[16]{0:T(128)} %bitcast.26), channel_id=1, source_target_pairs={{0,16},{16,0},{1,17},{17,1},{2,18},{18,2},{3,19},{19,3},{4,20},{20... | collective-permute-start | bytes 200 | tf_op jit(solution)/shard_map/ppermute | solution.py:413
  6.3 7.7 %collective-permute-start.3 = (bf16[2,128,256]{2,1,0:T(8,128)(2,1)S(1)}, bf16[2,128,256]{2,1,0:T(8,128)(2,1)S(1)}, u32[]{:S(2)}, u32[]{:S(2)}) collective-permute-start(bf16[2,128,256]{2,1,0:T(8,128)(2,1)S(1)} %bitcast.29), channel_id=1, source_target_pairs={{0,3},{1,2},{2,1},{3,0},{4,7},{5,6},{6,5},{7,4},{8,11},{9,10},{10,... | collective-permute-start | bytes 393224 | tf_op jit(solution)/shard_map/ppermute | solution.py:438
  13.1 5.7 %collective-permute-start.4 = (bf16[2,128,256]{2,1,0:T(8,128)(2,1)S(1)}, bf16[2,128,256]{2,1,0:T(8,128)(2,1)S(1)}, u32[]{:S(2)}, u32[]{:S(2)}) collective-permute-start(bf16[2,128,256]{2,1,0:T(8,128)(2,1)S(1)} %bitcast.30), channel_id=1, source_target_pairs={{0,1},{1,0},{2,3},{3,2},{4,5},{5,4},{6,7},{7,6},{8,9},{9,8},{10,11... | collective-permute-start | bytes 393224 | tf_op jit(solution)/shard_map/ppermute | solution.py:438
  13.7 5.3 %collective-permute-start.5 = (bf16[2,128,256]{2,1,0:T(8,128)(2,1)S(1)}, bf16[2,128,256]{2,1,0:T(8,128)(2,1)S(1)}, u32[]{:S(2)}, u32[]{:S(2)}) collective-permute-start(bf16[2,128,256]{2,1,0:T(8,128)(2,1)S(1)} %bitcast.20), channel_id=1, source_target_pairs={{0,2},{1,3},{2,0},{3,1},{4,6},{5,7},{6,4},{7,5},{8,10},{9,11},{10,... | collective-permute-start | bytes 393224 | tf_op jit(solution)/shard_map/ppermute | solution.py:438
  19.1 5.0 %collective-permute-start.6 = (bf16[2,128,256]{2,1,0:T(8,128)(2,1)S(1)}, bf16[2,128,256]{2,1,0:T(8,128)(2,1)S(1)}, u32[]{:S(2)}, u32[]{:S(2)}) collective-permute-start(bf16[2,128,256]{2,1,0:T(8,128)(2,1)S(1)} %get-tuple-element.40), channel_id=1, source_target_pairs={{0,4},{1,5},{2,6},{3,7},{4,0},{5,1},{6,2},{7,3},{8,12},{9,13},{10,... | collective-permute-start | bytes 393224 | tf_op jit(solution)/shard_map/ppermute | solution.py:529
  23.0 8.6 %copy-start.1 = (bf16[256,256]{1,0:T(8,128)(2,1)S(1)}, bf16[256,256]{1,0:T(8,128)(2,1)}, u32[]{:S(2)}) copy-start(bf16[256,256]{1,0:T(8,128)(2,1)} %refs_3_.1) | copy-start | bytes 393220
  24.2 11.1 %copy-start = (bf16[256,256]{1,0:T(8,128)(2,1)S(1)}, bf16[256,256]{1,0:T(8,128)(2,1)}, u32[]{:S(2)}) copy-start(bf16[256,256]{1,0:T(8,128)(2,1)} %refs_11_.1) | copy-start | bytes 393220
  24.2 11.1 %copy-start.2 = (s32[1,16,8]{1,2,0:T(8,128)S(1)}, s32[1,16,8]{1,2,0:T(8,128)}, u32[]{:S(2)}) copy-start(s32[1,16,8]{1,2,0:T(8,128)} %param.11) | copy-start | bytes 1540
  24.2 7.3 %collective-permute-start.7 = (bf16[2,128,256]{2,1,0:T(8,128)(2,1)S(1)}, bf16[2,128,256]{2,1,0:T(8,128)(2,1)S(1)}, u32[]{:S(2)}, u32[]{:S(2)}) collective-permute-start(bf16[2,128,256]{2,1,0:T(8,128)(2,1)S(1)} %get-tuple-element.44), channel_id=1, source_target_pairs={{0,8},{1,9},{2,10},{3,11},{4,12},{5,13},{6,14},{7,15},{8,0},{9,1},... | collective-permute-start | bytes 393224 | tf_op jit(solution)/shard_map/ppermute | solution.py:532
  26.9 10.6 %collective-permute-start.11 = (bf16[2,128,256]{2,1,0:T(8,128)(2,1)S(1)}, bf16[2,128,256]{2,1,0:T(8,128)(2,1)S(1)}, u32[]{:S(2)}, u32[]{:S(2)}) collective-permute-start(bf16[2,128,256]{2,1,0:T(8,128)(2,1)S(1)} %get-tuple-element.45), channel_id=1, source_target_pairs={{16,17},{17,18},{18,19},{19,20},{20,21},{21,22},{22,23},{23,24},{2... | collective-permute-start | bytes 393224 | tf_op jit(solution)/shard_map/ppermute | solution.py:521
  27.5 10.0 %collective-permute-start.12 = (bf16[2,128,256]{2,1,0:T(8,128)(2,1)S(1)}, bf16[2,128,256]{2,1,0:T(8,128)(2,1)S(1)}, u32[]{:S(2)}, u32[]{:S(2)}) collective-permute-start(bf16[2,128,256]{2,1,0:T(8,128)(2,1)S(1)} %get-tuple-element.46), channel_id=1, source_target_pairs={{17,16},{18,17},{19,18},{20,19},{21,20},{22,21},{23,22},{24,23},{2... | collective-permute-start | bytes 393224 | tf_op jit(solution)/shard_map/ppermute | solution.py:521
  31.8 7.0 %collective-permute-start.10 = (bf16[2,128,256]{2,1,0:T(8,128)(2,1)S(1)}, bf16[2,128,256]{2,1,0:T(8,128)(2,1)S(1)}, u32[]{:S(2)}, u32[]{:S(2)}) collective-permute-start(bf16[2,128,256]{2,1,0:T(8,128)(2,1)S(1)} %shard_map.91.refs_5_.refs_0_), channel_id=1, source_target_pairs={{0,3},{1,2},{2,1},{3,0},{4,7},{5,6},{6,5},{7,4},{8,11},{9,10},{10,... | collective-permute-start | bytes 393224 | tf_op jit(solution)/shard_map/ppermute | solution.py:536
  33.7 6.3 %collective-permute-start.9 = (bf16[2,128,256]{2,1,0:T(8,128)(2,1)S(1)}, bf16[2,128,256]{2,1,0:T(8,128)(2,1)S(1)}, u32[]{:S(2)}, u32[]{:S(2)}) collective-permute-start(bf16[2,128,256]{2,1,0:T(8,128)(2,1)S(1)} %shard_map.91.refs_5_.refs_0_), channel_id=1, source_target_pairs={{0,2},{1,3},{2,0},{3,1},{4,6},{5,7},{6,4},{7,5},{8,10},{9,11},{10,... | collective-permute-start | bytes 393224 | tf_op jit(solution)/shard_map/ppermute | solution.py:536
  34.8 5.2 %collective-permute-start.8 = (bf16[2,128,256]{2,1,0:T(8,128)(2,1)S(1)}, bf16[2,128,256]{2,1,0:T(8,128)(2,1)S(1)}, u32[]{:S(2)}, u32[]{:S(2)}) collective-permute-start(bf16[2,128,256]{2,1,0:T(8,128)(2,1)S(1)} %shard_map.91.refs_5_.refs_0_), channel_id=1, source_target_pairs={{0,1},{1,0},{2,3},{3,2},{4,5},{5,4},{6,7},{7,6},{8,9},{9,8},{10,11... | collective-permute-start | bytes 393224 | tf_op jit(solution)/shard_map/ppermute | solution.py:536
  37.5 4.9 %copy-start.3 = (s32[1,16]{1,0:T(1,128)S(1)}, s32[1,16]{1,0:T(1,128)}, u32[]{:S(2)}) copy-start(s32[1,16]{1,0:T(1,128)} %param.12) | copy-start | bytes 196
  40.0 2.4 %collective-permute-start.13 = (bf16[1536,256]{1,0:T(8,128)(2,1)S(1)}, bf16[1536,256]{1,0:T(8,128)(2,1)S(1)}, u32[]{:S(2)}, u32[]{:S(2)}) collective-permute-start(bf16[1536,256]{1,0:T(8,128)(2,1)S(1)} %shard_map.94), channel_id=1, source_target_pairs={{0,16},{16,0},{1,17},{17,1},{2,18},{18,2},{3,19},{19,3},{4,20},{20... | collective-permute-start | bytes 2359304 | tf_op jit(solution)/shard_map/ppermute | solution.py:547

commit v8 on v7

--- a/solution.py
+++ b/solution.py
@@ -202,9 +202,9 @@
         finish(copies)
 
 
-def fill_found(codes_ref, found_ref):
+def fill_found(codes_ref, found_ref, wanted):
     pairs, cells = codes_ref.shape
-    for cell in range(cells):
+    for cell in wanted:
         for code in range(9):
             found_ref[9 * cell + code] = cells * pairs
         for pair in range(pairs):
@@ -233,7 +233,7 @@
 def short_kernel(lines, codes_ref, radial_ref, *refs):
     line_refs, (w_ref, message_ref, found_ref) = refs[:lines], refs[lines:]
     cells, slots, channels = message_ref.shape
-    fill_found(codes_ref, found_ref)
+    fill_found(codes_ref, found_ref, range(cells))
     carried = None
     for start in range(2, cells, 2):
         taken = [line_ref[(start - 1) * slots : (start + 1) * slots, :] for line_ref in line_refs]
@@ -250,7 +250,7 @@
 def fill_ends(slots, codes_ref, radial_ref, line_refs, outer, handed_ref, base, w_ref, found_ref, ends_ref):
     slab, slabs = lax.axis_index("grp"), lax.axis_size("grp")
     cells = codes_ref.shape[1]
-    fill_found(codes_ref, found_ref)
+    fill_found(codes_ref, found_ref, (0, 1, cells - 2, cells - 1))
     for side, start in enumerate((0, cells)):
         taken = []
         for line, line_ref in enumerate(line_refs):
@@ -330,32 +330,59 @@
     return whole
 
 
-def near_kernel(blocks, *refs):
-    energies, (table_ref, out_ref, turned_ref) = refs[:blocks], refs[blocks:]
-    for place, energy in enumerate(energies):
-        turned_ref[place] = energy[...].astype(F32).T.astype(BF16)
+def near_kernel(own, others, *refs):
+    refs = list(refs)
+    energies = [refs.pop(0) for _ in own]
+    handed_ref = refs.pop(0) if others else None
+    start_ref = refs.pop(0) if others else None
+    table_ref, out_ref, turned_ref = refs
+    rows = table_ref.shape[1]
+    places = [*own, *others]
+    for index in range(len(places)):
+        if index < len(own):
+            energy = energies[index][...]
+        else:
+            first = (index - len(own)) * rows
+            energy = handed_ref[first : first + rows, :]
+        turned_ref[index] = energy.astype(F32).T.astype(BF16)
     atoms = out_ref.shape[1]
     tile = math.gcd(atoms, 512)
     for start in range(0, atoms, tile):
-        total = None
-        for place in range(blocks):
-            part = jnp.dot(turned_ref[place], table_ref[place, :, start : start + tile], preferred_element_type=F32)
+        span = slice(start, start + tile)
+        total = start_ref[:, span] if others else None
+        for index, place in enumerate(places):
+            part = jnp.dot(turned_ref[index], table_ref[place, :, span], preferred_element_type=F32)
             total = part if total is None else total + part
-        out_ref[:, start : start + tile] = total
-
-
-def final_kernel(blocks, lines, scale, counts_ref, codes_ref, near_ref, message_ref, handed_ref, table_ref, *refs):
+        out_ref[:, span] = total
+
+
+def near_call(own, others, energies, table, handed=(), start=(), held=()):
+    rows, atoms = table.shape[1:]
+    channels = energies[0].shape[-1]
+    (total,) = call(
+        functools.partial(near_kernel, own, others),
+        [(VMEM, ((channels, atoms), F32))],
+        in_vmem([*[energy.reshape(rows, channels) for energy in energies], *handed, *start, table]),
+        [pltpu.VMEM((len(own) + len(others), channels, rows), BF16)],
+        held,
+    )
+    return total
+
+
+def final_kernel(
+    places, base, lines, scale, counts_ref, codes_ref, near_ref, message_ref, handed_ref, ends_from_ref, table_ref, *refs
+):
     radial_ref, line_refs, outer, w_ref = refs[0], refs[1 : 1 + lines], refs[1 + lines : 3 + lines], refs[3 + lines]
     out_ref, turned_ref, result_ref, found_ref, ends_ref, semaphores = refs[4 + lines :]
     masked_ref = line_refs[0]
     cells, slots, channels = out_ref.shape
     rows = table_ref.shape[1]
-    for place in range(blocks):
-        turned_ref[place] = handed_ref[place * rows : (place + 1) * rows, :].astype(F32).T.astype(BF16)
+    for index in range(len(places)):
+        turned_ref[index] = handed_ref[index * rows : (index + 1) * rows, :].astype(F32).T.astype(BF16)
     ends_ref[:2] = message_ref[:2]
     ends_ref[2:] = message_ref[cells - 2 :]
     fill_ends(
-        slots, codes_ref, radial_ref, line_refs, outer, handed_ref, blocks * rows, w_ref, found_ref, ends_ref
+        slots, codes_ref, radial_ref, line_refs, outer, ends_from_ref, base, w_ref, found_ref, ends_ref
     )
     slot_ids = lax.broadcasted_iota(jnp.int32, (slots, channels), 0)
     group = math.gcd(cells, 2)
@@ -364,8 +391,8 @@
     for first in range(0, cells, group):
         span = slice(first * slots, (first + group) * slots)
         total = near_ref[:, span]
-        for place in range(blocks):
-            total = total + jnp.dot(turned_ref[place], table_ref[blocks + place, :, span], preferred_element_type=F32)
+        for index, place in enumerate(places):
+            total = total + jnp.dot(turned_ref[index], table_ref[place, :, span], preferred_element_type=F32)
         for cell in range(first, first + group):
             value = total[:, (cell - first) * slots : (cell - first + 1) * slots].T * scale
             value += ends_ref[cell] if cell < 2 else ends_ref[cell - cells + 4] if cell >= cells - 2 else message_ref[cell]
@@ -378,15 +405,16 @@
     finish(leaving)
 
 
-def final_call(counts, codes, near, message, handed, table, radial, lines, outer, w_msg, scale):
-    blocks, rows = table.shape[0] // 2, table.shape[1]
+def final_call(
+    places, base, counts, codes, near, message, handed, ends_from, table, radial, lines, outer, w_msg, scale
+):
     cells, slots, channels = message.shape
     (result,) = call(
-        functools.partial(final_kernel, blocks, len(lines), scale),
+        functools.partial(final_kernel, places, base, len(lines), scale),
         [(HBM, (message.shape, BF16))],
-        [(SMEM, counts), (SMEM, codes)] + in_vmem([near, message, handed, table, radial, *lines, *outer, w_msg]),
+        [(SMEM, counts), (SMEM, codes)] + in_vmem([near, message, handed, ends_from, table, radial, *lines, *outer, w_msg]),
         [
-            pltpu.VMEM((blocks, channels, rows), BF16),
+            pltpu.VMEM((len(places), channels, table.shape[1]), BF16),
             pltpu.VMEM(message.shape, BF16),
             pltpu.SMEM((9 * cells,), jnp.int32),
             pltpu.VMEM((4, slots, channels), F32),
@@ -420,7 +448,7 @@
         sibling_counts = jnp.where(even, near[1][0], near[0][0])
         sibling_features = jnp.where(even, near[1][1], near[0][1])
 
-    blocks = 4 if dev_count % 4 == 0 else 2
+    blocks = 4
     digits = [("grp", 1, 2), ("dev", 1, blocks)]
     twos = [("dev", blocks << bit) for bit in range((dev_count // blocks).bit_length() - 1)]
     twos += [("grp", 2 << bit) for bit in range((slabs // 2).bit_length() - 1)]
@@ -544,17 +572,19 @@
         [pltpu.SMEM((9 * cells,), jnp.int32)],
         [energy, tables],
     )
-    handed = lax.ppermute(stacked([*energies, *(outer if slabs == 2 else [])], [message]), "grp", swap)
-    energies = [part.reshape(2 * block, channels) for part in energies]
-    (near_sum,) = call(
-        functools.partial(near_kernel, blocks),
-        [(VMEM, ((channels, atoms), F32))],
-        in_vmem([*energies, tables]),
-        [pltpu.VMEM((blocks, channels, 2 * block), BF16)],
-        [message],
+    soon, late = [0], list(range(1, blocks))
+    soon_energies, late_energies = [energies[place] for place in soon], [energies[place] for place in late]
+    handed = lax.ppermute(stacked([*soon_energies, *(outer if slabs == 2 else [])], [message]), "grp", swap)
+    near_sum = near_call(soon, [], soon_energies, tables, held=[message])
+    handed_late = lax.ppermute(stacked(late_energies, [near_sum]), "grp", swap)
+    near_sum = near_call(
+        late, [blocks + place for place in soon], late_energies, tables, [handed], [near_sum]
     )
     scale = 8.0 / math.sqrt(wave_count)
-    result = final_call(counts, codes, near_sum, message, handed, tables, radial, lines, outer, w_msg, scale)
+    result = final_call(
+        [blocks + place for place in late], len(soon) * 2 * block, counts, codes, near_sum, message, handed_late, handed,
+        tables, radial, lines, outer, w_msg, scale,
+    )
     return result[None]
 
 

time: 46.5 us -> 45.4 us (0.976)
  waiting for transfers between devices: 9.51 us -> 8.37 us
    ppermute x3, waiting for transfers between devices: 2.45 us -> 1.84 us  [body(): lax.ppermute(energy, 'dev', pairs_at('dev', 1, place))]
    ppermute x1 -> x2, waiting for transfers between devices: 0.94 us -> 0.36 us  [the longest x1 0.36 us: body(): handed_late = lax.ppermute(stacked(late_energies, [near_sum]), 'grp', swap)]
    pallas_call x14 -> x16, Pallas kernels: 21.9 us -> 22 us  [call(): pl.pallas_call(without_held, in_specs=[place for place, _ in operands], o...]
  transfers between devices with their start and end apart: 14 -> 15, of which waited for: 8 -> 8; matrix products, arithmetic and copies ran while one was open for 0% -> 0% of each run, Pallas kernels for 35% -> 37%
where the time goes in v8:
time: 45.4 us; the launch traced here: 45.2 us
  Pallas kernels  22 us (48%)
  starting transfers between devices  14.5 us (32%)
  waiting for transfers between devices  8.37 us (18%)
    pallas_call x16, Pallas kernels, call(): pl.pallas_call(without_held, in_specs=[place for place, _ in operands], o...  22 us
    ppermute x3, starting transfers between devices, sent(): lax.ppermute(part.reshape(2, block, channels), 'dev', pairs_at('dev', 1,...  4.17 us
    ppermute x3, starting transfers between devices, body(): lax.ppermute(energy, 'dev', pairs_at('dev', 1, place))  3.55 us
    ppermute x1, waiting for transfers between devices, body(): pieces = [total, lax.ppermute(half_total, axis, pairs_at(axis, stride, 1))]  3.34 us
    ppermute x1, starting transfers between devices, body(): pieces = [total, lax.ppermute(half_total, axis, pairs_at(axis, stride, 1))]  2.66 us
    ppermute x3, waiting for transfers between devices, body(): lax.ppermute(energy, 'dev', pairs_at('dev', 1, place))  1.84 us
    ppermute x1, starting transfers between devices, body(): lax.ppermute(half_total, axis, pairs_at(axis, stride, 1))  1.64 us
    ppermute x3, waiting for transfers between devices, sent(): lax.ppermute(part.reshape(2, block, channels), 'dev', pairs_at('dev', 1,...  1.64 us
  transfers between devices with their start and end apart: 15, of which 8 were waited for; matrix products, arithmetic and copies ran while one was open for 0% of the time, Pallas kernels for 37%

profile of v8, /device:TPU:0, one launch (start us, length us, event | category | flops | bytes accessed | tf_op | source)
XLA Modules:
  0.0 45.2 jit_solution(6660419528434725558)
XLA Ops:
  0.0 0.5 %collective-permute-start.1 = (bf16[16,128,256]{2,1,0:T(8,128)(2,1)}, bf16[16,128,256]{2,1,0:T(8,128)(2,1)S(1)}, u32[]{:S(2)}, u32[]{:S(2)}) collective-permute-start(bf16[16,128,256]{2,1,0:T(8,128)(2,1)} %bitcast.32), channel_id=1, source_target_pairs={{0,16},{16,0},{1,17},{17,1},{2,18},{18,2},{3,19},{19,3},{4,20},{20... | collective-permute-start | bytes 3145736 | tf_op jit(solution)/shard_map/ppermute | solution.py:442
  0.5 0.5 %collective-permute-start = (s32[16]{0:T(128)}, s32[16]{0:T(128)S(1)}, u32[]{:S(2)}, u32[]{:S(2)}) collective-permute-start(s32[16]{0:T(128)} %bitcast.26), channel_id=1, source_target_pairs={{0,16},{16,0},{1,17},{17,1},{2,18},{18,2},{3,19},{19,3},{4,20},{20... | collective-permute-start | bytes 200 | tf_op jit(solution)/shard_map/ppermute | solution.py:441
  1.0 3.5 %shard_map.82 = (bf16[2048,256]{1,0:T(8,128)(2,1)S(1)}, bf16[32,2048]{1,0:T(8,128)(2,1)S(1)}, bf16[1024,32]{1,0:T(8,128)(2,1)S(1)}, bf16[8,256,2048]{2,1,0:T(8,1...) custom-call(s32[3,1024]{1,0:T(4,128)} %refs_0_.1, f32[3,16,128]{2,1,0:T(8,128)} %bitcast.35, s32[16]{0:T(128)} %bitcast.27, ...), custom_call_target="tpu_custom_call" | custom-call | tf_op jit(solution)/shard_map/pallas_call | solution.py:29
  4.5 1.9 %shard_map.83 = (bf16[2048,256]{1,0:T(8,128)(2,1)S(1)}, bf16[32,2048]{1,0:T(8,128)(2,1)S(1)}, bf16[256,256]{1,0:T(8,128)(2,1)S(1)}) custom-call(s32[16]{0:T(128)S(1)} %collective-permute-done.refs_0_, bf16[16,128,256]{2,1,0:T(8,128)(2,1)S(1)} %collective-permute-done.1.refs_1_, f32[3,16,128]{2,1,0:T(8,128)S(1)} %collective-permute-done.2.refs_2_, ...), custom_call_target="tpu_custom_call" | custom-call | tf_op jit(solution)/shard_map/pallas_call | solution.py:29
  6.3 3.5 %collective-permute-start.3 = (bf16[2,128,256]{2,1,0:T(8,128)(2,1)S(1)}, bf16[2,128,256]{2,1,0:T(8,128)(2,1)S(1)}, u32[]{:S(2)}, u32[]{:S(2)}) collective-permute-start(bf16[2,128,256]{2,1,0:T(8,128)(2,1)S(1)} %bitcast.29), channel_id=1, source_target_pairs={{0,3},{1,2},{2,1},{3,0},{4,7},{5,6},{6,5},{7,4},{8,11},{9,10},{10,... | collective-permute-start | bytes 393224 | tf_op jit(solution)/shard_map/ppermute | solution.py:466
  9.9 1.1 %shard_map.84.refs_6_ = bf16[256,256]{1,0:T(8,128)(2,1)S(1)} custom-call(bf16[1024,32]{1,0:T(8,128)(2,1)S(1)} %get-tuple-element.26.refs_3_.refs_0_.refs_2_, bf16[32,2048]{1,0:T(8,128)(2,1)S(1)} %get-tuple-element.30.refs_1_.refs_3_, bf16[2048,256]{1,0:T(8,128)(2,1)S(1)} %get-tuple-element.31.refs_2_.refs_4_.refs_3_.refs_9_, ...), custom_call_target="tpu_custom_call" | custom-call | tf_op jit(solution)/shard_map/pallas_call | solution.py:29
  11.0 2.1 %shard_map.85 = (bf16[8,256,2048]{2,1,0:T(8,128)(2,1)S(1)}, bf16[256,256]{1,0:T(8,128)(2,1)S(1)}) custom-call(bf16[1024,32]{1,0:T(8,128)(2,1)S(1)} %get-tuple-element.26.refs_3_.refs_0_.refs_2_, bf16[32,2048]{1,0:T(8,128)(2,1)S(1)} %get-tuple-element.27.refs_1_, ...), custom_call_target="tpu_custom_call", output_to_operand_aliasing={{0}: (5, {})} | custom-call | tf_op jit(solution)/shard_map/pallas_call | solution.py:29
  13.1 0.6 %collective-permute-start.4 = (bf16[2,128,256]{2,1,0:T(8,128)(2,1)S(1)}, bf16[2,128,256]{2,1,0:T(8,128)(2,1)S(1)}, u32[]{:S(2)}, u32[]{:S(2)}) collective-permute-start(bf16[2,128,256]{2,1,0:T(8,128)(2,1)S(1)} %bitcast.30), channel_id=1, source_target_pairs={{0,1},{1,0},{2,3},{3,2},{4,5},{5,4},{6,7},{7,6},{8,9},{9,8},{10,11... | collective-permute-start | bytes 393224 | tf_op jit(solution)/shard_map/ppermute | solution.py:466
  13.7 0.3 collective-permute-done.3.refs_6_.refs_3_
  14.0 2.1 %shard_map.86 = (bf16[8,256,2048]{2,1,0:T(8,128)(2,1)S(1)}, f32[256,256]{1,0:T(8,128)S(1)}) custom-call(bf16[1024,32]{1,0:T(8,128)(2,1)S(1)} %get-tuple-element.26.refs_3_.refs_0_.refs_2_, bf16[32,2048]{1,0:T(8,128)(2,1)S(1)} %get-tuple-element.27.refs_1_, ...), custom_call_target="tpu_custom_call", output_to_operand_aliasing={{0}: (5, {})} | custom-call | tf_op jit(solution)/shard_map/pallas_call | solution.py:29
  16.1 1.5 %shard_map.87.refs_4_.refs_2_ = bf16[8,256,2048]{2,1,0:T(8,128)(2,1)S(1)} custom-call(bf16[1024,32]{1,0:T(8,128)(2,1)S(1)} %get-tuple-element.26.refs_3_.refs_0_.refs_2_, bf16[32,2048]{1,0:T(8,128)(2,1)S(1)} %get-tuple-element.27.refs_1_, bf16[8,256,2048]{2,1,0:T(8,128)(2,1)S(1)} %get-tuple-element.38.refs_2_, ...), custom_call_target="tpu_custom_call", output_to_operand_aliasing={{}: (2, {})} | custom-call | tf_op jit(solution)/shard_map/pallas_call | solution.py:29
  17.7 1.1 %collective-permute-done.4.refs_1_ = bf16[2,128,256]{2,1,0:T(8,128)(2,1)S(1)} collective-permute-done((bf16[2,128,256]{2,1,0:T(8,128)(2,1)S(1)}, bf16[2,128,256]{2,1,0:T(8,128)(2,1)S(1)}, u32[]{:S(2)}, u32[]{:S(2)}) %collective-permute-start.4) | collective-permute-done | bytes 131104 | tf_op jit(solution)/shard_map/ppermute | solution.py:466
  18.8 0.3 collective-permute-done.5.refs_2_
  19.1 1.6 %collective-permute-start.6 = (bf16[2,128,256]{2,1,0:T(8,128)(2,1)S(1)}, bf16[2,128,256]{2,1,0:T(8,128)(2,1)S(1)}, u32[]{:S(2)}, u32[]{:S(2)}) collective-permute-start(bf16[2,128,256]{2,1,0:T(8,128)(2,1)S(1)} %get-tuple-element.40), channel_id=1, source_target_pairs={{0,4},{1,5},{2,6},{3,7},{4,0},{5,1},{6,2},{7,3},{8,12},{9,13},{10,... | collective-permute-start | bytes 393224 | tf_op jit(solution)/shard_map/ppermute | solution.py:557
  20.7 2.2 %shard_map.89 = (bf16[8,256,2048]{2,1,0:T(8,128)(2,1)S(1)}, bf16[2,128,256]{2,1,0:T(8,128)(2,1)S(1)}, bf16[2,128,256]{2,1,0:T(8,128)(2,1)S(1)}, bf16[129,128,128]{2,1,0:T(8,128)(2,1)S(1)}) custom-call(bf16[1024,32]{1,0:T(8,128)(2,1)S(1)} %get-tuple-element.26.refs_3_.refs_0_.refs_2_, ...), custom_call_target="tpu_custom_call", output_to_operand_aliasing={{0}: (2, {})} | custom-call | tf_op jit(solution)/shard_map/pallas_call | solution.py:29
  23.0 1.2 %collective-permute-done.6.refs_1_ = bf16[2,128,256]{2,1,0:T(8,128)(2,1)S(1)} collective-permute-done((bf16[2,128,256]{2,1,0:T(8,128)(2,1)S(1)}, bf16[2,128,256]{2,1,0:T(8,128)(2,1)S(1)}, u32[]{:S(2)}, u32[]{:S(2)}) %collective-permute-start.6) | collective-permute-done | bytes 131104 | tf_op jit(solution)/shard_map/ppermute | solution.py:557
  24.2 2.7 %collective-permute-start.7 = (bf16[2,128,256]{2,1,0:T(8,128)(2,1)S(1)}, bf16[2,128,256]{2,1,0:T(8,128)(2,1)S(1)}, u32[]{:S(2)}, u32[]{:S(2)}) collective-permute-start(bf16[2,128,256]{2,1,0:T(8,128)(2,1)S(1)} %get-tuple-element.44), channel_id=1, source_target_pairs={{0,8},{1,9},{2,10},{3,11},{4,12},{5,13},{6,14},{7,15},{8,0},{9,1},... | collective-permute-start | bytes 393224 | tf_op jit(solution)/shard_map/ppermute | solution.py:560
  26.8 0.7 %collective-permute-start.11 = (bf16[2,128,256]{2,1,0:T(8,128)(2,1)S(1)}, bf16[2,128,256]{2,1,0:T(8,128)(2,1)S(1)}, u32[]{:S(2)}, u32[]{:S(2)}) collective-permute-start(bf16[2,128,256]{2,1,0:T(8,128)(2,1)S(1)} %get-tuple-element.45), channel_id=1, source_target_pairs={{16,17},{17,18},{18,19},{19,20},{20,21},{21,22},{22,23},{23,24},{2... | collective-permute-start | bytes 393224 | tf_op jit(solution)/shard_map/ppermute | solution.py:549
  27.5 0.7 %collective-permute-start.12 = (bf16[2,128,256]{2,1,0:T(8,128)(2,1)S(1)}, bf16[2,128,256]{2,1,0:T(8,128)(2,1)S(1)}, u32[]{:S(2)}, u32[]{:S(2)}) collective-permute-start(bf16[2,128,256]{2,1,0:T(8,128)(2,1)S(1)} %get-tuple-element.46), channel_id=1, source_target_pairs={{17,16},{18,17},{19,18},{20,19},{21,20},{22,21},{23,22},{24,23},{2... | collective-permute-start | bytes 393224 | tf_op jit(solution)/shard_map/ppermute | solution.py:549
  28.2 3.3 %collective-permute-done.7.refs_1_ = bf16[2,128,256]{2,1,0:T(8,128)(2,1)S(1)} collective-permute-done((bf16[2,128,256]{2,1,0:T(8,128)(2,1)S(1)}, bf16[2,128,256]{2,1,0:T(8,128)(2,1)S(1)}, u32[]{:S(2)}, u32[]{:S(2)}) %collective-permute-start.7) | collective-permute-done | bytes 131104 | tf_op jit(solution)/shard_map/ppermute | solution.py:560
  31.5 0.2 shard_map.91.refs_5_.refs_0_
  31.7 2.1 %collective-permute-start.10 = (bf16[2,128,256]{2,1,0:T(8,128)(2,1)S(1)}, bf16[2,128,256]{2,1,0:T(8,128)(2,1)S(1)}, u32[]{:S(2)}, u32[]{:S(2)}) collective-permute-start(bf16[2,128,256]{2,1,0:T(8,128)(2,1)S(1)} %shard_map.91.refs_5_.refs_0_), channel_id=1, source_target_pairs={{0,3},{1,2},{2,1},{3,0},{4,7},{5,6},{6,5},{7,4},{8,11},{9,10},{10,... | collective-permute-start | bytes 393224 | tf_op jit(solution)/shard_map/ppermute | solution.py:564
  33.9 0.9 %collective-permute-start.9 = (bf16[2,128,256]{2,1,0:T(8,128)(2,1)S(1)}, bf16[2,128,256]{2,1,0:T(8,128)(2,1)S(1)}, u32[]{:S(2)}, u32[]{:S(2)}) collective-permute-start(bf16[2,128,256]{2,1,0:T(8,128)(2,1)S(1)} %shard_map.91.refs_5_.refs_0_), channel_id=1, source_target_pairs={{0,2},{1,3},{2,0},{3,1},{4,6},{5,7},{6,4},{7,5},{8,10},{9,11},{10,... | collective-permute-start | bytes 393224 | tf_op jit(solution)/shard_map/ppermute | solution.py:564
  34.8 0.5 %collective-permute-start.8 = (bf16[2,128,256]{2,1,0:T(8,128)(2,1)S(1)}, bf16[2,128,256]{2,1,0:T(8,128)(2,1)S(1)}, u32[]{:S(2)}, u32[]{:S(2)}) collective-permute-start(bf16[2,128,256]{2,1,0:T(8,128)(2,1)S(1)} %shard_map.91.refs_5_.refs_0_), channel_id=1, source_target_pairs={{0,1},{1,0},{2,3},{3,2},{4,5},{5,4},{6,7},{7,6},{8,9},{9,8},{10,11... | collective-permute-start | bytes 393224 | tf_op jit(solution)/shard_map/ppermute | solution.py:564
  35.3 2.1 %shard_map.92.refs_3_.refs_2_ = f32[16,128,256]{2,1,0:T(8,128)S(1)} custom-call(s32[8,16]{1,0:T(8,128)S(1)} %bitcast.24, bf16[129,128,128]{2,1,0:T(8,128)(2,1)S(1)} %get-tuple-element.42.refs_3_.refs_5_.refs_1_.refs_7_, bf16[2048,256]{1,0:T(8,128)(2,1)S(1)} %get-tuple-element.28.refs_2_.refs_3_.refs_8_, ...), custom_call_target="tpu_custom_call" | custom-call | tf_op jit(solution)/shard_map/pallas_call | solution.py:29
  37.5 0.1 collective-permute-start.13
  37.6 0.5 %shard_map.94.refs_4_.refs_3_ = f32[256,2048]{1,0:T(8,128)S(1)} custom-call(bf16[256,256]{1,0:T(8,128)(2,1)S(1)} %bitcast.18, bf16[8,256,2048]{2,1,0:T(8,128)(2,1)S(1)} %get-tuple-element.41.refs_2_.refs_4_.refs_6_.refs_1_.refs_5_, f32[16,128,256]{2,1,0:T(8,128)S(1)} %shard_map.92.refs_3_.refs_2_), custom_call_target="tpu_custom_call" | custom-call | tf_op jit(solution)/shard_map/pallas_call | solution.py:29
  38.1 0.6 %collective-permute-done.10.refs_2_ = bf16[2,128,256]{2,1,0:T(8,128)(2,1)S(1)} collective-permute-done((bf16[2,128,256]{2,1,0:T(8,128)(2,1)S(1)}, bf16[2,128,256]{2,1,0:T(8,128)(2,1)S(1)}, u32[]{:S(2)}, u32[]{:S(2)}) %collective-permute-start.10) | collective-permute-done | bytes 131104 | tf_op jit(solution)/shard_map/ppermute | solution.py:564
  38.7 1.2 %collective-permute-done.9.refs_1_ = bf16[2,128,256]{2,1,0:T(8,128)(2,1)S(1)} collective-permute-done((bf16[2,128,256]{2,1,0:T(8,128)(2,1)S(1)}, bf16[2,128,256]{2,1,0:T(8,128)(2,1)S(1)}, u32[]{:S(2)}, u32[]{:S(2)}) %collective-permute-start.9) | collective-permute-done | bytes 131104 | tf_op jit(solution)/shard_map/ppermute | solution.py:564
  40.0 1.3 %shard_map.95.refs_2_ = f32[256,2048]{1,0:T(8,128)S(1)} custom-call(bf16[256,256]{1,0:T(8,128)(2,1)S(1)} %bitcast.23, bf16[256,256]{1,0:T(8,128)(2,1)S(1)} %bitcast.22, bf16[256,256]{1,0:T(8,128)(2,1)S(1)} %bitcast.21, bf16[768,256]{1,0:T(8,128)(2,1)S(1)} %collective-permute-done.13.refs_3_.refs_5_, f32[256,2048]{1,0:T(8,128)S(1)} %shard_map.94.refs_4_.refs_3_, ...), custom_call_target="tpu_custom_call" | custom-call | tf_op jit(solution)/shard_map/pallas_call | solution.py:29
  41.4 0.4 collective-permute-done.14.refs_4_
  41.7 3.3 %shard_map.97 = bf16[16,128,256]{2,1,0:T(8,128)(2,1)} custom-call(s32[16]{0:T(128)S(1)} %bitcast.28, s32[8,16]{1,0:T(8,128)S(1)} %bitcast.25, f32[256,2048]{1,0:T(8,128)S(1)} %shard_map.95.refs_2_, f32[16,128,256]{2,1,0:T(8,128)S(1)} %shard_map.92.refs_3_.refs_2_, bf16[768,256]{1,0:T(8,128)(2,1)S(1)} %collective-permute-done.14.refs_4_, ...), custom_call_target="tpu_custom_call" | custom-call | tf_op jit(solution)/shard_map/pallas_call | solution.py:29
  (22 shorter events, 0.4 us)
Async XLA Ops:
  0.0 4.5 %collective-permute-start.1 = (bf16[16,128,256]{2,1,0:T(8,128)(2,1)}, bf16[16,128,256]{2,1,0:T(8,128)(2,1)S(1)}, u32[]{:S(2)}, u32[]{:S(2)}) collective-permute-start(bf16[16,128,256]{2,1,0:T(8,128)(2,1)} %bitcast.32), channel_id=1, source_target_pairs={{0,16},{16,0},{1,17},{17,1},{2,18},{18,2},{3,19},{19,3},{4,20},{20... | collective-permute-start | bytes 3145736 | tf_op jit(solution)/shard_map/ppermute | solution.py:442
  0.5 4.0 %collective-permute-start.2 = (f32[3,16,128]{2,1,0:T(8,128)}, f32[3,16,128]{2,1,0:T(8,128)S(1)}, u32[]{:S(2)}, u32[]{:S(2)}) collective-permute-start(f32[3,16,128]{2,1,0:T(8,128)} %bitcast.34), channel_id=1, source_target_pairs={{0,16},{16,0},{1,17},{17,1},{2,18},{18,2},{3,19},{19,3},{4,20},{20... | collective-permute-start | bytes 73736 | tf_op jit(solution)/shard_map/ppermute | solution.py:439
  0.5 3.9 %collective-permute-start = (s32[16]{0:T(128)}, s32[16]{0:T(128)S(1)}, u32[]{:S(2)}, u32[]{:S(2)}) collective-permute-start(s32[16]{0:T(128)} %bitcast.26), channel_id=1, source_target_pairs={{0,16},{16,0},{1,17},{17,1},{2,18},{18,2},{3,19},{19,3},{4,20},{20... | collective-permute-start | bytes 200 | tf_op jit(solution)/shard_map/ppermute | solution.py:441
  6.3 7.7 %collective-permute-start.3 = (bf16[2,128,256]{2,1,0:T(8,128)(2,1)S(1)}, bf16[2,128,256]{2,1,0:T(8,128)(2,1)S(1)}, u32[]{:S(2)}, u32[]{:S(2)}) collective-permute-start(bf16[2,128,256]{2,1,0:T(8,128)(2,1)S(1)} %bitcast.29), channel_id=1, source_target_pairs={{0,3},{1,2},{2,1},{3,0},{4,7},{5,6},{6,5},{7,4},{8,11},{9,10},{10,... | collective-permute-start | bytes 393224 | tf_op jit(solution)/shard_map/ppermute | solution.py:466
  13.1 5.7 %collective-permute-start.4 = (bf16[2,128,256]{2,1,0:T(8,128)(2,1)S(1)}, bf16[2,128,256]{2,1,0:T(8,128)(2,1)S(1)}, u32[]{:S(2)}, u32[]{:S(2)}) collective-permute-start(bf16[2,128,256]{2,1,0:T(8,128)(2,1)S(1)} %bitcast.30), channel_id=1, source_target_pairs={{0,1},{1,0},{2,3},{3,2},{4,5},{5,4},{6,7},{7,6},{8,9},{9,8},{10,11... | collective-permute-start | bytes 393224 | tf_op jit(solution)/shard_map/ppermute | solution.py:466
  13.7 5.3 %collective-permute-start.5 = (bf16[2,128,256]{2,1,0:T(8,128)(2,1)S(1)}, bf16[2,128,256]{2,1,0:T(8,128)(2,1)S(1)}, u32[]{:S(2)}, u32[]{:S(2)}) collective-permute-start(bf16[2,128,256]{2,1,0:T(8,128)(2,1)S(1)} %bitcast.20), channel_id=1, source_target_pairs={{0,2},{1,3},{2,0},{3,1},{4,6},{5,7},{6,4},{7,5},{8,10},{9,11},{10,... | collective-permute-start | bytes 393224 | tf_op jit(solution)/shard_map/ppermute | solution.py:466
  19.1 5.0 %collective-permute-start.6 = (bf16[2,128,256]{2,1,0:T(8,128)(2,1)S(1)}, bf16[2,128,256]{2,1,0:T(8,128)(2,1)S(1)}, u32[]{:S(2)}, u32[]{:S(2)}) collective-permute-start(bf16[2,128,256]{2,1,0:T(8,128)(2,1)S(1)} %get-tuple-element.40), channel_id=1, source_target_pairs={{0,4},{1,5},{2,6},{3,7},{4,0},{5,1},{6,2},{7,3},{8,12},{9,13},{10,... | collective-permute-start | bytes 393224 | tf_op jit(solution)/shard_map/ppermute | solution.py:557
  22.9 8.6 %copy-start.1 = (bf16[256,256]{1,0:T(8,128)(2,1)S(1)}, bf16[256,256]{1,0:T(8,128)(2,1)}, u32[]{:S(2)}) copy-start(bf16[256,256]{1,0:T(8,128)(2,1)} %refs_3_.1) | copy-start | bytes 393220
  24.2 11.1 %copy-start = (bf16[256,256]{1,0:T(8,128)(2,1)S(1)}, bf16[256,256]{1,0:T(8,128)(2,1)}, u32[]{:S(2)}) copy-start(bf16[256,256]{1,0:T(8,128)(2,1)} %refs_12_.1) | copy-start | bytes 393220
  24.2 11.1 %copy-start.2 = (s32[1,16,8]{1,2,0:T(8,128)S(1)}, s32[1,16,8]{1,2,0:T(8,128)}, u32[]{:S(2)}) copy-start(s32[1,16,8]{1,2,0:T(8,128)} %param.11) | copy-start | bytes 1540
  24.2 7.3 %collective-permute-start.7 = (bf16[2,128,256]{2,1,0:T(8,128)(2,1)S(1)}, bf16[2,128,256]{2,1,0:T(8,128)(2,1)S(1)}, u32[]{:S(2)}, u32[]{:S(2)}) collective-permute-start(bf16[2,128,256]{2,1,0:T(8,128)(2,1)S(1)} %get-tuple-element.44), channel_id=1, source_target_pairs={{0,8},{1,9},{2,10},{3,11},{4,12},{5,13},{6,14},{7,15},{8,0},{9,1},... | collective-permute-start | bytes 393224 | tf_op jit(solution)/shard_map/ppermute | solution.py:560
  26.8 10.6 %collective-permute-start.11 = (bf16[2,128,256]{2,1,0:T(8,128)(2,1)S(1)}, bf16[2,128,256]{2,1,0:T(8,128)(2,1)S(1)}, u32[]{:S(2)}, u32[]{:S(2)}) collective-permute-start(bf16[2,128,256]{2,1,0:T(8,128)(2,1)S(1)} %get-tuple-element.45), channel_id=1, source_target_pairs={{16,17},{17,18},{18,19},{19,20},{20,21},{21,22},{22,23},{23,24},{2... | collective-permute-start | bytes 393224 | tf_op jit(solution)/shard_map/ppermute | solution.py:549
  27.5 9.9 %collective-permute-start.12 = (bf16[2,128,256]{2,1,0:T(8,128)(2,1)S(1)}, bf16[2,128,256]{2,1,0:T(8,128)(2,1)S(1)}, u32[]{:S(2)}, u32[]{:S(2)}) collective-permute-start(bf16[2,128,256]{2,1,0:T(8,128)(2,1)S(1)} %get-tuple-element.46), channel_id=1, source_target_pairs={{17,16},{18,17},{19,18},{20,19},{21,20},{22,21},{23,22},{24,23},{2... | collective-permute-start | bytes 393224 | tf_op jit(solution)/shard_map/ppermute | solution.py:549
  31.7 7.0 %collective-permute-start.10 = (bf16[2,128,256]{2,1,0:T(8,128)(2,1)S(1)}, bf16[2,128,256]{2,1,0:T(8,128)(2,1)S(1)}, u32[]{:S(2)}, u32[]{:S(2)}) collective-permute-start(bf16[2,128,256]{2,1,0:T(8,128)(2,1)S(1)} %shard_map.91.refs_5_.refs_0_), channel_id=1, source_target_pairs={{0,3},{1,2},{2,1},{3,0},{4,7},{5,6},{6,5},{7,4},{8,11},{9,10},{10,... | collective-permute-start | bytes 393224 | tf_op jit(solution)/shard_map/ppermute | solution.py:564
  33.9 6.1 %collective-permute-start.9 = (bf16[2,128,256]{2,1,0:T(8,128)(2,1)S(1)}, bf16[2,128,256]{2,1,0:T(8,128)(2,1)S(1)}, u32[]{:S(2)}, u32[]{:S(2)}) collective-permute-start(bf16[2,128,256]{2,1,0:T(8,128)(2,1)S(1)} %shard_map.91.refs_5_.refs_0_), channel_id=1, source_target_pairs={{0,2},{1,3},{2,0},{3,1},{4,6},{5,7},{6,4},{7,5},{8,10},{9,11},{10,... | collective-permute-start | bytes 393224 | tf_op jit(solution)/shard_map/ppermute | solution.py:564
  34.8 5.2 %collective-permute-start.8 = (bf16[2,128,256]{2,1,0:T(8,128)(2,1)S(1)}, bf16[2,128,256]{2,1,0:T(8,128)(2,1)S(1)}, u32[]{:S(2)}, u32[]{:S(2)}) collective-permute-start(bf16[2,128,256]{2,1,0:T(8,128)(2,1)S(1)} %shard_map.91.refs_5_.refs_0_), channel_id=1, source_target_pairs={{0,1},{1,0},{2,3},{3,2},{4,5},{5,4},{6,7},{7,6},{8,9},{9,8},{10,11... | collective-permute-start | bytes 393224 | tf_op jit(solution)/shard_map/ppermute | solution.py:564
  37.5 2.5 %collective-permute-start.13 = (bf16[768,256]{1,0:T(8,128)(2,1)S(1)}, bf16[768,256]{1,0:T(8,128)(2,1)S(1)}, u32[]{:S(2)}, u32[]{:S(2)}) collective-permute-start(bf16[768,256]{1,0:T(8,128)(2,1)S(1)} %shard_map.93), channel_id=1, source_target_pairs={{0,16},{16,0},{1,17},{17,1},{2,18},{18,2},{3,19},{19,3},{4,20},{20... | collective-permute-start | bytes 1179656 | tf_op jit(solution)/shard_map/ppermute | solution.py:577
  38.1 3.7 %copy-start.3 = (s32[1,16]{1,0:T(1,128)S(1)}, s32[1,16]{1,0:T(1,128)}, u32[]{:S(2)}) copy-start(s32[1,16]{1,0:T(1,128)} %param.12) | copy-start | bytes 196
  40.0 1.8 %collective-permute-start.14 = (bf16[768,256]{1,0:T(8,128)(2,1)S(1)}, bf16[768,256]{1,0:T(8,128)(2,1)S(1)}, u32[]{:S(2)}, u32[]{:S(2)}) collective-permute-start(bf16[768,256]{1,0:T(8,128)(2,1)S(1)} %shard_map.96), channel_id=1, source_target_pairs={{0,16},{16,0},{1,17},{17,1},{2,18},{18,2},{3,19},{19,3},{4,20},{20... | collective-permute-start | bytes 1179656 | tf_op jit(solution)/shard_map/ppermute | solution.py:579

commit v9 on v8

--- a/solution.py
+++ b/solution.py
@@ -146,11 +146,12 @@
     fill_waves(waves_ref, padded_ref, turned_ref, flips)
     copies[1].wait()
     fill_places(offsets_ref, places_ref, dev * cells, slab, *lengths)
-    copies[2].wait()
-    copies[3].wait()
-    fill_masked(counts_ref, features_ref, masked_ref)
-    for place, sums_ref in zip(early, sums):
+    for index, (place, sums_ref) in enumerate(zip(early, sums)):
         fill_table(turned_ref[place * block : (place + 1) * block, :], places_ref, table_ref.at[place])
+        if index == 0:
+            copies[2].wait()
+            copies[3].wait()
+            fill_masked(counts_ref, features_ref, masked_ref)
         sums_ref[...] = sums_of(table_ref.at[place], masked_ref)
 
 

time: 45.4 us -> 45.4 us (level)
  no operation moved by 1% of the time
where the time goes in v9:
time: 45.4 us; the launch traced here: 45.2 us
  Pallas kernels  21.8 us (48%)
  starting transfers between devices  14.6 us (32%)
  waiting for transfers between devices  8.35 us (18%)
    pallas_call x16, Pallas kernels, call(): pl.pallas_call(without_held, in_specs=[place for place, _ in operands], o...  21.8 us
    ppermute x3, starting transfers between devices, sent(): lax.ppermute(part.reshape(2, block, channels), 'dev', pairs_at('dev', 1,...  4.17 us
    ppermute x3, starting transfers between devices, body(): lax.ppermute(energy, 'dev', pairs_at('dev', 1, place))  3.55 us
    ppermute x1, waiting for transfers between devices, body(): pieces = [total, lax.ppermute(half_total, axis, pairs_at(axis, stride, 1))]  3.34 us
    ppermute x1, starting transfers between devices, body(): pieces = [total, lax.ppermute(half_total, axis, pairs_at(axis, stride, 1))]  2.84 us
    ppermute x3, waiting for transfers between devices, body(): lax.ppermute(energy, 'dev', pairs_at('dev', 1, place))  1.84 us
    ppermute x1, starting transfers between devices, body(): lax.ppermute(half_total, axis, pairs_at(axis, stride, 1))  1.64 us
    ppermute x3, waiting for transfers between devices, sent(): lax.ppermute(part.reshape(2, block, channels), 'dev', pairs_at('dev', 1,...  1.63 us
  transfers between devices with their start and end apart: 15, of which 8 were waited for; matrix products, arithmetic and copies ran while one was open for 0% of the time, Pallas kernels for 37%

profile of v9, /device:TPU:0, one launch (start us, length us, event | category | flops | bytes accessed | tf_op | source)
XLA Modules:
  0.0 45.2 jit_solution(13580914294484544711)
XLA Ops:
  0.0 0.5 %collective-permute-start.1 = (bf16[16,128,256]{2,1,0:T(8,128)(2,1)}, bf16[16,128,256]{2,1,0:T(8,128)(2,1)S(1)}, u32[]{:S(2)}, u32[]{:S(2)}) collective-permute-start(bf16[16,128,256]{2,1,0:T(8,128)(2,1)} %bitcast.32), channel_id=1, source_target_pairs={{0,16},{16,0},{1,17},{17,1},{2,18},{18,2},{3,19},{19,3},{4,20},{20... | collective-permute-start | bytes 3145736 | tf_op jit(solution)/shard_map/ppermute | solution.py:443
  0.5 0.5 %collective-permute-start = (s32[16]{0:T(128)}, s32[16]{0:T(128)S(1)}, u32[]{:S(2)}, u32[]{:S(2)}) collective-permute-start(s32[16]{0:T(128)} %bitcast.26), channel_id=1, source_target_pairs={{0,16},{16,0},{1,17},{17,1},{2,18},{18,2},{3,19},{19,3},{4,20},{20... | collective-permute-start | bytes 200 | tf_op jit(solution)/shard_map/ppermute | solution.py:442
  1.0 3.3 %shard_map.82 = (bf16[2048,256]{1,0:T(8,128)(2,1)S(1)}, bf16[32,2048]{1,0:T(8,128)(2,1)S(1)}, bf16[1024,32]{1,0:T(8,128)(2,1)S(1)}, bf16[8,256,2048]{2,1,0:T(8,1...) custom-call(s32[3,1024]{1,0:T(4,128)} %refs_0_.1, f32[3,16,128]{2,1,0:T(8,128)} %bitcast.35, s32[16]{0:T(128)} %bitcast.27, ...), custom_call_target="tpu_custom_call" | custom-call | tf_op jit(solution)/shard_map/pallas_call | solution.py:29
  4.3 1.9 %shard_map.83 = (bf16[2048,256]{1,0:T(8,128)(2,1)S(1)}, bf16[32,2048]{1,0:T(8,128)(2,1)S(1)}, bf16[256,256]{1,0:T(8,128)(2,1)S(1)}) custom-call(s32[16]{0:T(128)S(1)} %collective-permute-done.refs_0_, bf16[16,128,256]{2,1,0:T(8,128)(2,1)S(1)} %collective-permute-done.1.refs_1_, f32[3,16,128]{2,1,0:T(8,128)S(1)} %collective-permute-done.2.refs_2_, ...), custom_call_target="tpu_custom_call" | custom-call | tf_op jit(solution)/shard_map/pallas_call | solution.py:29
  6.1 3.5 %collective-permute-start.3 = (bf16[2,128,256]{2,1,0:T(8,128)(2,1)S(1)}, bf16[2,128,256]{2,1,0:T(8,128)(2,1)S(1)}, u32[]{:S(2)}, u32[]{:S(2)}) collective-permute-start(bf16[2,128,256]{2,1,0:T(8,128)(2,1)S(1)} %bitcast.29), channel_id=1, source_target_pairs={{0,3},{1,2},{2,1},{3,0},{4,7},{5,6},{6,5},{7,4},{8,11},{9,10},{10,... | collective-permute-start | bytes 393224 | tf_op jit(solution)/shard_map/ppermute | solution.py:467
  9.7 1.1 %shard_map.84.refs_6_ = bf16[256,256]{1,0:T(8,128)(2,1)S(1)} custom-call(bf16[1024,32]{1,0:T(8,128)(2,1)S(1)} %get-tuple-element.26.refs_3_.refs_0_.refs_2_, bf16[32,2048]{1,0:T(8,128)(2,1)S(1)} %get-tuple-element.30.refs_1_.refs_3_, bf16[2048,256]{1,0:T(8,128)(2,1)S(1)} %get-tuple-element.31.refs_2_.refs_4_.refs_3_.refs_9_, ...), custom_call_target="tpu_custom_call" | custom-call | tf_op jit(solution)/shard_map/pallas_call | solution.py:29
  10.8 2.1 %shard_map.85 = (bf16[8,256,2048]{2,1,0:T(8,128)(2,1)S(1)}, bf16[256,256]{1,0:T(8,128)(2,1)S(1)}) custom-call(bf16[1024,32]{1,0:T(8,128)(2,1)S(1)} %get-tuple-element.26.refs_3_.refs_0_.refs_2_, bf16[32,2048]{1,0:T(8,128)(2,1)S(1)} %get-tuple-element.27.refs_1_, ...), custom_call_target="tpu_custom_call", output_to_operand_aliasing={{0}: (5, {})} | custom-call | tf_op jit(solution)/shard_map/pallas_call | solution.py:29
  12.9 0.6 %collective-permute-start.4 = (bf16[2,128,256]{2,1,0:T(8,128)(2,1)S(1)}, bf16[2,128,256]{2,1,0:T(8,128)(2,1)S(1)}, u32[]{:S(2)}, u32[]{:S(2)}) collective-permute-start(bf16[2,128,256]{2,1,0:T(8,128)(2,1)S(1)} %bitcast.30), channel_id=1, source_target_pairs={{0,1},{1,0},{2,3},{3,2},{4,5},{5,4},{6,7},{7,6},{8,9},{9,8},{10,11... | collective-permute-start | bytes 393224 | tf_op jit(solution)/shard_map/ppermute | solution.py:467
  13.5 0.3 collective-permute-done.3.refs_6_.refs_3_
  13.8 2.1 %shard_map.86 = (bf16[8,256,2048]{2,1,0:T(8,128)(2,1)S(1)}, f32[256,256]{1,0:T(8,128)S(1)}) custom-call(bf16[1024,32]{1,0:T(8,128)(2,1)S(1)} %get-tuple-element.26.refs_3_.refs_0_.refs_2_, bf16[32,2048]{1,0:T(8,128)(2,1)S(1)} %get-tuple-element.27.refs_1_, ...), custom_call_target="tpu_custom_call", output_to_operand_aliasing={{0}: (5, {})} | custom-call | tf_op jit(solution)/shard_map/pallas_call | solution.py:29
  15.9 1.5 %shard_map.87.refs_4_.refs_2_ = bf16[8,256,2048]{2,1,0:T(8,128)(2,1)S(1)} custom-call(bf16[1024,32]{1,0:T(8,128)(2,1)S(1)} %get-tuple-element.26.refs_3_.refs_0_.refs_2_, bf16[32,2048]{1,0:T(8,128)(2,1)S(1)} %get-tuple-element.27.refs_1_, bf16[8,256,2048]{2,1,0:T(8,128)(2,1)S(1)} %get-tuple-element.38.refs_2_, ...), custom_call_target="tpu_custom_call", output_to_operand_aliasing={{}: (2, {})} | custom-call | tf_op jit(solution)/shard_map/pallas_call | solution.py:29
  17.5 1.1 %collective-permute-done.4.refs_1_ = bf16[2,128,256]{2,1,0:T(8,128)(2,1)S(1)} collective-permute-done((bf16[2,128,256]{2,1,0:T(8,128)(2,1)S(1)}, bf16[2,128,256]{2,1,0:T(8,128)(2,1)S(1)}, u32[]{:S(2)}, u32[]{:S(2)}) %collective-permute-start.4) | collective-permute-done | bytes 131104 | tf_op jit(solution)/shard_map/ppermute | solution.py:467
  18.6 0.2 collective-permute-done.5.refs_2_
  18.9 1.6 %collective-permute-start.6 = (bf16[2,128,256]{2,1,0:T(8,128)(2,1)S(1)}, bf16[2,128,256]{2,1,0:T(8,128)(2,1)S(1)}, u32[]{:S(2)}, u32[]{:S(2)}) collective-permute-start(bf16[2,128,256]{2,1,0:T(8,128)(2,1)S(1)} %get-tuple-element.40), channel_id=1, source_target_pairs={{0,4},{1,5},{2,6},{3,7},{4,0},{5,1},{6,2},{7,3},{8,12},{9,13},{10,... | collective-permute-start | bytes 393224 | tf_op jit(solution)/shard_map/ppermute | solution.py:558
  20.5 2.2 %shard_map.89 = (bf16[8,256,2048]{2,1,0:T(8,128)(2,1)S(1)}, bf16[2,128,256]{2,1,0:T(8,128)(2,1)S(1)}, bf16[2,128,256]{2,1,0:T(8,128)(2,1)S(1)}, bf16[129,128,128]{2,1,0:T(8,128)(2,1)S(1)}) custom-call(bf16[1024,32]{1,0:T(8,128)(2,1)S(1)} %get-tuple-element.26.refs_3_.refs_0_.refs_2_, ...), custom_call_target="tpu_custom_call", output_to_operand_aliasing={{0}: (2, {})} | custom-call | tf_op jit(solution)/shard_map/pallas_call | solution.py:29
  22.7 1.2 %collective-permute-done.6.refs_1_ = bf16[2,128,256]{2,1,0:T(8,128)(2,1)S(1)} collective-permute-done((bf16[2,128,256]{2,1,0:T(8,128)(2,1)S(1)}, bf16[2,128,256]{2,1,0:T(8,128)(2,1)S(1)}, u32[]{:S(2)}, u32[]{:S(2)}) %collective-permute-start.6) | collective-permute-done | bytes 131104 | tf_op jit(solution)/shard_map/ppermute | solution.py:558
  24.0 2.8 %collective-permute-start.7 = (bf16[2,128,256]{2,1,0:T(8,128)(2,1)S(1)}, bf16[2,128,256]{2,1,0:T(8,128)(2,1)S(1)}, u32[]{:S(2)}, u32[]{:S(2)}) collective-permute-start(bf16[2,128,256]{2,1,0:T(8,128)(2,1)S(1)} %get-tuple-element.44), channel_id=1, source_target_pairs={{0,8},{1,9},{2,10},{3,11},{4,12},{5,13},{6,14},{7,15},{8,0},{9,1},... | collective-permute-start | bytes 393224 | tf_op jit(solution)/shard_map/ppermute | solution.py:561
  26.8 0.7 %collective-permute-start.11 = (bf16[2,128,256]{2,1,0:T(8,128)(2,1)S(1)}, bf16[2,128,256]{2,1,0:T(8,128)(2,1)S(1)}, u32[]{:S(2)}, u32[]{:S(2)}) collective-permute-start(bf16[2,128,256]{2,1,0:T(8,128)(2,1)S(1)} %get-tuple-element.45), channel_id=1, source_target_pairs={{16,17},{17,18},{18,19},{19,20},{20,21},{21,22},{22,23},{23,24},{2... | collective-permute-start | bytes 393224 | tf_op jit(solution)/shard_map/ppermute | solution.py:550
  27.5 0.7 %collective-permute-start.12 = (bf16[2,128,256]{2,1,0:T(8,128)(2,1)S(1)}, bf16[2,128,256]{2,1,0:T(8,128)(2,1)S(1)}, u32[]{:S(2)}, u32[]{:S(2)}) collective-permute-start(bf16[2,128,256]{2,1,0:T(8,128)(2,1)S(1)} %get-tuple-element.46), channel_id=1, source_target_pairs={{17,16},{18,17},{19,18},{20,19},{21,20},{22,21},{23,22},{24,23},{2... | collective-permute-start | bytes 393224 | tf_op jit(solution)/shard_map/ppermute | solution.py:550
  28.2 3.3 %collective-permute-done.7.refs_1_ = bf16[2,128,256]{2,1,0:T(8,128)(2,1)S(1)} collective-permute-done((bf16[2,128,256]{2,1,0:T(8,128)(2,1)S(1)}, bf16[2,128,256]{2,1,0:T(8,128)(2,1)S(1)}, u32[]{:S(2)}, u32[]{:S(2)}) %collective-permute-start.7) | collective-permute-done | bytes 131104 | tf_op jit(solution)/shard_map/ppermute | solution.py:561
  31.5 0.2 shard_map.91.refs_5_.refs_0_
  31.7 2.1 %collective-permute-start.10 = (bf16[2,128,256]{2,1,0:T(8,128)(2,1)S(1)}, bf16[2,128,256]{2,1,0:T(8,128)(2,1)S(1)}, u32[]{:S(2)}, u32[]{:S(2)}) collective-permute-start(bf16[2,128,256]{2,1,0:T(8,128)(2,1)S(1)} %shard_map.91.refs_5_.refs_0_), channel_id=1, source_target_pairs={{0,3},{1,2},{2,1},{3,0},{4,7},{5,6},{6,5},{7,4},{8,11},{9,10},{10,... | collective-permute-start | bytes 393224 | tf_op jit(solution)/shard_map/ppermute | solution.py:565
  33.8 0.9 %collective-permute-start.9 = (bf16[2,128,256]{2,1,0:T(8,128)(2,1)S(1)}, bf16[2,128,256]{2,1,0:T(8,128)(2,1)S(1)}, u32[]{:S(2)}, u32[]{:S(2)}) collective-permute-start(bf16[2,128,256]{2,1,0:T(8,128)(2,1)S(1)} %shard_map.91.refs_5_.refs_0_), channel_id=1, source_target_pairs={{0,2},{1,3},{2,0},{3,1},{4,6},{5,7},{6,4},{7,5},{8,10},{9,11},{10,... | collective-permute-start | bytes 393224 | tf_op jit(solution)/shard_map/ppermute | solution.py:565
  34.7 0.5 %collective-permute-start.8 = (bf16[2,128,256]{2,1,0:T(8,128)(2,1)S(1)}, bf16[2,128,256]{2,1,0:T(8,128)(2,1)S(1)}, u32[]{:S(2)}, u32[]{:S(2)}) collective-permute-start(bf16[2,128,256]{2,1,0:T(8,128)(2,1)S(1)} %shard_map.91.refs_5_.refs_0_), channel_id=1, source_target_pairs={{0,1},{1,0},{2,3},{3,2},{4,5},{5,4},{6,7},{7,6},{8,9},{9,8},{10,11... | collective-permute-start | bytes 393224 | tf_op jit(solution)/shard_map/ppermute | solution.py:565
  35.3 2.1 %shard_map.92.refs_3_.refs_2_ = f32[16,128,256]{2,1,0:T(8,128)S(1)} custom-call(s32[8,16]{1,0:T(8,128)S(1)} %bitcast.24, bf16[129,128,128]{2,1,0:T(8,128)(2,1)S(1)} %get-tuple-element.42.refs_3_.refs_5_.refs_1_.refs_7_, bf16[2048,256]{1,0:T(8,128)(2,1)S(1)} %get-tuple-element.28.refs_2_.refs_3_.refs_8_, ...), custom_call_target="tpu_custom_call" | custom-call | tf_op jit(solution)/shard_map/pallas_call | solution.py:29
  37.6 0.5 %shard_map.94.refs_4_.refs_3_ = f32[256,2048]{1,0:T(8,128)S(1)} custom-call(bf16[256,256]{1,0:T(8,128)(2,1)S(1)} %bitcast.18, bf16[8,256,2048]{2,1,0:T(8,128)(2,1)S(1)} %get-tuple-element.41.refs_2_.refs_4_.refs_6_.refs_1_.refs_5_, f32[16,128,256]{2,1,0:T(8,128)S(1)} %shard_map.92.refs_3_.refs_2_), custom_call_target="tpu_custom_call" | custom-call | tf_op jit(solution)/shard_map/pallas_call | solution.py:29
  38.0 0.6 %collective-permute-done.10.refs_2_ = bf16[2,128,256]{2,1,0:T(8,128)(2,1)S(1)} collective-permute-done((bf16[2,128,256]{2,1,0:T(8,128)(2,1)S(1)}, bf16[2,128,256]{2,1,0:T(8,128)(2,1)S(1)}, u32[]{:S(2)}, u32[]{:S(2)}) %collective-permute-start.10) | collective-permute-done | bytes 131104 | tf_op jit(solution)/shard_map/ppermute | solution.py:565
  38.7 1.2 %collective-permute-done.9.refs_1_ = bf16[2,128,256]{2,1,0:T(8,128)(2,1)S(1)} collective-permute-done((bf16[2,128,256]{2,1,0:T(8,128)(2,1)S(1)}, bf16[2,128,256]{2,1,0:T(8,128)(2,1)S(1)}, u32[]{:S(2)}, u32[]{:S(2)}) %collective-permute-start.9) | collective-permute-done | bytes 131104 | tf_op jit(solution)/shard_map/ppermute | solution.py:565
  39.9 0.1 collective-permute-start.14
  40.0 1.3 %shard_map.95.refs_2_ = f32[256,2048]{1,0:T(8,128)S(1)} custom-call(bf16[256,256]{1,0:T(8,128)(2,1)S(1)} %bitcast.23, bf16[256,256]{1,0:T(8,128)(2,1)S(1)} %bitcast.22, bf16[256,256]{1,0:T(8,128)(2,1)S(1)} %bitcast.21, bf16[768,256]{1,0:T(8,128)(2,1)S(1)} %collective-permute-done.13.refs_3_.refs_5_, f32[256,2048]{1,0:T(8,128)S(1)} %shard_map.94.refs_4_.refs_3_, ...), custom_call_target="tpu_custom_call" | custom-call | tf_op jit(solution)/shard_map/pallas_call | solution.py:29
  41.4 0.3 collective-permute-done.14.refs_4_
  41.7 3.3 %shard_map.97 = bf16[16,128,256]{2,1,0:T(8,128)(2,1)} custom-call(s32[16]{0:T(128)S(1)} %bitcast.28, s32[8,16]{1,0:T(8,128)S(1)} %bitcast.25, f32[256,2048]{1,0:T(8,128)S(1)} %shard_map.95.refs_2_, f32[16,128,256]{2,1,0:T(8,128)S(1)} %shard_map.92.refs_3_.refs_2_, bf16[768,256]{1,0:T(8,128)(2,1)S(1)} %collective-permute-done.14.refs_4_, ...), custom_call_target="tpu_custom_call" | custom-call | tf_op jit(solution)/shard_map/pallas_call | solution.py:29
  (22 shorter events, 0.4 us)
Async XLA Ops:
  0.0 4.3 %collective-permute-start.1 = (bf16[16,128,256]{2,1,0:T(8,128)(2,1)}, bf16[16,128,256]{2,1,0:T(8,128)(2,1)S(1)}, u32[]{:S(2)}, u32[]{:S(2)}) collective-permute-start(bf16[16,128,256]{2,1,0:T(8,128)(2,1)} %bitcast.32), channel_id=1, source_target_pairs={{0,16},{16,0},{1,17},{17,1},{2,18},{18,2},{3,19},{19,3},{4,20},{20... | collective-permute-start | bytes 3145736 | tf_op jit(solution)/shard_map/ppermute | solution.py:443
  0.5 3.8 %collective-permute-start.2 = (f32[3,16,128]{2,1,0:T(8,128)}, f32[3,16,128]{2,1,0:T(8,128)S(1)}, u32[]{:S(2)}, u32[]{:S(2)}) collective-permute-start(f32[3,16,128]{2,1,0:T(8,128)} %bitcast.34), channel_id=1, source_target_pairs={{0,16},{16,0},{1,17},{17,1},{2,18},{18,2},{3,19},{19,3},{4,20},{20... | collective-permute-start | bytes 73736 | tf_op jit(solution)/shard_map/ppermute | solution.py:440
  0.5 3.7 %collective-permute-start = (s32[16]{0:T(128)}, s32[16]{0:T(128)S(1)}, u32[]{:S(2)}, u32[]{:S(2)}) collective-permute-start(s32[16]{0:T(128)} %bitcast.26), channel_id=1, source_target_pairs={{0,16},{16,0},{1,17},{17,1},{2,18},{18,2},{3,19},{19,3},{4,20},{20... | collective-permute-start | bytes 200 | tf_op jit(solution)/shard_map/ppermute | solution.py:442
  6.1 7.7 %collective-permute-start.3 = (bf16[2,128,256]{2,1,0:T(8,128)(2,1)S(1)}, bf16[2,128,256]{2,1,0:T(8,128)(2,1)S(1)}, u32[]{:S(2)}, u32[]{:S(2)}) collective-permute-start(bf16[2,128,256]{2,1,0:T(8,128)(2,1)S(1)} %bitcast.29), channel_id=1, source_target_pairs={{0,3},{1,2},{2,1},{3,0},{4,7},{5,6},{6,5},{7,4},{8,11},{9,10},{10,... | collective-permute-start | bytes 393224 | tf_op jit(solution)/shard_map/ppermute | solution.py:467
  12.9 5.7 %collective-permute-start.4 = (bf16[2,128,256]{2,1,0:T(8,128)(2,1)S(1)}, bf16[2,128,256]{2,1,0:T(8,128)(2,1)S(1)}, u32[]{:S(2)}, u32[]{:S(2)}) collective-permute-start(bf16[2,128,256]{2,1,0:T(8,128)(2,1)S(1)} %bitcast.30), channel_id=1, source_target_pairs={{0,1},{1,0},{2,3},{3,2},{4,5},{5,4},{6,7},{7,6},{8,9},{9,8},{10,11... | collective-permute-start | bytes 393224 | tf_op jit(solution)/shard_map/ppermute | solution.py:467
  13.5 5.3 %collective-permute-start.5 = (bf16[2,128,256]{2,1,0:T(8,128)(2,1)S(1)}, bf16[2,128,256]{2,1,0:T(8,128)(2,1)S(1)}, u32[]{:S(2)}, u32[]{:S(2)}) collective-permute-start(bf16[2,128,256]{2,1,0:T(8,128)(2,1)S(1)} %bitcast.20), channel_id=1, source_target_pairs={{0,2},{1,3},{2,0},{3,1},{4,6},{5,7},{6,4},{7,5},{8,10},{9,11},{10,... | collective-permute-start | bytes 393224 | tf_op jit(solution)/shard_map/ppermute | solution.py:467
  18.9 5.0 %collective-permute-start.6 = (bf16[2,128,256]{2,1,0:T(8,128)(2,1)S(1)}, bf16[2,128,256]{2,1,0:T(8,128)(2,1)S(1)}, u32[]{:S(2)}, u32[]{:S(2)}) collective-permute-start(bf16[2,128,256]{2,1,0:T(8,128)(2,1)S(1)} %get-tuple-element.40), channel_id=1, source_target_pairs={{0,4},{1,5},{2,6},{3,7},{4,0},{5,1},{6,2},{7,3},{8,12},{9,13},{10,... | collective-permute-start | bytes 393224 | tf_op jit(solution)/shard_map/ppermute | solution.py:558
  22.7 8.8 %copy-start.1 = (bf16[256,256]{1,0:T(8,128)(2,1)S(1)}, bf16[256,256]{1,0:T(8,128)(2,1)}, u32[]{:S(2)}) copy-start(bf16[256,256]{1,0:T(8,128)(2,1)} %refs_3_.1) | copy-start | bytes 393220
  24.0 11.3 %copy-start = (bf16[256,256]{1,0:T(8,128)(2,1)S(1)}, bf16[256,256]{1,0:T(8,128)(2,1)}, u32[]{:S(2)}) copy-start(bf16[256,256]{1,0:T(8,128)(2,1)} %refs_12_.1) | copy-start | bytes 393220
  24.0 11.3 %copy-start.2 = (s32[1,16,8]{1,2,0:T(8,128)S(1)}, s32[1,16,8]{1,2,0:T(8,128)}, u32[]{:S(2)}) copy-start(s32[1,16,8]{1,2,0:T(8,128)} %param.11) | copy-start | bytes 1540
  24.0 7.5 %collective-permute-start.7 = (bf16[2,128,256]{2,1,0:T(8,128)(2,1)S(1)}, bf16[2,128,256]{2,1,0:T(8,128)(2,1)S(1)}, u32[]{:S(2)}, u32[]{:S(2)}) collective-permute-start(bf16[2,128,256]{2,1,0:T(8,128)(2,1)S(1)} %get-tuple-element.44), channel_id=1, source_target_pairs={{0,8},{1,9},{2,10},{3,11},{4,12},{5,13},{6,14},{7,15},{8,0},{9,1},... | collective-permute-start | bytes 393224 | tf_op jit(solution)/shard_map/ppermute | solution.py:561
  26.8 10.6 %collective-permute-start.11 = (bf16[2,128,256]{2,1,0:T(8,128)(2,1)S(1)}, bf16[2,128,256]{2,1,0:T(8,128)(2,1)S(1)}, u32[]{:S(2)}, u32[]{:S(2)}) collective-permute-start(bf16[2,128,256]{2,1,0:T(8,128)(2,1)S(1)} %get-tuple-element.45), channel_id=1, source_target_pairs={{16,17},{17,18},{18,19},{19,20},{20,21},{21,22},{22,23},{23,24},{2... | collective-permute-start | bytes 393224 | tf_op jit(solution)/shard_map/ppermute | solution.py:550
  27.5 9.9 %collective-permute-start.12 = (bf16[2,128,256]{2,1,0:T(8,128)(2,1)S(1)}, bf16[2,128,256]{2,1,0:T(8,128)(2,1)S(1)}, u32[]{:S(2)}, u32[]{:S(2)}) collective-permute-start(bf16[2,128,256]{2,1,0:T(8,128)(2,1)S(1)} %get-tuple-element.46), channel_id=1, source_target_pairs={{17,16},{18,17},{19,18},{20,19},{21,20},{22,21},{23,22},{24,23},{2... | collective-permute-start | bytes 393224 | tf_op jit(solution)/shard_map/ppermute | solution.py:550
  31.7 7.0 %collective-permute-start.10 = (bf16[2,128,256]{2,1,0:T(8,128)(2,1)S(1)}, bf16[2,128,256]{2,1,0:T(8,128)(2,1)S(1)}, u32[]{:S(2)}, u32[]{:S(2)}) collective-permute-start(bf16[2,128,256]{2,1,0:T(8,128)(2,1)S(1)} %shard_map.91.refs_5_.refs_0_), channel_id=1, source_target_pairs={{0,3},{1,2},{2,1},{3,0},{4,7},{5,6},{6,5},{7,4},{8,11},{9,10},{10,... | collective-permute-start | bytes 393224 | tf_op jit(solution)/shard_map/ppermute | solution.py:565
  33.8 6.1 %collective-permute-start.9 = (bf16[2,128,256]{2,1,0:T(8,128)(2,1)S(1)}, bf16[2,128,256]{2,1,0:T(8,128)(2,1)S(1)}, u32[]{:S(2)}, u32[]{:S(2)}) collective-permute-start(bf16[2,128,256]{2,1,0:T(8,128)(2,1)S(1)} %shard_map.91.refs_5_.refs_0_), channel_id=1, source_target_pairs={{0,2},{1,3},{2,0},{3,1},{4,6},{5,7},{6,4},{7,5},{8,10},{9,11},{10,... | collective-permute-start | bytes 393224 | tf_op jit(solution)/shard_map/ppermute | solution.py:565
  34.7 5.2 %collective-permute-start.8 = (bf16[2,128,256]{2,1,0:T(8,128)(2,1)S(1)}, bf16[2,128,256]{2,1,0:T(8,128)(2,1)S(1)}, u32[]{:S(2)}, u32[]{:S(2)}) collective-permute-start(bf16[2,128,256]{2,1,0:T(8,128)(2,1)S(1)} %shard_map.91.refs_5_.refs_0_), channel_id=1, source_target_pairs={{0,1},{1,0},{2,3},{3,2},{4,5},{5,4},{6,7},{7,6},{8,9},{9,8},{10,11... | collective-permute-start | bytes 393224 | tf_op jit(solution)/shard_map/ppermute | solution.py:565
  37.5 2.5 %collective-permute-start.13 = (bf16[768,256]{1,0:T(8,128)(2,1)S(1)}, bf16[768,256]{1,0:T(8,128)(2,1)S(1)}, u32[]{:S(2)}, u32[]{:S(2)}) collective-permute-start(bf16[768,256]{1,0:T(8,128)(2,1)S(1)} %shard_map.93), channel_id=1, source_target_pairs={{0,16},{16,0},{1,17},{17,1},{2,18},{18,2},{3,19},{19,3},{4,20},{20... | collective-permute-start | bytes 1179656 | tf_op jit(solution)/shard_map/ppermute | solution.py:578
  38.0 3.7 %copy-start.3 = (s32[1,16]{1,0:T(1,128)S(1)}, s32[1,16]{1,0:T(1,128)}, u32[]{:S(2)}) copy-start(s32[1,16]{1,0:T(1,128)} %param.12) | copy-start | bytes 196
  39.9 1.8 %collective-permute-start.14 = (bf16[768,256]{1,0:T(8,128)(2,1)S(1)}, bf16[768,256]{1,0:T(8,128)(2,1)S(1)}, u32[]{:S(2)}, u32[]{:S(2)}) collective-permute-start(bf16[768,256]{1,0:T(8,128)(2,1)S(1)} %shard_map.96), channel_id=1, source_target_pairs={{0,16},{16,0},{1,17},{17,1},{2,18},{18,2},{3,19},{19,3},{4,20},{20... | collective-permute-start | bytes 1179656 | tf_op jit(solution)/shard_map/ppermute | solution.py:580
